TPU v7x, 32 devices: a whole 2x2x4 slice. The times are simulated.
32 devices in a mesh: row: 4 (over z), col: 8 (over y, x, core).
Axes of the slice: x: 2, y: 2, z: 4, core: 2. Of those that a mesh axis runs over, the one named last changes fastest.
Arguments:
- new_keys: bfloat16 [256, 28672], P('col', 'row'), may hold values from -6 to 6
- precision: bfloat16 [28672, 28672], P('row', 'col'), may hold values from -0.03125 to 0.03125
- stored_keys: bfloat16 [8, 256, 28672], P('row', None, 'col'), may hold values from -0.03125 to 0.03125
- pair_batch: int32 [4, 6], replicated, may hold values from 0 to 7, as said below
- pair_count: int32 [4], replicated, may hold values from 2 to 6, as said below
- batch_length: int32 [8], replicated, may hold values from 64 to 256
- batch_slot: int32 [8], replicated, may hold values from 0 to 7, each once
Outputs:
- whitened: bfloat16 [256, 28672], P('row', 'col')
- intersections: float32 [4, 6, 64, 256], P('row', None, 'col')
Inputs may be any that keep to these rules, and one draw needn't show every extreme that they name: `pair_batch`: the ids in one block's row are distinct; ids at places at or beyond the block's count are ignored. `pair_count`: some block lists exactly 6 batches. `batch_slot`: every store slot belongs to exactly one batch.
All inputs are finite; a program needn't handle non-finite values.
Results may differ from a plain program's by a relative error of at most 0.0029.
Values may be sent and summed in bfloat16 or wider, within the bound.
No kernel may reach another device: no remote copies, remote signals or barrier semaphores. Data moves between devices by JAX's collectives and lax.ppermute only.
A program may use at most 128 MiB of HBM per device.

v0:
```python
import jax
import jax.numpy as jnp
from jax import lax
from jax.sharding import PartitionSpec as P


def against_store(rows, stored_keys):
    return jnp.einsum("kd,qjd->qkj", rows, stored_keys, preferred_element_type=jnp.float32)


def select_pairs(table, slots, lengths, count):
    picked = jnp.take(table, slots, axis=0)
    places = jnp.arange(slots.shape[0], dtype=jnp.int32)
    columns = jnp.arange(table.shape[-1], dtype=jnp.int32)
    keep = (places < count)[:, None, None] & (columns[None, None, :] < lengths[:, None, None])
    return jnp.where(keep, picked, jnp.zeros_like(picked))


def shards(new_keys, precision, stored_keys, pair_batch, pair_count, batch_length, batch_slot):
    row_count = lax.axis_size("row")
    col_count = lax.axis_size("col")
    row_index = lax.axis_index("row")
    total_keys = new_keys.shape[0] * col_count
    block_keys = total_keys // row_count
    partial_value = jnp.dot(
        lax.all_gather(new_keys, "col", axis=0, tiled=True),
        precision,
        preferred_element_type=jnp.float32,
    )
    every_row = lax.psum(partial_value, "row").astype(jnp.bfloat16)
    whitened = lax.dynamic_slice_in_dim(every_row, row_index * block_keys, block_keys, 0)
    terms = against_store(every_row, stored_keys)
    local_batches = terms.shape[0]
    batch_keys = terms.shape[2]
    blocks = terms.reshape(local_batches, row_count, block_keys, batch_keys)
    listed = pair_batch[row_index]
    slots = batch_slot[listed]
    lengths = batch_length[listed]
    count = pair_count[row_index]
    routed = lax.all_to_all(blocks, "row", split_axis=1, concat_axis=0, tiled=True)
    picked = select_pairs(routed[:, 0], slots, lengths, count)
    shares = lax.psum_scatter(picked, "col", scatter_dimension=1, tiled=True)
    return (whitened, shares[None])


def solution(mesh):
    placed = (P("col", "row"), P("row", "col"), P("row", None, "col"), P(), P(), P(), P())
    return jax.shard_map(
        shards,
        mesh=mesh,
        in_specs=placed,
        out_specs=(P("row", "col"), P("row", None, "col", None)),
        check_vma=False,
    )
```

profile of v0, /device:TPU:0, one launch (start us, length us, event | category | flops | bytes accessed | tf_op | source)
XLA Modules:
  0.0 263.1 jit_solution(18069127330231890873)
XLA Ops:
  7.2 0.0 copy-start
  7.2 0.0 all-gather.2.cloned.1.call-start
  7.2 0.7 all-gather.2.cloned.1.call-update
  7.9 1.2 dynamic_slice.10
  9.2 0.7 fusion.3
  9.9 37.3 %all-gather.2.cloned.1.call-done = bf16[256,7168]{1,0:T(8,128)(2,1)} async-done(((bf16[32,7168]{1,0:T(8,128)(2,1)}), bf16[256,7168]{1,0:T(8,128)(2,1)}) %all-gather.2.cloned.1.call-update) | async-done | bytes 3670032 | tf_op jit(solution)/shard_map/all_gather | solution.py:26
  47.1 24.1 %fusion.5 = f32[256,3584]{1,0:T(8,128)} fusion(bf16[256,7168]{1,0:T(8,128)(2,1)} %all-gather.2.cloned.1.call-done, bf16[7168,3584]{1,0:T(8,128)(2,1)} %param.8), kind=kOutput, calls=%fused_computation.18 | convolution fusion | flops 13153337344 | bytes 58720256 | tf_op jit(solution)/shard_map/dot_general | solution.py:25
  71.3 131.0 %all-reduce.1 = bf16[256,3584]{1,0:T(8,128)(2,1)S(1)} all-reduce(f32[256,3584]{1,0:T(8,128)} %fusion.5), channel_id=1, replica_groups=mesh['row'=4,'col'=8] {'row'}, use_global_device_ids=true, to_apply=%region_0.0 | all-reduce | flops 917504 | bytes 5505024 | tf_op jit(solution)/shard_map/psum | solution.py:30
  202.3 0.0 copy-start.1
  202.3 3.2 %fusion = f32[256,2,256]{2,0,1:T(8,128)S(1)} fusion(bf16[2,256,3584]{2,1,0:T(8,128)(2,1)} %param.9, bf16[256,3584]{1,0:T(8,128)(2,1)S(1)} %all-reduce.1), kind=kOutput, calls=%fused_computation.3 | convolution fusion | flops 939524096 | bytes 6029312 | tf_op jit(solution)/shard_map/kd,qjd->qkj/dot_general | solution.py:8
  205.5 0.8 copy.9
  206.3 3.5 %all-to-all-start = ((f32[2,4,64,256]{3,2,0,1:T(8,128)}), f32[2,4,64,256]{3,2,0,1:T(8,128)S(1)}, u32[]{:S(2)}, u32[]{:S(2)}) async-start(f32[2,4,64,256]{3,2,0,1:T(8,128)} %copy.9), calls=%async_computation | async-start | bytes 1048576 | tf_op jit(solution)/shard_map/all_to_all | solution.py:40
  209.8 0.0 reduce-scatter.2.cloned.1.call-start
  209.8 0.7 iota_compare_fusion.1
  210.5 0.0 copy-done
  210.5 0.6 gather_fusion.1
  211.1 0.0 copy-done.1
  211.2 0.6 gather_fusion
  211.8 0.1 fusion.2
  211.9 10.7 %all-to-all-done = f32[2,4,64,256]{3,2,0,1:T(8,128)S(1)} async-done(((f32[2,4,64,256]{3,2,0,1:T(8,128)}), f32[2,4,64,256]{3,2,0,1:T(8,128)S(1)}, u32[]{:S(2)}, u32[]{:S(2)}) %all-to-all-start) | async-done | bytes 524320 | tf_op jit(solution)/shard_map/all_to_all | solution.py:40
  222.6 0.6 gather_fusion.2
  223.2 0.9 select_select_fusion
  224.1 0.0 reduce-scatter.2.cloned.1.call-update
  224.1 0.8 constant_dynamic-slice_fusion
  224.9 31.3 %reduce-scatter.2.cloned.1.call-done = f32[6,8,256]{2,1,0:T(8,128)} async-done(((f32[6,64,256]{2,1,0:T(8,128)}), f32[6,8,256]{2,1,0:T(8,128)}) %reduce-scatter.2.cloned.1.call-update) | async-done | bytes 49168 | tf_op jit(solution)/shard_map/reduce_scatter | solution.py:42
  (4 shorter events, 0.0 us)
Async XLA Ops:
  7.2 203.3 %copy-start = (s32[8]{0:T(128)S(1)}, s32[8]{0:T(128)}, u32[]{:S(2)}) copy-start(s32[8]{0:T(128)} %param.13) | copy-start | bytes 100
  7.2 40.0 %all-gather.2.cloned.1.call-start = ((), (), s32[]{:S(2)}) async-start(), calls=%async_computation.2 | async-start | bytes 4128768 | tf_op jit(solution)/shard_map/all_gather | solution.py:26
  202.3 8.9 %copy-start.1 = (s32[8]{0:T(128)S(1)}, s32[8]{0:T(128)}, u32[]{:S(2)}) copy-start(s32[8]{0:T(128)} %param.12) | copy-start | bytes 100
  206.3 16.3 %all-to-all-start = ((f32[2,4,64,256]{3,2,0,1:T(8,128)}), f32[2,4,64,256]{3,2,0,1:T(8,128)S(1)}, u32[]{:S(2)}, u32[]{:S(2)}) async-start(f32[2,4,64,256]{3,2,0,1:T(8,128)} %copy.9), calls=%async_computation | async-start | bytes 1048576 | tf_op jit(solution)/shard_map/all_to_all | solution.py:40
  209.8 46.4 %reduce-scatter.2.cloned.1.call-start = ((), (), s32[]{:S(2)}) async-start(), calls=%async_computation.3 | async-start | bytes 442368 | tf_op jit(solution)/shard_map/reduce_scatter | solution.py:42
Sparse Core Ops, SparseCore 0:
  9.9 37.2 all-gather.1
  224.2 31.9 reduce-scatter.1
where the time goes:
time: 263 us
  blocking collectives  131 us (50%)
  waiting for transfers between devices  80 us (30%)
  matrix products  27.3 us (10%)
  between operations  14.1 us (5%)
  local copies, waits for them, and re-layouts  4.76 us (2%)
  starting transfers between devices  3.55 us (1%)
    psum x1, blocking collectives, shards(): every_row = lax.psum(partial_value, 'row').astype(jnp.bfloat16)  131 us
    all_gather x1, waiting for transfers between devices, shards(): lax.all_gather(new_keys, 'col', axis=0, tiled=True)  37.3 us
    reduce_scatter x1, waiting for transfers between devices, shards(): shares = lax.psum_scatter(picked, 'col', scatter_dimension=1, tiled=True)  31.3 us
    dot_general x1, matrix products, shards(): jnp.dot(lax.all_gather(new_keys, 'col', axis=0, tiled=True), precision, p...  24.1 us
    all_to_all x1, waiting for transfers between devices, shards(): lax.all_to_all(blocks, 'row', split_axis=1, concat_axis=0, tiled=True)  10.7 us
  transfers between devices with their start and end apart: 3, of which 3 were waited for; matrix products, arithmetic and copies ran while one was open for 2% of the time, Pallas kernels for 0%

commit v1 on v0

v1 whole, which is shorter than its diff:
```python
import functools

import jax
import jax.numpy as jnp
from jax import lax
from jax.experimental import pallas as pl
from jax.experimental.pallas import tpu as pltpu
from jax.sharding import PartitionSpec as P

PARTS = 7
STEPS = 7


def flipped(array, bit, count):
    return lax.ppermute(array, "col", [(c, c ^ bit) for c in range(count)])


def gathered(new_keys, col_count, col_index):
    rows = new_keys.shape[0]
    if col_count != 8:
        return [lax.all_gather(new_keys, "col", axis=0, tiled=True)], [jnp.int32(0)]
    half = rows // 2
    by_x = flipped(new_keys, 2, 8)
    by_y = flipped(new_keys, 4, 8)
    by_core = flipped(new_keys, 1, 8)
    low = flipped(by_x[:half], 4, 8)
    high = flipped(by_y[half:], 2, 8)
    x_core = flipped(by_x, 1, 8)
    y_core = flipped(by_y, 1, 8)
    low_core = flipped(low, 1, 8)
    high_core = flipped(high, 1, 8)
    pieces = [new_keys, by_core, by_x, x_core, by_y, y_core, low, high, low_core, high_core]
    of = [0, 1, 2, 3, 4, 5, 6, 6, 7, 7]
    within = [0] * 7 + [half, 0, half]
    return pieces, [(col_index ^ f) * rows + w for f, w in zip(of, within)]


def product_kernel(count, starts_ref, *refs):
    pieces, weights_ref, wide_ref, sent_ref, keys_ref = refs[:count], *refs[count:]
    step = pl.program_id(0)
    for i, piece in enumerate(pieces):
        size = piece.shape[0]
        keys_ref[pl.ds(pl.multiple_of(starts_ref[i], 16), size), :] = piece[...]
    part = jnp.dot(keys_ref[...], weights_ref[...], preferred_element_type=jnp.float32)

    @pl.when(step == 0)
    def _():
        wide_ref[...] = part

    @pl.when(step > 0)
    def _():
        wide_ref[...] += part

    @pl.when(step == pl.num_programs(0) - 1)
    def _():
        sent_ref[...] = wide_ref[...].astype(sent_ref.dtype)


def product(pieces, starts, weights, part, keys, wire):
    depth, columns = weights.shape
    deep, wide = depth // STEPS, columns // PARTS
    grid_spec = pltpu.PrefetchScalarGridSpec(
        num_scalar_prefetch=1,
        grid=(STEPS,),
        in_specs=[pl.BlockSpec((p.shape[0], deep), lambda k, s: (0, k)) for p in pieces]
        + [pl.BlockSpec((deep, wide), lambda k, s: (k, part))],
        out_specs=[pl.BlockSpec((keys, wide), lambda k, s: (0, 0))] * 2,
        scratch_shapes=[pltpu.VMEM((keys, deep), pieces[0].dtype)],
    )
    return pl.pallas_call(
        functools.partial(product_kernel, len(pieces)),
        grid_spec=grid_spec,
        out_shape=[
            jax.ShapeDtypeStruct((keys, wide), jnp.float32),
            jax.ShapeDtypeStruct((keys, wide), wire),
        ],
        compiler_params=pltpu.CompilerParams(vmem_limit_bytes=24 * 2**20),
        cost_estimate=pl.CostEstimate(
            flops=2 * keys * depth * wide,
            bytes_accessed=2 * depth * (keys + wide) + 6 * keys * wide,
            transcendentals=0,
        ),
        name="product",
    )(starts, *pieces, weights)


def summed(wide, sent, row_count, wire, inner):
    half = row_count // 2
    total = wide
    for hop in range(half - 1):
        came = lax.ppermute(sent, "row", [(hop, hop + 1), (row_count - 1 - hop, row_count - 2 - hop)])
        total = total + came.astype(jnp.float32)
        sent = total.astype(wire)
    came = lax.ppermute(sent, "row", [(half - 1, half), (half, half - 1)])
    final = (total + came.astype(jnp.float32)).astype(jnp.bfloat16)
    for hop in range(half - 1):
        low, high = half - 1 - hop, half + hop
        came = lax.ppermute(final, "row", [(low, low - 1), (high, high + 1)])
        last = hop == half - 2
        if last:
            return final, came
        final = jnp.where(inner[hop], final, came)
    return final, final


def contract_kernel(first, at_ref, final_ref, came_ref, stored_ref, *refs):
    terms_ref, whitened_ref, rows_ref = refs[-3:]
    own, start = at_ref[0], at_ref[1]

    @pl.when(own != 0)
    def _():
        rows_ref[...] = final_ref[...]

    @pl.when(own == 0)
    def _():
        rows_ref[...] = came_ref[...]

    batches, slots, wide = stored_ref.shape
    term = lax.dot_general(
        rows_ref[...],
        stored_ref[...].reshape(batches * slots, wide),
        (((1,), (1,)), ((), ())),
        preferred_element_type=jnp.float32,
    )
    terms_ref[...] = term if first else refs[0][...] + term
    whitened_ref[...] = rows_ref[pl.ds(pl.multiple_of(start, 16), whitened_ref.shape[0]), :]


def contract(at, final, came, stored, terms, whitened, part, block):
    keys, wide = final.shape
    batches, slots, columns = stored.shape
    first = terms is None
    whole = pl.BlockSpec((keys, wide), lambda i, s: (0, 0))
    sums = pl.BlockSpec((keys, batches * slots), lambda i, s: (0, 0))
    in_specs = [whole, whole, pl.BlockSpec((batches, slots, wide), lambda i, s: (0, 0, part))]
    operands = [at, final, came, stored]
    aliases = {}
    if not first:
        in_specs += [sums, pl.BlockSpec(memory_space=pl.ANY)]
        operands += [terms, whitened]
        aliases = {4: 0, 5: 1}
    return pl.pallas_call(
        functools.partial(contract_kernel, first),
        grid_spec=pltpu.PrefetchScalarGridSpec(
            num_scalar_prefetch=1,
            grid=(1,),
            in_specs=in_specs,
            out_specs=[sums, pl.BlockSpec((block, wide), lambda i, s: (0, part))],
            scratch_shapes=[pltpu.VMEM((keys, wide), jnp.bfloat16)],
        ),
        out_shape=[
            jax.ShapeDtypeStruct((keys, batches * slots), jnp.float32),
            jax.ShapeDtypeStruct((block, columns), jnp.bfloat16),
        ],
        input_output_aliases=aliases,
        compiler_params=pltpu.CompilerParams(vmem_limit_bytes=24 * 2**20),
        cost_estimate=pl.CostEstimate(
            flops=2 * keys * wide * batches * slots,
            bytes_accessed=2 * wide * (2 * keys + batches * slots) + 8 * keys * batches * slots,
            transcendentals=0,
        ),
        name="contract",
    )(*operands)


def select_kernel(count, row_ref, batch_ref, used_ref, length_ref, slot_ref, *refs):
    parts, out_ref, held_ref = refs[:count], refs[count], refs[count + 1]
    batches, rows, slots = held_ref.shape[1:]
    for i, part in enumerate(parts):
        for b in range(batches):
            held_ref[i, b] = part[0, :, b * slots : (b + 1) * slots]
    row = row_ref[0]
    column = lax.broadcasted_iota(jnp.int32, (rows, slots), 1)
    for place in range(out_ref.shape[1]):
        batch = batch_ref[row, place]
        slot = slot_ref[batch]
        owner = lax.div(slot, batches)
        shift = lax.rem(row - owner + count, count)
        length = jnp.where(place < used_ref[row], length_ref[batch], 0)
        value = held_ref[shift, slot - owner * batches]
        out_ref[0, place] = jnp.where(column < length, value, 0.0)


def selected(parts, row_index, pair_batch, pair_count, batch_length, batch_slot, batches):
    count = len(parts)
    _, rows, wide = parts[0].shape
    slots = wide // batches
    places = pair_batch.shape[1]
    return pl.pallas_call(
        functools.partial(select_kernel, count),
        grid_spec=pltpu.PrefetchScalarGridSpec(
            num_scalar_prefetch=5,
            grid=(1,),
            in_specs=[pl.BlockSpec((1, rows, wide), lambda i, *s: (0, 0, 0))] * count,
            out_specs=pl.BlockSpec((1, places, rows, slots), lambda i, *s: (0, 0, 0, 0)),
            scratch_shapes=[pltpu.VMEM((count, batches, rows, slots), jnp.float32)],
        ),
        out_shape=jax.ShapeDtypeStruct((1, places, rows, slots), jnp.float32),
        name="select",
    )(row_index[None], pair_batch, pair_count, batch_length, batch_slot, *parts)


def shards(new_keys, precision, stored_keys, pair_batch, pair_count, batch_length, batch_slot):
    row_count = lax.axis_size("row")
    col_count = lax.axis_size("col")
    row_index = lax.axis_index("row")
    col_index = lax.axis_index("col")
    keys = new_keys.shape[0] * col_count
    block = keys // row_count
    batches = stored_keys.shape[0]
    half = row_count // 2
    wire = jnp.bfloat16 if row_count <= 4 else jnp.float32

    away = jnp.where(row_index < half, half - 1 - row_index, row_index - half)
    inner = [away <= hop for hop in range(half)]
    at = jnp.stack([(away < half - 1).astype(jnp.int32), row_index * block])

    pieces, starts = gathered(new_keys, col_count, col_index)
    starts = jnp.stack(starts)
    terms = whitened = None
    for part in range(PARTS):
        wide, sent = product(pieces, starts, precision, part, keys, wire)
        final, came = summed(wide, sent, row_count, wire, inner)
        terms, whitened = contract(at, final, came, stored_keys, terms, whitened, part, block)

    share = block // col_count
    sums = terms.reshape(row_count, col_count, share, terms.shape[1])
    bit = 1
    while bit < col_count:
        pairs = sums.reshape(row_count, sums.shape[1] // 2, 2, share, sums.shape[3])
        mine = (col_index // bit) % 2
        kept = lax.dynamic_index_in_dim(pairs, mine, 2, keepdims=False)
        left = lax.dynamic_index_in_dim(pairs, 1 - mine, 2, keepdims=False)
        sums = kept + flipped(left, bit, col_count)
        bit *= 2
    sums = sums[:, 0]
    parts = []
    for shift in range(row_count):
        part = lax.dynamic_slice_in_dim(sums, (row_index + shift) % row_count, 1, 0)
        if shift:
            part = lax.ppermute(part, "row", [(r, (r + shift) % row_count) for r in range(row_count)])
        parts.append(part)
    shares = selected(parts, row_index, pair_batch, pair_count, batch_length, batch_slot, batches)
    return (whitened, shares)


def solution(mesh):
    placed = (P("col", "row"), P("row", "col"), P("row", None, "col"), P(), P(), P(), P())
    return jax.shard_map(
        shards,
        mesh=mesh,
        in_specs=placed,
        out_specs=(P("row", "col"), P("row", None, "col", None)),
        check_vma=False,
    )
```

time: 263 us -> 178 us (0.68)
  blocking collectives: 131 us -> 0 us
  Pallas kernels: 0 us -> 69.3 us
  starting transfers between devices: 3.55 us -> 41.3 us
  matrix products: 27.3 us -> 0 us
  waiting for transfers between devices: 80 us -> 56.7 us
  between operations: 14.1 us -> 1.16 us
    psum x1 -> x0, blocking collectives: 131 us -> none  [shards(): every_row = lax.psum(partial_value, 'row').astype(jnp.bfloat16)]
    pallas_call x0 -> x15, Pallas kernels: none -> 69.3 us  [the longest x7 54.8 us: product(): pl.pallas_call(functools.partial(product_kernel, len(pieces)), grid_spec=...]
    ppermute x0 -> x36, waiting for transfers between devices: none -> 56.7 us  [the longest x7 24.8 us: summed(): came = lax.ppermute(final, 'row', [(low, low - 1), (high, high + 1)])]
    ppermute x0 -> x36, starting transfers between devices: none -> 41.3 us  [the longest x7 11.3 us: summed(): lax.ppermute(sent, 'row', [(hop, hop + 1), (row_count - 1 - hop, row_coun...]
    all_gather x1 -> x0, waiting for transfers between devices: 37.3 us -> none  [shards(): lax.all_gather(new_keys, 'col', axis=0, tiled=True)]
    reduce_scatter x1 -> x0, waiting for transfers between devices: 31.3 us -> none  [shards(): shares = lax.psum_scatter(picked, 'col', scatter_dimension=1, tiled=True)]
    dot_general x2 -> x0, matrix products: 27.3 us -> none  [the longest x1 24.1 us: shards(): jnp.dot(lax.all_gather(new_keys, 'col', axis=0, tiled=True), precision, p...]
    all_to_all x1 -> x0, waiting for transfers between devices: 10.7 us -> none  [shards(): lax.all_to_all(blocks, 'row', split_axis=1, concat_axis=0, tiled=True)]
  transfers between devices with their start and end apart: 3 -> 36, of which waited for: 3 -> 19; matrix products, arithmetic and copies ran while one was open for 2% -> 1% of each run, Pallas kernels for 0% -> 33%
where the time goes in v1:
time: 178 us; the launch traced here: 176 us
  Pallas kernels  69.3 us (39%)
  waiting for transfers between devices  56.7 us (32%)
  starting transfers between devices  41.3 us (23%)
  local copies, waits for them, and re-layouts  6.48 us (4%)
    pallas_call x7, Pallas kernels, product(): pl.pallas_call(functools.partial(product_kernel, len(pieces)), grid_spec=...  54.8 us
    ppermute x7, waiting for transfers between devices, summed(): came = lax.ppermute(final, 'row', [(low, low - 1), (high, high + 1)])  24.8 us
    ppermute x12, waiting for transfers between devices, flipped(): return lax.ppermute(array, 'col', [(c, c ^ bit) for c in range(count)])  23.5 us
    pallas_call x7, Pallas kernels, contract(): pl.pallas_call(functools.partial(contract_kernel, first), grid_spec=pltpu...  12.3 us
    ppermute x7, starting transfers between devices, summed(): lax.ppermute(sent, 'row', [(hop, hop + 1), (row_count - 1 - hop, row_coun...  11.3 us
    ppermute x12, starting transfers between devices, flipped(): return lax.ppermute(array, 'col', [(c, c ^ bit) for c in range(count)])  11.2 us
    ppermute x7, starting transfers between devices, summed(): came = lax.ppermute(final, 'row', [(low, low - 1), (high, high + 1)])  9.02 us
    ppermute x7, waiting for transfers between devices, summed(): lax.ppermute(sent, 'row', [(hop, hop + 1), (row_count - 1 - hop, row_coun...  6.9 us
  transfers between devices with their start and end apart: 36, of which 19 were waited for; matrix products, arithmetic and copies ran while one was open for 1% of the time, Pallas kernels for 33%

profile of v1, /device:TPU:0, one launch (start us, length us, event | category | flops | bytes accessed | tf_op | source)
XLA Modules:
  0.0 176.4 jit_solution(5939005051407481837)
XLA Ops:
  0.6 3.0 %collective-permute-start.1 = (bf16[32,7168]{1,0:T(8,128)(2,1)}, bf16[32,7168]{1,0:T(8,128)(2,1)S(1)}, u32[]{:S(2)}, u32[]{:S(2)}) collective-permute-start(bf16[32,7168]{1,0:T(8,128)(2,1)} %refs_0_.13), channel_id=1, source_target_pairs={{0,2},{1,3},{2,0},{3,1},{4,6},{5,7},{6,4},{7,5},{8,10},{9,11},{10,... | collective-permute-start | bytes 1376264 | tf_op jit(solution)/shard_map/ppermute | solution.py:15
  3.6 1.5 collective-permute-start.3
  5.2 9.2 %collective-permute-done.1.refs_2_ = bf16[32,7168]{1,0:T(8,128)(2,1)S(1)} collective-permute-done((bf16[32,7168]{1,0:T(8,128)(2,1)}, bf16[32,7168]{1,0:T(8,128)(2,1)S(1)}, u32[]{:S(2)}, u32[]{:S(2)}) %collective-permute-start.1) | collective-permute-done | bytes 458784 | tf_op jit(solution)/shard_map/ppermute | solution.py:15
  14.4 1.8 %collective-permute-start.5 = (bf16[16,7168]{1,0:T(8,128)(2,1)S(1)}, bf16[16,7168]{1,0:T(8,128)(2,1)S(1)}, u32[]{:S(2)}, u32[]{:S(2)}) collective-permute-start(bf16[16,7168]{1,0:T(8,128)(2,1)S(1)} %slice.8), channel_id=1, source_target_pairs={{0,4},{1,5},{2,6},{3,7},{4,0},{5,1},{6,2},{7,3},{8,12},{9,13},{10,... | collective-permute-start | bytes 688136 | tf_op jit(solution)/shard_map/ppermute | solution.py:15
  16.2 1.6 collective-permute-start.6
  18.3 2.9 %collective-permute-done.5.refs_6_ = bf16[16,7168]{1,0:T(8,128)(2,1)S(1)} collective-permute-done((bf16[16,7168]{1,0:T(8,128)(2,1)S(1)}, bf16[16,7168]{1,0:T(8,128)(2,1)S(1)}, u32[]{:S(2)}, u32[]{:S(2)}) %collective-permute-start.5) | collective-permute-done | bytes 229408 | tf_op jit(solution)/shard_map/ppermute | solution.py:15
  21.2 1.3 collective-permute-done.6.refs_7_
  22.7 1.3 collective-permute-done.8.refs_9_
  24.0 1.0 copy-done.2
  25.0 7.8 %product.13 = (f32[256,512]{1,0:T(8,128)S(1)}, bf16[256,512]{1,0:T(8,128)(2,1)S(1)}) custom-call(s32[10]{0:T(128)S(1)} %stack.59.starts_ref, bf16[32,7168]{1,0:T(8,128)(2,1)S(1)} %copy-done.2, bf16[32,7168]{1,0:T(8,128)(2,1)S(1)} %collective-permute-done.refs_1_, bf16[32,7168]{1,0:T(8,128)(2,1)S(1)} %collective-permute-done.1.refs_2_, ...), custom_call_target="tpu_custom_call" | custom-call | flops 1879048192 | bytes 11796480 | tf_op jit(solution)/shard_map/product/pallas_call | solution.py:70
  32.8 3.5 %collective-permute-start.27 = (bf16[256,512]{1,0:T(8,128)(2,1)S(1)}, bf16[256,512]{1,0:T(8,128)(2,1)S(1)}, u32[]{:S(2)}, u32[]{:S(2)}) collective-permute-start(bf16[256,512]{1,0:T(8,128)(2,1)S(1)} %get-tuple-element.43), channel_id=1, source_target_pairs={{0,8},{24,16},{1,9},{25,17},{2,10},{26,18},{3,11},{27,19},{4,12},{... | collective-permute-start | bytes 786440 | tf_op jit(solution)/shard_map/ppermute | solution.py:91
  36.4 7.8 %product.12 = (f32[256,512]{1,0:T(8,128)S(1)}, bf16[256,512]{1,0:T(8,128)(2,1)S(1)}) custom-call(s32[10]{0:T(128)S(1)} %stack.59.starts_ref, bf16[32,7168]{1,0:T(8,128)(2,1)S(1)} %copy-done.2, bf16[32,7168]{1,0:T(8,128)(2,1)S(1)} %collective-permute-done.refs_1_, bf16[32,7168]{1,0:T(8,128)(2,1)S(1)} %collective-permute-done.1.refs_2_, ...), custom_call_target="tpu_custom_call" | custom-call | flops 1879048192 | bytes 11796480 | tf_op jit(solution)/shard_map/product/pallas_call | solution.py:70
  44.2 1.3 collective-permute-start.24
  45.5 7.8 %product.11 = (f32[256,512]{1,0:T(8,128)S(1)}, bf16[256,512]{1,0:T(8,128)(2,1)S(1)}) custom-call(s32[10]{0:T(128)S(1)} %stack.59.starts_ref, bf16[32,7168]{1,0:T(8,128)(2,1)S(1)} %copy-done.2, bf16[32,7168]{1,0:T(8,128)(2,1)S(1)} %collective-permute-done.refs_1_, bf16[32,7168]{1,0:T(8,128)(2,1)S(1)} %collective-permute-done.1.refs_2_, ...), custom_call_target="tpu_custom_call" | custom-call | flops 1879048192 | bytes 11796480 | tf_op jit(solution)/shard_map/product/pallas_call | solution.py:70
  53.4 1.3 collective-permute-start.21
  54.7 7.8 %product.10 = (f32[256,512]{1,0:T(8,128)S(1)}, bf16[256,512]{1,0:T(8,128)(2,1)S(1)}) custom-call(s32[10]{0:T(128)S(1)} %stack.59.starts_ref, bf16[32,7168]{1,0:T(8,128)(2,1)S(1)} %copy-done.2, bf16[32,7168]{1,0:T(8,128)(2,1)S(1)} %collective-permute-done.refs_1_, bf16[32,7168]{1,0:T(8,128)(2,1)S(1)} %collective-permute-done.1.refs_2_, ...), custom_call_target="tpu_custom_call" | custom-call | flops 1879048192 | bytes 11796480 | tf_op jit(solution)/shard_map/product/pallas_call | solution.py:70
  62.5 1.3 collective-permute-start.18
  63.8 7.8 %product.9 = (f32[256,512]{1,0:T(8,128)S(1)}, bf16[256,512]{1,0:T(8,128)(2,1)S(1)}) custom-call(s32[10]{0:T(128)S(1)} %stack.59.starts_ref, bf16[32,7168]{1,0:T(8,128)(2,1)S(1)} %copy-done.2, bf16[32,7168]{1,0:T(8,128)(2,1)S(1)} %collective-permute-done.refs_1_, bf16[32,7168]{1,0:T(8,128)(2,1)S(1)} %collective-permute-done.1.refs_2_, ...), custom_call_target="tpu_custom_call" | custom-call | flops 1879048192 | bytes 11796480 | tf_op jit(solution)/shard_map/product/pallas_call | solution.py:70
  71.7 1.3 collective-permute-start.15
  73.0 7.8 %product.8 = (f32[256,512]{1,0:T(8,128)S(1)}, bf16[256,512]{1,0:T(8,128)(2,1)S(1)}) custom-call(s32[10]{0:T(128)S(1)} %stack.59.starts_ref, bf16[32,7168]{1,0:T(8,128)(2,1)S(1)} %copy-done.2, bf16[32,7168]{1,0:T(8,128)(2,1)S(1)} %collective-permute-done.refs_1_, bf16[32,7168]{1,0:T(8,128)(2,1)S(1)} %collective-permute-done.1.refs_2_, ...), custom_call_target="tpu_custom_call" | custom-call | flops 1879048192 | bytes 11796480 | tf_op jit(solution)/shard_map/product/pallas_call | solution.py:70
  80.8 7.8 %product.7 = (f32[256,512]{1,0:T(8,128)S(1)}, bf16[256,512]{1,0:T(8,128)(2,1)S(1)}) custom-call(s32[10]{0:T(128)S(1)} %stack.59.starts_ref, bf16[32,7168]{1,0:T(8,128)(2,1)S(1)} %copy-done.2, bf16[32,7168]{1,0:T(8,128)(2,1)S(1)} %collective-permute-done.refs_1_, bf16[32,7168]{1,0:T(8,128)(2,1)S(1)} %collective-permute-done.1.refs_2_, ...), custom_call_target="tpu_custom_call" | custom-call | flops 1879048192 | bytes 11796480 | tf_op jit(solution)/shard_map/product/pallas_call | solution.py:70
  88.7 1.3 collective-permute-start.12
  90.1 1.3 collective-permute-start.9
  91.5 0.7 collective-permute-start.28
  92.3 0.7 collective-permute-start.25
  93.0 0.7 collective-permute-start.22
  93.8 2.8 %collective-permute-done.12 = bf16[256,512]{1,0:T(8,128)(2,1)S(1)} collective-permute-done((bf16[256,512]{1,0:T(8,128)(2,1)S(1)}, bf16[256,512]{1,0:T(8,128)(2,1)S(1)}, u32[]{:S(2)}, u32[]{:S(2)}) %collective-permute-start.12) | collective-permute-done | bytes 262176 | tf_op jit(solution)/shard_map/ppermute | solution.py:91
  96.6 0.7 collective-permute-start.19
  97.4 4.1 %collective-permute-done.9 = bf16[256,512]{1,0:T(8,128)(2,1)S(1)} collective-permute-done((bf16[256,512]{1,0:T(8,128)(2,1)S(1)}, bf16[256,512]{1,0:T(8,128)(2,1)S(1)}, u32[]{:S(2)}, u32[]{:S(2)}) %collective-permute-start.9) | collective-permute-done | bytes 262176 | tf_op jit(solution)/shard_map/ppermute | solution.py:91
  101.4 0.7 collective-permute-start.16
  102.2 0.7 collective-permute-start.13
  103.0 0.7 collective-permute-start.10
  103.8 1.3 collective-permute-start.29
  105.3 1.3 collective-permute-start.26
  106.7 1.3 collective-permute-start.23
  108.1 1.3 collective-permute-start.20
  109.6 1.3 collective-permute-start.17
  110.9 9.4 %collective-permute-done.29.came_ref = bf16[256,512]{1,0:T(8,128)(2,1)S(1)} collective-permute-done((bf16[256,512]{1,0:T(8,128)(2,1)S(1)}, bf16[256,512]{1,0:T(8,128)(2,1)S(1)}, u32[]{:S(2)}, u32[]{:S(2)}) %collective-permute-start.29) | collective-permute-done | bytes 262176 | tf_op jit(solution)/shard_map/ppermute | solution.py:98
  120.3 1.3 collective-permute-start.14
  121.7 4.2 %collective-permute-done.26.came_ref = bf16[256,512]{1,0:T(8,128)(2,1)S(1)} collective-permute-done((bf16[256,512]{1,0:T(8,128)(2,1)S(1)}, bf16[256,512]{1,0:T(8,128)(2,1)S(1)}, u32[]{:S(2)}, u32[]{:S(2)}) %collective-permute-start.26) | collective-permute-done | bytes 262176 | tf_op jit(solution)/shard_map/ppermute | solution.py:98
  125.9 1.3 collective-permute-start.11
  127.3 2.0 %copy-done = bf16[2,256,3584]{2,1,0:T(8,128)(2,1)S(1)} copy-done((bf16[2,256,3584]{2,1,0:T(8,128)(2,1)S(1)}, bf16[2,256,3584]{2,1,0:T(8,128)(2,1)}, u32[]{:S(2)}) %copy-start) | copy-done | bytes 3670040
  129.4 1.4 contract.7
  130.7 2.0 %copy-done.1 = bf16[2,256,3584]{2,1,0:T(8,128)(2,1)S(1)} copy-done((bf16[2,256,3584]{2,1,0:T(8,128)(2,1)S(1)}, bf16[2,256,3584]{2,1,0:T(8,128)(2,1)}, u32[]{:S(2)}) %copy-start.1) | copy-done | bytes 3670040
  132.8 1.4 contract.8
  134.1 2.3 %contract.9 = (f32[256,512]{1,0:T(8,128)S(1)}, bf16[64,3584]{1,0:T(8,128)(2,1)}) custom-call(s32[2]{0:T(128)S(1)} %pad_add_fusion.at_ref, bf16[256,512]{1,0:T(8,128)(2,1)S(1)} %add_convert_fusion.2.final_ref, bf16[256,512]{1,0:T(8,128)(2,1)} %collective-permute-done.23.came_ref, ...), custom_call_target="tpu_custom_call", output_to_operand_aliasing={{0}: (4, {}), {1}: (5, {})} | custom-call | flops 134217728 | bytes 2097152 | tf_op jit(solution)/shard_map/contract/pallas_call | solution.py:142
  136.4 0.8 collective-permute-done.20.came_ref
  137.3 2.3 %contract.10 = (f32[256,512]{1,0:T(8,128)S(1)}, bf16[64,3584]{1,0:T(8,128)(2,1)}) custom-call(s32[2]{0:T(128)S(1)} %pad_add_fusion.at_ref, bf16[256,512]{1,0:T(8,128)(2,1)S(1)} %add_convert_fusion.3.final_ref, bf16[256,512]{1,0:T(8,128)(2,1)} %collective-permute-done.20.came_ref, ...), custom_call_target="tpu_custom_call", output_to_operand_aliasing={{0}: (4, {}), {1}: (5, {})} | custom-call | flops 134217728 | bytes 2097152 | tf_op jit(solution)/shard_map/contract/pallas_call | solution.py:142
  139.5 3.8 %collective-permute-done.17.came_ref = bf16[256,512]{1,0:T(8,128)(2,1)} collective-permute-done((bf16[256,512]{1,0:T(8,128)(2,1)S(1)}, bf16[256,512]{1,0:T(8,128)(2,1)}, u32[]{:S(2)}, u32[]{:S(2)}) %collective-permute-start.17) | collective-permute-done | bytes 262176 | tf_op jit(solution)/shard_map/ppermute | solution.py:98
  143.3 2.3 %contract.11 = (f32[256,512]{1,0:T(8,128)S(1)}, bf16[64,3584]{1,0:T(8,128)(2,1)}) custom-call(s32[2]{0:T(128)S(1)} %pad_add_fusion.at_ref, bf16[256,512]{1,0:T(8,128)(2,1)S(1)} %add_convert_fusion.4.final_ref, bf16[256,512]{1,0:T(8,128)(2,1)} %collective-permute-done.17.came_ref, ...), custom_call_target="tpu_custom_call", output_to_operand_aliasing={{0}: (4, {}), {1}: (5, {})} | custom-call | flops 134217728 | bytes 2097152 | tf_op jit(solution)/shard_map/contract/pallas_call | solution.py:142
  145.6 3.2 %collective-permute-done.14.came_ref = bf16[256,512]{1,0:T(8,128)(2,1)S(1)} collective-permute-done((bf16[256,512]{1,0:T(8,128)(2,1)S(1)}, bf16[256,512]{1,0:T(8,128)(2,1)S(1)}, u32[]{:S(2)}, u32[]{:S(2)}) %collective-permute-start.14) | collective-permute-done | bytes 262176 | tf_op jit(solution)/shard_map/ppermute | solution.py:98
  148.8 1.4 contract.12
  150.2 3.4 %collective-permute-done.11.came_ref = bf16[256,512]{1,0:T(8,128)(2,1)S(1)} collective-permute-done((bf16[256,512]{1,0:T(8,128)(2,1)S(1)}, bf16[256,512]{1,0:T(8,128)(2,1)S(1)}, u32[]{:S(2)}, u32[]{:S(2)}) %collective-permute-start.11) | collective-permute-done | bytes 262176 | tf_op jit(solution)/shard_map/ppermute | solution.py:98
  153.5 1.4 contract.13
  155.1 1.5 collective-permute-done.30
  156.6 1.6 collective-permute-start.31
  158.2 4.0 %collective-permute-done.31 = f32[4,2,8,512]{3,2,1,0:T(8,128)S(1)} collective-permute-done((f32[4,2,8,512]{3,2,1,0:T(8,128)S(1)}, f32[4,2,8,512]{3,2,1,0:T(8,128)S(1)}, u32[]{:S(2)}, u32[]{:S(2)}) %collective-permute-start.31) | collective-permute-done | bytes 131104 | tf_op jit(solution)/shard_map/ppermute | solution.py:15
  162.2 1.1 collective-permute-start.32
  163.4 3.2 %collective-permute-done.32 = f32[4,1,8,512]{3,2,1,0:T(8,128)S(1)} collective-permute-done((f32[4,1,8,512]{3,2,1,0:T(8,128)S(1)}, f32[4,1,8,512]{3,2,1,0:T(8,128)S(1)}, u32[]{:S(2)}, u32[]{:S(2)}) %collective-permute-start.32) | collective-permute-done | bytes 65568 | tf_op jit(solution)/shard_map/ppermute | solution.py:15
  167.2 1.1 collective-permute-start.33
  168.3 1.4 collective-permute-start.34
  169.7 2.5 %collective-permute-start.35 = (f32[1,8,512]{2,1,0:T(8,128)S(1)}, f32[1,8,512]{2,1,0:T(8,128)S(1)}, u32[]{:S(2)}, u32[]{:S(2)}) collective-permute-start(f32[1,8,512]{2,1,0:T(8,128)S(1)} %get-tuple-element.58), channel_id=1, source_target_pairs={{0,24},{8,0},{16,8},{24,16},{1,25},{9,1},{17,9},{25,17},{2,26},{10... | collective-permute-start | bytes 49160 | tf_op jit(solution)/shard_map/ppermute | solution.py:241
  173.0 0.7 collective-permute-done.35.refs_3_
  174.3 2.1 %select.25 = f32[1,6,8,256]{3,2,1,0:T(8,128)} custom-call(s32[1]{0:T(128)} %bitcast.12.row_ref, s32[4,6]{1,0:T(4,128)} %batch_ref.1, s32[4]{0:T(128)} %used_ref.1, s32[8]{0:T(128)} %length_ref.1, s32[8]{0:T(128)} %slot_ref.1, f32[1,8,512]{2,1,0:T(8,128)} %get-tuple-element.61.refs_0_, f32[1,8,512]{2,1,0:T(8,128)} %copy-done.3, f32[1,8,512]{2,1,0:T(8,128)} %copy-done.4, ...), custom_call_target="tpu_custom_call" | custom-call | tf_op jit(solution)/shard_map/select/pallas_call | solution.py:189
  (60 shorter events, 4.4 us)
Async XLA Ops:
  0.6 13.7 %collective-permute-start.1 = (bf16[32,7168]{1,0:T(8,128)(2,1)}, bf16[32,7168]{1,0:T(8,128)(2,1)S(1)}, u32[]{:S(2)}, u32[]{:S(2)}) collective-permute-start(bf16[32,7168]{1,0:T(8,128)(2,1)} %refs_0_.13), channel_id=1, source_target_pairs={{0,2},{1,3},{2,0},{3,1},{4,6},{5,7},{6,4},{7,5},{8,10},{9,11},{10,... | collective-permute-start | bytes 1376264 | tf_op jit(solution)/shard_map/ppermute | solution.py:15
  3.6 12.6 %collective-permute-start.3 = (bf16[32,7168]{1,0:T(8,128)(2,1)}, bf16[32,7168]{1,0:T(8,128)(2,1)S(1)}, u32[]{:S(2)}, u32[]{:S(2)}) collective-permute-start(bf16[32,7168]{1,0:T(8,128)(2,1)} %refs_0_.13), channel_id=1, source_target_pairs={{0,4},{1,5},{2,6},{3,7},{4,0},{5,1},{6,2},{7,3},{8,12},{9,13},{10,... | collective-permute-start | bytes 1376264 | tf_op jit(solution)/shard_map/ppermute | solution.py:15
  5.2 17.4 %collective-permute-start = (bf16[32,7168]{1,0:T(8,128)(2,1)}, bf16[32,7168]{1,0:T(8,128)(2,1)S(1)}, u32[]{:S(2)}, u32[]{:S(2)}) collective-permute-start(bf16[32,7168]{1,0:T(8,128)(2,1)} %refs_0_.13), channel_id=1, source_target_pairs={{0,1},{1,0},{2,3},{3,2},{4,5},{5,4},{6,7},{7,6},{8,9},{9,8},{10,11... | collective-permute-start | bytes 1376264 | tf_op jit(solution)/shard_map/ppermute | solution.py:15
  14.4 6.9 %collective-permute-start.5 = (bf16[16,7168]{1,0:T(8,128)(2,1)S(1)}, bf16[16,7168]{1,0:T(8,128)(2,1)S(1)}, u32[]{:S(2)}, u32[]{:S(2)}) collective-permute-start(bf16[16,7168]{1,0:T(8,128)(2,1)S(1)} %slice.8), channel_id=1, source_target_pairs={{0,4},{1,5},{2,6},{3,7},{4,0},{5,1},{6,2},{7,3},{8,12},{9,13},{10,... | collective-permute-start | bytes 688136 | tf_op jit(solution)/shard_map/ppermute | solution.py:15
  16.2 6.3 %collective-permute-start.6 = (bf16[16,7168]{1,0:T(8,128)(2,1)S(1)}, bf16[16,7168]{1,0:T(8,128)(2,1)S(1)}, u32[]{:S(2)}, u32[]{:S(2)}) collective-permute-start(bf16[16,7168]{1,0:T(8,128)(2,1)S(1)} %slice.9), channel_id=1, source_target_pairs={{0,2},{1,3},{2,0},{3,1},{4,6},{5,7},{6,4},{7,5},{8,10},{9,11},{10,... | collective-permute-start | bytes 688136 | tf_op jit(solution)/shard_map/ppermute | solution.py:15
  17.8 6.2 %collective-permute-start.2 = (bf16[32,7168]{1,0:T(8,128)(2,1)S(1)}, bf16[32,7168]{1,0:T(8,128)(2,1)S(1)}, u32[]{:S(2)}, u32[]{:S(2)}) collective-permute-start(bf16[32,7168]{1,0:T(8,128)(2,1)S(1)} %collective-permute-done.1.refs_2_), channel_id=1, source_target_pairs={{0,1},{1,0},{2,3},{3,2},{4,5},{5,4},{6,7},{7,6},{8,9},{9,8},{10,11... | collective-permute-start | bytes 1376264 | tf_op jit(solution)/shard_map/ppermute | solution.py:15
  17.8 6.2 %collective-permute-start.4 = (bf16[32,7168]{1,0:T(8,128)(2,1)S(1)}, bf16[32,7168]{1,0:T(8,128)(2,1)S(1)}, u32[]{:S(2)}, u32[]{:S(2)}) collective-permute-start(bf16[32,7168]{1,0:T(8,128)(2,1)S(1)} %collective-permute-done.3.refs_4_), channel_id=1, source_target_pairs={{0,1},{1,0},{2,3},{3,2},{4,5},{5,4},{6,7},{7,6},{8,9},{9,8},{10,11... | collective-permute-start | bytes 1376264 | tf_op jit(solution)/shard_map/ppermute | solution.py:15
  21.2 1.5 collective-permute-start.7
  22.5 1.5 collective-permute-start.8
  24.0 1.0 copy-start.2
  32.8 55.8 %collective-permute-start.27 = (bf16[256,512]{1,0:T(8,128)(2,1)S(1)}, bf16[256,512]{1,0:T(8,128)(2,1)S(1)}, u32[]{:S(2)}, u32[]{:S(2)}) collective-permute-start(bf16[256,512]{1,0:T(8,128)(2,1)S(1)} %get-tuple-element.43), channel_id=1, source_target_pairs={{0,8},{24,16},{1,9},{25,17},{2,10},{26,18},{3,11},{27,19},{4,12},{... | collective-permute-start | bytes 786440 | tf_op jit(solution)/shard_map/ppermute | solution.py:91
  44.2 45.9 %collective-permute-start.24 = (bf16[256,512]{1,0:T(8,128)(2,1)S(1)}, bf16[256,512]{1,0:T(8,128)(2,1)S(1)}, u32[]{:S(2)}, u32[]{:S(2)}) collective-permute-start(bf16[256,512]{1,0:T(8,128)(2,1)S(1)} %get-tuple-element.41), channel_id=1, source_target_pairs={{0,8},{24,16},{1,9},{25,17},{2,10},{26,18},{3,11},{27,19},{4,12},{... | collective-permute-start | bytes 786440 | tf_op jit(solution)/shard_map/ppermute | solution.py:91
  53.4 38.1 %collective-permute-start.21 = (bf16[256,512]{1,0:T(8,128)(2,1)S(1)}, bf16[256,512]{1,0:T(8,128)(2,1)S(1)}, u32[]{:S(2)}, u32[]{:S(2)}) collective-permute-start(bf16[256,512]{1,0:T(8,128)(2,1)S(1)} %get-tuple-element.39), channel_id=1, source_target_pairs={{0,8},{24,16},{1,9},{25,17},{2,10},{26,18},{3,11},{27,19},{4,12},{... | collective-permute-start | bytes 786440 | tf_op jit(solution)/shard_map/ppermute | solution.py:91
  62.5 29.7 %collective-permute-start.18 = (bf16[256,512]{1,0:T(8,128)(2,1)S(1)}, bf16[256,512]{1,0:T(8,128)(2,1)S(1)}, u32[]{:S(2)}, u32[]{:S(2)}) collective-permute-start(bf16[256,512]{1,0:T(8,128)(2,1)S(1)} %get-tuple-element.37), channel_id=1, source_target_pairs={{0,8},{24,16},{1,9},{25,17},{2,10},{26,18},{3,11},{27,19},{4,12},{... | collective-permute-start | bytes 786440 | tf_op jit(solution)/shard_map/ppermute | solution.py:91
  71.7 21.4 %collective-permute-start.15 = (bf16[256,512]{1,0:T(8,128)(2,1)S(1)}, bf16[256,512]{1,0:T(8,128)(2,1)S(1)}, u32[]{:S(2)}, u32[]{:S(2)}) collective-permute-start(bf16[256,512]{1,0:T(8,128)(2,1)S(1)} %get-tuple-element.35), channel_id=1, source_target_pairs={{0,8},{24,16},{1,9},{25,17},{2,10},{26,18},{3,11},{27,19},{4,12},{... | collective-permute-start | bytes 786440 | tf_op jit(solution)/shard_map/ppermute | solution.py:91
  88.7 7.9 %collective-permute-start.12 = (bf16[256,512]{1,0:T(8,128)(2,1)S(1)}, bf16[256,512]{1,0:T(8,128)(2,1)S(1)}, u32[]{:S(2)}, u32[]{:S(2)}) collective-permute-start(bf16[256,512]{1,0:T(8,128)(2,1)S(1)} %get-tuple-element.33), channel_id=1, source_target_pairs={{0,8},{24,16},{1,9},{25,17},{2,10},{26,18},{3,11},{27,19},{4,12},{... | collective-permute-start | bytes 786440 | tf_op jit(solution)/shard_map/ppermute | solution.py:91
  90.1 11.4 %collective-permute-start.9 = (bf16[256,512]{1,0:T(8,128)(2,1)S(1)}, bf16[256,512]{1,0:T(8,128)(2,1)S(1)}, u32[]{:S(2)}, u32[]{:S(2)}) collective-permute-start(bf16[256,512]{1,0:T(8,128)(2,1)S(1)} %get-tuple-element.31), channel_id=1, source_target_pairs={{0,8},{24,16},{1,9},{25,17},{2,10},{26,18},{3,11},{27,19},{4,12},{... | collective-permute-start | bytes 786440 | tf_op jit(solution)/shard_map/ppermute | solution.py:91
  91.5 10.7 %collective-permute-start.28 = (bf16[256,512]{1,0:T(8,128)(2,1)S(1)}, bf16[256,512]{1,0:T(8,128)(2,1)S(1)}, u32[]{:S(2)}, u32[]{:S(2)}) collective-permute-start(bf16[256,512]{1,0:T(8,128)(2,1)S(1)} %fusion.6), channel_id=1, source_target_pairs={{8,16},{16,8},{9,17},{17,9},{10,18},{18,10},{11,19},{19,11},{12,20... | collective-permute-start | bytes 786440 | tf_op jit(solution)/shard_map/ppermute | solution.py:94
  92.3 10.8 %collective-permute-start.25 = (bf16[256,512]{1,0:T(8,128)(2,1)S(1)}, bf16[256,512]{1,0:T(8,128)(2,1)S(1)}, u32[]{:S(2)}, u32[]{:S(2)}) collective-permute-start(bf16[256,512]{1,0:T(8,128)(2,1)S(1)} %fusion.5), channel_id=1, source_target_pairs={{8,16},{16,8},{9,17},{17,9},{10,18},{18,10},{11,19},{19,11},{12,20... | collective-permute-start | bytes 786440 | tf_op jit(solution)/shard_map/ppermute | solution.py:94
  93.0 10.8 %collective-permute-start.22 = (bf16[256,512]{1,0:T(8,128)(2,1)S(1)}, bf16[256,512]{1,0:T(8,128)(2,1)S(1)}, u32[]{:S(2)}, u32[]{:S(2)}) collective-permute-start(bf16[256,512]{1,0:T(8,128)(2,1)S(1)} %fusion.4), channel_id=1, source_target_pairs={{8,16},{16,8},{9,17},{17,9},{10,18},{18,10},{11,19},{19,11},{12,20... | collective-permute-start | bytes 786440 | tf_op jit(solution)/shard_map/ppermute | solution.py:94
  96.6 8.6 %collective-permute-start.19 = (bf16[256,512]{1,0:T(8,128)(2,1)S(1)}, bf16[256,512]{1,0:T(8,128)(2,1)S(1)}, u32[]{:S(2)}, u32[]{:S(2)}) collective-permute-start(bf16[256,512]{1,0:T(8,128)(2,1)S(1)} %fusion.3), channel_id=1, source_target_pairs={{8,16},{16,8},{9,17},{17,9},{10,18},{18,10},{11,19},{19,11},{12,20... | collective-permute-start | bytes 786440 | tf_op jit(solution)/shard_map/ppermute | solution.py:94
  101.4 5.3 %collective-permute-start.16 = (bf16[256,512]{1,0:T(8,128)(2,1)S(1)}, bf16[256,512]{1,0:T(8,128)(2,1)S(1)}, u32[]{:S(2)}, u32[]{:S(2)}) collective-permute-start(bf16[256,512]{1,0:T(8,128)(2,1)S(1)} %fusion.2), channel_id=1, source_target_pairs={{8,16},{16,8},{9,17},{17,9},{10,18},{18,10},{11,19},{19,11},{12,20... | collective-permute-start | bytes 786440 | tf_op jit(solution)/shard_map/ppermute | solution.py:94
  102.2 5.9 %collective-permute-start.13 = (bf16[256,512]{1,0:T(8,128)(2,1)S(1)}, bf16[256,512]{1,0:T(8,128)(2,1)S(1)}, u32[]{:S(2)}, u32[]{:S(2)}) collective-permute-start(bf16[256,512]{1,0:T(8,128)(2,1)S(1)} %fusion.1), channel_id=1, source_target_pairs={{8,16},{16,8},{9,17},{17,9},{10,18},{18,10},{11,19},{19,11},{12,20... | collective-permute-start | bytes 786440 | tf_op jit(solution)/shard_map/ppermute | solution.py:94
  103.0 6.5 %collective-permute-start.10 = (bf16[256,512]{1,0:T(8,128)(2,1)S(1)}, bf16[256,512]{1,0:T(8,128)(2,1)S(1)}, u32[]{:S(2)}, u32[]{:S(2)}) collective-permute-start(bf16[256,512]{1,0:T(8,128)(2,1)S(1)} %fusion), channel_id=1, source_target_pairs={{8,16},{16,8},{9,17},{17,9},{10,18},{18,10},{11,19},{19,11},{12,20... | collective-permute-start | bytes 786440 | tf_op jit(solution)/shard_map/ppermute | solution.py:94
  103.8 16.5 %collective-permute-start.29 = (bf16[256,512]{1,0:T(8,128)(2,1)S(1)}, bf16[256,512]{1,0:T(8,128)(2,1)S(1)}, u32[]{:S(2)}, u32[]{:S(2)}) collective-permute-start(bf16[256,512]{1,0:T(8,128)(2,1)S(1)} %add_convert_fusion.final_ref), channel_id=1, source_target_pairs={{8,0},{16,24},{9,1},{17,25},{10,2},{18,26},{11,3},{19,27},{12,4},{... | collective-permute-start | bytes 786440 | tf_op jit(solution)/shard_map/ppermute | solution.py:98
  105.3 20.6 %collective-permute-start.26 = (bf16[256,512]{1,0:T(8,128)(2,1)S(1)}, bf16[256,512]{1,0:T(8,128)(2,1)S(1)}, u32[]{:S(2)}, u32[]{:S(2)}) collective-permute-start(bf16[256,512]{1,0:T(8,128)(2,1)S(1)} %add_convert_fusion.1.final_ref), channel_id=1, source_target_pairs={{8,0},{16,24},{9,1},{17,25},{10,2},{18,26},{11,3},{19,27},{12,4},{... | collective-permute-start | bytes 786440 | tf_op jit(solution)/shard_map/ppermute | solution.py:98
  106.7 27.4 %collective-permute-start.23 = (bf16[256,512]{1,0:T(8,128)(2,1)S(1)}, bf16[256,512]{1,0:T(8,128)(2,1)}, u32[]{:S(2)}, u32[]{:S(2)}) collective-permute-start(bf16[256,512]{1,0:T(8,128)(2,1)S(1)} %add_convert_fusion.2.final_ref), channel_id=1, source_target_pairs={{8,0},{16,24},{9,1},{17,25},{10,2},{18,26},{11,3},{19,27},{12,4},{... | collective-permute-start | bytes 786440 | tf_op jit(solution)/shard_map/ppermute | solution.py:98
  108.1 29.1 %collective-permute-start.20 = (bf16[256,512]{1,0:T(8,128)(2,1)S(1)}, bf16[256,512]{1,0:T(8,128)(2,1)}, u32[]{:S(2)}, u32[]{:S(2)}) collective-permute-start(bf16[256,512]{1,0:T(8,128)(2,1)S(1)} %add_convert_fusion.3.final_ref), channel_id=1, source_target_pairs={{8,0},{16,24},{9,1},{17,25},{10,2},{18,26},{11,3},{19,27},{12,4},{... | collective-permute-start | bytes 786440 | tf_op jit(solution)/shard_map/ppermute | solution.py:98
  109.6 33.7 %collective-permute-start.17 = (bf16[256,512]{1,0:T(8,128)(2,1)S(1)}, bf16[256,512]{1,0:T(8,128)(2,1)}, u32[]{:S(2)}, u32[]{:S(2)}) collective-permute-start(bf16[256,512]{1,0:T(8,128)(2,1)S(1)} %add_convert_fusion.4.final_ref), channel_id=1, source_target_pairs={{8,0},{16,24},{9,1},{17,25},{10,2},{18,26},{11,3},{19,27},{12,4},{... | collective-permute-start | bytes 786440 | tf_op jit(solution)/shard_map/ppermute | solution.py:98
  120.3 28.5 %collective-permute-start.14 = (bf16[256,512]{1,0:T(8,128)(2,1)S(1)}, bf16[256,512]{1,0:T(8,128)(2,1)S(1)}, u32[]{:S(2)}, u32[]{:S(2)}) collective-permute-start(bf16[256,512]{1,0:T(8,128)(2,1)S(1)} %add_convert_fusion.5.final_ref), channel_id=1, source_target_pairs={{8,0},{16,24},{9,1},{17,25},{10,2},{18,26},{11,3},{19,27},{12,4},{... | collective-permute-start | bytes 786440 | tf_op jit(solution)/shard_map/ppermute | solution.py:98
  125.9 27.6 %collective-permute-start.11 = (bf16[256,512]{1,0:T(8,128)(2,1)S(1)}, bf16[256,512]{1,0:T(8,128)(2,1)S(1)}, u32[]{:S(2)}, u32[]{:S(2)}) collective-permute-start(bf16[256,512]{1,0:T(8,128)(2,1)S(1)} %add_convert_fusion.6.final_ref), channel_id=1, source_target_pairs={{8,0},{16,24},{9,1},{17,25},{10,2},{18,26},{11,3},{19,27},{12,4},{... | collective-permute-start | bytes 786440 | tf_op jit(solution)/shard_map/ppermute | solution.py:98
  127.3 2.0 %copy-start = (bf16[2,256,3584]{2,1,0:T(8,128)(2,1)S(1)}, bf16[2,256,3584]{2,1,0:T(8,128)(2,1)}, u32[]{:S(2)}) copy-start(bf16[2,256,3584]{2,1,0:T(8,128)(2,1)} %stored_ref.13) | copy-start | bytes 11010052
  130.7 2.0 %copy-start.1 = (bf16[2,256,3584]{2,1,0:T(8,128)(2,1)S(1)}, bf16[2,256,3584]{2,1,0:T(8,128)(2,1)}, u32[]{:S(2)}) copy-start(bf16[2,256,3584]{2,1,0:T(8,128)(2,1)} %stored_ref.13) | copy-start | bytes 11010052
  154.9 1.6 collective-permute-start.30
  156.6 5.6 %collective-permute-start.31 = (f32[4,2,8,512]{3,2,1,0:T(8,128)S(1)}, f32[4,2,8,512]{3,2,1,0:T(8,128)S(1)}, u32[]{:S(2)}, u32[]{:S(2)}) collective-permute-start(f32[4,2,8,512]{3,2,1,0:T(8,128)S(1)} %dynamic-slice_bitcast_fusion.1), channel_id=1, source_target_pairs={{0,2},{1,3},{2,0},{3,1},{4,6},{5,7},{6,4},{7,5},{8,10},{9,11},{10,... | collective-permute-start | bytes 393224 | tf_op jit(solution)/shard_map/ppermute | solution.py:15
  162.2 4.3 %collective-permute-start.32 = (f32[4,1,8,512]{3,2,1,0:T(8,128)S(1)}, f32[4,1,8,512]{3,2,1,0:T(8,128)S(1)}, u32[]{:S(2)}, u32[]{:S(2)}) collective-permute-start(f32[4,1,8,512]{3,2,1,0:T(8,128)S(1)} %constant_dynamic-slice_fusion), channel_id=1, source_target_pairs={{0,4},{1,5},{2,6},{3,7},{4,0},{5,1},{6,2},{7,3},{8,12},{9,13},{10,... | collective-permute-start | bytes 196616 | tf_op jit(solution)/shard_map/ppermute | solution.py:15
  167.2 5.5 %collective-permute-start.33 = (f32[1,8,512]{2,1,0:T(8,128)S(1)}, f32[1,8,512]{2,1,0:T(8,128)S(1)}, u32[]{:S(2)}, u32[]{:S(2)}) collective-permute-start(f32[1,8,512]{2,1,0:T(8,128)S(1)} %get-tuple-element.60), channel_id=1, source_target_pairs={{0,8},{8,16},{16,24},{24,0},{1,9},{9,17},{17,25},{25,1},{2,10},{10... | collective-permute-start | bytes 49160 | tf_op jit(solution)/shard_map/ppermute | solution.py:241
  168.3 4.6 %collective-permute-start.34 = (f32[1,8,512]{2,1,0:T(8,128)S(1)}, f32[1,8,512]{2,1,0:T(8,128)S(1)}, u32[]{:S(2)}, u32[]{:S(2)}) collective-permute-start(f32[1,8,512]{2,1,0:T(8,128)S(1)} %get-tuple-element.59), channel_id=1, source_target_pairs={{0,16},{8,24},{16,0},{24,8},{1,17},{9,25},{17,1},{25,9},{2,18},{10... | collective-permute-start | bytes 49160 | tf_op jit(solution)/shard_map/ppermute | solution.py:241
  169.7 4.0 %collective-permute-start.35 = (f32[1,8,512]{2,1,0:T(8,128)S(1)}, f32[1,8,512]{2,1,0:T(8,128)S(1)}, u32[]{:S(2)}, u32[]{:S(2)}) collective-permute-start(f32[1,8,512]{2,1,0:T(8,128)S(1)} %get-tuple-element.58), channel_id=1, source_target_pairs={{0,24},{8,0},{16,8},{24,16},{1,25},{9,1},{17,9},{25,17},{2,26},{10... | collective-permute-start | bytes 49160 | tf_op jit(solution)/shard_map/ppermute | solution.py:241
  172.7 1.0 copy-start.3
  173.0 0.7 copy-start.4
  173.7 0.6 copy-start.5

commit v2 on v1

v2 whole, which is shorter than its diff:
```python
import functools

import jax
import jax.numpy as jnp
from jax import lax
from jax.experimental import pallas as pl
from jax.experimental.pallas import tpu as pltpu
from jax.sharding import PartitionSpec as P

PARTS = 5
STEPS = 7
SLOTS = 4
LANES = 128
VMEM = pl.BlockSpec(memory_space=pltpu.VMEM)
ANY = pl.BlockSpec(memory_space=pl.ANY)
SMEM = pl.BlockSpec(memory_space=pltpu.SMEM)


def flipped(array, bit, count):
    return lax.ppermute(array, "col", [(c, c ^ bit) for c in range(count)])


def gathered(new_keys, col_count, col_index):
    rows = new_keys.shape[0]
    if col_count != 8:
        return [lax.all_gather(new_keys, "col", axis=0, tiled=True)], [jnp.int32(0)]
    half = rows // 2
    by_x = flipped(new_keys, 2, 8)
    by_y = flipped(new_keys, 4, 8)
    by_core = flipped(new_keys, 1, 8)
    low = flipped(by_x[:half], 4, 8)
    high = flipped(by_y[half:], 2, 8)
    x_core = flipped(by_x, 1, 8)
    y_core = flipped(by_y, 1, 8)
    low_core = flipped(low, 1, 8)
    high_core = flipped(high, 1, 8)
    pieces = [new_keys, by_core, by_x, x_core, by_y, y_core, low, high, low_core, high_core]
    of = [0, 1, 2, 3, 4, 5, 6, 6, 7, 7]
    within = [0] * 7 + [half, 0, half]
    return pieces, [(col_index ^ f) * rows + w for f, w in zip(of, within)]


def ranges(columns):
    tiles = columns // LANES
    count = min(PARTS, tiles)
    ends = [(tiles * (i + 1) + count // 2) // count * LANES for i in range(count)]
    return list(zip([0] + ends[:-1], ends))


def params():
    return pltpu.CompilerParams(vmem_limit_bytes=32 * 2**20)


def assemble_kernel(count, starts_ref, *refs):
    keys_ref = refs[count]
    for i, piece in enumerate(refs[:count]):
        keys_ref[pl.ds(pl.multiple_of(starts_ref[i], 16), piece.shape[0]), :] = piece[...]


def assembled(pieces, starts, keys):
    return pl.pallas_call(
        functools.partial(assemble_kernel, len(pieces)),
        in_specs=[SMEM] + [VMEM] * len(pieces),
        out_specs=VMEM,
        out_shape=jax.ShapeDtypeStruct((keys, pieces[0].shape[1]), pieces[0].dtype),
        compiler_params=params(),
        name="assemble",
    )(starts, *pieces)


def product_kernel(left, keys_ref, weights_ref, after_ref, wide_ref, sent_ref, held_ref, arrived):
    wide = wide_ref.shape[1]
    deep = held_ref.shape[1]

    def copy(step):
        return pltpu.make_async_copy(
            weights_ref.at[pl.ds(step * deep, deep), pl.ds(left, wide)],
            held_ref.at[step % SLOTS],
            arrived.at[step % SLOTS],
        )

    for step in range(min(SLOTS, STEPS)):
        copy(step).start()
    for step in range(STEPS):
        copy(step).wait()
        part = jnp.dot(
            keys_ref[:, step * deep : (step + 1) * deep],
            held_ref[step % SLOTS],
            preferred_element_type=jnp.float32,
        )
        if step + SLOTS < STEPS:
            copy(step + SLOTS).start()
        total = part if step == 0 else wide_ref[...] + part
        wide_ref[...] = total
        if step == STEPS - 1:
            sent_ref[...] = total.astype(sent_ref.dtype)


def product(keys, weights, span, wire, after):
    depth = weights.shape[0]
    rows, wide = keys.shape[0], span[1] - span[0]
    return pl.pallas_call(
        functools.partial(product_kernel, span[0]),
        in_specs=[VMEM, ANY, ANY],
        out_specs=[VMEM, VMEM],
        out_shape=[
            jax.ShapeDtypeStruct((rows, wide), jnp.float32),
            jax.ShapeDtypeStruct((rows, wide), wire),
        ],
        scratch_shapes=[
            pltpu.VMEM((SLOTS, depth // STEPS, wide), weights.dtype),
            pltpu.SemaphoreType.DMA((SLOTS,)),
        ],
        compiler_params=params(),
        cost_estimate=pl.CostEstimate(
            flops=2 * rows * depth * wide,
            bytes_accessed=2 * depth * (rows + wide) + 6 * rows * wide,
            transcendentals=0,
        ),
        name="product",
    )(keys, weights, after)


def add_kernel(wide_ref, came_ref, after_ref, total_ref, sent_ref):
    total = wide_ref[...] + came_ref[...].astype(jnp.float32)
    total_ref[...] = total
    sent_ref[...] = total.astype(sent_ref.dtype)


def added(wide, came, wire, after):
    return pl.pallas_call(
        add_kernel,
        in_specs=[VMEM, VMEM, ANY],
        out_specs=[VMEM, VMEM],
        out_shape=[jax.ShapeDtypeStruct(wide.shape, jnp.float32), jax.ShapeDtypeStruct(wide.shape, wire)],
        compiler_params=params(),
        name="added",
    )(wide, came, after)


def final_kernel(wide_ref, came_ref, after_ref, final_ref):
    final_ref[...] = (wide_ref[...] + came_ref[...].astype(jnp.float32)).astype(final_ref.dtype)


def finished(wide, came, after):
    return pl.pallas_call(
        final_kernel,
        in_specs=[VMEM, VMEM, ANY],
        out_specs=VMEM,
        out_shape=jax.ShapeDtypeStruct(wide.shape, jnp.bfloat16),
        compiler_params=params(),
        name="finished",
    )(wide, came, after)


def contract_kernel(span, done, at_ref, final_ref, came_ref, stored_ref, after_ref, *refs):
    before = refs[: done[0]]
    pieces = refs[done[0] : done[0] + done[1]]
    terms_ref, whitened_ref, rows_ref = refs[-3:]
    start = at_ref[1]

    @pl.when(at_ref[0] != 0)
    def _():
        rows_ref[...] = final_ref[...]

    @pl.when(at_ref[0] == 0)
    def _():
        rows_ref[...] = came_ref[...]

    batches, slots, _ = stored_ref.shape
    wide = span[1] - span[0]
    term = lax.dot_general(
        rows_ref[...],
        stored_ref[:, :, span[0] : span[1]].reshape(batches * slots, wide),
        (((1,), (1,)), ((), ())),
        preferred_element_type=jnp.float32,
    )
    terms_ref[...] = before[0][...] + term if before else term
    block = whitened_ref.shape[0]
    left = 0
    for piece in pieces:
        whitened_ref[:, left : left + piece.shape[1]] = piece[...]
        left += piece.shape[1]
    whitened_ref[:, left : left + wide] = rows_ref[pl.ds(pl.multiple_of(start, 16), block), :]


def contract(at, final, came, stored, terms, pieces, span, block, after):
    keys, wide = final.shape
    sums = stored.shape[0] * stored.shape[1]
    before = [] if terms is None else [terms]
    columns = wide + sum(p.shape[1] for p in pieces)
    return pl.pallas_call(
        functools.partial(contract_kernel, span, (len(before), len(pieces))),
        in_specs=[SMEM, VMEM, VMEM, VMEM, ANY] + [VMEM] * (len(before) + len(pieces)),
        out_specs=[VMEM, VMEM],
        out_shape=[
            jax.ShapeDtypeStruct((keys, sums), jnp.float32),
            jax.ShapeDtypeStruct((block, columns), jnp.bfloat16),
        ],
        scratch_shapes=[pltpu.VMEM((keys, wide), jnp.bfloat16)],
        compiler_params=params(),
        name="contract",
    )(at, final, came, stored, after, *before, *pieces)


def in_order(row_count, wire, inner, make, spans, close):
    half = row_count // 2
    count = len(spans)
    made, after = {}, None

    def sum_of(part, hop):
        nonlocal after
        wide, came = made[part]
        if hop < half - 1:
            wide, sent = added(wide, came, wire, after)
            after = sent
            made[part] = (wide, step_in(sent, hop + 1))
        elif hop == half - 1:
            final = finished(wide, came, after)
            after = final
            made[part] = (final, step_out(final, 0))
        else:
            final, came = made[part]
            final = jnp.where(inner[hop - half], final, came)
            made[part] = (final, step_out(final, hop - half + 1))

    def step_in(sent, hop):
        if hop == half - 1:
            pairs = [(half - 1, half), (half, half - 1)]
        else:
            pairs = [(hop, hop + 1), (row_count - 1 - hop, row_count - 2 - hop)]
        return lax.ppermute(sent, "row", pairs)

    def step_out(final, hop):
        low, high = half - 1 - hop, half + hop
        if low == 0:
            return final
        return lax.ppermute(final, "row", [(low, low - 1), (high, high + 1)])

    stages = 2 * half - 2
    for tick in range(count + stages + 2):
        for hop in range(stages):
            part = tick - 2 - hop
            if 0 <= part < count:
                sum_of(part, hop)
        if tick < count:
            wide, sent = make(tick, after)
            after = sent
            made[tick] = (wide, step_in(sent, 0))
        part = tick - 2 - stages
        if 0 <= part < count:
            after = close(part, *made[part], after)


def select_kernel(count, row_ref, batch_ref, used_ref, length_ref, slot_ref, *refs):
    parts, out_ref, held_ref = refs[:count], refs[count], refs[count + 1]
    batches, rows, slots = held_ref.shape[1:]
    for i, part in enumerate(parts):
        for b in range(batches):
            held_ref[i, b] = part[0, :, b * slots : (b + 1) * slots]
    row = row_ref[0]
    column = lax.broadcasted_iota(jnp.int32, (rows, slots), 1)
    for place in range(out_ref.shape[1]):
        batch = batch_ref[row, place]
        slot = slot_ref[batch]
        owner = lax.div(slot, batches)
        shift = lax.rem(row - owner + count, count)
        length = jnp.where(place < used_ref[row], length_ref[batch], 0)
        value = held_ref[shift, slot - owner * batches]
        out_ref[0, place] = jnp.where(column < length, value, 0.0)


def selected(parts, row_index, pair_batch, pair_count, batch_length, batch_slot, batches):
    count = len(parts)
    _, rows, wide = parts[0].shape
    slots = wide // batches
    places = pair_batch.shape[1]
    return pl.pallas_call(
        functools.partial(select_kernel, count),
        in_specs=[SMEM] * 5 + [VMEM] * count,
        out_specs=VMEM,
        out_shape=jax.ShapeDtypeStruct((1, places, rows, slots), jnp.float32),
        scratch_shapes=[pltpu.VMEM((count, batches, rows, slots), jnp.float32)],
        name="select",
    )(row_index[None], pair_batch, pair_count, batch_length, batch_slot, *parts)


def shards(new_keys, precision, stored_keys, pair_batch, pair_count, batch_length, batch_slot):
    row_count = lax.axis_size("row")
    col_count = lax.axis_size("col")
    row_index = lax.axis_index("row")
    col_index = lax.axis_index("col")
    total_keys = new_keys.shape[0] * col_count
    block = total_keys // row_count
    batches = stored_keys.shape[0]
    half = row_count // 2
    wire = jnp.bfloat16 if row_count <= 4 else jnp.float32

    away = jnp.where(row_index < half, half - 1 - row_index, row_index - half)
    inner = [away <= hop for hop in range(half)]
    at = jnp.stack([(away < half - 1).astype(jnp.int32), row_index * block])

    pieces, starts = gathered(new_keys, col_count, col_index)
    keys = assembled(pieces, jnp.stack(starts), total_keys)
    spans = ranges(precision.shape[1])
    whitened = []
    terms = None

    def make(part, after):
        return product(keys, precision, spans[part], wire, at if after is None else after)

    def close(part, final, came, after):
        nonlocal terms
        before = whitened if part == len(spans) - 1 else []
        terms, rows = contract(at, final, came, stored_keys, terms, before, spans[part], block, after)
        whitened.append(rows)
        return rows

    in_order(row_count, wire, inner, make, spans, close)

    share = block // col_count
    sums = terms.reshape(row_count, col_count, share, terms.shape[1])
    bit = 1
    while bit < col_count:
        if col_count == 8 and bit == 2:
            other = [lax.dynamic_index_in_dim(sums, (col_index // 2) ^ f, 1, keepdims=False) for f in range(4)]
            sums = other[0] + sum(flipped(other[f], 2 * f, col_count) for f in (3, 2, 1))
            sums = sums[:, None]
            break
        pairs = sums.reshape(row_count, sums.shape[1] // 2, 2, share, sums.shape[3])
        mine = (col_index // bit) % 2
        kept = lax.dynamic_index_in_dim(pairs, mine, 2, keepdims=False)
        left = lax.dynamic_index_in_dim(pairs, 1 - mine, 2, keepdims=False)
        sums = kept + flipped(left, bit, col_count)
        bit *= 2
    sums = sums[:, 0]
    parts = []
    for shift in range(row_count):
        part = lax.dynamic_slice_in_dim(sums, (row_index + shift) % row_count, 1, 0)
        if shift:
            part = lax.ppermute(part, "row", [(r, (r + shift) % row_count) for r in range(row_count)])
        parts.append(part)
    shares = selected(parts, row_index, pair_batch, pair_count, batch_length, batch_slot, batches)
    return (whitened[-1], shares)


def solution(mesh):
    placed = (P("col", "row"), P("row", "col"), P("row", None, "col"), P(), P(), P(), P())
    return jax.shard_map(
        shards,
        mesh=mesh,
        in_specs=placed,
        out_specs=(P("row", "col"), P("row", None, "col", None)),
        check_vma=False,
    )
```

time: 178 us -> 155 us (0.87)
  Pallas kernels: 69.3 us -> 38.2 us
  waiting for transfers between devices: 56.7 us -> 64.9 us
  starting transfers between devices: 41.3 us -> 45.5 us
  local copies, waits for them, and re-layouts: 6.48 us -> 4.47 us
    pallas_call x15 -> x22, Pallas kernels: 69.3 us -> 38.2 us  [the longest x5 29.4 us: product(): pl.pallas_call(functools.partial(product_kernel, span[0]), in_specs=[VMEM...]
    ppermute x21 -> x15, waiting for transfers between devices: 31.7 us -> 39.9 us  [the longest x5 27.9 us: step_out(): return lax.ppermute(final, 'row', [(low, low - 1), (high, high + 1)])]
    ppermute x21 -> x15, starting transfers between devices: 25.1 us -> 29.7 us  [the longest x10 23 us: step_in(): return lax.ppermute(sent, 'row', pairs)]
    unnamed x12, local copies, waits for them, and re-layouts: 5.69 us -> 3.66 us
    ppermute x12 -> x13, waiting for transfers between devices: 23.5 us -> 22.1 us  [flipped(): return lax.ppermute(array, 'col', [(c, c ^ bit) for c in range(count)])]
    ppermute x12 -> x13, starting transfers between devices: 11.2 us -> 12.1 us  [flipped(): return lax.ppermute(array, 'col', [(c, c ^ bit) for c in range(count)])]
  transfers between devices with their start and end apart: 36 -> 31, of which waited for: 19 -> 14; matrix products, arithmetic and copies ran while one was open for 1% -> 0% of each run, Pallas kernels for 33% -> 18%
where the time goes in v2:
time: 155 us; the launch traced here: 154 us
  waiting for transfers between devices  64.9 us (42%)
  starting transfers between devices  45.5 us (29%)
  Pallas kernels  38.2 us (25%)
  local copies, waits for them, and re-layouts  4.47 us (3%)
    pallas_call x5, Pallas kernels, product(): pl.pallas_call(functools.partial(product_kernel, span[0]), in_specs=[VMEM...  29.4 us
    ppermute x5, waiting for transfers between devices, step_out(): return lax.ppermute(final, 'row', [(low, low - 1), (high, high + 1)])  27.9 us
    ppermute x10, starting transfers between devices, step_in(): return lax.ppermute(sent, 'row', pairs)  23 us
    ppermute x13, waiting for transfers between devices, flipped(): return lax.ppermute(array, 'col', [(c, c ^ bit) for c in range(count)])  22.1 us
    ppermute x13, starting transfers between devices, flipped(): return lax.ppermute(array, 'col', [(c, c ^ bit) for c in range(count)])  12.1 us
    ppermute x10, waiting for transfers between devices, step_in(): return lax.ppermute(sent, 'row', pairs)  12 us
    ppermute x5, starting transfers between devices, step_out(): return lax.ppermute(final, 'row', [(low, low - 1), (high, high + 1)])  6.64 us
    pallas_call x5, Pallas kernels, contract(): pl.pallas_call(functools.partial(contract_kernel, span, (len(before), len...  5.61 us
  transfers between devices with their start and end apart: 31, of which 14 were waited for; matrix products, arithmetic and copies ran while one was open for 0% of the time, Pallas kernels for 18%

profile of v2, /device:TPU:0, one launch (start us, length us, event | category | flops | bytes accessed | tf_op | source)
XLA Modules:
  0.0 154.4 jit_solution(11911179696909510318)
XLA Ops:
  0.6 3.0 %collective-permute-start.1 = (bf16[32,7168]{1,0:T(8,128)(2,1)}, bf16[32,7168]{1,0:T(8,128)(2,1)S(1)}, u32[]{:S(2)}, u32[]{:S(2)}) collective-permute-start(bf16[32,7168]{1,0:T(8,128)(2,1)} %refs_0_.1), channel_id=1, source_target_pairs={{0,2},{1,3},{2,0},{3,1},{4,6},{5,7},{6,4},{7,5},{8,10},{9,11},{10,... | collective-permute-start | bytes 1376264 | tf_op jit(solution)/shard_map/ppermute | solution.py:20
  3.6 1.5 collective-permute-start.3
  5.2 9.2 %collective-permute-done.1.refs_2_ = bf16[32,7168]{1,0:T(8,128)(2,1)S(1)} collective-permute-done((bf16[32,7168]{1,0:T(8,128)(2,1)}, bf16[32,7168]{1,0:T(8,128)(2,1)S(1)}, u32[]{:S(2)}, u32[]{:S(2)}) %collective-permute-start.1) | collective-permute-done | bytes 458784 | tf_op jit(solution)/shard_map/ppermute | solution.py:20
  14.4 1.8 %collective-permute-start.5 = (bf16[16,7168]{1,0:T(8,128)(2,1)S(1)}, bf16[16,7168]{1,0:T(8,128)(2,1)S(1)}, u32[]{:S(2)}, u32[]{:S(2)}) collective-permute-start(bf16[16,7168]{1,0:T(8,128)(2,1)S(1)} %slice.8), channel_id=1, source_target_pairs={{0,4},{1,5},{2,6},{3,7},{4,0},{5,1},{6,2},{7,3},{8,12},{9,13},{10,... | collective-permute-start | bytes 688136 | tf_op jit(solution)/shard_map/ppermute | solution.py:20
  16.2 0.5 collective-permute-start.4
  16.7 1.6 %collective-permute-start.6 = (bf16[16,7168]{1,0:T(8,128)(2,1)S(1)}, bf16[16,7168]{1,0:T(8,128)(2,1)S(1)}, u32[]{:S(2)}, u32[]{:S(2)}) collective-permute-start(bf16[16,7168]{1,0:T(8,128)(2,1)S(1)} %slice.9), channel_id=1, source_target_pairs={{0,2},{1,3},{2,0},{3,1},{4,6},{5,7},{6,4},{7,5},{8,10},{9,11},{10,... | collective-permute-start | bytes 688136 | tf_op jit(solution)/shard_map/ppermute | solution.py:20
  18.3 2.9 %collective-permute-done.5.refs_6_ = bf16[16,7168]{1,0:T(8,128)(2,1)S(1)} collective-permute-done((bf16[16,7168]{1,0:T(8,128)(2,1)S(1)}, bf16[16,7168]{1,0:T(8,128)(2,1)S(1)}, u32[]{:S(2)}, u32[]{:S(2)}) %collective-permute-start.5) | collective-permute-done | bytes 229408 | tf_op jit(solution)/shard_map/ppermute | solution.py:20
  21.2 3.1 %collective-permute-done.6.refs_7_ = bf16[16,7168]{1,0:T(8,128)(2,1)S(1)} collective-permute-done((bf16[16,7168]{1,0:T(8,128)(2,1)S(1)}, bf16[16,7168]{1,0:T(8,128)(2,1)S(1)}, u32[]{:S(2)}, u32[]{:S(2)}) %collective-permute-start.6) | collective-permute-done | bytes 229408 | tf_op jit(solution)/shard_map/ppermute | solution.py:20
  24.3 0.1 stack.59.starts_ref
  24.4 0.1 pad_add_fusion.after_ref.at_ref
  24.5 1.3 collective-permute-done.8.refs_9_
  25.8 1.0 copy-done.2
  26.8 0.8 assemble.1.keys_ref
  27.6 6.1 %product.5 = (f32[256,768]{1,0:T(8,128)S(1)}, bf16[256,768]{1,0:T(8,128)(2,1)S(1)}) custom-call(bf16[256,7168]{1,0:T(8,128)(2,1)S(1)} %assemble.1.keys_ref, bf16[7168,3584]{1,0:T(8,128)(2,1)} %weights_ref.9, s32[2]{0:T(128)S(1)} %pad_add_fusion.after_ref.at_ref), custom_call_target="tpu_custom_call" | custom-call | flops 2818572288 | bytes 15859712 | tf_op jit(solution)/shard_map/product/pallas_call | solution.py:102
  33.8 3.5 %collective-permute-start.10 = (bf16[256,768]{1,0:T(8,128)(2,1)S(1)}, bf16[256,768]{1,0:T(8,128)(2,1)S(1)}, u32[]{:S(2)}, u32[]{:S(2)}) collective-permute-start(bf16[256,768]{1,0:T(8,128)(2,1)S(1)} %get-tuple-element.32.after_ref), channel_id=1, source_target_pairs={{0,8},{24,16},{1,9},{25,17},{2,10},{26,18},{3,11},{27,19},{4,12},{... | collective-permute-start | bytes 1179656 | tf_op jit(solution)/shard_map/ppermute | solution.py:232
  37.3 5.4 %product.6 = (f32[256,640]{1,0:T(8,128)S(1)}, bf16[256,640]{1,0:T(8,128)(2,1)S(1)}) custom-call(bf16[256,7168]{1,0:T(8,128)(2,1)S(1)} %assemble.1.keys_ref, bf16[7168,3584]{1,0:T(8,128)(2,1)} %weights_ref.9, bf16[256,768]{1,0:T(8,128)(2,1)S(1)} %get-tuple-element.32.after_ref), custom_call_target="tpu_custom_call" | custom-call | flops 2348810240 | bytes 13828096 | tf_op jit(solution)/shard_map/product/pallas_call | solution.py:102
  42.7 1.3 collective-permute-start.9
  44.0 2.7 %collective-permute-done.10.came_ref = bf16[256,768]{1,0:T(8,128)(2,1)S(1)} collective-permute-done((bf16[256,768]{1,0:T(8,128)(2,1)S(1)}, bf16[256,768]{1,0:T(8,128)(2,1)S(1)}, u32[]{:S(2)}, u32[]{:S(2)}) %collective-permute-start.10) | collective-permute-done | bytes 393248 | tf_op jit(solution)/shard_map/ppermute | solution.py:232
  46.7 0.1 added.5
  46.8 0.7 collective-permute-start.13
  47.5 6.1 %product.7 = (f32[256,768]{1,0:T(8,128)S(1)}, bf16[256,768]{1,0:T(8,128)(2,1)S(1)}) custom-call(bf16[256,7168]{1,0:T(8,128)(2,1)S(1)} %assemble.1.keys_ref, bf16[7168,3584]{1,0:T(8,128)(2,1)} %weights_ref.9, bf16[256,768]{1,0:T(8,128)(2,1)S(1)} %get-tuple-element.36.after_ref), custom_call_target="tpu_custom_call" | custom-call | flops 2818572288 | bytes 15859712 | tf_op jit(solution)/shard_map/product/pallas_call | solution.py:102
  53.7 7.2 %collective-permute-start.12 = (bf16[256,768]{1,0:T(8,128)(2,1)S(1)}, bf16[256,768]{1,0:T(8,128)(2,1)S(1)}, u32[]{:S(2)}, u32[]{:S(2)}) collective-permute-start(bf16[256,768]{1,0:T(8,128)(2,1)S(1)} %get-tuple-element.37.after_ref), channel_id=1, source_target_pairs={{0,8},{24,16},{1,9},{25,17},{2,10},{26,18},{3,11},{27,19},{4,12},{... | collective-permute-start | bytes 1179656 | tf_op jit(solution)/shard_map/ppermute | solution.py:232
  60.9 0.1 added.6
  61.0 0.7 collective-permute-start.11
  61.8 1.5 collective-permute-start.18
  63.3 5.4 %product.8 = (f32[256,640]{1,0:T(8,128)S(1)}, bf16[256,640]{1,0:T(8,128)(2,1)S(1)}) custom-call(bf16[256,7168]{1,0:T(8,128)(2,1)S(1)} %assemble.1.keys_ref, bf16[7168,3584]{1,0:T(8,128)(2,1)} %weights_ref.9, bf16[256,768]{1,0:T(8,128)(2,1)S(1)} %finished.5.after_ref.final_ref), custom_call_target="tpu_custom_call" | custom-call | flops 2348810240 | bytes 13828096 | tf_op jit(solution)/shard_map/product/pallas_call | solution.py:102
  68.7 0.1 added.7
  68.8 0.7 collective-permute-start.16
  69.6 6.3 %product.9 = (f32[256,768]{1,0:T(8,128)S(1)}, bf16[256,768]{1,0:T(8,128)(2,1)S(1)}) custom-call(bf16[256,7168]{1,0:T(8,128)(2,1)S(1)} %assemble.1.keys_ref, bf16[7168,3584]{1,0:T(8,128)(2,1)} %weights_ref.9, bf16[256,640]{1,0:T(8,128)(2,1)S(1)} %finished.6.after_ref.final_ref), custom_call_target="tpu_custom_call" | custom-call | flops 2818572288 | bytes 15859712 | tf_op jit(solution)/shard_map/product/pallas_call | solution.py:102
  75.9 6.3 %collective-permute-start.14 = (bf16[256,768]{1,0:T(8,128)(2,1)S(1)}, bf16[256,768]{1,0:T(8,128)(2,1)S(1)}, u32[]{:S(2)}, u32[]{:S(2)}) collective-permute-start(bf16[256,768]{1,0:T(8,128)(2,1)S(1)} %get-tuple-element.45.after_ref), channel_id=1, source_target_pairs={{0,8},{24,16},{1,9},{25,17},{2,10},{26,18},{3,11},{27,19},{4,12},{... | collective-permute-start | bytes 1179656 | tf_op jit(solution)/shard_map/ppermute | solution.py:232
  82.1 1.3 collective-permute-start.17
  83.5 1.3 collective-permute-start.15
  84.8 1.0 contract.5
  85.8 9.3 %collective-permute-done.17.came_ref = bf16[256,640]{1,0:T(8,128)(2,1)S(1)} collective-permute-done((bf16[256,640]{1,0:T(8,128)(2,1)S(1)}, bf16[256,640]{1,0:T(8,128)(2,1)S(1)}, u32[]{:S(2)}, u32[]{:S(2)}) %collective-permute-start.17) | collective-permute-done | bytes 327712 | tf_op jit(solution)/shard_map/ppermute | solution.py:232
  95.0 0.1 added.8
  95.2 0.1 finished.7.after_ref.final_ref
  95.3 1.3 collective-permute-start.20
  96.6 1.0 contract.6
  97.6 0.1 added.9
  97.7 0.7 collective-permute-start.19
  98.4 0.7 collective-permute-start.21
  99.2 5.8 %collective-permute-done.20.came_ref = bf16[256,768]{1,0:T(8,128)(2,1)S(1)} collective-permute-done((bf16[256,768]{1,0:T(8,128)(2,1)S(1)}, bf16[256,768]{1,0:T(8,128)(2,1)S(1)}, u32[]{:S(2)}, u32[]{:S(2)}) %collective-permute-start.20) | collective-permute-done | bytes 393248 | tf_op jit(solution)/shard_map/ppermute | solution.py:238
  104.9 1.0 contract.7
  106.0 1.3 collective-permute-start.22
  107.3 1.3 collective-permute-start.23
  108.6 22.1 %collective-permute-done.23.came_ref = bf16[256,640]{1,0:T(8,128)(2,1)S(1)} collective-permute-done((bf16[256,640]{1,0:T(8,128)(2,1)S(1)}, bf16[256,640]{1,0:T(8,128)(2,1)S(1)}, u32[]{:S(2)}, u32[]{:S(2)}) %collective-permute-start.23) | collective-permute-done | bytes 327712 | tf_op jit(solution)/shard_map/ppermute | solution.py:238
  130.7 2.0 %copy-done.1 = bf16[2,256,3584]{2,1,0:T(8,128)(2,1)S(1)} copy-done((bf16[2,256,3584]{2,1,0:T(8,128)(2,1)S(1)}, bf16[2,256,3584]{2,1,0:T(8,128)(2,1)}, u32[]{:S(2)}) %copy-start.1) | copy-done | bytes 3670040
  132.7 1.0 contract.8
  133.7 1.7 %contract.9 = (f32[256,512]{1,0:T(8,128)S(1)}, bf16[64,3584]{1,0:T(8,128)(2,1)}) custom-call(s32[2]{0:T(128)S(1)} %pad_add_fusion.after_ref.at_ref, bf16[256,768]{1,0:T(8,128)(2,1)S(1)} %finished.9.after_ref.final_ref, bf16[256,768]{1,0:T(8,128)(2,1)S(1)} %collective-permute-done.22.came_ref, bf16[2,256,3584]{2,1,0:T(8,128)(2,1)S(1)} %copy-done.1, ...), custom_call_target="tpu_custom_call" | custom-call | tf_op jit(solution)/shard_map/contract/pallas_call | solution.py:192
  135.5 0.1 collective-permute-start.24
  135.6 1.5 collective-permute-done.24
  137.2 1.6 %collective-permute-start.27 = (f32[4,8,512]{2,1,0:T(8,128)S(1)}, f32[4,8,512]{2,1,0:T(8,128)S(1)}, u32[]{:S(2)}, u32[]{:S(2)}) collective-permute-start(f32[4,8,512]{2,1,0:T(8,128)S(1)} %get-tuple-element.65), channel_id=1, source_target_pairs={{0,2},{1,3},{2,0},{3,1},{4,6},{5,7},{6,4},{7,5},{8,10},{9,11},{10,... | collective-permute-start | bytes 196616 | tf_op jit(solution)/shard_map/ppermute | solution.py:20
  138.8 1.1 collective-permute-start.25
  139.8 0.9 collective-permute-start.26
  140.7 1.2 collective-permute-done.27
  141.9 2.1 %collective-permute-done.25 = f32[4,8,512]{2,1,0:T(8,128)S(1)} collective-permute-done((f32[4,8,512]{2,1,0:T(8,128)S(1)}, f32[4,8,512]{2,1,0:T(8,128)S(1)}, u32[]{:S(2)}, u32[]{:S(2)}) %collective-permute-start.25) | collective-permute-done | bytes 65568 | tf_op jit(solution)/shard_map/ppermute | solution.py:20
  144.0 0.8 collective-permute-done.26
  144.8 0.6 constant_dynamic-slice_fusion
  145.5 3.0 %collective-permute-start.29 = (f32[1,8,512]{2,1,0:T(8,128)S(1)}, f32[1,8,512]{2,1,0:T(8,128)S(1)}, u32[]{:S(2)}, u32[]{:S(2)}) collective-permute-start(f32[1,8,512]{2,1,0:T(8,128)S(1)} %get-tuple-element.68), channel_id=1, source_target_pairs={{0,16},{8,24},{16,0},{24,8},{1,17},{9,25},{17,1},{25,9},{2,18},{10... | collective-permute-start | bytes 49160 | tf_op jit(solution)/shard_map/ppermute | solution.py:341
  148.5 0.8 collective-permute-start.30
  149.3 1.7 %collective-permute-done.28.refs_1_ = f32[1,8,512]{2,1,0:T(8,128)S(1)} collective-permute-done((f32[1,8,512]{2,1,0:T(8,128)S(1)}, f32[1,8,512]{2,1,0:T(8,128)S(1)}, u32[]{:S(2)}, u32[]{:S(2)}) %collective-permute-start.28) | collective-permute-done | bytes 16416 | tf_op jit(solution)/shard_map/ppermute | solution.py:341
  151.0 1.2 collective-permute-done.30.refs_3_
  152.2 0.6 copy-done.5
  152.8 1.5 select.17
  (42 shorter events, 0.5 us)
Async XLA Ops:
  0.6 13.7 %collective-permute-start.1 = (bf16[32,7168]{1,0:T(8,128)(2,1)}, bf16[32,7168]{1,0:T(8,128)(2,1)S(1)}, u32[]{:S(2)}, u32[]{:S(2)}) collective-permute-start(bf16[32,7168]{1,0:T(8,128)(2,1)} %refs_0_.1), channel_id=1, source_target_pairs={{0,2},{1,3},{2,0},{3,1},{4,6},{5,7},{6,4},{7,5},{8,10},{9,11},{10,... | collective-permute-start | bytes 1376264 | tf_op jit(solution)/shard_map/ppermute | solution.py:20
  3.6 12.6 %collective-permute-start.3 = (bf16[32,7168]{1,0:T(8,128)(2,1)}, bf16[32,7168]{1,0:T(8,128)(2,1)S(1)}, u32[]{:S(2)}, u32[]{:S(2)}) collective-permute-start(bf16[32,7168]{1,0:T(8,128)(2,1)} %refs_0_.1), channel_id=1, source_target_pairs={{0,4},{1,5},{2,6},{3,7},{4,0},{5,1},{6,2},{7,3},{8,12},{9,13},{10,... | collective-permute-start | bytes 1376264 | tf_op jit(solution)/shard_map/ppermute | solution.py:20
  5.2 19.3 %collective-permute-start = (bf16[32,7168]{1,0:T(8,128)(2,1)}, bf16[32,7168]{1,0:T(8,128)(2,1)S(1)}, u32[]{:S(2)}, u32[]{:S(2)}) collective-permute-start(bf16[32,7168]{1,0:T(8,128)(2,1)} %refs_0_.1), channel_id=1, source_target_pairs={{0,1},{1,0},{2,3},{3,2},{4,5},{5,4},{6,7},{7,6},{8,9},{9,8},{10,11... | collective-permute-start | bytes 1376264 | tf_op jit(solution)/shard_map/ppermute | solution.py:20
  14.4 6.9 %collective-permute-start.5 = (bf16[16,7168]{1,0:T(8,128)(2,1)S(1)}, bf16[16,7168]{1,0:T(8,128)(2,1)S(1)}, u32[]{:S(2)}, u32[]{:S(2)}) collective-permute-start(bf16[16,7168]{1,0:T(8,128)(2,1)S(1)} %slice.8), channel_id=1, source_target_pairs={{0,4},{1,5},{2,6},{3,7},{4,0},{5,1},{6,2},{7,3},{8,12},{9,13},{10,... | collective-permute-start | bytes 688136 | tf_op jit(solution)/shard_map/ppermute | solution.py:20
  16.2 8.3 %collective-permute-start.2 = (bf16[32,7168]{1,0:T(8,128)(2,1)S(1)}, bf16[32,7168]{1,0:T(8,128)(2,1)S(1)}, u32[]{:S(2)}, u32[]{:S(2)}) collective-permute-start(bf16[32,7168]{1,0:T(8,128)(2,1)S(1)} %collective-permute-done.1.refs_2_), channel_id=1, source_target_pairs={{0,1},{1,0},{2,3},{3,2},{4,5},{5,4},{6,7},{7,6},{8,9},{9,8},{10,11... | collective-permute-start | bytes 1376264 | tf_op jit(solution)/shard_map/ppermute | solution.py:20
  16.2 8.3 %collective-permute-start.4 = (bf16[32,7168]{1,0:T(8,128)(2,1)S(1)}, bf16[32,7168]{1,0:T(8,128)(2,1)S(1)}, u32[]{:S(2)}, u32[]{:S(2)}) collective-permute-start(bf16[32,7168]{1,0:T(8,128)(2,1)S(1)} %collective-permute-done.3.refs_4_), channel_id=1, source_target_pairs={{0,1},{1,0},{2,3},{3,2},{4,5},{5,4},{6,7},{7,6},{8,9},{9,8},{10,11... | collective-permute-start | bytes 1376264 | tf_op jit(solution)/shard_map/ppermute | solution.py:20
  16.7 7.6 %collective-permute-start.6 = (bf16[16,7168]{1,0:T(8,128)(2,1)S(1)}, bf16[16,7168]{1,0:T(8,128)(2,1)S(1)}, u32[]{:S(2)}, u32[]{:S(2)}) collective-permute-start(bf16[16,7168]{1,0:T(8,128)(2,1)S(1)} %slice.9), channel_id=1, source_target_pairs={{0,2},{1,3},{2,0},{3,1},{4,6},{5,7},{6,4},{7,5},{8,10},{9,11},{10,... | collective-permute-start | bytes 688136 | tf_op jit(solution)/shard_map/ppermute | solution.py:20
  21.2 3.3 %collective-permute-start.7 = (bf16[16,7168]{1,0:T(8,128)(2,1)S(1)}, bf16[16,7168]{1,0:T(8,128)(2,1)S(1)}, u32[]{:S(2)}, u32[]{:S(2)}) collective-permute-start(bf16[16,7168]{1,0:T(8,128)(2,1)S(1)} %collective-permute-done.5.refs_6_), channel_id=1, source_target_pairs={{0,1},{1,0},{2,3},{3,2},{4,5},{5,4},{6,7},{7,6},{8,9},{9,8},{10,11... | collective-permute-start | bytes 688136 | tf_op jit(solution)/shard_map/ppermute | solution.py:20
  24.3 1.5 collective-permute-start.8
  25.8 1.0 copy-start.2
  33.8 12.9 %collective-permute-start.10 = (bf16[256,768]{1,0:T(8,128)(2,1)S(1)}, bf16[256,768]{1,0:T(8,128)(2,1)S(1)}, u32[]{:S(2)}, u32[]{:S(2)}) collective-permute-start(bf16[256,768]{1,0:T(8,128)(2,1)S(1)} %get-tuple-element.32.after_ref), channel_id=1, source_target_pairs={{0,8},{24,16},{1,9},{25,17},{2,10},{26,18},{3,11},{27,19},{4,12},{... | collective-permute-start | bytes 1179656 | tf_op jit(solution)/shard_map/ppermute | solution.py:232
  42.7 18.2 %collective-permute-start.9 = (bf16[256,640]{1,0:T(8,128)(2,1)S(1)}, bf16[256,640]{1,0:T(8,128)(2,1)S(1)}, u32[]{:S(2)}, u32[]{:S(2)}) collective-permute-start(bf16[256,640]{1,0:T(8,128)(2,1)S(1)} %get-tuple-element.34.after_ref), channel_id=1, source_target_pairs={{0,8},{24,16},{1,9},{25,17},{2,10},{26,18},{3,11},{27,19},{4,12},{... | collective-permute-start | bytes 983048 | tf_op jit(solution)/shard_map/ppermute | solution.py:232
  46.8 14.9 %collective-permute-start.13 = (bf16[256,768]{1,0:T(8,128)(2,1)S(1)}, bf16[256,768]{1,0:T(8,128)(2,1)S(1)}, u32[]{:S(2)}, u32[]{:S(2)}) collective-permute-start(bf16[256,768]{1,0:T(8,128)(2,1)S(1)} %get-tuple-element.36.after_ref), channel_id=1, source_target_pairs={{8,16},{16,8},{9,17},{17,9},{10,18},{18,10},{11,19},{19,11},{12,20... | collective-permute-start | bytes 1179656 | tf_op jit(solution)/shard_map/ppermute | solution.py:232
  53.7 15.0 %collective-permute-start.12 = (bf16[256,768]{1,0:T(8,128)(2,1)S(1)}, bf16[256,768]{1,0:T(8,128)(2,1)S(1)}, u32[]{:S(2)}, u32[]{:S(2)}) collective-permute-start(bf16[256,768]{1,0:T(8,128)(2,1)S(1)} %get-tuple-element.37.after_ref), channel_id=1, source_target_pairs={{0,8},{24,16},{1,9},{25,17},{2,10},{26,18},{3,11},{27,19},{4,12},{... | collective-permute-start | bytes 1179656 | tf_op jit(solution)/shard_map/ppermute | solution.py:232
  61.0 8.5 %collective-permute-start.11 = (bf16[256,640]{1,0:T(8,128)(2,1)S(1)}, bf16[256,640]{1,0:T(8,128)(2,1)S(1)}, u32[]{:S(2)}, u32[]{:S(2)}) collective-permute-start(bf16[256,640]{1,0:T(8,128)(2,1)S(1)} %get-tuple-element.39.after_ref), channel_id=1, source_target_pairs={{8,16},{16,8},{9,17},{17,9},{10,18},{18,10},{11,19},{19,11},{12,20... | collective-permute-start | bytes 983048 | tf_op jit(solution)/shard_map/ppermute | solution.py:232
  61.8 23.0 %collective-permute-start.18 = (bf16[256,768]{1,0:T(8,128)(2,1)S(1)}, bf16[256,768]{1,0:T(8,128)(2,1)S(1)}, u32[]{:S(2)}, u32[]{:S(2)}) collective-permute-start(bf16[256,768]{1,0:T(8,128)(2,1)S(1)} %finished.5.after_ref.final_ref), channel_id=1, source_target_pairs={{8,0},{16,24},{9,1},{17,25},{10,2},{18,26},{11,3},{19,27},{12,4},{... | collective-permute-start | bytes 1179656 | tf_op jit(solution)/shard_map/ppermute | solution.py:238
  68.8 26.4 %collective-permute-start.16 = (bf16[256,768]{1,0:T(8,128)(2,1)S(1)}, bf16[256,768]{1,0:T(8,128)(2,1)S(1)}, u32[]{:S(2)}, u32[]{:S(2)}) collective-permute-start(bf16[256,768]{1,0:T(8,128)(2,1)S(1)} %get-tuple-element.43.after_ref), channel_id=1, source_target_pairs={{8,16},{16,8},{9,17},{17,9},{10,18},{18,10},{11,19},{19,11},{12,20... | collective-permute-start | bytes 1179656 | tf_op jit(solution)/shard_map/ppermute | solution.py:232
  69.6 15.2 %copy-start = (bf16[2,256,3584]{2,1,0:T(8,128)(2,1)S(1)}, bf16[2,256,3584]{2,1,0:T(8,128)(2,1)}, u32[]{:S(2)}) copy-start(bf16[2,256,3584]{2,1,0:T(8,128)(2,1)} %stored_ref.9) | copy-start | bytes 11010052
  75.9 21.7 %collective-permute-start.14 = (bf16[256,768]{1,0:T(8,128)(2,1)S(1)}, bf16[256,768]{1,0:T(8,128)(2,1)S(1)}, u32[]{:S(2)}, u32[]{:S(2)}) collective-permute-start(bf16[256,768]{1,0:T(8,128)(2,1)S(1)} %get-tuple-element.45.after_ref), channel_id=1, source_target_pairs={{0,8},{24,16},{1,9},{25,17},{2,10},{26,18},{3,11},{27,19},{4,12},{... | collective-permute-start | bytes 1179656 | tf_op jit(solution)/shard_map/ppermute | solution.py:232
  82.1 12.9 %collective-permute-start.17 = (bf16[256,640]{1,0:T(8,128)(2,1)S(1)}, bf16[256,640]{1,0:T(8,128)(2,1)S(1)}, u32[]{:S(2)}, u32[]{:S(2)}) collective-permute-start(bf16[256,640]{1,0:T(8,128)(2,1)S(1)} %get-tuple-element.42.after_ref), channel_id=1, source_target_pairs={{0,8},{24,16},{1,9},{25,17},{2,10},{26,18},{3,11},{27,19},{4,12},{... | collective-permute-start | bytes 983048 | tf_op jit(solution)/shard_map/ppermute | solution.py:232
  83.5 13.1 %collective-permute-start.15 = (bf16[256,640]{1,0:T(8,128)(2,1)S(1)}, bf16[256,640]{1,0:T(8,128)(2,1)S(1)}, u32[]{:S(2)}, u32[]{:S(2)}) collective-permute-start(bf16[256,640]{1,0:T(8,128)(2,1)S(1)} %finished.6.after_ref.final_ref), channel_id=1, source_target_pairs={{8,0},{16,24},{9,1},{17,25},{10,2},{18,26},{11,3},{19,27},{12,4},{... | collective-permute-start | bytes 983048 | tf_op jit(solution)/shard_map/ppermute | solution.py:238
  95.3 9.7 %collective-permute-start.20 = (bf16[256,768]{1,0:T(8,128)(2,1)S(1)}, bf16[256,768]{1,0:T(8,128)(2,1)S(1)}, u32[]{:S(2)}, u32[]{:S(2)}) collective-permute-start(bf16[256,768]{1,0:T(8,128)(2,1)S(1)} %finished.7.after_ref.final_ref), channel_id=1, source_target_pairs={{8,0},{16,24},{9,1},{17,25},{10,2},{18,26},{11,3},{19,27},{12,4},{... | collective-permute-start | bytes 1179656 | tf_op jit(solution)/shard_map/ppermute | solution.py:238
  97.7 8.2 %collective-permute-start.19 = (bf16[256,768]{1,0:T(8,128)(2,1)S(1)}, bf16[256,768]{1,0:T(8,128)(2,1)S(1)}, u32[]{:S(2)}, u32[]{:S(2)}) collective-permute-start(bf16[256,768]{1,0:T(8,128)(2,1)S(1)} %get-tuple-element.53.after_ref), channel_id=1, source_target_pairs={{8,16},{16,8},{9,17},{17,9},{10,18},{18,10},{11,19},{19,11},{12,20... | collective-permute-start | bytes 1179656 | tf_op jit(solution)/shard_map/ppermute | solution.py:232
  98.4 0.7 collective-permute-start.21
  106.0 27.7 %collective-permute-start.22 = (bf16[256,768]{1,0:T(8,128)(2,1)S(1)}, bf16[256,768]{1,0:T(8,128)(2,1)S(1)}, u32[]{:S(2)}, u32[]{:S(2)}) collective-permute-start(bf16[256,768]{1,0:T(8,128)(2,1)S(1)} %finished.9.after_ref.final_ref), channel_id=1, source_target_pairs={{8,0},{16,24},{9,1},{17,25},{10,2},{18,26},{11,3},{19,27},{12,4},{... | collective-permute-start | bytes 1179656 | tf_op jit(solution)/shard_map/ppermute | solution.py:238
  107.3 23.4 %collective-permute-start.23 = (bf16[256,640]{1,0:T(8,128)(2,1)S(1)}, bf16[256,640]{1,0:T(8,128)(2,1)S(1)}, u32[]{:S(2)}, u32[]{:S(2)}) collective-permute-start(bf16[256,640]{1,0:T(8,128)(2,1)S(1)} %finished.8.after_ref.final_ref), channel_id=1, source_target_pairs={{8,0},{16,24},{9,1},{17,25},{10,2},{18,26},{11,3},{19,27},{12,4},{... | collective-permute-start | bytes 983048 | tf_op jit(solution)/shard_map/ppermute | solution.py:238
  130.7 2.0 %copy-start.1 = (bf16[2,256,3584]{2,1,0:T(8,128)(2,1)S(1)}, bf16[2,256,3584]{2,1,0:T(8,128)(2,1)}, u32[]{:S(2)}) copy-start(bf16[2,256,3584]{2,1,0:T(8,128)(2,1)} %stored_ref.9) | copy-start | bytes 11010052
  135.5 1.6 %collective-permute-start.24 = (f32[4,4,8,512]{3,2,0,1:T(8,128)S(1)}, f32[4,4,8,512]{3,2,0,1:T(8,128)S(1)}, u32[]{:S(2)}, u32[]{:S(2)}) collective-permute-start(f32[4,4,8,512]{3,2,0,1:T(8,128)S(1)} %bitcast.28), channel_id=1, source_target_pairs={{0,1},{1,0},{2,3},{3,2},{4,5},{5,4},{6,7},{7,6},{8,9},{9,8},{10,11... | collective-permute-start | bytes 786440 | tf_op jit(solution)/shard_map/ppermute | solution.py:20
  137.2 4.7 %collective-permute-start.27 = (f32[4,8,512]{2,1,0:T(8,128)S(1)}, f32[4,8,512]{2,1,0:T(8,128)S(1)}, u32[]{:S(2)}, u32[]{:S(2)}) collective-permute-start(f32[4,8,512]{2,1,0:T(8,128)S(1)} %get-tuple-element.65), channel_id=1, source_target_pairs={{0,2},{1,3},{2,0},{3,1},{4,6},{5,7},{6,4},{7,5},{8,10},{9,11},{10,... | collective-permute-start | bytes 196616 | tf_op jit(solution)/shard_map/ppermute | solution.py:20
  138.8 5.2 %collective-permute-start.25 = (f32[4,8,512]{2,1,0:T(8,128)S(1)}, f32[4,8,512]{2,1,0:T(8,128)S(1)}, u32[]{:S(2)}, u32[]{:S(2)}) collective-permute-start(f32[4,8,512]{2,1,0:T(8,128)S(1)} %get-tuple-element.66), channel_id=1, source_target_pairs={{0,6},{1,7},{2,4},{3,5},{4,2},{5,3},{6,0},{7,1},{8,14},{9,15},{10,... | collective-permute-start | bytes 196616 | tf_op jit(solution)/shard_map/ppermute | solution.py:20
  139.8 5.0 %collective-permute-start.26 = (f32[4,8,512]{2,1,0:T(8,128)S(1)}, f32[4,8,512]{2,1,0:T(8,128)S(1)}, u32[]{:S(2)}, u32[]{:S(2)}) collective-permute-start(f32[4,8,512]{2,1,0:T(8,128)S(1)} %get-tuple-element.64), channel_id=1, source_target_pairs={{0,4},{1,5},{2,6},{3,7},{4,0},{5,1},{6,2},{7,3},{8,12},{9,13},{10,... | collective-permute-start | bytes 196616 | tf_op jit(solution)/shard_map/ppermute | solution.py:20
  145.5 5.5 %collective-permute-start.28 = (f32[1,8,512]{2,1,0:T(8,128)S(1)}, f32[1,8,512]{2,1,0:T(8,128)S(1)}, u32[]{:S(2)}, u32[]{:S(2)}) collective-permute-start(f32[1,8,512]{2,1,0:T(8,128)S(1)} %get-tuple-element.69), channel_id=1, source_target_pairs={{0,8},{8,16},{16,24},{24,0},{1,9},{9,17},{17,25},{25,1},{2,10},{10... | collective-permute-start | bytes 49160 | tf_op jit(solution)/shard_map/ppermute | solution.py:341
  145.5 5.5 %collective-permute-start.29 = (f32[1,8,512]{2,1,0:T(8,128)S(1)}, f32[1,8,512]{2,1,0:T(8,128)S(1)}, u32[]{:S(2)}, u32[]{:S(2)}) collective-permute-start(f32[1,8,512]{2,1,0:T(8,128)S(1)} %get-tuple-element.68), channel_id=1, source_target_pairs={{0,16},{8,24},{16,0},{24,8},{1,17},{9,25},{17,1},{25,9},{2,18},{10... | collective-permute-start | bytes 49160 | tf_op jit(solution)/shard_map/ppermute | solution.py:341
  148.5 3.7 %collective-permute-start.30 = (f32[1,8,512]{2,1,0:T(8,128)S(1)}, f32[1,8,512]{2,1,0:T(8,128)S(1)}, u32[]{:S(2)}, u32[]{:S(2)}) collective-permute-start(f32[1,8,512]{2,1,0:T(8,128)S(1)} %get-tuple-element.67), channel_id=1, source_target_pairs={{0,24},{8,0},{16,8},{24,16},{1,25},{9,1},{17,9},{25,17},{2,26},{10... | collective-permute-start | bytes 49160 | tf_op jit(solution)/shard_map/ppermute | solution.py:341
  151.0 1.2 copy-start.3
  151.0 1.2 copy-start.4
  152.2 0.6 copy-start.5

commit v3 on v2

--- a/solution.py
+++ b/solution.py
@@ -10,6 +10,9 @@
 PARTS = 5
 STEPS = 7
 SLOTS = 4
+HOP = 8 * 2**20
+PIECES = 4
+EARLY = ((0,), (1,))
 LANES = 128
 VMEM = pl.BlockSpec(memory_space=pltpu.VMEM)
 ANY = pl.BlockSpec(memory_space=pl.ANY)
@@ -20,16 +23,19 @@
     return lax.ppermute(array, "col", [(c, c ^ bit) for c in range(count)])
 
 
-def gathered(new_keys, col_count, col_index):
+def gathered(new_keys, col_count, col_index, fetch):
     rows = new_keys.shape[0]
     if col_count != 8:
-        return [lax.all_gather(new_keys, "col", axis=0, tiled=True)], [jnp.int32(0)]
+        return [new_keys, lax.all_gather(new_keys, "col", axis=0, tiled=True)], [jnp.int32(0)] * 2, new_keys
     half = rows // 2
     by_x = flipped(new_keys, 2, 8)
     by_y = flipped(new_keys, 4, 8)
     by_core = flipped(new_keys, 1, 8)
-    low = flipped(by_x[:half], 4, 8)
-    high = flipped(by_y[half:], 2, 8)
+    after = fetch(0, by_core)
+    low, high = halved(by_x, by_y, after)
+    after = fetch(1, low)
+    low = flipped(low, 4, 8)
+    high = flipped(high, 2, 8)
     x_core = flipped(by_x, 1, 8)
     y_core = flipped(by_y, 1, 8)
     low_core = flipped(low, 1, 8)
@@ -37,7 +43,57 @@
     pieces = [new_keys, by_core, by_x, x_core, by_y, y_core, low, high, low_core, high_core]
     of = [0, 1, 2, 3, 4, 5, 6, 6, 7, 7]
     within = [0] * 7 + [half, 0, half]
-    return pieces, [(col_index ^ f) * rows + w for f, w in zip(of, within)]
+    return pieces, [(col_index ^ f) * rows + w for f, w in zip(of, within)], after
+
+
+def halved_kernel(x_ref, y_ref, after_ref, low_ref, high_ref):
+    half = low_ref.shape[0]
+    low_ref[...] = x_ref[:half]
+    high_ref[...] = y_ref[half:]
+
+
+def halved(by_x, by_y, after):
+    rows, depth = by_x.shape
+    return pl.pallas_call(
+        halved_kernel,
+        in_specs=[VMEM, VMEM, ANY],
+        out_specs=[VMEM, VMEM],
+        out_shape=[jax.ShapeDtypeStruct((rows // 2, depth), by_x.dtype)] * 2,
+        compiler_params=params(),
+        cost_estimate=cost(),
+        name="halved",
+    )(by_x, by_y, after)
+
+
+def fetch_kernel(spans, weights_ref, after_ref, *refs):
+    token_ref, arrived = refs[-2:]
+    token_ref[...] = jnp.zeros_like(token_ref)
+    copies = []
+    for i, (span, ref) in enumerate(zip(spans, refs[:-2])):
+        deep = ref.shape[0] // PIECES
+        for k in range(PIECES):
+            rows = pl.ds(k * deep, deep)
+            source = weights_ref.at[rows, pl.ds(span[0], span[1] - span[0])]
+            copies.append(pltpu.make_async_copy(source, ref.at[rows, :], arrived.at[i * PIECES + k]))
+    for copy in copies:
+        copy.start()
+    for copy in copies:
+        copy.wait()
+
+
+def fetched(weights, spans, after):
+    depth = weights.shape[0]
+    return pl.pallas_call(
+        functools.partial(fetch_kernel, spans),
+        in_specs=[ANY, ANY],
+        out_specs=[VMEM] * (len(spans) + 1),
+        out_shape=[jax.ShapeDtypeStruct((depth, e - b), weights.dtype) for b, e in spans]
+        + [jax.ShapeDtypeStruct((8, LANES), jnp.float32)],
+        scratch_shapes=[pltpu.SemaphoreType.DMA((PIECES * len(spans),))],
+        compiler_params=params(),
+        cost_estimate=cost(),
+        name="fetch",
+    )(weights, after)
 
 
 def ranges(columns):
@@ -47,30 +103,41 @@
     return list(zip([0] + ends[:-1], ends))
 
 
+def cost(size=1):
+    return pl.CostEstimate(flops=1, bytes_accessed=size, transcendentals=0)
+
+
 def params():
-    return pltpu.CompilerParams(vmem_limit_bytes=32 * 2**20)
-
-
-def assemble_kernel(count, starts_ref, *refs):
-    keys_ref = refs[count]
-    for i, piece in enumerate(refs[:count]):
-        keys_ref[pl.ds(pl.multiple_of(starts_ref[i], 16), piece.shape[0]), :] = piece[...]
-
-
-def assembled(pieces, starts, keys):
-    return pl.pallas_call(
-        functools.partial(assemble_kernel, len(pieces)),
-        in_specs=[SMEM] + [VMEM] * len(pieces),
+    return pltpu.CompilerParams(vmem_limit_bytes=12 * 2**20)
+
+
+def assemble_kernel(count, starts_ref, after_ref, own_ref, *refs):
+    pieces, keys_ref, arrived = refs[:count], refs[count], refs[count + 1]
+    own = pl.ds(pl.multiple_of(starts_ref[0], 16), own_ref.shape[0])
+    copy = pltpu.make_async_copy(own_ref, keys_ref.at[own, :], arrived)
+    copy.start()
+    copy.wait()
+    for i, piece in enumerate(pieces):
+        keys_ref[pl.ds(pl.multiple_of(starts_ref[i + 1], 16), piece.shape[0]), :] = piece[...]
+
+
+def assembled(pieces, starts, keys, after):
+    return pl.pallas_call(
+        functools.partial(assemble_kernel, len(pieces) - 1),
+        in_specs=[SMEM, ANY, ANY] + [VMEM] * (len(pieces) - 1),
         out_specs=VMEM,
         out_shape=jax.ShapeDtypeStruct((keys, pieces[0].shape[1]), pieces[0].dtype),
-        compiler_params=params(),
+        scratch_shapes=[pltpu.SemaphoreType.DMA],
+        compiler_params=params(),
+        cost_estimate=cost(),
         name="assemble",
-    )(starts, *pieces)
-
-
-def product_kernel(left, keys_ref, weights_ref, after_ref, wide_ref, sent_ref, held_ref, arrived):
+    )(starts, after, *pieces)
+
+
+def product_kernel(left, early, keys_ref, weights_ref, stored_ref, after_ref, *refs):
+    wide_ref, sent_ref, columns_ref, held_ref, arrived = refs
     wide = wide_ref.shape[1]
-    deep = held_ref.shape[1]
+    deep = keys_ref.shape[1] // STEPS
 
     def copy(step):
         return pltpu.make_async_copy(
@@ -79,46 +146,51 @@
             arrived.at[step % SLOTS],
         )
 
-    for step in range(min(SLOTS, STEPS)):
-        copy(step).start()
+    other = pltpu.make_async_copy(stored_ref.at[:, :, pl.ds(left, wide)], columns_ref, arrived.at[SLOTS])
+    if not early:
+        for step in range(min(SLOTS, STEPS)):
+            copy(step).start()
+    other.start()
     for step in range(STEPS):
-        copy(step).wait()
+        if early:
+            weights = weights_ref[step * deep : (step + 1) * deep, :]
+        else:
+            copy(step).wait()
+            weights = held_ref[step % SLOTS]
         part = jnp.dot(
             keys_ref[:, step * deep : (step + 1) * deep],
-            held_ref[step % SLOTS],
+            weights,
             preferred_element_type=jnp.float32,
         )
-        if step + SLOTS < STEPS:
+        if not early and step + SLOTS < STEPS:
             copy(step + SLOTS).start()
         total = part if step == 0 else wide_ref[...] + part
         wide_ref[...] = total
         if step == STEPS - 1:
             sent_ref[...] = total.astype(sent_ref.dtype)
-
-
-def product(keys, weights, span, wire, after):
+    other.wait()
+
+
+def product(keys, weights, early, stored, span, wire, after):
     depth = weights.shape[0]
     rows, wide = keys.shape[0], span[1] - span[0]
     return pl.pallas_call(
-        functools.partial(product_kernel, span[0]),
-        in_specs=[VMEM, ANY, ANY],
-        out_specs=[VMEM, VMEM],
+        functools.partial(product_kernel, span[0], early),
+        in_specs=[VMEM, VMEM if early else ANY, ANY, ANY],
+        out_specs=[VMEM, VMEM, VMEM],
         out_shape=[
             jax.ShapeDtypeStruct((rows, wide), jnp.float32),
             jax.ShapeDtypeStruct((rows, wide), wire),
+            jax.ShapeDtypeStruct(stored.shape[:2] + (wide,), stored.dtype),
         ],
         scratch_shapes=[
-            pltpu.VMEM((SLOTS, depth // STEPS, wide), weights.dtype),
-            pltpu.SemaphoreType.DMA((SLOTS,)),
+            pltpu.VMEM((SLOTS, 16 if early else depth // STEPS, wide), weights.dtype),
+            pltpu.SemaphoreType.DMA((SLOTS + 1,)),
         ],
         compiler_params=params(),
-        cost_estimate=pl.CostEstimate(
-            flops=2 * rows * depth * wide,
-            bytes_accessed=2 * depth * (rows + wide) + 6 * rows * wide,
-            transcendentals=0,
-        ),
+        cost_estimate=cost(),
         name="product",
-    )(keys, weights, after)
+    )(keys, weights, stored, after)
 
 
 def add_kernel(wide_ref, came_ref, after_ref, total_ref, sent_ref):
@@ -134,6 +206,7 @@
         out_specs=[VMEM, VMEM],
         out_shape=[jax.ShapeDtypeStruct(wide.shape, jnp.float32), jax.ShapeDtypeStruct(wide.shape, wire)],
         compiler_params=params(),
+        cost_estimate=cost(HOP),
         name="added",
     )(wide, came, after)
 
@@ -149,11 +222,12 @@
         out_specs=VMEM,
         out_shape=jax.ShapeDtypeStruct(wide.shape, jnp.bfloat16),
         compiler_params=params(),
+        cost_estimate=cost(HOP),
         name="finished",
     )(wide, came, after)
 
 
-def contract_kernel(span, done, at_ref, final_ref, came_ref, stored_ref, after_ref, *refs):
+def contract_kernel(done, at_ref, final_ref, came_ref, stored_ref, after_ref, *refs):
     before = refs[: done[0]]
     pieces = refs[done[0] : done[0] + done[1]]
     terms_ref, whitened_ref, rows_ref = refs[-3:]
@@ -167,11 +241,10 @@
     def _():
         rows_ref[...] = came_ref[...]
 
-    batches, slots, _ = stored_ref.shape
-    wide = span[1] - span[0]
+    batches, slots, wide = stored_ref.shape
     term = lax.dot_general(
         rows_ref[...],
-        stored_ref[:, :, span[0] : span[1]].reshape(batches * slots, wide),
+        stored_ref[...].reshape(batches * slots, wide),
         (((1,), (1,)), ((), ())),
         preferred_element_type=jnp.float32,
     )
@@ -184,13 +257,13 @@
     whitened_ref[:, left : left + wide] = rows_ref[pl.ds(pl.multiple_of(start, 16), block), :]
 
 
-def contract(at, final, came, stored, terms, pieces, span, block, after):
+def contract(at, final, came, stored, terms, pieces, block, after):
     keys, wide = final.shape
     sums = stored.shape[0] * stored.shape[1]
     before = [] if terms is None else [terms]
     columns = wide + sum(p.shape[1] for p in pieces)
     return pl.pallas_call(
-        functools.partial(contract_kernel, span, (len(before), len(pieces))),
+        functools.partial(contract_kernel, (len(before), len(pieces))),
         in_specs=[SMEM, VMEM, VMEM, VMEM, ANY] + [VMEM] * (len(before) + len(pieces)),
         out_specs=[VMEM, VMEM],
         out_shape=[
@@ -199,6 +272,7 @@
         ],
         scratch_shapes=[pltpu.VMEM((keys, wide), jnp.bfloat16)],
         compiler_params=params(),
+        cost_estimate=cost(HOP),
         name="contract",
     )(at, final, came, stored, after, *before, *pieces)
 
@@ -281,6 +355,7 @@
         out_specs=VMEM,
         out_shape=jax.ShapeDtypeStruct((1, places, rows, slots), jnp.float32),
         scratch_shapes=[pltpu.VMEM((count, batches, rows, slots), jnp.float32)],
+        cost_estimate=cost(),
         name="select",
     )(row_index[None], pair_batch, pair_count, batch_length, batch_slot, *parts)
 
@@ -300,19 +375,32 @@
     inner = [away <= hop for hop in range(half)]
     at = jnp.stack([(away < half - 1).astype(jnp.int32), row_index * block])
 
-    pieces, starts = gathered(new_keys, col_count, col_index)
-    keys = assembled(pieces, jnp.stack(starts), total_keys)
     spans = ranges(precision.shape[1])
+    early = {}
+
+    def fetch(turn, after):
+        parts = [p for p in EARLY[turn] if p < len(spans)]
+        *held, token = fetched(precision, [spans[p] for p in parts], after)
+        early.update(zip(parts, held))
+        return token
+
+    pieces, starts, after = gathered(new_keys, col_count, col_index, fetch)
+    keys = assembled(pieces, jnp.stack(starts), total_keys, after)
     whitened = []
+    columns = []
     terms = None
 
     def make(part, after):
-        return product(keys, precision, spans[part], wire, at if after is None else after)
+        weights = early.get(part, precision)
+        after = at if after is None else after
+        *made, held = product(keys, weights, part in early, stored_keys, spans[part], wire, after)
+        columns.append(held)
+        return made
 
     def close(part, final, came, after):
         nonlocal terms
         before = whitened if part == len(spans) - 1 else []
-        terms, rows = contract(at, final, came, stored_keys, terms, before, spans[part], block, after)
+        terms, rows = contract(at, final, came, columns[part], terms, before, block, after)
         whitened.append(rows)
         return rows
 

time: 155 us -> 157 us (1.013)
  waiting for transfers between devices: 64.9 us -> 60.2 us
  local copies, waits for them, and re-layouts: 4.47 us -> 8.77 us
  Pallas kernels: 38.2 us -> 41.9 us
    ppermute x13, waiting for transfers between devices: 22.1 us -> 12.6 us  [flipped(): return lax.ppermute(array, 'col', [(c, c ^ bit) for c in range(count)])]
    unnamed x12 -> x18, local copies, waits for them, and re-layouts: 3.66 us -> 7.99 us
    pallas_call x11 -> x14, Pallas kernels: 35.8 us -> 39.5 us  [the longest x5 24.2 us: product(): pl.pallas_call(functools.partial(product_kernel, span[0], early), in_spec...]
    ppermute x10, waiting for transfers between devices: 12 us -> 15.1 us  [step_in(): return lax.ppermute(sent, 'row', pairs)]
    ppermute x5, waiting for transfers between devices: 27.9 us -> 29.6 us  [step_out(): return lax.ppermute(final, 'row', [(low, low - 1), (high, high + 1)])]
  transfers between devices with their start and end apart: 31 -> 31, of which waited for: 14 -> 13; matrix products, arithmetic and copies ran while one was open for 0% -> 0% of each run, Pallas kernels for 18% -> 22%
where the time goes in v3:
time: 157 us
  waiting for transfers between devices  60.2 us (38%)
  starting transfers between devices  44.3 us (28%)
  Pallas kernels  41.9 us (27%)
  local copies, waits for them, and re-layouts  8.77 us (6%)
    ppermute x5, waiting for transfers between devices, step_out(): return lax.ppermute(final, 'row', [(low, low - 1), (high, high + 1)])  29.6 us
    pallas_call x5, Pallas kernels, product(): pl.pallas_call(functools.partial(product_kernel, span[0], early), in_spec...  24.2 us
    ppermute x10, starting transfers between devices, step_in(): return lax.ppermute(sent, 'row', pairs)  23 us
    ppermute x10, waiting for transfers between devices, step_in(): return lax.ppermute(sent, 'row', pairs)  15.1 us
    ppermute x13, waiting for transfers between devices, flipped(): return lax.ppermute(array, 'col', [(c, c ^ bit) for c in range(count)])  12.6 us
    ppermute x13, starting transfers between devices, flipped(): return lax.ppermute(array, 'col', [(c, c ^ bit) for c in range(count)])  10.9 us
    pallas_call x2, Pallas kernels, fetched(): pl.pallas_call(functools.partial(fetch_kernel, spans), in_specs=[ANY, ANY...  8.21 us
    unnamed x18, local copies, waits for them, and re-layouts  7.99 us
  transfers between devices with their start and end apart: 31, of which 13 were waited for; matrix products, arithmetic and copies ran while one was open for 0% of the time, Pallas kernels for 22%

profile of v3, /device:TPU:0, one launch (start us, length us, event | category | flops | bytes accessed | tf_op | source)
XLA Modules:
  0.0 156.5 jit_solution(5728127319231584162)
XLA Ops:
  0.6 0.5 collective-permute-start.2
  1.1 2.6 %collective-permute-start = (bf16[32,7168]{1,0:T(8,128)(2,1)}, bf16[32,7168]{1,0:T(8,128)(2,1)S(1)}, u32[]{:S(2)}, u32[]{:S(2)}) collective-permute-start(bf16[32,7168]{1,0:T(8,128)(2,1)} %own_ref.1), channel_id=1, source_target_pairs={{0,2},{1,3},{2,0},{3,1},{4,6},{5,7},{6,4},{7,5},{8,10},{9,11},{10,... | collective-permute-start | bytes 1376264 | tf_op jit(solution)/shard_map/ppermute | solution.py:23
  3.7 1.5 collective-permute-start.1
  5.2 4.3 %fetch.2 = (bf16[7168,768]{1,0:T(8,128)(2,1)S(1)}, f32[8,128]{1,0:T(8,128)S(1)}) custom-call(bf16[7168,3584]{1,0:T(8,128)(2,1)} %weights_ref.9, bf16[32,7168]{1,0:T(8,128)(2,1)S(1)} %collective-permute-done.2.after_ref.refs_0_), custom_call_target="tpu_custom_call" | custom-call | flops 1 | bytes 1 | tf_op jit(solution)/shard_map/fetch/pallas_call | solution.py:86
  9.5 4.1 %copy-done.1 = bf16[7168,768]{1,0:T(8,128)(2,1)} copy-done((bf16[7168,768]{1,0:T(8,128)(2,1)}, bf16[7168,768]{1,0:T(8,128)(2,1)S(1)}, u32[]{:S(2)}) %copy-start.1) | copy-done | bytes 11010072
  13.7 1.4 collective-permute-done.x_ref.refs_1_
  15.0 1.5 collective-permute-done.1.y_ref.refs_3_
  16.5 1.6 %collective-permute-start.5 = (bf16[16,7168]{1,0:T(8,128)(2,1)S(1)}, bf16[16,7168]{1,0:T(8,128)(2,1)S(1)}, u32[]{:S(2)}, u32[]{:S(2)}) collective-permute-start(bf16[16,7168]{1,0:T(8,128)(2,1)S(1)} %get-tuple-element.44.after_ref), channel_id=1, source_target_pairs={{0,4},{1,5},{2,6},{3,7},{4,0},{5,1},{6,2},{7,3},{8,12},{9,13},{10,... | collective-permute-start | bytes 688136 | tf_op jit(solution)/shard_map/ppermute | solution.py:23
  18.1 0.5 collective-permute-start.6
  18.7 0.5 collective-permute-start.4
  19.2 4.3 %collective-permute-done.5.refs_5_ = bf16[16,7168]{1,0:T(8,128)(2,1)S(1)} collective-permute-done((bf16[16,7168]{1,0:T(8,128)(2,1)S(1)}, bf16[16,7168]{1,0:T(8,128)(2,1)S(1)}, u32[]{:S(2)}, u32[]{:S(2)}) %collective-permute-start.5) | collective-permute-done | bytes 229408 | tf_op jit(solution)/shard_map/ppermute | solution.py:23
  23.5 1.2 collective-permute-done.6.refs_6_
  24.7 0.1 stack.59.starts_ref
  24.9 3.9 %fetch.3 = (bf16[7168,640]{1,0:T(8,128)(2,1)S(1)}, f32[8,128]{1,0:T(8,128)S(1)}) custom-call(bf16[7168,3584]{1,0:T(8,128)(2,1)} %weights_ref.9, bf16[16,7168]{1,0:T(8,128)(2,1)S(1)} %get-tuple-element.44.after_ref), custom_call_target="tpu_custom_call" | custom-call | flops 1 | bytes 1 | tf_op jit(solution)/shard_map/fetch/pallas_call | solution.py:86
  28.9 1.0 assemble.1.keys_ref
  29.9 1.2 slice-done.1
  31.1 0.7 slice-done.2
  31.9 1.3 copy-done
  33.2 3.1 %product.5 = (f32[256,768]{1,0:T(8,128)S(1)}, bf16[256,768]{1,0:T(8,128)(2,1)S(1)}, bf16[2,256,768]{2,1,0:T(8,128)(2,1)S(1)}) custom-call(bf16[256,7168]{1,0:T(8,128)(2,1)S(1)} %assemble.1.keys_ref, bf16[7168,768]{1,0:T(8,128)(2,1)S(1)} %bitcast.28, bf16[2,256,3584]{2,1,0:T(8,128)(2,1)S(1)} %copy-done, s32[2]{0:T(128)S(1)} %pad_add_fusion.after_ref.at_ref), custom_call_target="tpu_custom_call" | custom-call | flops 1 | bytes 1 | tf_op jit(solution)/shard_map/product/pallas_call | solution.py:177
  36.3 3.5 %collective-permute-start.10 = (bf16[256,768]{1,0:T(8,128)(2,1)S(1)}, bf16[256,768]{1,0:T(8,128)(2,1)S(1)}, u32[]{:S(2)}, u32[]{:S(2)}) collective-permute-start(bf16[256,768]{1,0:T(8,128)(2,1)S(1)} %get-tuple-element.49.after_ref), channel_id=1, source_target_pairs={{0,8},{24,16},{1,9},{25,17},{2,10},{26,18},{3,11},{27,19},{4,12},{... | collective-permute-start | bytes 1179656 | tf_op jit(solution)/shard_map/ppermute | solution.py:306
  39.8 3.2 %product.6 = (f32[256,640]{1,0:T(8,128)S(1)}, bf16[256,640]{1,0:T(8,128)(2,1)S(1)}, bf16[2,256,640]{2,1,0:T(8,128)(2,1)S(1)}) custom-call(bf16[256,7168]{1,0:T(8,128)(2,1)S(1)} %assemble.1.keys_ref, bf16[7168,640]{1,0:T(8,128)(2,1)S(1)} %get-tuple-element.47.weights_ref, bf16[2,256,3584]{2,1,0:T(8,128)(2,1)S(1)} %copy-done, ...), custom_call_target="tpu_custom_call" | custom-call | flops 1 | bytes 1 | tf_op jit(solution)/shard_map/product/pallas_call | solution.py:177
  43.0 1.3 collective-permute-start.9
  44.3 4.9 %collective-permute-done.10.came_ref = bf16[256,768]{1,0:T(8,128)(2,1)S(1)} collective-permute-done((bf16[256,768]{1,0:T(8,128)(2,1)S(1)}, bf16[256,768]{1,0:T(8,128)(2,1)S(1)}, u32[]{:S(2)}, u32[]{:S(2)}) %collective-permute-start.10) | collective-permute-done | bytes 393248 | tf_op jit(solution)/shard_map/ppermute | solution.py:306
  49.2 0.1 added.5
  49.3 0.7 collective-permute-start.13
  50.0 6.2 %product.7 = (f32[256,768]{1,0:T(8,128)S(1)}, bf16[256,768]{1,0:T(8,128)(2,1)S(1)}, bf16[2,256,768]{2,1,0:T(8,128)(2,1)S(1)}) custom-call(bf16[256,7168]{1,0:T(8,128)(2,1)S(1)} %assemble.1.keys_ref, bf16[7168,3584]{1,0:T(8,128)(2,1)} %weights_ref.9, bf16[2,256,3584]{2,1,0:T(8,128)(2,1)S(1)} %copy-done, bf16[256,768]{1,0:T(8,128)(2,1)S(1)} %get-tuple-element.53.after_ref), custom_call_target="tpu_custom_call" | custom-call | flops 1 | bytes 1 | tf_op jit(solution)/shard_map/product/pallas_call | solution.py:177
  56.2 7.2 %collective-permute-start.12 = (bf16[256,768]{1,0:T(8,128)(2,1)S(1)}, bf16[256,768]{1,0:T(8,128)(2,1)S(1)}, u32[]{:S(2)}, u32[]{:S(2)}) collective-permute-start(bf16[256,768]{1,0:T(8,128)(2,1)S(1)} %get-tuple-element.54.after_ref), channel_id=1, source_target_pairs={{0,8},{24,16},{1,9},{25,17},{2,10},{26,18},{3,11},{27,19},{4,12},{... | collective-permute-start | bytes 1179656 | tf_op jit(solution)/shard_map/ppermute | solution.py:306
  63.5 0.1 added.6
  63.6 0.7 collective-permute-start.11
  64.3 1.5 collective-permute-start.18
  65.8 5.5 %product.8 = (f32[256,640]{1,0:T(8,128)S(1)}, bf16[256,640]{1,0:T(8,128)(2,1)S(1)}, bf16[2,256,640]{2,1,0:T(8,128)(2,1)S(1)}) custom-call(bf16[256,7168]{1,0:T(8,128)(2,1)S(1)} %assemble.1.keys_ref, bf16[7168,3584]{1,0:T(8,128)(2,1)} %weights_ref.9, bf16[2,256,3584]{2,1,0:T(8,128)(2,1)S(1)} %copy-done, bf16[256,768]{1,0:T(8,128)(2,1)S(1)} %finished.5.after_ref.final_ref), custom_call_target="tpu_custom_call" | custom-call | flops 1 | bytes 1 | tf_op jit(solution)/shard_map/product/pallas_call | solution.py:177
  71.3 0.1 added.7
  71.4 0.7 collective-permute-start.16
  72.2 6.2 %product.9 = (f32[256,768]{1,0:T(8,128)S(1)}, bf16[256,768]{1,0:T(8,128)(2,1)S(1)}, bf16[2,256,768]{2,1,0:T(8,128)(2,1)S(1)}) custom-call(bf16[256,7168]{1,0:T(8,128)(2,1)S(1)} %assemble.1.keys_ref, bf16[7168,3584]{1,0:T(8,128)(2,1)} %weights_ref.9, bf16[2,256,3584]{2,1,0:T(8,128)(2,1)S(1)} %copy-done, bf16[256,640]{1,0:T(8,128)(2,1)S(1)} %finished.6.after_ref.final_ref), custom_call_target="tpu_custom_call" | custom-call | flops 1 | bytes 1 | tf_op jit(solution)/shard_map/product/pallas_call | solution.py:177
  78.4 6.2 %collective-permute-start.14 = (bf16[256,768]{1,0:T(8,128)(2,1)S(1)}, bf16[256,768]{1,0:T(8,128)(2,1)S(1)}, u32[]{:S(2)}, u32[]{:S(2)}) collective-permute-start(bf16[256,768]{1,0:T(8,128)(2,1)S(1)} %get-tuple-element.62.after_ref), channel_id=1, source_target_pairs={{0,8},{24,16},{1,9},{25,17},{2,10},{26,18},{3,11},{27,19},{4,12},{... | collective-permute-start | bytes 1179656 | tf_op jit(solution)/shard_map/ppermute | solution.py:306
  84.6 1.3 collective-permute-start.17
  86.0 1.3 collective-permute-start.15
  87.3 1.0 contract.5
  88.3 10.1 %collective-permute-done.17.came_ref = bf16[256,640]{1,0:T(8,128)(2,1)S(1)} collective-permute-done((bf16[256,640]{1,0:T(8,128)(2,1)S(1)}, bf16[256,640]{1,0:T(8,128)(2,1)S(1)}, u32[]{:S(2)}, u32[]{:S(2)}) %collective-permute-start.17) | collective-permute-done | bytes 327712 | tf_op jit(solution)/shard_map/ppermute | solution.py:306
  98.4 0.1 added.8
  98.6 1.3 collective-permute-start.20
  99.9 1.0 contract.6
  100.9 0.1 added.9
  101.0 0.7 collective-permute-start.19
  101.7 0.7 collective-permute-start.21
  102.5 6.4 %collective-permute-done.20.came_ref = bf16[256,768]{1,0:T(8,128)(2,1)S(1)} collective-permute-done((bf16[256,768]{1,0:T(8,128)(2,1)S(1)}, bf16[256,768]{1,0:T(8,128)(2,1)S(1)}, u32[]{:S(2)}, u32[]{:S(2)}) %collective-permute-start.20) | collective-permute-done | bytes 393248 | tf_op jit(solution)/shard_map/ppermute | solution.py:312
  108.9 1.0 contract.7
  110.0 1.3 collective-permute-start.22
  111.3 1.3 collective-permute-start.23
  112.6 23.2 %collective-permute-done.23.came_ref = bf16[256,640]{1,0:T(8,128)(2,1)} collective-permute-done((bf16[256,640]{1,0:T(8,128)(2,1)S(1)}, bf16[256,640]{1,0:T(8,128)(2,1)}, u32[]{:S(2)}, u32[]{:S(2)}) %collective-permute-start.23) | collective-permute-done | bytes 327712 | tf_op jit(solution)/shard_map/ppermute | solution.py:312
  135.8 1.4 contract.8
  137.2 1.7 %contract.9 = (f32[256,512]{1,0:T(8,128)S(1)}, bf16[64,3584]{1,0:T(8,128)(2,1)}) custom-call(s32[2]{0:T(128)S(1)} %pad_add_fusion.after_ref.at_ref, bf16[256,768]{1,0:T(8,128)(2,1)S(1)} %finished.9.after_ref.final_ref, bf16[256,768]{1,0:T(8,128)(2,1)S(1)} %collective-permute-done.22.came_ref, bf16[2,256,768]{2,1,0:T(8,128)(2,1)S(1)} %get-tuple-element.77.stored_ref, ...), custom_call_target="tpu_custom_call" | custom-call | flops 1 | bytes 8388608 | tf_op jit(solution)/shard_map/contract/pallas_call | solution.py:265
  139.1 1.5 collective-permute-done.24
  140.8 2.0 %collective-permute-start.26 = (f32[4,8,512]{2,1,0:T(8,128)S(1)}, f32[4,8,512]{2,1,0:T(8,128)S(1)}, u32[]{:S(2)}, u32[]{:S(2)}) collective-permute-start(f32[4,8,512]{2,1,0:T(8,128)S(1)} %get-tuple-element.86), channel_id=1, source_target_pairs={{0,4},{1,5},{2,6},{3,7},{4,0},{5,1},{6,2},{7,3},{8,12},{9,13},{10,... | collective-permute-start | bytes 196616 | tf_op jit(solution)/shard_map/ppermute | solution.py:23
  142.7 1.5 collective-permute-start.27
  144.3 2.2 %collective-permute-done.25 = f32[4,8,512]{2,1,0:T(8,128)S(1)} collective-permute-done((f32[4,8,512]{2,1,0:T(8,128)S(1)}, f32[4,8,512]{2,1,0:T(8,128)S(1)}, u32[]{:S(2)}, u32[]{:S(2)}) %collective-permute-start.25) | collective-permute-done | bytes 65568 | tf_op jit(solution)/shard_map/ppermute | solution.py:23
  146.5 0.5 collective-permute-done.27
  147.0 0.6 constant_dynamic-slice_fusion
  147.6 3.0 %collective-permute-start.29 = (f32[1,8,512]{2,1,0:T(8,128)S(1)}, f32[1,8,512]{2,1,0:T(8,128)S(1)}, u32[]{:S(2)}, u32[]{:S(2)}) collective-permute-start(f32[1,8,512]{2,1,0:T(8,128)S(1)} %get-tuple-element.90), channel_id=1, source_target_pairs={{0,16},{8,24},{16,0},{24,8},{1,17},{9,25},{17,1},{25,9},{2,18},{10... | collective-permute-start | bytes 49160 | tf_op jit(solution)/shard_map/ppermute | solution.py:429
  150.7 0.8 collective-permute-start.30
  151.5 1.7 %collective-permute-done.28.refs_1_ = f32[1,8,512]{2,1,0:T(8,128)S(1)} collective-permute-done((f32[1,8,512]{2,1,0:T(8,128)S(1)}, f32[1,8,512]{2,1,0:T(8,128)S(1)}, u32[]{:S(2)}, u32[]{:S(2)}) %collective-permute-start.28) | collective-permute-done | bytes 16416 | tf_op jit(solution)/shard_map/ppermute | solution.py:429
  153.2 1.2 collective-permute-done.30.refs_3_
  154.4 0.6 copy-done.5
  155.0 1.5 select.17
  (50 shorter events, 0.8 us)
Async XLA Ops:
  0.6 4.6 %collective-permute-start.2 = (bf16[32,7168]{1,0:T(8,128)(2,1)}, bf16[32,7168]{1,0:T(8,128)(2,1)S(1)}, u32[]{:S(2)}, u32[]{:S(2)}) collective-permute-start(bf16[32,7168]{1,0:T(8,128)(2,1)} %own_ref.1), channel_id=1, source_target_pairs={{0,1},{1,0},{2,3},{3,2},{4,5},{5,4},{6,7},{7,6},{8,9},{9,8},{10,11... | collective-permute-start | bytes 1376264 | tf_op jit(solution)/shard_map/ppermute | solution.py:23
  1.1 13.9 %collective-permute-start = (bf16[32,7168]{1,0:T(8,128)(2,1)}, bf16[32,7168]{1,0:T(8,128)(2,1)S(1)}, u32[]{:S(2)}, u32[]{:S(2)}) collective-permute-start(bf16[32,7168]{1,0:T(8,128)(2,1)} %own_ref.1), channel_id=1, source_target_pairs={{0,2},{1,3},{2,0},{3,1},{4,6},{5,7},{6,4},{7,5},{8,10},{9,11},{10,... | collective-permute-start | bytes 1376264 | tf_op jit(solution)/shard_map/ppermute | solution.py:23
  3.7 12.8 %collective-permute-start.1 = (bf16[32,7168]{1,0:T(8,128)(2,1)}, bf16[32,7168]{1,0:T(8,128)(2,1)S(1)}, u32[]{:S(2)}, u32[]{:S(2)}) collective-permute-start(bf16[32,7168]{1,0:T(8,128)(2,1)} %own_ref.1), channel_id=1, source_target_pairs={{0,4},{1,5},{2,6},{3,7},{4,0},{5,1},{6,2},{7,3},{8,12},{9,13},{10,... | collective-permute-start | bytes 1376264 | tf_op jit(solution)/shard_map/ppermute | solution.py:23
  9.5 4.1 %copy-start.1 = (bf16[7168,768]{1,0:T(8,128)(2,1)}, bf16[7168,768]{1,0:T(8,128)(2,1)S(1)}, u32[]{:S(2)}) copy-start(bf16[7168,768]{1,0:T(8,128)(2,1)S(1)} %get-tuple-element.48.weights_ref) | copy-start | bytes 33030148
  16.5 6.9 %collective-permute-start.5 = (bf16[16,7168]{1,0:T(8,128)(2,1)S(1)}, bf16[16,7168]{1,0:T(8,128)(2,1)S(1)}, u32[]{:S(2)}, u32[]{:S(2)}) collective-permute-start(bf16[16,7168]{1,0:T(8,128)(2,1)S(1)} %get-tuple-element.44.after_ref), channel_id=1, source_target_pairs={{0,4},{1,5},{2,6},{3,7},{4,0},{5,1},{6,2},{7,3},{8,12},{9,13},{10,... | collective-permute-start | bytes 688136 | tf_op jit(solution)/shard_map/ppermute | solution.py:23
  18.1 6.6 %collective-permute-start.6 = (bf16[16,7168]{1,0:T(8,128)(2,1)S(1)}, bf16[16,7168]{1,0:T(8,128)(2,1)S(1)}, u32[]{:S(2)}, u32[]{:S(2)}) collective-permute-start(bf16[16,7168]{1,0:T(8,128)(2,1)S(1)} %get-tuple-element.46), channel_id=1, source_target_pairs={{0,2},{1,3},{2,0},{3,1},{4,6},{5,7},{6,4},{7,5},{8,10},{9,11},{10,... | collective-permute-start | bytes 688136 | tf_op jit(solution)/shard_map/ppermute | solution.py:23
  18.7 10.2 %collective-permute-start.3 = (bf16[32,7168]{1,0:T(8,128)(2,1)S(1)}, bf16[32,7168]{1,0:T(8,128)(2,1)S(1)}, u32[]{:S(2)}, u32[]{:S(2)}) collective-permute-start(bf16[32,7168]{1,0:T(8,128)(2,1)S(1)} %collective-permute-done.x_ref.refs_1_), channel_id=1, source_target_pairs={{0,1},{1,0},{2,3},{3,2},{4,5},{5,4},{6,7},{7,6},{8,9},{9,8},{10,11... | collective-permute-start | bytes 1376264 | tf_op jit(solution)/shard_map/ppermute | solution.py:23
  18.7 10.2 %collective-permute-start.4 = (bf16[32,7168]{1,0:T(8,128)(2,1)S(1)}, bf16[32,7168]{1,0:T(8,128)(2,1)S(1)}, u32[]{:S(2)}, u32[]{:S(2)}) collective-permute-start(bf16[32,7168]{1,0:T(8,128)(2,1)S(1)} %collective-permute-done.1.y_ref.refs_3_), channel_id=1, source_target_pairs={{0,1},{1,0},{2,3},{3,2},{4,5},{5,4},{6,7},{7,6},{8,9},{9,8},{10,11... | collective-permute-start | bytes 1376264 | tf_op jit(solution)/shard_map/ppermute | solution.py:23
  23.5 5.4 %collective-permute-start.7 = (bf16[16,7168]{1,0:T(8,128)(2,1)S(1)}, bf16[16,7168]{1,0:T(8,128)(2,1)S(1)}, u32[]{:S(2)}, u32[]{:S(2)}) collective-permute-start(bf16[16,7168]{1,0:T(8,128)(2,1)S(1)} %collective-permute-done.5.refs_5_), channel_id=1, source_target_pairs={{0,1},{1,0},{2,3},{3,2},{4,5},{5,4},{6,7},{7,6},{8,9},{9,8},{10,11... | collective-permute-start | bytes 688136 | tf_op jit(solution)/shard_map/ppermute | solution.py:23
  24.7 4.1 %collective-permute-start.8 = (bf16[16,7168]{1,0:T(8,128)(2,1)S(1)}, bf16[16,7168]{1,0:T(8,128)(2,1)S(1)}, u32[]{:S(2)}, u32[]{:S(2)}) collective-permute-start(bf16[16,7168]{1,0:T(8,128)(2,1)S(1)} %collective-permute-done.6.refs_6_), channel_id=1, source_target_pairs={{0,1},{1,0},{2,3},{3,2},{4,5},{5,4},{6,7},{7,6},{8,9},{9,8},{10,11... | collective-permute-start | bytes 688136 | tf_op jit(solution)/shard_map/ppermute | solution.py:23
  24.8 5.1 %slice-start = ((s8[11010048]{0:T(1024)(128)(4,1)}), s8[4194304]{0:T(1024)(128)(4,1)S(1)}, s32[]{:S(2)}) async-start(s8[11010048]{0:T(1024)(128)(4,1)} %bitcast.27), calls=%async_computation | async-start | bytes 8388608
  24.9 4.0 %copy-start.2 = (bf16[32,7168]{1,0:T(8,128)(2,1)S(1)}, bf16[32,7168]{1,0:T(8,128)(2,1)}, u32[]{:S(2)}) copy-start(bf16[32,7168]{1,0:T(8,128)(2,1)} %own_ref.1) | copy-start | bytes 1376260
  24.9 6.3 %slice-start.1 = ((s8[11010048]{0:T(1024)(128)(4,1)}), s8[4194304]{0:T(1024)(128)(4,1)S(1)}, s32[]{:S(2)}) async-start(s8[11010048]{0:T(1024)(128)(4,1)} %bitcast.27), calls=%async_computation.1 | async-start | bytes 8388608
  24.9 7.0 %slice-start.2 = ((s8[11010048]{0:T(1024)(128)(4,1)}), s8[2621440]{0:T(1024)(128)(4,1)S(1)}, s32[]{:S(2)}) async-start(s8[11010048]{0:T(1024)(128)(4,1)} %bitcast.27), calls=%async_computation.2 | async-start | bytes 5242880
  28.8 4.4 %copy-start = (bf16[2,256,3584]{2,1,0:T(8,128)(2,1)S(1)}, bf16[2,256,3584]{2,1,0:T(8,128)(2,1)}, u32[]{:S(2)}) copy-start(bf16[2,256,3584]{2,1,0:T(8,128)(2,1)} %stored_ref.9) | copy-start | bytes 11010052
  36.3 12.9 %collective-permute-start.10 = (bf16[256,768]{1,0:T(8,128)(2,1)S(1)}, bf16[256,768]{1,0:T(8,128)(2,1)S(1)}, u32[]{:S(2)}, u32[]{:S(2)}) collective-permute-start(bf16[256,768]{1,0:T(8,128)(2,1)S(1)} %get-tuple-element.49.after_ref), channel_id=1, source_target_pairs={{0,8},{24,16},{1,9},{25,17},{2,10},{26,18},{3,11},{27,19},{4,12},{... | collective-permute-start | bytes 1179656 | tf_op jit(solution)/shard_map/ppermute | solution.py:306
  43.0 20.5 %collective-permute-start.9 = (bf16[256,640]{1,0:T(8,128)(2,1)S(1)}, bf16[256,640]{1,0:T(8,128)(2,1)S(1)}, u32[]{:S(2)}, u32[]{:S(2)}) collective-permute-start(bf16[256,640]{1,0:T(8,128)(2,1)S(1)} %get-tuple-element.51.after_ref), channel_id=1, source_target_pairs={{0,8},{24,16},{1,9},{25,17},{2,10},{26,18},{3,11},{27,19},{4,12},{... | collective-permute-start | bytes 983048 | tf_op jit(solution)/shard_map/ppermute | solution.py:306
  49.3 14.9 %collective-permute-start.13 = (bf16[256,768]{1,0:T(8,128)(2,1)S(1)}, bf16[256,768]{1,0:T(8,128)(2,1)S(1)}, u32[]{:S(2)}, u32[]{:S(2)}) collective-permute-start(bf16[256,768]{1,0:T(8,128)(2,1)S(1)} %get-tuple-element.53.after_ref), channel_id=1, source_target_pairs={{8,16},{16,8},{9,17},{17,9},{10,18},{18,10},{11,19},{19,11},{12,20... | collective-permute-start | bytes 1179656 | tf_op jit(solution)/shard_map/ppermute | solution.py:306
  56.2 15.1 %collective-permute-start.12 = (bf16[256,768]{1,0:T(8,128)(2,1)S(1)}, bf16[256,768]{1,0:T(8,128)(2,1)S(1)}, u32[]{:S(2)}, u32[]{:S(2)}) collective-permute-start(bf16[256,768]{1,0:T(8,128)(2,1)S(1)} %get-tuple-element.54.after_ref), channel_id=1, source_target_pairs={{0,8},{24,16},{1,9},{25,17},{2,10},{26,18},{3,11},{27,19},{4,12},{... | collective-permute-start | bytes 1179656 | tf_op jit(solution)/shard_map/ppermute | solution.py:306
  63.6 8.6 %collective-permute-start.11 = (bf16[256,640]{1,0:T(8,128)(2,1)S(1)}, bf16[256,640]{1,0:T(8,128)(2,1)S(1)}, u32[]{:S(2)}, u32[]{:S(2)}) collective-permute-start(bf16[256,640]{1,0:T(8,128)(2,1)S(1)} %get-tuple-element.56.after_ref), channel_id=1, source_target_pairs={{8,16},{16,8},{9,17},{17,9},{10,18},{18,10},{11,19},{19,11},{12,20... | collective-permute-start | bytes 983048 | tf_op jit(solution)/shard_map/ppermute | solution.py:306
  64.3 22.9 %collective-permute-start.18 = (bf16[256,768]{1,0:T(8,128)(2,1)S(1)}, bf16[256,768]{1,0:T(8,128)(2,1)S(1)}, u32[]{:S(2)}, u32[]{:S(2)}) collective-permute-start(bf16[256,768]{1,0:T(8,128)(2,1)S(1)} %finished.5.after_ref.final_ref), channel_id=1, source_target_pairs={{8,0},{16,24},{9,1},{17,25},{10,2},{18,26},{11,3},{19,27},{12,4},{... | collective-permute-start | bytes 1179656 | tf_op jit(solution)/shard_map/ppermute | solution.py:312
  71.4 27.1 %collective-permute-start.16 = (bf16[256,768]{1,0:T(8,128)(2,1)S(1)}, bf16[256,768]{1,0:T(8,128)(2,1)S(1)}, u32[]{:S(2)}, u32[]{:S(2)}) collective-permute-start(bf16[256,768]{1,0:T(8,128)(2,1)S(1)} %get-tuple-element.60.after_ref), channel_id=1, source_target_pairs={{8,16},{16,8},{9,17},{17,9},{10,18},{18,10},{11,19},{19,11},{12,20... | collective-permute-start | bytes 1179656 | tf_op jit(solution)/shard_map/ppermute | solution.py:306
  78.4 22.5 %collective-permute-start.14 = (bf16[256,768]{1,0:T(8,128)(2,1)S(1)}, bf16[256,768]{1,0:T(8,128)(2,1)S(1)}, u32[]{:S(2)}, u32[]{:S(2)}) collective-permute-start(bf16[256,768]{1,0:T(8,128)(2,1)S(1)} %get-tuple-element.62.after_ref), channel_id=1, source_target_pairs={{0,8},{24,16},{1,9},{25,17},{2,10},{26,18},{3,11},{27,19},{4,12},{... | collective-permute-start | bytes 1179656 | tf_op jit(solution)/shard_map/ppermute | solution.py:306
  84.6 13.7 %collective-permute-start.17 = (bf16[256,640]{1,0:T(8,128)(2,1)S(1)}, bf16[256,640]{1,0:T(8,128)(2,1)S(1)}, u32[]{:S(2)}, u32[]{:S(2)}) collective-permute-start(bf16[256,640]{1,0:T(8,128)(2,1)S(1)} %get-tuple-element.59.after_ref), channel_id=1, source_target_pairs={{0,8},{24,16},{1,9},{25,17},{2,10},{26,18},{3,11},{27,19},{4,12},{... | collective-permute-start | bytes 983048 | tf_op jit(solution)/shard_map/ppermute | solution.py:306
  86.0 13.9 %collective-permute-start.15 = (bf16[256,640]{1,0:T(8,128)(2,1)S(1)}, bf16[256,640]{1,0:T(8,128)(2,1)S(1)}, u32[]{:S(2)}, u32[]{:S(2)}) collective-permute-start(bf16[256,640]{1,0:T(8,128)(2,1)S(1)} %finished.6.after_ref.final_ref), channel_id=1, source_target_pairs={{8,0},{16,24},{9,1},{17,25},{10,2},{18,26},{11,3},{19,27},{12,4},{... | collective-permute-start | bytes 983048 | tf_op jit(solution)/shard_map/ppermute | solution.py:312
  98.6 10.3 %collective-permute-start.20 = (bf16[256,768]{1,0:T(8,128)(2,1)S(1)}, bf16[256,768]{1,0:T(8,128)(2,1)S(1)}, u32[]{:S(2)}, u32[]{:S(2)}) collective-permute-start(bf16[256,768]{1,0:T(8,128)(2,1)S(1)} %finished.7.after_ref.final_ref), channel_id=1, source_target_pairs={{8,0},{16,24},{9,1},{17,25},{10,2},{18,26},{11,3},{19,27},{12,4},{... | collective-permute-start | bytes 1179656 | tf_op jit(solution)/shard_map/ppermute | solution.py:312
  101.0 8.9 %collective-permute-start.19 = (bf16[256,768]{1,0:T(8,128)(2,1)S(1)}, bf16[256,768]{1,0:T(8,128)(2,1)S(1)}, u32[]{:S(2)}, u32[]{:S(2)}) collective-permute-start(bf16[256,768]{1,0:T(8,128)(2,1)S(1)} %get-tuple-element.72.after_ref), channel_id=1, source_target_pairs={{8,16},{16,8},{9,17},{17,9},{10,18},{18,10},{11,19},{19,11},{12,20... | collective-permute-start | bytes 1179656 | tf_op jit(solution)/shard_map/ppermute | solution.py:306
  101.7 0.7 collective-permute-start.21
  110.0 27.2 %collective-permute-start.22 = (bf16[256,768]{1,0:T(8,128)(2,1)S(1)}, bf16[256,768]{1,0:T(8,128)(2,1)S(1)}, u32[]{:S(2)}, u32[]{:S(2)}) collective-permute-start(bf16[256,768]{1,0:T(8,128)(2,1)S(1)} %finished.9.after_ref.final_ref), channel_id=1, source_target_pairs={{8,0},{16,24},{9,1},{17,25},{10,2},{18,26},{11,3},{19,27},{12,4},{... | collective-permute-start | bytes 1179656 | tf_op jit(solution)/shard_map/ppermute | solution.py:312
  111.3 24.5 %collective-permute-start.23 = (bf16[256,640]{1,0:T(8,128)(2,1)S(1)}, bf16[256,640]{1,0:T(8,128)(2,1)}, u32[]{:S(2)}, u32[]{:S(2)}) collective-permute-start(bf16[256,640]{1,0:T(8,128)(2,1)S(1)} %finished.8.after_ref.final_ref), channel_id=1, source_target_pairs={{8,0},{16,24},{9,1},{17,25},{10,2},{18,26},{11,3},{19,27},{12,4},{... | collective-permute-start | bytes 983048 | tf_op jit(solution)/shard_map/ppermute | solution.py:312
  139.0 1.6 %collective-permute-start.24 = (f32[4,4,8,512]{3,2,0,1:T(8,128)S(1)}, f32[4,4,8,512]{3,2,0,1:T(8,128)S(1)}, u32[]{:S(2)}, u32[]{:S(2)}) collective-permute-start(f32[4,4,8,512]{3,2,0,1:T(8,128)S(1)} %bitcast.30), channel_id=1, source_target_pairs={{0,1},{1,0},{2,3},{3,2},{4,5},{5,4},{6,7},{7,6},{8,9},{9,8},{10,11... | collective-permute-start | bytes 786440 | tf_op jit(solution)/shard_map/ppermute | solution.py:23
  140.7 5.8 %collective-permute-start.25 = (f32[4,8,512]{2,1,0:T(8,128)S(1)}, f32[4,8,512]{2,1,0:T(8,128)S(1)}, u32[]{:S(2)}, u32[]{:S(2)}) collective-permute-start(f32[4,8,512]{2,1,0:T(8,128)S(1)} %get-tuple-element.88), channel_id=1, source_target_pairs={{0,6},{1,7},{2,4},{3,5},{4,2},{5,3},{6,0},{7,1},{8,14},{9,15},{10,... | collective-permute-start | bytes 196616 | tf_op jit(solution)/shard_map/ppermute | solution.py:23
  140.8 5.7 %collective-permute-start.26 = (f32[4,8,512]{2,1,0:T(8,128)S(1)}, f32[4,8,512]{2,1,0:T(8,128)S(1)}, u32[]{:S(2)}, u32[]{:S(2)}) collective-permute-start(f32[4,8,512]{2,1,0:T(8,128)S(1)} %get-tuple-element.86), channel_id=1, source_target_pairs={{0,4},{1,5},{2,6},{3,7},{4,0},{5,1},{6,2},{7,3},{8,12},{9,13},{10,... | collective-permute-start | bytes 196616 | tf_op jit(solution)/shard_map/ppermute | solution.py:23
  142.7 4.3 %collective-permute-start.27 = (f32[4,8,512]{2,1,0:T(8,128)S(1)}, f32[4,8,512]{2,1,0:T(8,128)S(1)}, u32[]{:S(2)}, u32[]{:S(2)}) collective-permute-start(f32[4,8,512]{2,1,0:T(8,128)S(1)} %get-tuple-element.87), channel_id=1, source_target_pairs={{0,2},{1,3},{2,0},{3,1},{4,6},{5,7},{6,4},{7,5},{8,10},{9,11},{10,... | collective-permute-start | bytes 196616 | tf_op jit(solution)/shard_map/ppermute | solution.py:23
  147.6 5.5 %collective-permute-start.28 = (f32[1,8,512]{2,1,0:T(8,128)S(1)}, f32[1,8,512]{2,1,0:T(8,128)S(1)}, u32[]{:S(2)}, u32[]{:S(2)}) collective-permute-start(f32[1,8,512]{2,1,0:T(8,128)S(1)} %get-tuple-element.91), channel_id=1, source_target_pairs={{0,8},{8,16},{16,24},{24,0},{1,9},{9,17},{17,25},{25,1},{2,10},{10... | collective-permute-start | bytes 49160 | tf_op jit(solution)/shard_map/ppermute | solution.py:429
  147.6 5.5 %collective-permute-start.29 = (f32[1,8,512]{2,1,0:T(8,128)S(1)}, f32[1,8,512]{2,1,0:T(8,128)S(1)}, u32[]{:S(2)}, u32[]{:S(2)}) collective-permute-start(f32[1,8,512]{2,1,0:T(8,128)S(1)} %get-tuple-element.90), channel_id=1, source_target_pairs={{0,16},{8,24},{16,0},{24,8},{1,17},{9,25},{17,1},{25,9},{2,18},{10... | collective-permute-start | bytes 49160 | tf_op jit(solution)/shard_map/ppermute | solution.py:429
  150.7 3.7 %collective-permute-start.30 = (f32[1,8,512]{2,1,0:T(8,128)S(1)}, f32[1,8,512]{2,1,0:T(8,128)S(1)}, u32[]{:S(2)}, u32[]{:S(2)}) collective-permute-start(f32[1,8,512]{2,1,0:T(8,128)S(1)} %get-tuple-element.89), channel_id=1, source_target_pairs={{0,24},{8,0},{16,8},{24,16},{1,25},{9,1},{17,9},{25,17},{2,26},{10... | collective-permute-start | bytes 49160 | tf_op jit(solution)/shard_map/ppermute | solution.py:429
  153.2 1.2 copy-start.3
  153.2 1.2 copy-start.4
  154.4 0.6 copy-start.5

commit v4 on v0

v4 whole, which is shorter than its diff:
```python
import functools

import jax
import jax.numpy as jnp
from jax import lax
from jax.experimental import pallas as pl
from jax.experimental.pallas import tpu as pltpu
from jax.sharding import PartitionSpec as P

PARTS = 4
STEPS = 7
SLOTS = 4
PIECES = 4
LANES = 128
VMEM = pl.BlockSpec(memory_space=pltpu.VMEM)
ANY = pl.BlockSpec(memory_space=pl.ANY)
SMEM = pl.BlockSpec(memory_space=pltpu.SMEM)


def flipped(array, bit, count):
    return lax.ppermute(array, "col", [(c, c ^ bit) for c in range(count)])


def gathered(new_keys, col_count, col_index, fetch):
    rows = new_keys.shape[0]
    if col_count != 8:
        own, after = fetch(new_keys)
        start = col_index * rows
        return [own, lax.all_gather(new_keys, "col", axis=0, tiled=True)], [start, jnp.int32(0)], after
    half = rows // 2
    by_x = flipped(new_keys, 2, 8)
    by_y = flipped(new_keys, 4, 8)
    by_core = flipped(new_keys, 1, 8)
    own, after = fetch(by_core)
    low, high = halved(by_x, by_y, after)
    low = flipped(low, 4, 8)
    high = flipped(high, 2, 8)
    x_core = flipped(by_x, 1, 8)
    y_core = flipped(by_y, 1, 8)
    low_core = flipped(low, 1, 8)
    high_core = flipped(high, 1, 8)
    pieces = [own, by_core, by_x, x_core, by_y, y_core, low, high, low_core, high_core]
    of = [0, 1, 2, 3, 4, 5, 6, 6, 7, 7]
    within = [0] * 7 + [half, 0, half]
    return pieces, [(col_index ^ f) * rows + w for f, w in zip(of, within)], after


def halved_kernel(x_ref, y_ref, after_ref, low_ref, high_ref):
    half = low_ref.shape[0]
    low_ref[...] = x_ref[:half]
    high_ref[...] = y_ref[half:]


def halved(by_x, by_y, after):
    rows, depth = by_x.shape
    return pl.pallas_call(
        halved_kernel,
        in_specs=[VMEM, VMEM, ANY],
        out_specs=[VMEM, VMEM],
        out_shape=[jax.ShapeDtypeStruct((rows // 2, depth), by_x.dtype)] * 2,
        compiler_params=params(),
        cost_estimate=cost(),
        name="halved",
    )(by_x, by_y, after)


def fetch_kernel(span, weights_ref, stored_ref, own_ref, after_ref, held_ref, batches_ref, keys_ref, token_ref, arrived):
    deep = held_ref.shape[0] // PIECES
    copies = [
        pltpu.make_async_copy(own_ref, keys_ref, arrived.at[PIECES]),
        pltpu.make_async_copy(stored_ref, batches_ref, arrived.at[PIECES + 1]),
    ]
    for k in range(PIECES):
        rows = pl.ds(k * deep, deep)
        source = weights_ref.at[rows, pl.ds(span[0], span[1] - span[0])]
        copies.append(pltpu.make_async_copy(source, held_ref.at[rows, :], arrived.at[k]))
    for copy in copies:
        copy.start()
    token_ref[...] = jnp.zeros_like(token_ref)
    for copy in copies:
        copy.wait()


def fetched(weights, stored, own, span, after):
    depth, wide = weights.shape[0], span[1] - span[0]
    return pl.pallas_call(
        functools.partial(fetch_kernel, span),
        in_specs=[ANY] * 4,
        out_specs=[VMEM] * 4,
        out_shape=[
            jax.ShapeDtypeStruct((depth, wide), weights.dtype),
            jax.ShapeDtypeStruct(stored.shape, stored.dtype),
            jax.ShapeDtypeStruct(own.shape, own.dtype),
            jax.ShapeDtypeStruct((8, LANES), jnp.float32),
        ],
        scratch_shapes=[pltpu.SemaphoreType.DMA((PIECES + 2,))],
        compiler_params=params(),
        cost_estimate=cost(),
        name="fetch",
    )(weights, stored, own, after)


def ranges(columns):
    tiles = columns // LANES
    count = max(n for n in range(1, PARTS + 1) if tiles % n == 0)
    wide = tiles // count * LANES
    return [(i * wide, (i + 1) * wide) for i in range(count)]


def cost():
    return pl.CostEstimate(flops=1, bytes_accessed=1, transcendentals=0)


def params():
    return pltpu.CompilerParams(vmem_limit_bytes=12 * 2**20)


def assemble_kernel(count, starts_ref, after_ref, *refs):
    keys_ref = refs[count]
    for i, piece in enumerate(refs[:count]):
        keys_ref[pl.ds(pl.multiple_of(starts_ref[i], 16), piece.shape[0]), :] = piece[...]


def assembled(pieces, starts, keys, after):
    return pl.pallas_call(
        functools.partial(assemble_kernel, len(pieces)),
        in_specs=[SMEM, ANY] + [VMEM] * len(pieces),
        out_specs=VMEM,
        out_shape=jax.ShapeDtypeStruct((keys, pieces[0].shape[1]), pieces[0].dtype),
        compiler_params=params(),
        cost_estimate=cost(),
        name="assemble",
    )(starts, after, *pieces)


def multiply(left, early, keys_ref, weights_ref, wide_ref, held_ref, arrived):
    wide = wide_ref.shape[1]
    deep = keys_ref.shape[1] // STEPS

    def copy(step):
        return pltpu.make_async_copy(
            weights_ref.at[pl.ds(step * deep, deep), pl.ds(left, wide)],
            held_ref.at[step % SLOTS],
            arrived.at[step % SLOTS],
        )

    if not early:
        for step in range(min(SLOTS, STEPS)):
            copy(step).start()
    for step in range(STEPS):
        if early:
            weights = weights_ref[step * deep : (step + 1) * deep, :]
        else:
            copy(step).wait()
            weights = held_ref[step % SLOTS]
        part = jnp.dot(
            keys_ref[:, step * deep : (step + 1) * deep],
            weights,
            preferred_element_type=jnp.float32,
        )
        if not early and step + SLOTS < STEPS:
            copy(step + SLOTS).start()
        wide_ref[...] = part if step == 0 else wide_ref[...] + part


def against(left, at_ref, final_ref, came_ref, stored_ref, before, terms_ref, piece_ref, rows_ref):
    @pl.when(at_ref[0] != 0)
    def _():
        rows_ref[...] = final_ref[...]

    @pl.when(at_ref[0] == 0)
    def _():
        rows_ref[...] = came_ref[...]

    batches, slots, _ = stored_ref.shape
    wide = rows_ref.shape[1]
    term = lax.dot_general(
        rows_ref[...],
        stored_ref[:, :, left : left + wide].reshape(batches * slots, wide),
        (((1,), (1,)), ((), ())),
        preferred_element_type=jnp.float32,
    )
    terms_ref[...] = before[0][...] + term if before else term
    piece_ref[...] = rows_ref[pl.ds(pl.multiple_of(at_ref[1], 16), piece_ref.shape[0]), :]


def work_kernel(product, contract, joined, at_ref, after_ref, *refs):
    refs = list(refs)
    take = lambda n: [refs.pop(0) for _ in range(n)]
    if product:
        factors = take(2)
    if contract:
        rows = take(3)
        before = take(contract[1])
        pieces = take(joined)
    if product:
        (wide_ref,) = take(1)
    if contract:
        terms_ref, piece_ref = take(2)
    if joined:
        (whole_ref,) = take(1)
    if product:
        multiply(*product, *factors, wide_ref, *take(2))
    if contract:
        against(contract[0], at_ref, *rows, before, terms_ref, piece_ref, *take(1))
    if joined:
        left = 0
        for piece in pieces + [piece_ref]:
            whole_ref[:, left : left + piece.shape[1]] = piece[...]
            left += piece.shape[1]


def work(at, after, product=None, contract=None, pieces=()):
    operands, specs, shapes, scratch = [at, after], [SMEM, ANY], [], []
    product_at = contract_at = None
    if product:
        keys, weights, early, span = product
        depth, rows, wide = weights.shape[0], keys.shape[0], span[1] - span[0]
        product_at = (span[0], early)
        operands += [keys, weights]
        specs += [VMEM, VMEM if early else ANY]
        shapes += [jax.ShapeDtypeStruct((rows, wide), jnp.float32)]
        scratch += [
            pltpu.VMEM((SLOTS, 16 if early else depth // STEPS, wide), weights.dtype),
            pltpu.SemaphoreType.DMA((SLOTS,)),
        ]
    if contract:
        final, came, stored, terms, left, block = contract
        rows, wide = final.shape
        before = [] if terms is None else [terms]
        contract_at = (left, len(before))
        operands += [final, came, stored, *before, *pieces]
        specs += [VMEM] * (3 + len(before) + len(pieces))
        shapes += [
            jax.ShapeDtypeStruct((rows, stored.shape[0] * stored.shape[1]), jnp.float32),
            jax.ShapeDtypeStruct((block, wide), jnp.bfloat16),
        ]
        scratch += [pltpu.VMEM((rows, wide), jnp.bfloat16)]
    if pieces:
        columns = sum(p.shape[1] for p in pieces) + wide
        shapes += [jax.ShapeDtypeStruct((block, columns), jnp.bfloat16)]
    return pl.pallas_call(
        functools.partial(work_kernel, product_at, contract_at, len(pieces)),
        in_specs=specs,
        out_specs=[VMEM] * len(shapes),
        out_shape=shapes,
        scratch_shapes=scratch,
        compiler_params=params(),
        cost_estimate=cost(),
        name="work",
    )(*operands)


def tick_kernel(names, outs, at_ref, after_ref, *refs):
    given = dict(zip(names, refs))
    made = dict(zip(outs, refs[len(names) :]))
    if "total" in made:
        total = given["wide"][...] + given["outer"][...].astype(jnp.float32)
        made["total"][...] = total
        made["across"][...] = total.astype(jnp.bfloat16)
    if "final" in made:
        final = (given["held"][...] + given["middle"][...].astype(jnp.float32)).astype(jnp.bfloat16)
        made["final"][...] = final
    if "along" in made:
        along = given["next"][...].astype(jnp.bfloat16)
        if "final" in made:
            along = jnp.where(at_ref[0] != 0, final, along)
        made["along"][...] = along


def tick(at, after, outs, **given):
    shape = next(iter(given.values())).shape
    wide = {"total": jnp.float32}
    made = pl.pallas_call(
        functools.partial(tick_kernel, tuple(given), outs),
        in_specs=[SMEM, ANY] + [VMEM] * len(given),
        out_specs=[VMEM] * len(outs),
        out_shape=[jax.ShapeDtypeStruct(shape, wide.get(name, jnp.bfloat16)) for name in outs],
        compiler_params=params(),
        cost_estimate=cost(),
        name="tick",
    )(at, after, *given.values())
    return dict(zip(outs, made))


def along_line(at, multiplied, contracted, count):
    wide, total, final = {}, {}, {}
    (wide[0],) = multiplied(0, at)
    outer = middle = None
    after = wide[0]
    for k in range(count + 2):
        outs, given = [], {}
        if 1 <= k <= count:
            outs += ["total", "across"]
            given.update(wide=wide[k - 1], outer=outer)
        if k >= 2:
            outs += ["final"]
            given.update(held=total[k - 2], middle=middle)
        if k < count:
            outs += ["along"]
            given.update(next=wide[k])
        made = tick(at, after, tuple(outs), **given)
        earlier = outer
        if k >= 2:
            final[k - 2] = made["final"]
        if 1 <= k <= count:
            total[k - 1] = made["total"]
            middle = lax.ppermute(made["across"], "row", [(1, 2), (2, 1)])
        pairs = ([(0, 1), (3, 2)] if k < count else []) + ([(1, 0), (2, 3)] if k >= 2 else [])
        sent = made["along"] if k < count else made["final"] if k >= 2 else made["across"]
        if pairs:
            outer = lax.ppermute(sent, "row", pairs)
        after = sent
        if k + 1 < count or k >= 3:
            product = k + 1 if k + 1 < count else None
            contract = (k - 3, final[k - 3], earlier) if k >= 3 else None
            out = multiplied(product, after, contract)
            if product is not None:
                wide[product] = out[0]
            after = out[-1]
    contracted(count - 1, final[count - 1], outer, after)


def select_kernel(count, row_ref, batch_ref, used_ref, length_ref, slot_ref, *refs):
    parts, out_ref, held_ref = refs[:count], refs[count], refs[count + 1]
    batches, rows, slots = held_ref.shape[1:]
    for i, part in enumerate(parts):
        for b in range(batches):
            held_ref[i, b] = part[0, :, b * slots : (b + 1) * slots]
    row = row_ref[0]
    column = lax.broadcasted_iota(jnp.int32, (rows, slots), 1)
    for place in range(out_ref.shape[1]):
        batch = batch_ref[row, place]
        slot = slot_ref[batch]
        owner = lax.div(slot, batches)
        shift = lax.rem(row - owner + count, count)
        length = jnp.where(place < used_ref[row], length_ref[batch], 0)
        value = held_ref[shift, slot - owner * batches]
        out_ref[0, place] = jnp.where(column < length, value, 0.0)


def selected(parts, row_index, pair_batch, pair_count, batch_length, batch_slot, batches):
    count = len(parts)
    _, rows, wide = parts[0].shape
    slots = wide // batches
    places = pair_batch.shape[1]
    return pl.pallas_call(
        functools.partial(select_kernel, count),
        in_specs=[SMEM] * 5 + [VMEM] * count,
        out_specs=VMEM,
        out_shape=jax.ShapeDtypeStruct((1, places, rows, slots), jnp.float32),
        scratch_shapes=[pltpu.VMEM((count, batches, rows, slots), jnp.float32)],
        cost_estimate=cost(),
        name="select",
    )(row_index[None], pair_batch, pair_count, batch_length, batch_slot, *parts)


def shards(new_keys, precision, stored_keys, pair_batch, pair_count, batch_length, batch_slot):
    row_count = lax.axis_size("row")
    col_count = lax.axis_size("col")
    row_index = lax.axis_index("row")
    col_index = lax.axis_index("col")
    total_keys = new_keys.shape[0] * col_count
    block = total_keys // row_count
    batches = stored_keys.shape[0]
    half = row_count // 2

    away = jnp.where(row_index < half, half - 1 - row_index, row_index - half)
    at = jnp.stack([(away == 0).astype(jnp.int32), row_index * block])
    spans = ranges(precision.shape[1])
    count = len(spans)
    early, stored, own, token = None, None, None, None

    def fetch(after):
        nonlocal early, stored, token
        early, stored, own, token = fetched(precision, stored_keys, new_keys, spans[0], after)
        return own, token

    pieces, starts, token = gathered(new_keys, col_count, col_index, fetch)
    order = list(range(1, len(pieces))) + [0]
    keys = assembled([pieces[i] for i in order], jnp.stack([starts[i] for i in order]), total_keys, token)
    terms = None
    whitened = []

    def multiplied(part, after, contract=None):
        nonlocal terms
        product = None
        if part is not None:
            product = (keys, precision if part else early, part == 0, spans[part])
        if contract is not None:
            number, final, came = contract
            contract = (final, came, stored, terms, spans[number][0], block)
        joined = whitened if contract is not None and number == count - 1 else []
        out = work(at, after, product, contract, joined)
        if contract is not None:
            first = 1 if product else 0
            terms = out[first]
            whitened.append(out[-1])
        return out

    def contracted(part, final, came, after):
        multiplied(None, after, (part, final, came))

    if row_count == 4:
        along_line(at, multiplied, contracted, count)
    else:
        after = at
        for part in range(count):
            (wide,) = multiplied(part, after)
            every = lax.psum(wide, "row").astype(jnp.bfloat16)
            contracted(part, every, every, wide)
            after = whitened[-1]

    share = block // col_count
    sums = terms.reshape(row_count, col_count, share, terms.shape[1])
    bit = 1
    while bit < col_count:
        if col_count == 8 and bit == 2:
            other = [lax.dynamic_index_in_dim(sums, (col_index // 2) ^ f, 1, keepdims=False) for f in range(4)]
            sums = other[0] + sum(flipped(other[f], 2 * f, col_count) for f in (3, 2, 1))
            sums = sums[:, None]
            break
        pairs = sums.reshape(row_count, sums.shape[1] // 2, 2, share, sums.shape[3])
        mine = (col_index // bit) % 2
        kept = lax.dynamic_index_in_dim(pairs, mine, 2, keepdims=False)
        left = lax.dynamic_index_in_dim(pairs, 1 - mine, 2, keepdims=False)
        sums = kept + flipped(left, bit, col_count)
        bit *= 2
    sums = sums[:, 0]
    parts = []
    for shift in range(row_count):
        part = lax.dynamic_slice_in_dim(sums, (row_index + shift) % row_count, 1, 0)
        if shift:
            part = lax.ppermute(part, "row", [(r, (r + shift) % row_count) for r in range(row_count)])
        parts.append(part)
    shares = selected(parts, row_index, pair_batch, pair_count, batch_length, batch_slot, batches)
    return (whitened[-1], shares)


def solution(mesh):
    placed = (P("col", "row"), P("row", "col"), P("row", None, "col"), P(), P(), P(), P())
    return jax.shard_map(
        shards,
        mesh=mesh,
        in_specs=placed,
        out_specs=(P("row", "col"), P("row", None, "col", None)),
        check_vma=False,
    )
```

time: 263 us -> 141 us (0.54)
  blocking collectives: 131 us -> 0 us
  Pallas kernels: 0 us -> 43.1 us
  waiting for transfers between devices: 80 us -> 43.3 us
  starting transfers between devices: 3.55 us -> 35.6 us
  matrix products: 27.3 us -> 0 us
  between operations: 14.1 us -> 0.97 us
  local copies, waits for them, and re-layouts: 4.76 us -> 17.5 us
    psum x1 -> x0, blocking collectives: 131 us -> none  [shards(): every_row = lax.psum(partial_value, 'row').astype(jnp.bfloat16)]
    ppermute x0 -> x26, waiting for transfers between devices: none -> 43.3 us  [the longest x6 29.1 us: along_line(): outer = lax.ppermute(sent, 'row', pairs)]
    pallas_call x0 -> x18, Pallas kernels: none -> 43.1 us  [the longest x8 30.6 us: work(): pl.pallas_call(functools.partial(work_kernel, product_at, contract_at, le...]
    all_gather x1 -> x0, waiting for transfers between devices: 37.3 us -> none  [shards(): lax.all_gather(new_keys, 'col', axis=0, tiled=True)]
    ppermute x0 -> x26, starting transfers between devices: none -> 35.6 us  [the longest x6 18.1 us: along_line(): outer = lax.ppermute(sent, 'row', pairs)]
    reduce_scatter x1 -> x0, waiting for transfers between devices: 31.3 us -> none  [shards(): shares = lax.psum_scatter(picked, 'col', scatter_dimension=1, tiled=True)]
    dot_general x2 -> x0, matrix products: 27.3 us -> none  [the longest x1 24.1 us: shards(): jnp.dot(lax.all_gather(new_keys, 'col', axis=0, tiled=True), precision, p...]
    unnamed x4 -> x20, local copies, waits for them, and re-layouts: 0.02 us -> 16.8 us
  transfers between devices with their start and end apart: 3 -> 26, of which waited for: 3 -> 16; matrix products, arithmetic and copies ran while one was open for 2% -> 0% of each run, Pallas kernels for 0% -> 21%
where the time goes in v4:
time: 141 us
  waiting for transfers between devices  43.3 us (31%)
  Pallas kernels  43.1 us (31%)
  starting transfers between devices  35.6 us (25%)
  local copies, waits for them, and re-layouts  17.5 us (12%)
    pallas_call x8, Pallas kernels, work(): pl.pallas_call(functools.partial(work_kernel, product_at, contract_at, le...  30.6 us
    ppermute x6, waiting for transfers between devices, along_line(): outer = lax.ppermute(sent, 'row', pairs)  29.1 us
    ppermute x6, starting transfers between devices, along_line(): outer = lax.ppermute(sent, 'row', pairs)  18.1 us
    unnamed x20, local copies, waits for them, and re-layouts  16.8 us
    ppermute x13, waiting for transfers between devices, flipped(): return lax.ppermute(array, 'col', [(c, c ^ bit) for c in range(count)])  12 us
    ppermute x13, starting transfers between devices, flipped(): return lax.ppermute(array, 'col', [(c, c ^ bit) for c in range(count)])  10.8 us
    pallas_call x1, Pallas kernels, fetched(): pl.pallas_call(functools.partial(fetch_kernel, span), in_specs=[ANY] * 4,...  5.36 us
    pallas_call x6, Pallas kernels, tick(): pl.pallas_call(functools.partial(tick_kernel, tuple(given), outs), in_spe...  4.39 us
  transfers between devices with their start and end apart: 26, of which 16 were waited for; matrix products, arithmetic and copies ran while one was open for 0% of the time, Pallas kernels for 21%

profile of v4, /device:TPU:0, one launch (start us, length us, event | category | flops | bytes accessed | tf_op | source)
XLA Modules:
  0.0 140.7 jit_solution(13007018809745223724)
XLA Ops:
  0.6 0.5 collective-permute-start
  1.1 2.6 %collective-permute-start.1 = (bf16[32,7168]{1,0:T(8,128)(2,1)}, bf16[32,7168]{1,0:T(8,128)(2,1)S(1)}, u32[]{:S(2)}, u32[]{:S(2)}) collective-permute-start(bf16[32,7168]{1,0:T(8,128)(2,1)} %own_ref.1), channel_id=1, source_target_pairs={{0,2},{1,3},{2,0},{3,1},{4,6},{5,7},{6,4},{7,5},{8,10},{9,11},{10,... | collective-permute-start | bytes 1376264 | tf_op jit(solution)/shard_map/ppermute | solution.py:21
  3.7 1.5 %collective-permute-start.3 = (bf16[32,7168]{1,0:T(8,128)(2,1)}, bf16[32,7168]{1,0:T(8,128)(2,1)S(1)}, u32[]{:S(2)}, u32[]{:S(2)}) collective-permute-start(bf16[32,7168]{1,0:T(8,128)(2,1)} %own_ref.1), channel_id=1, source_target_pairs={{0,4},{1,5},{2,6},{3,7},{4,0},{5,1},{6,2},{7,3},{8,12},{9,13},{10,... | collective-permute-start | bytes 1376264 | tf_op jit(solution)/shard_map/ppermute | solution.py:21
  5.2 2.0 %copy-done.5 = bf16[2,256,3584]{2,1,0:T(8,128)(2,1)S(1)} copy-done((bf16[2,256,3584]{2,1,0:T(8,128)(2,1)S(1)}, bf16[2,256,3584]{2,1,0:T(8,128)(2,1)}, u32[]{:S(2)}) %copy-start.5) | copy-done | bytes 3670040
  7.3 1.0 copy-done.6
  8.3 5.4 %fetch.1 = (bf16[7168,896]{1,0:T(8,128)(2,1)S(1)}, bf16[2,256,3584]{2,1,0:T(8,128)(2,1)S(1)}, bf16[32,7168]{1,0:T(8,128)(2,1)S(1)}, f32[8,128]{1,0:T(8,128)S(1)}) custom-call(bf16[7168,3584]{1,0:T(8,128)(2,1)} %refs_1_.5, bf16[2,256,3584]{2,1,0:T(8,128)(2,1)S(1)} %copy-done.5, bf16[32,7168]{1,0:T(8,128)(2,1)S(1)} %copy-done.6, ...), custom_call_target="tpu_custom_call" | custom-call | flops 1 | bytes 1 | tf_op jit(solution)/shard_map/fetch/pallas_call | solution.py:86
  13.7 1.8 %copy-done = bf16[2,256,3584]{2,1,0:T(8,128)(2,1)} copy-done((bf16[2,256,3584]{2,1,0:T(8,128)(2,1)}, bf16[2,256,3584]{2,1,0:T(8,128)(2,1)S(1)}, u32[]{:S(2)}) %copy-start) | copy-done | bytes 3670040
  15.4 4.6 %copy-done.3 = bf16[7168,896]{1,0:T(8,128)(2,1)} copy-done((bf16[7168,896]{1,0:T(8,128)(2,1)}, bf16[7168,896]{1,0:T(8,128)(2,1)S(1)}, u32[]{:S(2)}) %copy-start.3) | copy-done | bytes 12845080
  20.1 0.6 collective-permute-start.5
  20.7 1.4 %collective-permute-start.6 = (bf16[16,7168]{1,0:T(8,128)(2,1)S(1)}, bf16[16,7168]{1,0:T(8,128)(2,1)S(1)}, u32[]{:S(2)}, u32[]{:S(2)}) collective-permute-start(bf16[16,7168]{1,0:T(8,128)(2,1)S(1)} %get-tuple-element.32), channel_id=1, source_target_pairs={{0,2},{1,3},{2,0},{3,1},{4,6},{5,7},{6,4},{7,5},{8,10},{9,11},{10,... | collective-permute-start | bytes 688136 | tf_op jit(solution)/shard_map/ppermute | solution.py:21
  22.2 0.5 collective-permute-start.4
  22.7 4.9 %collective-permute-done.5.refs_5_ = bf16[16,7168]{1,0:T(8,128)(2,1)S(1)} collective-permute-done((bf16[16,7168]{1,0:T(8,128)(2,1)S(1)}, bf16[16,7168]{1,0:T(8,128)(2,1)S(1)}, u32[]{:S(2)}, u32[]{:S(2)}) %collective-permute-start.5) | collective-permute-done | bytes 229408 | tf_op jit(solution)/shard_map/ppermute | solution.py:21
  27.6 0.4 collective-permute-done.6.refs_6_
  28.0 0.1 collective-permute-start.8
  28.1 0.1 stack.59.starts_ref
  28.3 0.8 collective-permute-done.7.refs_7_
  29.1 0.6 collective-permute-done.8.refs_8_
  29.6 1.2 assemble.1.refs_0_
  30.9 4.6 %copy-done.4 = bf16[7168,896]{1,0:T(8,128)(2,1)S(1)} copy-done((bf16[7168,896]{1,0:T(8,128)(2,1)S(1)}, bf16[7168,896]{1,0:T(8,128)(2,1)}, u32[]{:S(2)}) %copy-start.4) | copy-done | bytes 12845080
  35.5 4.5 %work.8.after_ref.refs_0_ = f32[256,896]{1,0:T(8,128)S(1)} custom-call(s32[2]{0:T(128)S(1)} %pad_add_fusion.at_ref.after_ref, s32[2]{0:T(128)S(1)} %pad_add_fusion.at_ref.after_ref, bf16[256,7168]{1,0:T(8,128)(2,1)S(1)} %assemble.1.refs_0_, bf16[7168,896]{1,0:T(8,128)(2,1)S(1)} %copy-done.4), custom_call_target="tpu_custom_call" | custom-call | flops 1 | bytes 1 | tf_op jit(solution)/shard_map/work/pallas_call | solution.py:242
  40.1 0.6 tick.6.after_ref
  40.7 3.5 %collective-permute-start.9 = (bf16[256,896]{1,0:T(8,128)(2,1)S(1)}, bf16[256,896]{1,0:T(8,128)(2,1)S(1)}, u32[]{:S(2)}, u32[]{:S(2)}) collective-permute-start(bf16[256,896]{1,0:T(8,128)(2,1)S(1)} %tick.6.after_ref), channel_id=1, source_target_pairs={{0,8},{24,16},{1,9},{25,17},{2,10},{26,18},{3,11},{27,19},{4,12},{... | collective-permute-start | bytes 1376264 | tf_op jit(solution)/shard_map/ppermute | solution.py:312
  44.2 7.0 %work.9.after_ref.refs_2_.refs_0_ = f32[256,896]{1,0:T(8,128)S(1)} custom-call(s32[2]{0:T(128)S(1)} %pad_add_fusion.at_ref.after_ref, bf16[256,896]{1,0:T(8,128)(2,1)S(1)} %tick.6.after_ref, bf16[256,7168]{1,0:T(8,128)(2,1)S(1)} %assemble.1.refs_0_, bf16[7168,3584]{1,0:T(8,128)(2,1)} %refs_1_.5), custom_call_target="tpu_custom_call" | custom-call | flops 1 | bytes 1 | tf_op jit(solution)/shard_map/work/pallas_call | solution.py:242
  51.2 3.0 %collective-permute-done.9.refs_1_ = bf16[256,896]{1,0:T(8,128)(2,1)S(1)} collective-permute-done((bf16[256,896]{1,0:T(8,128)(2,1)S(1)}, bf16[256,896]{1,0:T(8,128)(2,1)S(1)}, u32[]{:S(2)}, u32[]{:S(2)}) %collective-permute-start.9) | collective-permute-done | bytes 458784 | tf_op jit(solution)/shard_map/ppermute | solution.py:312
  54.2 0.7 tick.7
  54.9 4.4 %collective-permute-start.10 = (bf16[256,896]{1,0:T(8,128)(2,1)S(1)}, bf16[256,896]{1,0:T(8,128)(2,1)S(1)}, u32[]{:S(2)}, u32[]{:S(2)}) collective-permute-start(bf16[256,896]{1,0:T(8,128)(2,1)S(1)} %get-tuple-element.35.after_ref), channel_id=1, source_target_pairs={{0,8},{24,16},{1,9},{25,17},{2,10},{26,18},{3,11},{27,19},{4,12},{... | collective-permute-start | bytes 1376264 | tf_op jit(solution)/shard_map/ppermute | solution.py:312
  59.3 0.9 collective-permute-start.11
  60.2 7.0 %work.10.after_ref.refs_4_.refs_0_ = f32[256,896]{1,0:T(8,128)S(1)} custom-call(s32[2]{0:T(128)S(1)} %pad_add_fusion.at_ref.after_ref, bf16[256,896]{1,0:T(8,128)(2,1)S(1)} %get-tuple-element.35.after_ref, bf16[256,7168]{1,0:T(8,128)(2,1)S(1)} %assemble.1.refs_0_, bf16[7168,3584]{1,0:T(8,128)(2,1)} %refs_1_.5), custom_call_target="tpu_custom_call" | custom-call | flops 1 | bytes 1 | tf_op jit(solution)/shard_map/work/pallas_call | solution.py:242
  67.3 1.3 collective-permute-done.10.refs_1_
  68.6 0.9 tick.8
  69.4 3.8 %collective-permute-start.12 = (bf16[256,896]{1,0:T(8,128)(2,1)S(1)}, bf16[256,896]{1,0:T(8,128)(2,1)S(1)}, u32[]{:S(2)}, u32[]{:S(2)}) collective-permute-start(bf16[256,896]{1,0:T(8,128)(2,1)S(1)} %get-tuple-element.38.after_ref), channel_id=1, source_target_pairs={{0,8},{24,16},{8,0},{16,24},{1,9},{25,17},{9,1},{17,25},{2,10},{26... | collective-permute-start | bytes 1376264 | tf_op jit(solution)/shard_map/ppermute | solution.py:312
  73.3 0.7 collective-permute-start.13
  73.9 7.0 %work.11.after_ref.refs_4_.refs_0_ = f32[256,896]{1,0:T(8,128)S(1)} custom-call(s32[2]{0:T(128)S(1)} %pad_add_fusion.at_ref.after_ref, bf16[256,896]{1,0:T(8,128)(2,1)S(1)} %get-tuple-element.38.after_ref, bf16[256,7168]{1,0:T(8,128)(2,1)S(1)} %assemble.1.refs_0_, bf16[7168,3584]{1,0:T(8,128)(2,1)} %refs_1_.5), custom_call_target="tpu_custom_call" | custom-call | flops 1 | bytes 1 | tf_op jit(solution)/shard_map/work/pallas_call | solution.py:242
  81.0 1.3 collective-permute-done.12.refs_1_
  82.3 0.9 tick.9
  83.2 3.7 %collective-permute-start.14 = (bf16[256,896]{1,0:T(8,128)(2,1)S(1)}, bf16[256,896]{1,0:T(8,128)(2,1)S(1)}, u32[]{:S(2)}, u32[]{:S(2)}) collective-permute-start(bf16[256,896]{1,0:T(8,128)(2,1)S(1)} %get-tuple-element.41.after_ref), channel_id=1, source_target_pairs={{0,8},{24,16},{8,0},{16,24},{1,9},{25,17},{9,1},{17,25},{2,10},{26... | collective-permute-start | bytes 1376264 | tf_op jit(solution)/shard_map/ppermute | solution.py:312
  86.9 0.7 collective-permute-start.15
  87.6 1.0 work.12
  88.7 6.4 %collective-permute-done.14.refs_1_ = bf16[256,896]{1,0:T(8,128)(2,1)S(1)} collective-permute-done((bf16[256,896]{1,0:T(8,128)(2,1)S(1)}, bf16[256,896]{1,0:T(8,128)(2,1)S(1)}, u32[]{:S(2)}, u32[]{:S(2)}) %collective-permute-start.14) | collective-permute-done | bytes 458784 | tf_op jit(solution)/shard_map/ppermute | solution.py:312
  95.1 0.7 tick.10
  95.8 0.7 collective-permute-start.16
  96.5 1.3 collective-permute-start.17
  97.8 1.1 work.13
  98.9 0.6 tick.11.after_ref.refs_0_
  99.5 1.3 collective-permute-start.18
  100.8 12.7 %collective-permute-done.17.refs_1_ = bf16[256,896]{1,0:T(8,128)(2,1)S(1)} collective-permute-done((bf16[256,896]{1,0:T(8,128)(2,1)S(1)}, bf16[256,896]{1,0:T(8,128)(2,1)S(1)}, u32[]{:S(2)}, u32[]{:S(2)}) %collective-permute-start.17) | collective-permute-done | bytes 458784 | tf_op jit(solution)/shard_map/ppermute | solution.py:312
  113.6 2.0 %copy-done.2 = bf16[2,256,3584]{2,1,0:T(8,128)(2,1)S(1)} copy-done((bf16[2,256,3584]{2,1,0:T(8,128)(2,1)S(1)}, bf16[2,256,3584]{2,1,0:T(8,128)(2,1)}, u32[]{:S(2)}) %copy-start.2) | copy-done | bytes 3670040
  115.6 1.0 work.14
  116.7 4.3 %collective-permute-done.18.refs_1_ = bf16[256,896]{1,0:T(8,128)(2,1)S(1)} collective-permute-done((bf16[256,896]{1,0:T(8,128)(2,1)S(1)}, bf16[256,896]{1,0:T(8,128)(2,1)S(1)}, u32[]{:S(2)}, u32[]{:S(2)}) %collective-permute-start.18) | collective-permute-done | bytes 458784 | tf_op jit(solution)/shard_map/ppermute | solution.py:312
  121.0 1.8 %work.15 = (f32[256,512]{1,0:T(8,128)S(1)}, bf16[64,896]{1,0:T(8,128)(2,1)}, bf16[64,3584]{1,0:T(8,128)(2,1)}) custom-call(s32[2]{0:T(128)S(1)} %pad_add_fusion.at_ref.after_ref, bf16[64,896]{1,0:T(8,128)(2,1)S(1)} %get-tuple-element.54.after_ref.refs_6_, bf16[256,896]{1,0:T(8,128)(2,1)S(1)} %tick.11.after_ref.refs_0_, ...), custom_call_target="tpu_custom_call" | custom-call | flops 1 | bytes 1 | tf_op jit(solution)/shard_map/work/pallas_call | solution.py:242
  123.0 1.5 %collective-permute-done.19 = f32[4,4,8,512]{3,2,0,1:T(8,128)S(1)} collective-permute-done((f32[4,4,8,512]{3,2,0,1:T(8,128)S(1)}, f32[4,4,8,512]{3,2,0,1:T(8,128)S(1)}, u32[]{:S(2)}, u32[]{:S(2)}) %collective-permute-start.19) | collective-permute-done | bytes 262176 | tf_op jit(solution)/shard_map/ppermute | solution.py:21
  124.5 1.9 %collective-permute-start.20 = (f32[4,8,512]{2,1,0:T(8,128)S(1)}, f32[4,8,512]{2,1,0:T(8,128)S(1)}, u32[]{:S(2)}, u32[]{:S(2)}) collective-permute-start(f32[4,8,512]{2,1,0:T(8,128)S(1)} %get-tuple-element.62), channel_id=1, source_target_pairs={{0,6},{1,7},{2,4},{3,5},{4,2},{5,3},{6,0},{7,1},{8,14},{9,15},{10,... | collective-permute-start | bytes 196616 | tf_op jit(solution)/shard_map/ppermute | solution.py:21
  126.4 1.1 collective-permute-start.21
  127.6 0.5 collective-permute-start.22
  128.1 1.7 %collective-permute-done.20 = f32[4,8,512]{2,1,0:T(8,128)S(1)} collective-permute-done((f32[4,8,512]{2,1,0:T(8,128)S(1)}, f32[4,8,512]{2,1,0:T(8,128)S(1)}, u32[]{:S(2)}, u32[]{:S(2)}) %collective-permute-start.20) | collective-permute-done | bytes 65568 | tf_op jit(solution)/shard_map/ppermute | solution.py:21
  129.8 1.2 collective-permute-done.21
  131.0 0.8 collective-permute-done.22
  131.8 0.6 constant_dynamic-slice_fusion
  132.5 1.9 %collective-permute-start.24 = (f32[1,8,512]{2,1,0:T(8,128)S(1)}, f32[1,8,512]{2,1,0:T(8,128)S(1)}, u32[]{:S(2)}, u32[]{:S(2)}) collective-permute-start(f32[1,8,512]{2,1,0:T(8,128)S(1)} %get-tuple-element.64), channel_id=1, source_target_pairs={{0,16},{8,24},{16,0},{24,8},{1,17},{9,25},{17,1},{25,9},{2,18},{10... | collective-permute-start | bytes 49160 | tf_op jit(solution)/shard_map/ppermute | solution.py:434
  134.4 1.9 %collective-permute-start.25 = (f32[1,8,512]{2,1,0:T(8,128)S(1)}, f32[1,8,512]{2,1,0:T(8,128)S(1)}, u32[]{:S(2)}, u32[]{:S(2)}) collective-permute-start(f32[1,8,512]{2,1,0:T(8,128)S(1)} %get-tuple-element.63), channel_id=1, source_target_pairs={{0,24},{8,0},{16,8},{24,16},{1,25},{9,1},{17,9},{25,17},{2,26},{10... | collective-permute-start | bytes 49160 | tf_op jit(solution)/shard_map/ppermute | solution.py:434
  136.3 1.7 %collective-permute-done.23.refs_1_ = f32[1,8,512]{2,1,0:T(8,128)S(1)} collective-permute-done((f32[1,8,512]{2,1,0:T(8,128)S(1)}, f32[1,8,512]{2,1,0:T(8,128)S(1)}, u32[]{:S(2)}, u32[]{:S(2)}) %collective-permute-start.23) | collective-permute-done | bytes 16416 | tf_op jit(solution)/shard_map/ppermute | solution.py:434
  138.0 0.6 collective-permute-done.25.refs_3_
  138.6 0.6 copy-done.9
  139.2 1.5 %select.17 = f32[1,6,8,256]{3,2,1,0:T(8,128)} custom-call(s32[1]{0:T(128)} %bitcast.12.row_ref, s32[4,6]{1,0:T(4,128)} %batch_ref.1, s32[4]{0:T(128)} %used_ref.1, s32[8]{0:T(128)} %length_ref.1, s32[8]{0:T(128)} %slot_ref.1, f32[1,8,512]{2,1,0:T(8,128)} %get-tuple-element.66.refs_0_, f32[1,8,512]{2,1,0:T(8,128)} %copy-done.7, f32[1,8,512]{2,1,0:T(8,128)} %copy-done.8, ...), custom_call_target="tpu_custom_call" | custom-call | flops 1 | bytes 1 | tf_op jit(solution)/shard_map/select/pallas_call | solution.py:347
  (34 shorter events, 0.4 us)
Async XLA Ops:
  0.6 4.6 %collective-permute-start = (bf16[32,7168]{1,0:T(8,128)(2,1)}, bf16[32,7168]{1,0:T(8,128)(2,1)S(1)}, u32[]{:S(2)}, u32[]{:S(2)}) collective-permute-start(bf16[32,7168]{1,0:T(8,128)(2,1)} %own_ref.1), channel_id=1, source_target_pairs={{0,1},{1,0},{2,3},{3,2},{4,5},{5,4},{6,7},{7,6},{8,9},{9,8},{10,11... | collective-permute-start | bytes 1376264 | tf_op jit(solution)/shard_map/ppermute | solution.py:21
  1.1 19.0 %collective-permute-start.1 = (bf16[32,7168]{1,0:T(8,128)(2,1)}, bf16[32,7168]{1,0:T(8,128)(2,1)S(1)}, u32[]{:S(2)}, u32[]{:S(2)}) collective-permute-start(bf16[32,7168]{1,0:T(8,128)(2,1)} %own_ref.1), channel_id=1, source_target_pairs={{0,2},{1,3},{2,0},{3,1},{4,6},{5,7},{6,4},{7,5},{8,10},{9,11},{10,... | collective-permute-start | bytes 1376264 | tf_op jit(solution)/shard_map/ppermute | solution.py:21
  3.7 16.4 %collective-permute-start.3 = (bf16[32,7168]{1,0:T(8,128)(2,1)}, bf16[32,7168]{1,0:T(8,128)(2,1)S(1)}, u32[]{:S(2)}, u32[]{:S(2)}) collective-permute-start(bf16[32,7168]{1,0:T(8,128)(2,1)} %own_ref.1), channel_id=1, source_target_pairs={{0,4},{1,5},{2,6},{3,7},{4,0},{5,1},{6,2},{7,3},{8,12},{9,13},{10,... | collective-permute-start | bytes 1376264 | tf_op jit(solution)/shard_map/ppermute | solution.py:21
  5.2 2.0 %copy-start.5 = (bf16[2,256,3584]{2,1,0:T(8,128)(2,1)S(1)}, bf16[2,256,3584]{2,1,0:T(8,128)(2,1)}, u32[]{:S(2)}) copy-start(bf16[2,256,3584]{2,1,0:T(8,128)(2,1)} %stored_ref.1) | copy-start | bytes 11010052
  7.3 1.0 copy-start.6
  13.7 1.8 %copy-start = (bf16[2,256,3584]{2,1,0:T(8,128)(2,1)}, bf16[2,256,3584]{2,1,0:T(8,128)(2,1)S(1)}, u32[]{:S(2)}) copy-start(bf16[2,256,3584]{2,1,0:T(8,128)(2,1)S(1)} %get-tuple-element.43.refs_2_) | copy-start | bytes 11010052
  15.4 4.6 %copy-start.3 = (bf16[7168,896]{1,0:T(8,128)(2,1)}, bf16[7168,896]{1,0:T(8,128)(2,1)S(1)}, u32[]{:S(2)}) copy-start(bf16[7168,896]{1,0:T(8,128)(2,1)S(1)} %get-tuple-element.34.refs_1_) | copy-start | bytes 38535172
  20.1 7.5 %collective-permute-start.5 = (bf16[16,7168]{1,0:T(8,128)(2,1)S(1)}, bf16[16,7168]{1,0:T(8,128)(2,1)S(1)}, u32[]{:S(2)}, u32[]{:S(2)}) collective-permute-start(bf16[16,7168]{1,0:T(8,128)(2,1)S(1)} %get-tuple-element.31), channel_id=1, source_target_pairs={{0,4},{1,5},{2,6},{3,7},{4,0},{5,1},{6,2},{7,3},{8,12},{9,13},{10,... | collective-permute-start | bytes 688136 | tf_op jit(solution)/shard_map/ppermute | solution.py:21
  20.7 7.3 %collective-permute-start.6 = (bf16[16,7168]{1,0:T(8,128)(2,1)S(1)}, bf16[16,7168]{1,0:T(8,128)(2,1)S(1)}, u32[]{:S(2)}, u32[]{:S(2)}) collective-permute-start(bf16[16,7168]{1,0:T(8,128)(2,1)S(1)} %get-tuple-element.32), channel_id=1, source_target_pairs={{0,2},{1,3},{2,0},{3,1},{4,6},{5,7},{6,4},{7,5},{8,10},{9,11},{10,... | collective-permute-start | bytes 688136 | tf_op jit(solution)/shard_map/ppermute | solution.py:21
  22.1 7.5 %collective-permute-start.2 = (bf16[32,7168]{1,0:T(8,128)(2,1)S(1)}, bf16[32,7168]{1,0:T(8,128)(2,1)S(1)}, u32[]{:S(2)}, u32[]{:S(2)}) collective-permute-start(bf16[32,7168]{1,0:T(8,128)(2,1)S(1)} %collective-permute-done.1.x_ref.refs_1_), channel_id=1, source_target_pairs={{0,1},{1,0},{2,3},{3,2},{4,5},{5,4},{6,7},{7,6},{8,9},{9,8},{10,11... | collective-permute-start | bytes 1376264 | tf_op jit(solution)/shard_map/ppermute | solution.py:21
  22.2 7.5 %collective-permute-start.4 = (bf16[32,7168]{1,0:T(8,128)(2,1)S(1)}, bf16[32,7168]{1,0:T(8,128)(2,1)S(1)}, u32[]{:S(2)}, u32[]{:S(2)}) collective-permute-start(bf16[32,7168]{1,0:T(8,128)(2,1)S(1)} %collective-permute-done.3.y_ref.refs_3_), channel_id=1, source_target_pairs={{0,1},{1,0},{2,3},{3,2},{4,5},{5,4},{6,7},{7,6},{8,9},{9,8},{10,11... | collective-permute-start | bytes 1376264 | tf_op jit(solution)/shard_map/ppermute | solution.py:21
  27.6 1.5 %collective-permute-start.7 = (bf16[16,7168]{1,0:T(8,128)(2,1)S(1)}, bf16[16,7168]{1,0:T(8,128)(2,1)S(1)}, u32[]{:S(2)}, u32[]{:S(2)}) collective-permute-start(bf16[16,7168]{1,0:T(8,128)(2,1)S(1)} %collective-permute-done.5.refs_5_), channel_id=1, source_target_pairs={{0,1},{1,0},{2,3},{3,2},{4,5},{5,4},{6,7},{7,6},{8,9},{9,8},{10,11... | collective-permute-start | bytes 688136 | tf_op jit(solution)/shard_map/ppermute | solution.py:21
  28.0 1.6 %collective-permute-start.8 = (bf16[16,7168]{1,0:T(8,128)(2,1)S(1)}, bf16[16,7168]{1,0:T(8,128)(2,1)}, u32[]{:S(2)}, u32[]{:S(2)}) collective-permute-start(bf16[16,7168]{1,0:T(8,128)(2,1)S(1)} %collective-permute-done.6.refs_6_), channel_id=1, source_target_pairs={{0,1},{1,0},{2,3},{3,2},{4,5},{5,4},{6,7},{7,6},{8,9},{9,8},{10,11... | collective-permute-start | bytes 688136 | tf_op jit(solution)/shard_map/ppermute | solution.py:21
  30.8 4.7 %copy-start.4 = (bf16[7168,896]{1,0:T(8,128)(2,1)S(1)}, bf16[7168,896]{1,0:T(8,128)(2,1)}, u32[]{:S(2)}) copy-start(bf16[7168,896]{1,0:T(8,128)(2,1)} %copy-done.3) | copy-start | bytes 38535172
  40.7 13.5 %collective-permute-start.9 = (bf16[256,896]{1,0:T(8,128)(2,1)S(1)}, bf16[256,896]{1,0:T(8,128)(2,1)S(1)}, u32[]{:S(2)}, u32[]{:S(2)}) collective-permute-start(bf16[256,896]{1,0:T(8,128)(2,1)S(1)} %tick.6.after_ref), channel_id=1, source_target_pairs={{0,8},{24,16},{1,9},{25,17},{2,10},{26,18},{3,11},{27,19},{4,12},{... | collective-permute-start | bytes 1376264 | tf_op jit(solution)/shard_map/ppermute | solution.py:312
  54.9 13.6 %collective-permute-start.10 = (bf16[256,896]{1,0:T(8,128)(2,1)S(1)}, bf16[256,896]{1,0:T(8,128)(2,1)S(1)}, u32[]{:S(2)}, u32[]{:S(2)}) collective-permute-start(bf16[256,896]{1,0:T(8,128)(2,1)S(1)} %get-tuple-element.35.after_ref), channel_id=1, source_target_pairs={{0,8},{24,16},{1,9},{25,17},{2,10},{26,18},{3,11},{27,19},{4,12},{... | collective-permute-start | bytes 1376264 | tf_op jit(solution)/shard_map/ppermute | solution.py:312
  59.3 9.2 %collective-permute-start.11 = (bf16[256,896]{1,0:T(8,128)(2,1)S(1)}, bf16[256,896]{1,0:T(8,128)(2,1)S(1)}, u32[]{:S(2)}, u32[]{:S(2)}) collective-permute-start(bf16[256,896]{1,0:T(8,128)(2,1)S(1)} %get-tuple-element.37), channel_id=1, source_target_pairs={{8,16},{16,8},{9,17},{17,9},{10,18},{18,10},{11,19},{19,11},{12,20... | collective-permute-start | bytes 1376264 | tf_op jit(solution)/shard_map/ppermute | solution.py:308
  69.4 12.9 %collective-permute-start.12 = (bf16[256,896]{1,0:T(8,128)(2,1)S(1)}, bf16[256,896]{1,0:T(8,128)(2,1)S(1)}, u32[]{:S(2)}, u32[]{:S(2)}) collective-permute-start(bf16[256,896]{1,0:T(8,128)(2,1)S(1)} %get-tuple-element.38.after_ref), channel_id=1, source_target_pairs={{0,8},{24,16},{8,0},{16,24},{1,9},{25,17},{9,1},{17,25},{2,10},{26... | collective-permute-start | bytes 1376264 | tf_op jit(solution)/shard_map/ppermute | solution.py:312
  73.3 9.1 %collective-permute-start.13 = (bf16[256,896]{1,0:T(8,128)(2,1)S(1)}, bf16[256,896]{1,0:T(8,128)(2,1)S(1)}, u32[]{:S(2)}, u32[]{:S(2)}) collective-permute-start(bf16[256,896]{1,0:T(8,128)(2,1)S(1)} %get-tuple-element.40), channel_id=1, source_target_pairs={{8,16},{16,8},{9,17},{17,9},{10,18},{18,10},{11,19},{19,11},{12,20... | collective-permute-start | bytes 1376264 | tf_op jit(solution)/shard_map/ppermute | solution.py:308
  81.0 6.6 %copy-start.1 = (bf16[2,256,3584]{2,1,0:T(8,128)(2,1)S(1)}, bf16[2,256,3584]{2,1,0:T(8,128)(2,1)}, u32[]{:S(2)}) copy-start(bf16[2,256,3584]{2,1,0:T(8,128)(2,1)} %copy-done) | copy-start | bytes 11010052
  83.2 11.9 %collective-permute-start.14 = (bf16[256,896]{1,0:T(8,128)(2,1)S(1)}, bf16[256,896]{1,0:T(8,128)(2,1)S(1)}, u32[]{:S(2)}, u32[]{:S(2)}) collective-permute-start(bf16[256,896]{1,0:T(8,128)(2,1)S(1)} %get-tuple-element.41.after_ref), channel_id=1, source_target_pairs={{0,8},{24,16},{8,0},{16,24},{1,9},{25,17},{9,1},{17,25},{2,10},{26... | collective-permute-start | bytes 1376264 | tf_op jit(solution)/shard_map/ppermute | solution.py:312
  86.9 8.2 %collective-permute-start.15 = (bf16[256,896]{1,0:T(8,128)(2,1)S(1)}, bf16[256,896]{1,0:T(8,128)(2,1)S(1)}, u32[]{:S(2)}, u32[]{:S(2)}) collective-permute-start(bf16[256,896]{1,0:T(8,128)(2,1)S(1)} %get-tuple-element.46), channel_id=1, source_target_pairs={{8,16},{16,8},{9,17},{17,9},{10,18},{18,10},{11,19},{19,11},{12,20... | collective-permute-start | bytes 1376264 | tf_op jit(solution)/shard_map/ppermute | solution.py:308
  95.8 3.1 %collective-permute-start.16 = (bf16[256,896]{1,0:T(8,128)(2,1)S(1)}, bf16[256,896]{1,0:T(8,128)(2,1)S(1)}, u32[]{:S(2)}, u32[]{:S(2)}) collective-permute-start(bf16[256,896]{1,0:T(8,128)(2,1)S(1)} %get-tuple-element.52), channel_id=1, source_target_pairs={{8,16},{16,8},{9,17},{17,9},{10,18},{18,10},{11,19},{19,11},{12,20... | collective-permute-start | bytes 1376264 | tf_op jit(solution)/shard_map/ppermute | solution.py:308
  96.5 17.1 %collective-permute-start.17 = (bf16[256,896]{1,0:T(8,128)(2,1)S(1)}, bf16[256,896]{1,0:T(8,128)(2,1)S(1)}, u32[]{:S(2)}, u32[]{:S(2)}) collective-permute-start(bf16[256,896]{1,0:T(8,128)(2,1)S(1)} %get-tuple-element.47.after_ref.refs_0_), channel_id=1, source_target_pairs={{8,0},{16,24},{9,1},{17,25},{10,2},{18,26},{11,3},{19,27},{12,4},{... | collective-permute-start | bytes 1376264 | tf_op jit(solution)/shard_map/ppermute | solution.py:312
  99.5 21.5 %collective-permute-start.18 = (bf16[256,896]{1,0:T(8,128)(2,1)S(1)}, bf16[256,896]{1,0:T(8,128)(2,1)S(1)}, u32[]{:S(2)}, u32[]{:S(2)}) collective-permute-start(bf16[256,896]{1,0:T(8,128)(2,1)S(1)} %tick.11.after_ref.refs_0_), channel_id=1, source_target_pairs={{8,0},{16,24},{9,1},{17,25},{10,2},{18,26},{11,3},{19,27},{12,4},{... | collective-permute-start | bytes 1376264 | tf_op jit(solution)/shard_map/ppermute | solution.py:312
  113.6 2.0 %copy-start.2 = (bf16[2,256,3584]{2,1,0:T(8,128)(2,1)S(1)}, bf16[2,256,3584]{2,1,0:T(8,128)(2,1)}, u32[]{:S(2)}) copy-start(bf16[2,256,3584]{2,1,0:T(8,128)(2,1)} %copy-done) | copy-start | bytes 11010052
  122.9 1.6 %collective-permute-start.19 = (f32[4,4,8,512]{3,2,0,1:T(8,128)S(1)}, f32[4,4,8,512]{3,2,0,1:T(8,128)S(1)}, u32[]{:S(2)}, u32[]{:S(2)}) collective-permute-start(f32[4,4,8,512]{3,2,0,1:T(8,128)S(1)} %bitcast.28), channel_id=1, source_target_pairs={{0,1},{1,0},{2,3},{3,2},{4,5},{5,4},{6,7},{7,6},{8,9},{9,8},{10,11... | collective-permute-start | bytes 786440 | tf_op jit(solution)/shard_map/ppermute | solution.py:21
  124.5 5.3 %collective-permute-start.20 = (f32[4,8,512]{2,1,0:T(8,128)S(1)}, f32[4,8,512]{2,1,0:T(8,128)S(1)}, u32[]{:S(2)}, u32[]{:S(2)}) collective-permute-start(f32[4,8,512]{2,1,0:T(8,128)S(1)} %get-tuple-element.62), channel_id=1, source_target_pairs={{0,6},{1,7},{2,4},{3,5},{4,2},{5,3},{6,0},{7,1},{8,14},{9,15},{10,... | collective-permute-start | bytes 196616 | tf_op jit(solution)/shard_map/ppermute | solution.py:21
  126.4 4.6 %collective-permute-start.21 = (f32[4,8,512]{2,1,0:T(8,128)S(1)}, f32[4,8,512]{2,1,0:T(8,128)S(1)}, u32[]{:S(2)}, u32[]{:S(2)}) collective-permute-start(f32[4,8,512]{2,1,0:T(8,128)S(1)} %get-tuple-element.60), channel_id=1, source_target_pairs={{0,4},{1,5},{2,6},{3,7},{4,0},{5,1},{6,2},{7,3},{8,12},{9,13},{10,... | collective-permute-start | bytes 196616 | tf_op jit(solution)/shard_map/ppermute | solution.py:21
  127.6 4.3 %collective-permute-start.22 = (f32[4,8,512]{2,1,0:T(8,128)S(1)}, f32[4,8,512]{2,1,0:T(8,128)S(1)}, u32[]{:S(2)}, u32[]{:S(2)}) collective-permute-start(f32[4,8,512]{2,1,0:T(8,128)S(1)} %get-tuple-element.61), channel_id=1, source_target_pairs={{0,2},{1,3},{2,0},{3,1},{4,6},{5,7},{6,4},{7,5},{8,10},{9,11},{10,... | collective-permute-start | bytes 196616 | tf_op jit(solution)/shard_map/ppermute | solution.py:21
  132.5 5.5 %collective-permute-start.23 = (f32[1,8,512]{2,1,0:T(8,128)S(1)}, f32[1,8,512]{2,1,0:T(8,128)S(1)}, u32[]{:S(2)}, u32[]{:S(2)}) collective-permute-start(f32[1,8,512]{2,1,0:T(8,128)S(1)} %get-tuple-element.65), channel_id=1, source_target_pairs={{0,8},{8,16},{16,24},{24,0},{1,9},{9,17},{17,25},{25,1},{2,10},{10... | collective-permute-start | bytes 49160 | tf_op jit(solution)/shard_map/ppermute | solution.py:434
  132.5 5.5 %collective-permute-start.24 = (f32[1,8,512]{2,1,0:T(8,128)S(1)}, f32[1,8,512]{2,1,0:T(8,128)S(1)}, u32[]{:S(2)}, u32[]{:S(2)}) collective-permute-start(f32[1,8,512]{2,1,0:T(8,128)S(1)} %get-tuple-element.64), channel_id=1, source_target_pairs={{0,16},{8,24},{16,0},{24,8},{1,17},{9,25},{17,1},{25,9},{2,18},{10... | collective-permute-start | bytes 49160 | tf_op jit(solution)/shard_map/ppermute | solution.py:434
  134.4 4.2 %collective-permute-start.25 = (f32[1,8,512]{2,1,0:T(8,128)S(1)}, f32[1,8,512]{2,1,0:T(8,128)S(1)}, u32[]{:S(2)}, u32[]{:S(2)}) collective-permute-start(f32[1,8,512]{2,1,0:T(8,128)S(1)} %get-tuple-element.63), channel_id=1, source_target_pairs={{0,24},{8,0},{16,8},{24,16},{1,25},{9,1},{17,9},{25,17},{2,26},{10... | collective-permute-start | bytes 49160 | tf_op jit(solution)/shard_map/ppermute | solution.py:434
  138.0 0.6 copy-start.7
  138.0 0.6 copy-start.8
  138.6 0.6 copy-start.9

commit v5 on v4

--- a/solution.py
+++ b/solution.py
@@ -10,7 +10,7 @@
 PARTS = 4
 STEPS = 7
 SLOTS = 4
-PIECES = 4
+AHEAD = 3
 LANES = 128
 VMEM = pl.BlockSpec(memory_space=pltpu.VMEM)
 ANY = pl.BlockSpec(memory_space=pl.ANY)
@@ -24,14 +24,14 @@
 def gathered(new_keys, col_count, col_index, fetch):
     rows = new_keys.shape[0]
     if col_count != 8:
-        own, after = fetch(new_keys)
+        after = fetch(new_keys)
         start = col_index * rows
-        return [own, lax.all_gather(new_keys, "col", axis=0, tiled=True)], [start, jnp.int32(0)], after
+        return [new_keys, lax.all_gather(new_keys, "col", axis=0, tiled=True)], [start, jnp.int32(0)], after
     half = rows // 2
     by_x = flipped(new_keys, 2, 8)
     by_y = flipped(new_keys, 4, 8)
     by_core = flipped(new_keys, 1, 8)
-    own, after = fetch(by_core)
+    after = fetch(by_core)
     low, high = halved(by_x, by_y, after)
     low = flipped(low, 4, 8)
     high = flipped(high, 2, 8)
@@ -39,7 +39,7 @@
     y_core = flipped(by_y, 1, 8)
     low_core = flipped(low, 1, 8)
     high_core = flipped(high, 1, 8)
-    pieces = [own, by_core, by_x, x_core, by_y, y_core, low, high, low_core, high_core]
+    pieces = [new_keys, by_core, by_x, x_core, by_y, y_core, low, high, low_core, high_core]
     of = [0, 1, 2, 3, 4, 5, 6, 6, 7, 7]
     within = [0] * 7 + [half, 0, half]
     return pieces, [(col_index ^ f) * rows + w for f, w in zip(of, within)], after
@@ -64,15 +64,12 @@
     )(by_x, by_y, after)
 
 
-def fetch_kernel(span, weights_ref, stored_ref, own_ref, after_ref, held_ref, batches_ref, keys_ref, token_ref, arrived):
-    deep = held_ref.shape[0] // PIECES
-    copies = [
-        pltpu.make_async_copy(own_ref, keys_ref, arrived.at[PIECES]),
-        pltpu.make_async_copy(stored_ref, batches_ref, arrived.at[PIECES + 1]),
-    ]
-    for k in range(PIECES):
+def fetch_kernel(left, weights_ref, after_ref, held_ref, token_ref, arrived):
+    deep = held_ref.shape[0] // AHEAD
+    copies = []
+    for k in range(AHEAD):
         rows = pl.ds(k * deep, deep)
-        source = weights_ref.at[rows, pl.ds(span[0], span[1] - span[0])]
+        source = weights_ref.at[rows, pl.ds(left, held_ref.shape[1])]
         copies.append(pltpu.make_async_copy(source, held_ref.at[rows, :], arrived.at[k]))
     for copy in copies:
         copy.start()
@@ -81,23 +78,20 @@
         copy.wait()
 
 
-def fetched(weights, stored, own, span, after):
-    depth, wide = weights.shape[0], span[1] - span[0]
+def fetched(weights, span, after):
     return pl.pallas_call(
-        functools.partial(fetch_kernel, span),
-        in_specs=[ANY] * 4,
-        out_specs=[VMEM] * 4,
+        functools.partial(fetch_kernel, span[0]),
+        in_specs=[ANY] * 2,
+        out_specs=[VMEM] * 2,
         out_shape=[
-            jax.ShapeDtypeStruct((depth, wide), weights.dtype),
-            jax.ShapeDtypeStruct(stored.shape, stored.dtype),
-            jax.ShapeDtypeStruct(own.shape, own.dtype),
+            jax.ShapeDtypeStruct((weights.shape[0] // STEPS * AHEAD, span[1] - span[0]), weights.dtype),
             jax.ShapeDtypeStruct((8, LANES), jnp.float32),
         ],
-        scratch_shapes=[pltpu.SemaphoreType.DMA((PIECES + 2,))],
+        scratch_shapes=[pltpu.SemaphoreType.DMA((AHEAD,))],
         compiler_params=params(),
         cost_estimate=cost(),
         name="fetch",
-    )(weights, stored, own, after)
+    )(weights, after)
 
 
 def ranges(columns):
@@ -112,7 +106,7 @@
 
 
 def params():
-    return pltpu.CompilerParams(vmem_limit_bytes=12 * 2**20)
+    return pltpu.CompilerParams(vmem_limit_bytes=10 * 2**20)
 
 
 def assemble_kernel(count, starts_ref, after_ref, *refs):
@@ -133,7 +127,7 @@
     )(starts, after, *pieces)
 
 
-def multiply(left, early, keys_ref, weights_ref, wide_ref, held_ref, arrived):
+def multiply(left, ahead, keys_ref, weights_ref, early, wide_ref, held_ref, arrived):
     wide = wide_ref.shape[1]
     deep = keys_ref.shape[1] // STEPS
 
@@ -144,12 +138,11 @@
             arrived.at[step % SLOTS],
         )
 
-    if not early:
-        for step in range(min(SLOTS, STEPS)):
-            copy(step).start()
+    for step in range(ahead, min(ahead + SLOTS, STEPS)):
+        copy(step).start()
     for step in range(STEPS):
-        if early:
-            weights = weights_ref[step * deep : (step + 1) * deep, :]
+        if step < ahead:
+            weights = early[0][step * deep : (step + 1) * deep, :]
         else:
             copy(step).wait()
             weights = held_ref[step % SLOTS]
@@ -158,7 +151,7 @@
             weights,
             preferred_element_type=jnp.float32,
         )
-        if not early and step + SLOTS < STEPS:
+        if step >= ahead and step + SLOTS < STEPS:
             copy(step + SLOTS).start()
         wide_ref[...] = part if step == 0 else wide_ref[...] + part
 
@@ -189,6 +182,7 @@
     take = lambda n: [refs.pop(0) for _ in range(n)]
     if product:
         factors = take(2)
+        early = take(1 if product[1] else 0)
     if contract:
         rows = take(3)
         before = take(contract[1])
@@ -200,7 +194,7 @@
     if joined:
         (whole_ref,) = take(1)
     if product:
-        multiply(*product, *factors, wide_ref, *take(2))
+        multiply(*product, *factors, early, wide_ref, *take(2))
     if contract:
         against(contract[0], at_ref, *rows, before, terms_ref, piece_ref, *take(1))
     if joined:
@@ -216,12 +210,12 @@
     if product:
         keys, weights, early, span = product
         depth, rows, wide = weights.shape[0], keys.shape[0], span[1] - span[0]
-        product_at = (span[0], early)
-        operands += [keys, weights]
-        specs += [VMEM, VMEM if early else ANY]
+        product_at = (span[0], AHEAD if early else 0)
+        operands += [keys, weights, *early]
+        specs += [VMEM, ANY] + [VMEM] * len(early)
         shapes += [jax.ShapeDtypeStruct((rows, wide), jnp.float32)]
         scratch += [
-            pltpu.VMEM((SLOTS, 16 if early else depth // STEPS, wide), weights.dtype),
+            pltpu.VMEM((SLOTS, depth // STEPS, wide), weights.dtype),
             pltpu.SemaphoreType.DMA((SLOTS,)),
         ]
     if contract:
@@ -321,38 +315,37 @@
     contracted(count - 1, final[count - 1], outer, after)
 
 
-def select_kernel(count, row_ref, batch_ref, used_ref, length_ref, slot_ref, *refs):
-    parts, out_ref, held_ref = refs[:count], refs[count], refs[count + 1]
-    batches, rows, slots = held_ref.shape[1:]
-    for i, part in enumerate(parts):
+def select_kernel(row_ref, batch_ref, used_ref, length_ref, slot_ref, kept_ref, came_ref, out_ref, held_ref):
+    count, batches, rows, slots = held_ref.shape
+    half = count // 2
+    for i in range(count):
+        part = kept_ref[i, 0] if i < half else came_ref[i - half, 0]
         for b in range(batches):
-            held_ref[i, b] = part[0, :, b * slots : (b + 1) * slots]
+            held_ref[i, b] = part[:, b * slots : (b + 1) * slots]
     row = row_ref[0]
     column = lax.broadcasted_iota(jnp.int32, (rows, slots), 1)
     for place in range(out_ref.shape[1]):
         batch = batch_ref[row, place]
         slot = slot_ref[batch]
         owner = lax.div(slot, batches)
-        shift = lax.rem(row - owner + count, count)
         length = jnp.where(place < used_ref[row], length_ref[batch], 0)
-        value = held_ref[shift, slot - owner * batches]
+        value = held_ref[owner ^ row, slot - owner * batches]
         out_ref[0, place] = jnp.where(column < length, value, 0.0)
 
 
-def selected(parts, row_index, pair_batch, pair_count, batch_length, batch_slot, batches):
-    count = len(parts)
-    _, rows, wide = parts[0].shape
+def selected(kept, came, row_index, pair_batch, pair_count, batch_length, batch_slot, batches):
+    half, _, rows, wide = kept.shape
     slots = wide // batches
     places = pair_batch.shape[1]
     return pl.pallas_call(
-        functools.partial(select_kernel, count),
-        in_specs=[SMEM] * 5 + [VMEM] * count,
+        select_kernel,
+        in_specs=[SMEM] * 5 + [VMEM] * 2,
         out_specs=VMEM,
         out_shape=jax.ShapeDtypeStruct((1, places, rows, slots), jnp.float32),
-        scratch_shapes=[pltpu.VMEM((count, batches, rows, slots), jnp.float32)],
+        scratch_shapes=[pltpu.VMEM((2 * half, batches, rows, slots), jnp.float32)],
         cost_estimate=cost(),
         name="select",
-    )(row_index[None], pair_batch, pair_count, batch_length, batch_slot, *parts)
+    )(row_index[None], pair_batch, pair_count, batch_length, batch_slot, kept, came)
 
 
 def shards(new_keys, precision, stored_keys, pair_batch, pair_count, batch_length, batch_slot):
@@ -369,12 +362,12 @@
     at = jnp.stack([(away == 0).astype(jnp.int32), row_index * block])
     spans = ranges(precision.shape[1])
     count = len(spans)
-    early, stored, own, token = None, None, None, None
+    early = []
 
     def fetch(after):
-        nonlocal early, stored, token
-        early, stored, own, token = fetched(precision, stored_keys, new_keys, spans[0], after)
-        return own, token
+        held, token = fetched(precision, spans[0], after)
+        early.append(held)
+        return token
 
     pieces, starts, token = gathered(new_keys, col_count, col_index, fetch)
     order = list(range(1, len(pieces))) + [0]
@@ -386,10 +379,10 @@
         nonlocal terms
         product = None
         if part is not None:
-            product = (keys, precision if part else early, part == 0, spans[part])
+            product = (keys, precision, [] if part else early, spans[part])
         if contract is not None:
             number, final, came = contract
-            contract = (final, came, stored, terms, spans[number][0], block)
+            contract = (final, came, stored_keys, terms, spans[number][0], block)
         joined = whitened if contract is not None and number == count - 1 else []
         out = work(at, after, product, contract, joined)
         if contract is not None:
@@ -426,14 +419,17 @@
         left = lax.dynamic_index_in_dim(pairs, 1 - mine, 2, keepdims=False)
         sums = kept + flipped(left, bit, col_count)
         bit *= 2
-    sums = sums[:, 0]
-    parts = []
-    for shift in range(row_count):
-        part = lax.dynamic_slice_in_dim(sums, (row_index + shift) % row_count, 1, 0)
-        if shift:
-            part = lax.ppermute(part, "row", [(r, (r + shift) % row_count) for r in range(row_count)])
-        parts.append(part)
-    shares = selected(parts, row_index, pair_batch, pair_count, batch_length, batch_slot, batches)
+    parts = [sums[None, :, 0]]
+    bit = 1
+    while bit < row_count:
+        sums = jnp.concatenate(parts)
+        pairs = sums.reshape(bit, sums.shape[1] // 2, 2, share, sums.shape[3])
+        mine = (row_index // bit) % 2
+        kept = lax.dynamic_index_in_dim(pairs, mine, 2, keepdims=False)
+        left = lax.dynamic_index_in_dim(pairs, 1 - mine, 2, keepdims=False)
+        parts = [kept, lax.ppermute(left, "row", [(r, r ^ bit) for r in range(row_count)])]
+        bit *= 2
+    shares = selected(*parts, row_index, pair_batch, pair_count, batch_length, batch_slot, batches)
     return (whitened[-1], shares)
 
 

time: 141 us -> 139 us (0.986)
  waiting for transfers between devices: 43.3 us -> 57.3 us
  local copies, waits for them, and re-layouts: 17.5 us -> 5.19 us
  starting transfers between devices: 35.6 us -> 31.9 us
    unnamed x20 -> x12, local copies, waits for them, and re-layouts: 16.8 us -> 5.05 us
    ppermute x3 -> x2, waiting for transfers between devices: 2.27 us -> 8.67 us  [shards(): lax.ppermute(left, 'row', [(r, r ^ bit) for r in range(row_count)])]
    ppermute x13, waiting for transfers between devices: 12 us -> 17.6 us  [flipped(): return lax.ppermute(array, 'col', [(c, c ^ bit) for c in range(count)])]
    ppermute x3 -> x2, starting transfers between devices: 3.83 us -> 0.07 us  [shards(): lax.ppermute(left, 'row', [(r, r ^ bit) for r in range(row_count)])]
    pallas_call x2, Pallas kernels: 6.88 us -> 4.09 us  [the longest x1 2.65 us: fetched(): pl.pallas_call(functools.partial(fetch_kernel, span[0]), in_specs=[ANY] *...]
    pallas_call x8, Pallas kernels: 30.6 us -> 32.8 us  [work(): pl.pallas_call(functools.partial(work_kernel, product_at, contract_at, le...]
    ppermute x6, waiting for transfers between devices: 29.1 us -> 31 us  [along_line(): outer = lax.ppermute(sent, 'row', pairs)]
  transfers between devices with their start and end apart: 26 -> 25, of which waited for: 16 -> 17; matrix products, arithmetic and copies ran while one was open for 0% -> 0% of each run, Pallas kernels for 21% -> 20%
where the time goes in v5:
time: 139 us
  waiting for transfers between devices  57.3 us (41%)
  Pallas kernels  42.6 us (31%)
  starting transfers between devices  31.9 us (23%)
  local copies, waits for them, and re-layouts  5.19 us (4%)
    pallas_call x8, Pallas kernels, work(): pl.pallas_call(functools.partial(work_kernel, product_at, contract_at, le...  32.8 us
    ppermute x6, waiting for transfers between devices, along_line(): outer = lax.ppermute(sent, 'row', pairs)  31 us
    ppermute x6, starting transfers between devices, along_line(): outer = lax.ppermute(sent, 'row', pairs)  18.1 us
    ppermute x13, waiting for transfers between devices, flipped(): return lax.ppermute(array, 'col', [(c, c ^ bit) for c in range(count)])  17.6 us
    ppermute x13, starting transfers between devices, flipped(): return lax.ppermute(array, 'col', [(c, c ^ bit) for c in range(count)])  10.9 us
    ppermute x2, waiting for transfers between devices, shards(): lax.ppermute(left, 'row', [(r, r ^ bit) for r in range(row_count)])  8.67 us
    unnamed x12, local copies, waits for them, and re-layouts  5.05 us
    pallas_call x6, Pallas kernels, tick(): pl.pallas_call(functools.partial(tick_kernel, tuple(given), outs), in_spe...  4.39 us
  transfers between devices with their start and end apart: 25, of which 17 were waited for; matrix products, arithmetic and copies ran while one was open for 0% of the time, Pallas kernels for 20%

profile of v5, /device:TPU:0, one launch (start us, length us, event | category | flops | bytes accessed | tf_op | source)
XLA Modules:
  0.0 138.7 jit_solution(16489594417719035563)
XLA Ops:
  0.6 0.5 collective-permute-start
  1.2 2.6 %collective-permute-start.1 = (bf16[32,7168]{1,0:T(8,128)(2,1)}, bf16[32,7168]{1,0:T(8,128)(2,1)S(1)}, u32[]{:S(2)}, u32[]{:S(2)}) collective-permute-start(bf16[32,7168]{1,0:T(8,128)(2,1)} %refs_9_.1), channel_id=1, source_target_pairs={{0,2},{1,3},{2,0},{3,1},{4,6},{5,7},{6,4},{7,5},{8,10},{9,11},{10,... | collective-permute-start | bytes 1376264 | tf_op jit(solution)/shard_map/ppermute | solution.py:21
  3.7 1.5 %collective-permute-start.3 = (bf16[32,7168]{1,0:T(8,128)(2,1)}, bf16[32,7168]{1,0:T(8,128)(2,1)S(1)}, u32[]{:S(2)}, u32[]{:S(2)}) collective-permute-start(bf16[32,7168]{1,0:T(8,128)(2,1)} %refs_9_.1), channel_id=1, source_target_pairs={{0,4},{1,5},{2,6},{3,7},{4,0},{5,1},{6,2},{7,3},{8,12},{9,13},{10,... | collective-permute-start | bytes 1376264 | tf_op jit(solution)/shard_map/ppermute | solution.py:21
  5.2 0.0 collective-permute-done.after_ref.refs_0_
  5.2 2.6 %fetch.1 = (bf16[3072,896]{1,0:T(8,128)(2,1)S(1)}, f32[8,128]{1,0:T(8,128)S(1)}) custom-call(bf16[7168,3584]{1,0:T(8,128)(2,1)} %refs_1_.7, bf16[32,7168]{1,0:T(8,128)(2,1)S(1)} %collective-permute-done.after_ref.refs_0_), custom_call_target="tpu_custom_call" | custom-call | flops 1 | bytes 1 | tf_op jit(solution)/shard_map/fetch/pallas_call | solution.py:82
  7.9 2.4 %copy-done.2 = bf16[3072,896]{1,0:T(8,128)(2,1)} copy-done((bf16[3072,896]{1,0:T(8,128)(2,1)}, bf16[3072,896]{1,0:T(8,128)(2,1)S(1)}, u32[]{:S(2)}) %copy-start.2) | copy-done | bytes 5505048
  10.3 4.7 %collective-permute-done.1.x_ref.refs_1_ = bf16[32,7168]{1,0:T(8,128)(2,1)S(1)} collective-permute-done((bf16[32,7168]{1,0:T(8,128)(2,1)}, bf16[32,7168]{1,0:T(8,128)(2,1)S(1)}, u32[]{:S(2)}, u32[]{:S(2)}) %collective-permute-start.1) | collective-permute-done | bytes 458784 | tf_op jit(solution)/shard_map/ppermute | solution.py:21
  15.0 1.5 %collective-permute-done.3.y_ref.refs_3_ = bf16[32,7168]{1,0:T(8,128)(2,1)S(1)} collective-permute-done((bf16[32,7168]{1,0:T(8,128)(2,1)}, bf16[32,7168]{1,0:T(8,128)(2,1)S(1)}, u32[]{:S(2)}, u32[]{:S(2)}) %collective-permute-start.3) | collective-permute-done | bytes 458784 | tf_op jit(solution)/shard_map/ppermute | solution.py:21
  16.6 1.6 %collective-permute-start.5 = (bf16[16,7168]{1,0:T(8,128)(2,1)S(1)}, bf16[16,7168]{1,0:T(8,128)(2,1)S(1)}, u32[]{:S(2)}, u32[]{:S(2)}) collective-permute-start(bf16[16,7168]{1,0:T(8,128)(2,1)S(1)} %get-tuple-element.29), channel_id=1, source_target_pairs={{0,4},{1,5},{2,6},{3,7},{4,0},{5,1},{6,2},{7,3},{8,12},{9,13},{10,... | collective-permute-start | bytes 688136 | tf_op jit(solution)/shard_map/ppermute | solution.py:21
  18.1 0.5 collective-permute-start.6
  18.7 0.0 collective-permute-start.2
  18.7 0.5 collective-permute-start.4
  19.2 4.3 %collective-permute-done.5.refs_5_ = bf16[16,7168]{1,0:T(8,128)(2,1)S(1)} collective-permute-done((bf16[16,7168]{1,0:T(8,128)(2,1)S(1)}, bf16[16,7168]{1,0:T(8,128)(2,1)S(1)}, u32[]{:S(2)}, u32[]{:S(2)}) %collective-permute-start.5) | collective-permute-done | bytes 229408 | tf_op jit(solution)/shard_map/ppermute | solution.py:21
  23.5 1.2 collective-permute-done.6.refs_6_
  24.7 0.1 stack.59.starts_ref
  24.8 0.1 pad_add_fusion.at_ref.after_ref
  24.9 0.1 collective-permute-done.7.refs_7_
  25.0 1.4 collective-permute-done.8.refs_8_
  26.3 1.3 assemble.1.refs_0_
  27.6 6.6 %work.8.after_ref.refs_0_ = f32[256,896]{1,0:T(8,128)S(1)} custom-call(s32[2]{0:T(128)S(1)} %pad_add_fusion.at_ref.after_ref, s32[2]{0:T(128)S(1)} %pad_add_fusion.at_ref.after_ref, bf16[256,7168]{1,0:T(8,128)(2,1)S(1)} %assemble.1.refs_0_, bf16[7168,3584]{1,0:T(8,128)(2,1)} %refs_1_.7, bf16[3072,896]{1,0:T(8,128)(2,1)S(1)} %copy-done.3), custom_call_target="tpu_custom_call" | custom-call | flops 1 | bytes 1 | tf_op jit(solution)/shard_map/work/pallas_call | solution.py:236
  34.2 0.6 tick.6.after_ref
  34.8 3.5 %collective-permute-start.9 = (bf16[256,896]{1,0:T(8,128)(2,1)S(1)}, bf16[256,896]{1,0:T(8,128)(2,1)S(1)}, u32[]{:S(2)}, u32[]{:S(2)}) collective-permute-start(bf16[256,896]{1,0:T(8,128)(2,1)S(1)} %tick.6.after_ref), channel_id=1, source_target_pairs={{0,8},{24,16},{1,9},{25,17},{2,10},{26,18},{3,11},{27,19},{4,12},{... | collective-permute-start | bytes 1376264 | tf_op jit(solution)/shard_map/ppermute | solution.py:306
  38.3 7.1 %work.9.after_ref.refs_2_.refs_0_ = f32[256,896]{1,0:T(8,128)S(1)} custom-call(s32[2]{0:T(128)S(1)} %pad_add_fusion.at_ref.after_ref, bf16[256,896]{1,0:T(8,128)(2,1)S(1)} %tick.6.after_ref, bf16[256,7168]{1,0:T(8,128)(2,1)S(1)} %assemble.1.refs_0_, bf16[7168,3584]{1,0:T(8,128)(2,1)} %refs_1_.7), custom_call_target="tpu_custom_call" | custom-call | flops 1 | bytes 1 | tf_op jit(solution)/shard_map/work/pallas_call | solution.py:236
  45.4 3.3 %collective-permute-done.9.refs_1_ = bf16[256,896]{1,0:T(8,128)(2,1)S(1)} collective-permute-done((bf16[256,896]{1,0:T(8,128)(2,1)S(1)}, bf16[256,896]{1,0:T(8,128)(2,1)S(1)}, u32[]{:S(2)}, u32[]{:S(2)}) %collective-permute-start.9) | collective-permute-done | bytes 458784 | tf_op jit(solution)/shard_map/ppermute | solution.py:306
  48.7 0.7 tick.7
  49.5 4.4 %collective-permute-start.10 = (bf16[256,896]{1,0:T(8,128)(2,1)S(1)}, bf16[256,896]{1,0:T(8,128)(2,1)S(1)}, u32[]{:S(2)}, u32[]{:S(2)}) collective-permute-start(bf16[256,896]{1,0:T(8,128)(2,1)S(1)} %get-tuple-element.32.after_ref), channel_id=1, source_target_pairs={{0,8},{24,16},{1,9},{25,17},{2,10},{26,18},{3,11},{27,19},{4,12},{... | collective-permute-start | bytes 1376264 | tf_op jit(solution)/shard_map/ppermute | solution.py:306
  53.9 0.9 collective-permute-start.11
  54.8 7.1 %work.10.after_ref.refs_4_.refs_0_ = f32[256,896]{1,0:T(8,128)S(1)} custom-call(s32[2]{0:T(128)S(1)} %pad_add_fusion.at_ref.after_ref, bf16[256,896]{1,0:T(8,128)(2,1)S(1)} %get-tuple-element.32.after_ref, bf16[256,7168]{1,0:T(8,128)(2,1)S(1)} %assemble.1.refs_0_, bf16[7168,3584]{1,0:T(8,128)(2,1)} %refs_1_.7), custom_call_target="tpu_custom_call" | custom-call | flops 1 | bytes 1 | tf_op jit(solution)/shard_map/work/pallas_call | solution.py:236
  61.9 1.6 %collective-permute-done.10.refs_1_ = bf16[256,896]{1,0:T(8,128)(2,1)S(1)} collective-permute-done((bf16[256,896]{1,0:T(8,128)(2,1)S(1)}, bf16[256,896]{1,0:T(8,128)(2,1)S(1)}, u32[]{:S(2)}, u32[]{:S(2)}) %collective-permute-start.10) | collective-permute-done | bytes 458784 | tf_op jit(solution)/shard_map/ppermute | solution.py:306
  63.5 0.9 tick.8
  64.4 3.8 %collective-permute-start.12 = (bf16[256,896]{1,0:T(8,128)(2,1)S(1)}, bf16[256,896]{1,0:T(8,128)(2,1)S(1)}, u32[]{:S(2)}, u32[]{:S(2)}) collective-permute-start(bf16[256,896]{1,0:T(8,128)(2,1)S(1)} %get-tuple-element.35.after_ref), channel_id=1, source_target_pairs={{0,8},{24,16},{8,0},{16,24},{1,9},{25,17},{9,1},{17,25},{2,10},{26... | collective-permute-start | bytes 1376264 | tf_op jit(solution)/shard_map/ppermute | solution.py:306
  68.2 0.7 collective-permute-start.13
  68.9 7.1 %work.11.after_ref.refs_4_.refs_0_ = f32[256,896]{1,0:T(8,128)S(1)} custom-call(s32[2]{0:T(128)S(1)} %pad_add_fusion.at_ref.after_ref, bf16[256,896]{1,0:T(8,128)(2,1)S(1)} %get-tuple-element.35.after_ref, bf16[256,7168]{1,0:T(8,128)(2,1)S(1)} %assemble.1.refs_0_, bf16[7168,3584]{1,0:T(8,128)(2,1)} %refs_1_.7), custom_call_target="tpu_custom_call" | custom-call | flops 1 | bytes 1 | tf_op jit(solution)/shard_map/work/pallas_call | solution.py:236
  76.0 0.0 copy-start
  76.0 1.7 %collective-permute-done.12.refs_1_ = bf16[256,896]{1,0:T(8,128)(2,1)S(1)} collective-permute-done((bf16[256,896]{1,0:T(8,128)(2,1)S(1)}, bf16[256,896]{1,0:T(8,128)(2,1)S(1)}, u32[]{:S(2)}, u32[]{:S(2)}) %collective-permute-start.12) | collective-permute-done | bytes 458784 | tf_op jit(solution)/shard_map/ppermute | solution.py:306
  77.7 0.9 tick.9
  78.6 3.7 %collective-permute-start.14 = (bf16[256,896]{1,0:T(8,128)(2,1)S(1)}, bf16[256,896]{1,0:T(8,128)(2,1)S(1)}, u32[]{:S(2)}, u32[]{:S(2)}) collective-permute-start(bf16[256,896]{1,0:T(8,128)(2,1)S(1)} %get-tuple-element.38.after_ref), channel_id=1, source_target_pairs={{0,8},{24,16},{8,0},{16,24},{1,9},{25,17},{9,1},{17,25},{2,10},{26... | collective-permute-start | bytes 1376264 | tf_op jit(solution)/shard_map/ppermute | solution.py:306
  82.3 0.7 collective-permute-start.15
  83.0 1.0 work.12
  84.1 6.8 %collective-permute-done.14.refs_1_ = bf16[256,896]{1,0:T(8,128)(2,1)S(1)} collective-permute-done((bf16[256,896]{1,0:T(8,128)(2,1)S(1)}, bf16[256,896]{1,0:T(8,128)(2,1)S(1)}, u32[]{:S(2)}, u32[]{:S(2)}) %collective-permute-start.14) | collective-permute-done | bytes 458784 | tf_op jit(solution)/shard_map/ppermute | solution.py:306
  90.9 0.7 tick.10
  91.7 0.7 collective-permute-start.16
  92.4 1.3 collective-permute-start.17
  93.7 1.1 work.13
  94.7 0.6 tick.11.after_ref.refs_0_
  95.4 1.3 collective-permute-start.18
  96.7 12.6 %collective-permute-done.17.refs_1_ = bf16[256,896]{1,0:T(8,128)(2,1)S(1)} collective-permute-done((bf16[256,896]{1,0:T(8,128)(2,1)S(1)}, bf16[256,896]{1,0:T(8,128)(2,1)S(1)}, u32[]{:S(2)}, u32[]{:S(2)}) %collective-permute-start.17) | collective-permute-done | bytes 458784 | tf_op jit(solution)/shard_map/ppermute | solution.py:306
  109.3 2.0 %copy-done.1 = bf16[2,256,3584]{2,1,0:T(8,128)(2,1)S(1)} copy-done((bf16[2,256,3584]{2,1,0:T(8,128)(2,1)S(1)}, bf16[2,256,3584]{2,1,0:T(8,128)(2,1)}, u32[]{:S(2)}) %copy-start.1) | copy-done | bytes 3670040
  111.4 1.1 work.14
  112.4 4.8 %collective-permute-done.18.refs_1_ = bf16[256,896]{1,0:T(8,128)(2,1)S(1)} collective-permute-done((bf16[256,896]{1,0:T(8,128)(2,1)S(1)}, bf16[256,896]{1,0:T(8,128)(2,1)S(1)}, u32[]{:S(2)}, u32[]{:S(2)}) %collective-permute-start.18) | collective-permute-done | bytes 458784 | tf_op jit(solution)/shard_map/ppermute | solution.py:306
  117.3 1.8 %work.15 = (f32[256,512]{1,0:T(8,128)S(1)}, bf16[64,896]{1,0:T(8,128)(2,1)}, bf16[64,3584]{1,0:T(8,128)(2,1)}) custom-call(s32[2]{0:T(128)S(1)} %pad_add_fusion.at_ref.after_ref, bf16[64,896]{1,0:T(8,128)(2,1)S(1)} %get-tuple-element.50.after_ref.refs_6_, bf16[256,896]{1,0:T(8,128)(2,1)S(1)} %tick.11.after_ref.refs_0_, ...), custom_call_target="tpu_custom_call" | custom-call | flops 1 | bytes 1 | tf_op jit(solution)/shard_map/work/pallas_call | solution.py:236
  119.1 0.1 collective-permute-start.19
  119.2 1.5 %collective-permute-done.19 = f32[4,4,8,512]{3,2,1,0:T(8,128)S(1)} collective-permute-done((f32[4,4,8,512]{3,2,1,0:T(8,128)S(1)}, f32[4,4,8,512]{3,2,1,0:T(8,128)S(1)}, u32[]{:S(2)}, u32[]{:S(2)}) %collective-permute-start.19) | collective-permute-done | bytes 262176 | tf_op jit(solution)/shard_map/ppermute | solution.py:21
  120.8 0.1 collective-permute-start.20
  120.8 2.1 %collective-permute-start.21 = (f32[4,8,512]{2,1,0:T(8,128)S(1)}, f32[4,8,512]{2,1,0:T(8,128)S(1)}, u32[]{:S(2)}, u32[]{:S(2)}) collective-permute-start(f32[4,8,512]{2,1,0:T(8,128)S(1)} %get-tuple-element.54), channel_id=1, source_target_pairs={{0,4},{1,5},{2,6},{3,7},{4,0},{5,1},{6,2},{7,3},{8,12},{9,13},{10,... | collective-permute-start | bytes 196616 | tf_op jit(solution)/shard_map/ppermute | solution.py:21
  123.0 1.3 collective-permute-start.22
  124.3 2.2 %collective-permute-done.20 = f32[4,8,512]{2,1,0:T(8,128)S(1)} collective-permute-done((f32[4,8,512]{2,1,0:T(8,128)S(1)}, f32[4,8,512]{2,1,0:T(8,128)S(1)}, u32[]{:S(2)}, u32[]{:S(2)}) %collective-permute-start.20) | collective-permute-done | bytes 65568 | tf_op jit(solution)/shard_map/ppermute | solution.py:21
  126.6 0.7 collective-permute-done.22
  127.3 0.1 collective-permute-start.23
  127.4 3.9 %collective-permute-done.23 = f32[1,2,8,512]{3,2,1,0:T(8,128)S(1)} collective-permute-done((f32[1,2,8,512]{3,2,1,0:T(8,128)S(1)}, f32[1,2,8,512]{3,2,1,0:T(8,128)S(1)}, u32[]{:S(2)}, u32[]{:S(2)}) %collective-permute-start.23) | collective-permute-done | bytes 32800 | tf_op jit(solution)/shard_map/ppermute | solution.py:430
  131.3 0.6 fusion
  131.9 4.8 %collective-permute-done.24.came_ref = f32[2,1,8,512]{3,2,1,0:T(8,128)S(1)} collective-permute-done((f32[2,1,8,512]{3,2,1,0:T(8,128)S(1)}, f32[2,1,8,512]{3,2,1,0:T(8,128)S(1)}, u32[]{:S(2)}, u32[]{:S(2)}) %collective-permute-start.24) | collective-permute-done | bytes 32800 | tf_op jit(solution)/shard_map/ppermute | solution.py:430
  136.7 0.6 copy-done.5
  137.3 1.4 %select.19 = f32[1,6,8,256]{3,2,1,0:T(8,128)} custom-call(s32[1]{0:T(128)} %bitcast.12.row_ref, s32[4,6]{1,0:T(4,128)} %batch_ref.1, s32[4]{0:T(128)} %used_ref.1, s32[8]{0:T(128)} %length_ref.1, s32[8]{0:T(128)} %slot_ref.1, f32[2,1,8,512]{3,2,1,0:T(8,128)} %get-tuple-element.58.kept_ref, f32[2,1,8,512]{3,2,1,0:T(8,128)} %copy-done.5), custom_call_target="tpu_custom_call" | custom-call | flops 1 | bytes 1 | tf_op jit(solution)/shard_map/select/pallas_call | solution.py:340
  (24 shorter events, 0.2 us)
Async XLA Ops:
  0.6 25.7 %copy-start.4 = (bf16[32,7168]{1,0:T(8,128)(2,1)S(1)}, bf16[32,7168]{1,0:T(8,128)(2,1)}, u32[]{:S(2)}) copy-start(bf16[32,7168]{1,0:T(8,128)(2,1)} %refs_9_.1) | copy-start | bytes 1376260
  0.6 4.6 %collective-permute-start = (bf16[32,7168]{1,0:T(8,128)(2,1)}, bf16[32,7168]{1,0:T(8,128)(2,1)S(1)}, u32[]{:S(2)}, u32[]{:S(2)}) collective-permute-start(bf16[32,7168]{1,0:T(8,128)(2,1)} %refs_9_.1), channel_id=1, source_target_pairs={{0,1},{1,0},{2,3},{3,2},{4,5},{5,4},{6,7},{7,6},{8,9},{9,8},{10,11... | collective-permute-start | bytes 1376264 | tf_op jit(solution)/shard_map/ppermute | solution.py:21
  1.2 13.9 %collective-permute-start.1 = (bf16[32,7168]{1,0:T(8,128)(2,1)}, bf16[32,7168]{1,0:T(8,128)(2,1)S(1)}, u32[]{:S(2)}, u32[]{:S(2)}) collective-permute-start(bf16[32,7168]{1,0:T(8,128)(2,1)} %refs_9_.1), channel_id=1, source_target_pairs={{0,2},{1,3},{2,0},{3,1},{4,6},{5,7},{6,4},{7,5},{8,10},{9,11},{10,... | collective-permute-start | bytes 1376264 | tf_op jit(solution)/shard_map/ppermute | solution.py:21
  3.7 12.8 %collective-permute-start.3 = (bf16[32,7168]{1,0:T(8,128)(2,1)}, bf16[32,7168]{1,0:T(8,128)(2,1)S(1)}, u32[]{:S(2)}, u32[]{:S(2)}) collective-permute-start(bf16[32,7168]{1,0:T(8,128)(2,1)} %refs_9_.1), channel_id=1, source_target_pairs={{0,4},{1,5},{2,6},{3,7},{4,0},{5,1},{6,2},{7,3},{8,12},{9,13},{10,... | collective-permute-start | bytes 1376264 | tf_op jit(solution)/shard_map/ppermute | solution.py:21
  7.9 2.4 %copy-start.2 = (bf16[3072,896]{1,0:T(8,128)(2,1)}, bf16[3072,896]{1,0:T(8,128)(2,1)S(1)}, u32[]{:S(2)}) copy-start(bf16[3072,896]{1,0:T(8,128)(2,1)S(1)} %get-tuple-element.31.refs_2_) | copy-start | bytes 16515076
  16.6 6.9 %collective-permute-start.5 = (bf16[16,7168]{1,0:T(8,128)(2,1)S(1)}, bf16[16,7168]{1,0:T(8,128)(2,1)S(1)}, u32[]{:S(2)}, u32[]{:S(2)}) collective-permute-start(bf16[16,7168]{1,0:T(8,128)(2,1)S(1)} %get-tuple-element.29), channel_id=1, source_target_pairs={{0,4},{1,5},{2,6},{3,7},{4,0},{5,1},{6,2},{7,3},{8,12},{9,13},{10,... | collective-permute-start | bytes 688136 | tf_op jit(solution)/shard_map/ppermute | solution.py:21
  18.1 6.6 %collective-permute-start.6 = (bf16[16,7168]{1,0:T(8,128)(2,1)S(1)}, bf16[16,7168]{1,0:T(8,128)(2,1)S(1)}, u32[]{:S(2)}, u32[]{:S(2)}) collective-permute-start(bf16[16,7168]{1,0:T(8,128)(2,1)S(1)} %get-tuple-element.30), channel_id=1, source_target_pairs={{0,2},{1,3},{2,0},{3,1},{4,6},{5,7},{6,4},{7,5},{8,10},{9,11},{10,... | collective-permute-start | bytes 688136 | tf_op jit(solution)/shard_map/ppermute | solution.py:21
  18.7 7.7 %collective-permute-start.2 = (bf16[32,7168]{1,0:T(8,128)(2,1)S(1)}, bf16[32,7168]{1,0:T(8,128)(2,1)S(1)}, u32[]{:S(2)}, u32[]{:S(2)}) collective-permute-start(bf16[32,7168]{1,0:T(8,128)(2,1)S(1)} %collective-permute-done.1.x_ref.refs_1_), channel_id=1, source_target_pairs={{0,1},{1,0},{2,3},{3,2},{4,5},{5,4},{6,7},{7,6},{8,9},{9,8},{10,11... | collective-permute-start | bytes 1376264 | tf_op jit(solution)/shard_map/ppermute | solution.py:21
  18.7 7.7 %collective-permute-start.4 = (bf16[32,7168]{1,0:T(8,128)(2,1)S(1)}, bf16[32,7168]{1,0:T(8,128)(2,1)S(1)}, u32[]{:S(2)}, u32[]{:S(2)}) collective-permute-start(bf16[32,7168]{1,0:T(8,128)(2,1)S(1)} %collective-permute-done.3.y_ref.refs_3_), channel_id=1, source_target_pairs={{0,1},{1,0},{2,3},{3,2},{4,5},{5,4},{6,7},{7,6},{8,9},{9,8},{10,11... | collective-permute-start | bytes 1376264 | tf_op jit(solution)/shard_map/ppermute | solution.py:21
  23.5 1.5 %collective-permute-start.7 = (bf16[16,7168]{1,0:T(8,128)(2,1)S(1)}, bf16[16,7168]{1,0:T(8,128)(2,1)S(1)}, u32[]{:S(2)}, u32[]{:S(2)}) collective-permute-start(bf16[16,7168]{1,0:T(8,128)(2,1)S(1)} %collective-permute-done.5.refs_5_), channel_id=1, source_target_pairs={{0,1},{1,0},{2,3},{3,2},{4,5},{5,4},{6,7},{7,6},{8,9},{9,8},{10,11... | collective-permute-start | bytes 688136 | tf_op jit(solution)/shard_map/ppermute | solution.py:21
  24.7 1.6 %collective-permute-start.8 = (bf16[16,7168]{1,0:T(8,128)(2,1)S(1)}, bf16[16,7168]{1,0:T(8,128)(2,1)}, u32[]{:S(2)}, u32[]{:S(2)}) collective-permute-start(bf16[16,7168]{1,0:T(8,128)(2,1)S(1)} %collective-permute-done.6.refs_6_), channel_id=1, source_target_pairs={{0,1},{1,0},{2,3},{3,2},{4,5},{5,4},{6,7},{7,6},{8,9},{9,8},{10,11... | collective-permute-start | bytes 688136 | tf_op jit(solution)/shard_map/ppermute | solution.py:21
  24.8 2.8 %copy-start.3 = (bf16[3072,896]{1,0:T(8,128)(2,1)S(1)}, bf16[3072,896]{1,0:T(8,128)(2,1)}, u32[]{:S(2)}) copy-start(bf16[3072,896]{1,0:T(8,128)(2,1)} %copy-done.2) | copy-start | bytes 16515076
  34.8 13.9 %collective-permute-start.9 = (bf16[256,896]{1,0:T(8,128)(2,1)S(1)}, bf16[256,896]{1,0:T(8,128)(2,1)S(1)}, u32[]{:S(2)}, u32[]{:S(2)}) collective-permute-start(bf16[256,896]{1,0:T(8,128)(2,1)S(1)} %tick.6.after_ref), channel_id=1, source_target_pairs={{0,8},{24,16},{1,9},{25,17},{2,10},{26,18},{3,11},{27,19},{4,12},{... | collective-permute-start | bytes 1376264 | tf_op jit(solution)/shard_map/ppermute | solution.py:306
  49.5 14.0 %collective-permute-start.10 = (bf16[256,896]{1,0:T(8,128)(2,1)S(1)}, bf16[256,896]{1,0:T(8,128)(2,1)S(1)}, u32[]{:S(2)}, u32[]{:S(2)}) collective-permute-start(bf16[256,896]{1,0:T(8,128)(2,1)S(1)} %get-tuple-element.32.after_ref), channel_id=1, source_target_pairs={{0,8},{24,16},{1,9},{25,17},{2,10},{26,18},{3,11},{27,19},{4,12},{... | collective-permute-start | bytes 1376264 | tf_op jit(solution)/shard_map/ppermute | solution.py:306
  53.9 9.6 %collective-permute-start.11 = (bf16[256,896]{1,0:T(8,128)(2,1)S(1)}, bf16[256,896]{1,0:T(8,128)(2,1)S(1)}, u32[]{:S(2)}, u32[]{:S(2)}) collective-permute-start(bf16[256,896]{1,0:T(8,128)(2,1)S(1)} %get-tuple-element.34), channel_id=1, source_target_pairs={{8,16},{16,8},{9,17},{17,9},{10,18},{18,10},{11,19},{19,11},{12,20... | collective-permute-start | bytes 1376264 | tf_op jit(solution)/shard_map/ppermute | solution.py:302
  64.4 13.4 %collective-permute-start.12 = (bf16[256,896]{1,0:T(8,128)(2,1)S(1)}, bf16[256,896]{1,0:T(8,128)(2,1)S(1)}, u32[]{:S(2)}, u32[]{:S(2)}) collective-permute-start(bf16[256,896]{1,0:T(8,128)(2,1)S(1)} %get-tuple-element.35.after_ref), channel_id=1, source_target_pairs={{0,8},{24,16},{8,0},{16,24},{1,9},{25,17},{9,1},{17,25},{2,10},{26... | collective-permute-start | bytes 1376264 | tf_op jit(solution)/shard_map/ppermute | solution.py:306
  68.2 9.5 %collective-permute-start.13 = (bf16[256,896]{1,0:T(8,128)(2,1)S(1)}, bf16[256,896]{1,0:T(8,128)(2,1)S(1)}, u32[]{:S(2)}, u32[]{:S(2)}) collective-permute-start(bf16[256,896]{1,0:T(8,128)(2,1)S(1)} %get-tuple-element.37), channel_id=1, source_target_pairs={{8,16},{16,8},{9,17},{17,9},{10,18},{18,10},{11,19},{19,11},{12,20... | collective-permute-start | bytes 1376264 | tf_op jit(solution)/shard_map/ppermute | solution.py:302
  76.0 7.0 %copy-start = (bf16[2,256,3584]{2,1,0:T(8,128)(2,1)S(1)}, bf16[2,256,3584]{2,1,0:T(8,128)(2,1)}, u32[]{:S(2)}) copy-start(bf16[2,256,3584]{2,1,0:T(8,128)(2,1)} %refs_2_.7) | copy-start | bytes 11010052
  78.6 12.3 %collective-permute-start.14 = (bf16[256,896]{1,0:T(8,128)(2,1)S(1)}, bf16[256,896]{1,0:T(8,128)(2,1)S(1)}, u32[]{:S(2)}, u32[]{:S(2)}) collective-permute-start(bf16[256,896]{1,0:T(8,128)(2,1)S(1)} %get-tuple-element.38.after_ref), channel_id=1, source_target_pairs={{0,8},{24,16},{8,0},{16,24},{1,9},{25,17},{9,1},{17,25},{2,10},{26... | collective-permute-start | bytes 1376264 | tf_op jit(solution)/shard_map/ppermute | solution.py:306
  82.3 8.6 %collective-permute-start.15 = (bf16[256,896]{1,0:T(8,128)(2,1)S(1)}, bf16[256,896]{1,0:T(8,128)(2,1)S(1)}, u32[]{:S(2)}, u32[]{:S(2)}) collective-permute-start(bf16[256,896]{1,0:T(8,128)(2,1)S(1)} %get-tuple-element.42), channel_id=1, source_target_pairs={{8,16},{16,8},{9,17},{17,9},{10,18},{18,10},{11,19},{19,11},{12,20... | collective-permute-start | bytes 1376264 | tf_op jit(solution)/shard_map/ppermute | solution.py:302
  91.7 3.1 %collective-permute-start.16 = (bf16[256,896]{1,0:T(8,128)(2,1)S(1)}, bf16[256,896]{1,0:T(8,128)(2,1)S(1)}, u32[]{:S(2)}, u32[]{:S(2)}) collective-permute-start(bf16[256,896]{1,0:T(8,128)(2,1)S(1)} %get-tuple-element.48), channel_id=1, source_target_pairs={{8,16},{16,8},{9,17},{17,9},{10,18},{18,10},{11,19},{19,11},{12,20... | collective-permute-start | bytes 1376264 | tf_op jit(solution)/shard_map/ppermute | solution.py:302
  92.4 17.0 %collective-permute-start.17 = (bf16[256,896]{1,0:T(8,128)(2,1)S(1)}, bf16[256,896]{1,0:T(8,128)(2,1)S(1)}, u32[]{:S(2)}, u32[]{:S(2)}) collective-permute-start(bf16[256,896]{1,0:T(8,128)(2,1)S(1)} %get-tuple-element.43.after_ref.refs_0_), channel_id=1, source_target_pairs={{8,0},{16,24},{9,1},{17,25},{10,2},{18,26},{11,3},{19,27},{12,4},{... | collective-permute-start | bytes 1376264 | tf_op jit(solution)/shard_map/ppermute | solution.py:306
  95.4 21.9 %collective-permute-start.18 = (bf16[256,896]{1,0:T(8,128)(2,1)S(1)}, bf16[256,896]{1,0:T(8,128)(2,1)S(1)}, u32[]{:S(2)}, u32[]{:S(2)}) collective-permute-start(bf16[256,896]{1,0:T(8,128)(2,1)S(1)} %tick.11.after_ref.refs_0_), channel_id=1, source_target_pairs={{8,0},{16,24},{9,1},{17,25},{10,2},{18,26},{11,3},{19,27},{12,4},{... | collective-permute-start | bytes 1376264 | tf_op jit(solution)/shard_map/ppermute | solution.py:306
  109.3 2.0 %copy-start.1 = (bf16[2,256,3584]{2,1,0:T(8,128)(2,1)S(1)}, bf16[2,256,3584]{2,1,0:T(8,128)(2,1)}, u32[]{:S(2)}) copy-start(bf16[2,256,3584]{2,1,0:T(8,128)(2,1)} %refs_2_.7) | copy-start | bytes 11010052
  119.1 1.6 %collective-permute-start.19 = (f32[4,4,8,512]{3,2,1,0:T(8,128)S(1)}, f32[4,4,8,512]{3,2,1,0:T(8,128)S(1)}, u32[]{:S(2)}, u32[]{:S(2)}) collective-permute-start(f32[4,4,8,512]{3,2,1,0:T(8,128)S(1)} %dynamic-slice_bitcast_fusion), channel_id=1, source_target_pairs={{0,1},{1,0},{2,3},{3,2},{4,5},{5,4},{6,7},{7,6},{8,9},{9,8},{10,11... | collective-permute-start | bytes 786440 | tf_op jit(solution)/shard_map/ppermute | solution.py:21
  120.8 5.8 %collective-permute-start.20 = (f32[4,8,512]{2,1,0:T(8,128)S(1)}, f32[4,8,512]{2,1,0:T(8,128)S(1)}, u32[]{:S(2)}, u32[]{:S(2)}) collective-permute-start(f32[4,8,512]{2,1,0:T(8,128)S(1)} %get-tuple-element.56), channel_id=1, source_target_pairs={{0,6},{1,7},{2,4},{3,5},{4,2},{5,3},{6,0},{7,1},{8,14},{9,15},{10,... | collective-permute-start | bytes 196616 | tf_op jit(solution)/shard_map/ppermute | solution.py:21
  120.8 5.7 %collective-permute-start.21 = (f32[4,8,512]{2,1,0:T(8,128)S(1)}, f32[4,8,512]{2,1,0:T(8,128)S(1)}, u32[]{:S(2)}, u32[]{:S(2)}) collective-permute-start(f32[4,8,512]{2,1,0:T(8,128)S(1)} %get-tuple-element.54), channel_id=1, source_target_pairs={{0,4},{1,5},{2,6},{3,7},{4,0},{5,1},{6,2},{7,3},{8,12},{9,13},{10,... | collective-permute-start | bytes 196616 | tf_op jit(solution)/shard_map/ppermute | solution.py:21
  123.0 4.3 %collective-permute-start.22 = (f32[4,8,512]{2,1,0:T(8,128)S(1)}, f32[4,8,512]{2,1,0:T(8,128)S(1)}, u32[]{:S(2)}, u32[]{:S(2)}) collective-permute-start(f32[4,8,512]{2,1,0:T(8,128)S(1)} %get-tuple-element.55), channel_id=1, source_target_pairs={{0,2},{1,3},{2,0},{3,1},{4,6},{5,7},{6,4},{7,5},{8,10},{9,11},{10,... | collective-permute-start | bytes 196616 | tf_op jit(solution)/shard_map/ppermute | solution.py:21
  127.3 4.0 %collective-permute-start.23 = (f32[1,2,8,512]{3,2,1,0:T(8,128)S(1)}, f32[1,2,8,512]{3,2,1,0:T(8,128)S(1)}, u32[]{:S(2)}, u32[]{:S(2)}) collective-permute-start(f32[1,2,8,512]{3,2,1,0:T(8,128)S(1)} %get-tuple-element.59), channel_id=1, source_target_pairs={{0,8},{8,0},{16,24},{24,16},{1,9},{9,1},{17,25},{25,17},{2,10},{10... | collective-permute-start | bytes 98312 | tf_op jit(solution)/shard_map/ppermute | solution.py:430
  131.9 4.8 %collective-permute-start.24 = (f32[2,1,8,512]{3,2,1,0:T(8,128)S(1)}, f32[2,1,8,512]{3,2,1,0:T(8,128)S(1)}, u32[]{:S(2)}, u32[]{:S(2)}) collective-permute-start(f32[2,1,8,512]{3,2,1,0:T(8,128)S(1)} %get-tuple-element.57), channel_id=1, source_target_pairs={{0,16},{8,24},{16,0},{24,8},{1,17},{9,25},{17,1},{25,9},{2,18},{10... | collective-permute-start | bytes 98312 | tf_op jit(solution)/shard_map/ppermute | solution.py:430
  136.7 0.6 copy-start.5

commit v6 on v5

--- a/solution.py
+++ b/solution.py
@@ -10,7 +10,6 @@
 PARTS = 4
 STEPS = 7
 SLOTS = 4
-AHEAD = 3
 LANES = 128
 VMEM = pl.BlockSpec(memory_space=pltpu.VMEM)
 ANY = pl.BlockSpec(memory_space=pl.ANY)
@@ -21,77 +20,49 @@
     return lax.ppermute(array, "col", [(c, c ^ bit) for c in range(count)])
 
 
-def gathered(new_keys, col_count, col_index, fetch):
+def gathered(new_keys, col_count, col_index):
     rows = new_keys.shape[0]
     if col_count != 8:
-        after = fetch(new_keys)
         start = col_index * rows
-        return [new_keys, lax.all_gather(new_keys, "col", axis=0, tiled=True)], [start, jnp.int32(0)], after
+        return [new_keys, lax.all_gather(new_keys, "col", axis=0, tiled=True)], [start, jnp.int32(0)]
     half = rows // 2
     by_x = flipped(new_keys, 2, 8)
     by_y = flipped(new_keys, 4, 8)
     by_core = flipped(new_keys, 1, 8)
-    after = fetch(by_core)
-    low, high = halved(by_x, by_y, after)
+    own, low, high = halved(new_keys, by_x, by_y)
     low = flipped(low, 4, 8)
     high = flipped(high, 2, 8)
     x_core = flipped(by_x, 1, 8)
     y_core = flipped(by_y, 1, 8)
     low_core = flipped(low, 1, 8)
     high_core = flipped(high, 1, 8)
-    pieces = [new_keys, by_core, by_x, x_core, by_y, y_core, low, high, low_core, high_core]
+    pieces = [own, by_core, by_x, x_core, by_y, y_core, low, high, low_core, high_core]
     of = [0, 1, 2, 3, 4, 5, 6, 6, 7, 7]
     within = [0] * 7 + [half, 0, half]
-    return pieces, [(col_index ^ f) * rows + w for f, w in zip(of, within)], after
-
-
-def halved_kernel(x_ref, y_ref, after_ref, low_ref, high_ref):
+    return pieces, [(col_index ^ f) * rows + w for f, w in zip(of, within)]
+
+
+def halved_kernel(own_ref, x_ref, y_ref, keys_ref, low_ref, high_ref):
+    keys_ref[...] = own_ref[...]
     half = low_ref.shape[0]
     low_ref[...] = x_ref[:half]
     high_ref[...] = y_ref[half:]
 
 
-def halved(by_x, by_y, after):
+def halved(own, by_x, by_y):
     rows, depth = by_x.shape
     return pl.pallas_call(
         halved_kernel,
-        in_specs=[VMEM, VMEM, ANY],
-        out_specs=[VMEM, VMEM],
-        out_shape=[jax.ShapeDtypeStruct((rows // 2, depth), by_x.dtype)] * 2,
+        in_specs=[VMEM] * 3,
+        out_specs=[VMEM] * 3,
+        out_shape=[
+            jax.ShapeDtypeStruct((rows, depth), own.dtype),
+            *[jax.ShapeDtypeStruct((rows // 2, depth), by_x.dtype)] * 2,
+        ],
         compiler_params=params(),
         cost_estimate=cost(),
         name="halved",
-    )(by_x, by_y, after)
-
-
-def fetch_kernel(left, weights_ref, after_ref, held_ref, token_ref, arrived):
-    deep = held_ref.shape[0] // AHEAD
-    copies = []
-    for k in range(AHEAD):
-        rows = pl.ds(k * deep, deep)
-        source = weights_ref.at[rows, pl.ds(left, held_ref.shape[1])]
-        copies.append(pltpu.make_async_copy(source, held_ref.at[rows, :], arrived.at[k]))
-    for copy in copies:
-        copy.start()
-    token_ref[...] = jnp.zeros_like(token_ref)
-    for copy in copies:
-        copy.wait()
-
-
-def fetched(weights, span, after):
-    return pl.pallas_call(
-        functools.partial(fetch_kernel, span[0]),
-        in_specs=[ANY] * 2,
-        out_specs=[VMEM] * 2,
-        out_shape=[
-            jax.ShapeDtypeStruct((weights.shape[0] // STEPS * AHEAD, span[1] - span[0]), weights.dtype),
-            jax.ShapeDtypeStruct((8, LANES), jnp.float32),
-        ],
-        scratch_shapes=[pltpu.SemaphoreType.DMA((AHEAD,))],
-        compiler_params=params(),
-        cost_estimate=cost(),
-        name="fetch",
-    )(weights, after)
+    )(own, by_x, by_y)
 
 
 def ranges(columns):
@@ -106,54 +77,54 @@
 
 
 def params():
-    return pltpu.CompilerParams(vmem_limit_bytes=10 * 2**20)
-
-
-def assemble_kernel(count, starts_ref, after_ref, *refs):
+    return pltpu.CompilerParams(vmem_limit_bytes=18 * 2**20)
+
+
+def assemble_kernel(count, starts_ref, *refs):
     keys_ref = refs[count]
     for i, piece in enumerate(refs[:count]):
         keys_ref[pl.ds(pl.multiple_of(starts_ref[i], 16), piece.shape[0]), :] = piece[...]
 
 
-def assembled(pieces, starts, keys, after):
+def assembled(pieces, starts, keys):
     return pl.pallas_call(
         functools.partial(assemble_kernel, len(pieces)),
-        in_specs=[SMEM, ANY] + [VMEM] * len(pieces),
+        in_specs=[SMEM] + [VMEM] * len(pieces),
         out_specs=VMEM,
         out_shape=jax.ShapeDtypeStruct((keys, pieces[0].shape[1]), pieces[0].dtype),
         compiler_params=params(),
         cost_estimate=cost(),
         name="assemble",
-    )(starts, after, *pieces)
-
-
-def multiply(left, ahead, keys_ref, weights_ref, early, wide_ref, held_ref, arrived):
+    )(starts, *pieces)
+
+
+def multiply(left, keys_ref, weights_ref, wide_ref, sent, held_ref, arrived):
     wide = wide_ref.shape[1]
     deep = keys_ref.shape[1] // STEPS
+    slots = held_ref.shape[0]
 
     def copy(step):
         return pltpu.make_async_copy(
             weights_ref.at[pl.ds(step * deep, deep), pl.ds(left, wide)],
-            held_ref.at[step % SLOTS],
-            arrived.at[step % SLOTS],
+            held_ref.at[step % slots],
+            arrived.at[step % slots],
         )
 
-    for step in range(ahead, min(ahead + SLOTS, STEPS)):
+    for step in range(slots):
         copy(step).start()
     for step in range(STEPS):
-        if step < ahead:
-            weights = early[0][step * deep : (step + 1) * deep, :]
-        else:
-            copy(step).wait()
-            weights = held_ref[step % SLOTS]
+        copy(step).wait()
         part = jnp.dot(
             keys_ref[:, step * deep : (step + 1) * deep],
-            weights,
+            held_ref[step % slots],
             preferred_element_type=jnp.float32,
         )
-        if step >= ahead and step + SLOTS < STEPS:
-            copy(step + SLOTS).start()
-        wide_ref[...] = part if step == 0 else wide_ref[...] + part
+        if step + slots < STEPS:
+            copy(step + slots).start()
+        total = part if step == 0 else wide_ref[...] + part
+        wide_ref[...] = total
+        if sent and step == STEPS - 1:
+            sent[0][...] = total.astype(sent[0].dtype)
 
 
 def against(left, at_ref, final_ref, came_ref, stored_ref, before, terms_ref, piece_ref, rows_ref):
@@ -182,19 +153,19 @@
     take = lambda n: [refs.pop(0) for _ in range(n)]
     if product:
         factors = take(2)
-        early = take(1 if product[1] else 0)
     if contract:
         rows = take(3)
         before = take(contract[1])
         pieces = take(joined)
     if product:
         (wide_ref,) = take(1)
+        sent = take(1 if product[1] else 0)
     if contract:
         terms_ref, piece_ref = take(2)
     if joined:
         (whole_ref,) = take(1)
     if product:
-        multiply(*product, *factors, early, wide_ref, *take(2))
+        multiply(product[0], *factors, wide_ref, sent, *take(2))
     if contract:
         against(contract[0], at_ref, *rows, before, terms_ref, piece_ref, *take(1))
     if joined:
@@ -208,15 +179,17 @@
     operands, specs, shapes, scratch = [at, after], [SMEM, ANY], [], []
     product_at = contract_at = None
     if product:
-        keys, weights, early, span = product
+        keys, weights, span, first = product
         depth, rows, wide = weights.shape[0], keys.shape[0], span[1] - span[0]
-        product_at = (span[0], AHEAD if early else 0)
-        operands += [keys, weights, *early]
-        specs += [VMEM, ANY] + [VMEM] * len(early)
+        product_at = (span[0], first)
+        operands += [keys, weights]
+        specs += [VMEM, ANY]
         shapes += [jax.ShapeDtypeStruct((rows, wide), jnp.float32)]
+        shapes += [jax.ShapeDtypeStruct((rows, wide), jnp.bfloat16)] * first
+        slots = STEPS if first else SLOTS
         scratch += [
-            pltpu.VMEM((SLOTS, depth // STEPS, wide), weights.dtype),
-            pltpu.SemaphoreType.DMA((SLOTS,)),
+            pltpu.VMEM((slots, depth // STEPS, wide), weights.dtype),
+            pltpu.SemaphoreType.DMA((slots,)),
         ]
     if contract:
         final, came, stored, terms, left, block = contract
@@ -279,10 +252,13 @@
 
 def along_line(at, multiplied, contracted, count):
     wide, total, final = {}, {}, {}
-    (wide[0],) = multiplied(0, at)
-    outer = middle = None
-    after = wide[0]
-    for k in range(count + 2):
+    wide[0], sent = multiplied(0, at)
+    outer = lax.ppermute(sent, "row", [(0, 1), (3, 2)])
+    middle, after = None, sent
+    if count > 1:
+        (wide[1],) = multiplied(1, after)
+        after = wide[1]
+    for k in range(1, count + 2):
         outs, given = [], {}
         if 1 <= k <= count:
             outs += ["total", "across"]
@@ -315,13 +291,11 @@
     contracted(count - 1, final[count - 1], outer, after)
 
 
-def select_kernel(row_ref, batch_ref, used_ref, length_ref, slot_ref, kept_ref, came_ref, out_ref, held_ref):
+def select_kernel(row_ref, batch_ref, used_ref, length_ref, slot_ref, sums_ref, out_ref, held_ref):
     count, batches, rows, slots = held_ref.shape
-    half = count // 2
     for i in range(count):
-        part = kept_ref[i, 0] if i < half else came_ref[i - half, 0]
         for b in range(batches):
-            held_ref[i, b] = part[:, b * slots : (b + 1) * slots]
+            held_ref[i, b] = sums_ref[i, :, b * slots : (b + 1) * slots]
     row = row_ref[0]
     column = lax.broadcasted_iota(jnp.int32, (rows, slots), 1)
     for place in range(out_ref.shape[1]):
@@ -329,23 +303,23 @@
         slot = slot_ref[batch]
         owner = lax.div(slot, batches)
         length = jnp.where(place < used_ref[row], length_ref[batch], 0)
-        value = held_ref[owner ^ row, slot - owner * batches]
+        value = held_ref[owner, slot - owner * batches]
         out_ref[0, place] = jnp.where(column < length, value, 0.0)
 
 
-def selected(kept, came, row_index, pair_batch, pair_count, batch_length, batch_slot, batches):
-    half, _, rows, wide = kept.shape
+def selected(sums, row_index, pair_batch, pair_count, batch_length, batch_slot, batches):
+    count, rows, wide = sums.shape
     slots = wide // batches
     places = pair_batch.shape[1]
     return pl.pallas_call(
         select_kernel,
-        in_specs=[SMEM] * 5 + [VMEM] * 2,
+        in_specs=[SMEM] * 5 + [VMEM],
         out_specs=VMEM,
         out_shape=jax.ShapeDtypeStruct((1, places, rows, slots), jnp.float32),
-        scratch_shapes=[pltpu.VMEM((2 * half, batches, rows, slots), jnp.float32)],
+        scratch_shapes=[pltpu.VMEM((count, batches, rows, slots), jnp.float32)],
         cost_estimate=cost(),
         name="select",
-    )(row_index[None], pair_batch, pair_count, batch_length, batch_slot, kept, came)
+    )(row_index[None], pair_batch, pair_count, batch_length, batch_slot, sums)
 
 
 def shards(new_keys, precision, stored_keys, pair_batch, pair_count, batch_length, batch_slot):
@@ -362,16 +336,10 @@
     at = jnp.stack([(away == 0).astype(jnp.int32), row_index * block])
     spans = ranges(precision.shape[1])
     count = len(spans)
-    early = []
-
-    def fetch(after):
-        held, token = fetched(precision, spans[0], after)
-        early.append(held)
-        return token
-
-    pieces, starts, token = gathered(new_keys, col_count, col_index, fetch)
+
+    pieces, starts = gathered(new_keys, col_count, col_index)
     order = list(range(1, len(pieces))) + [0]
-    keys = assembled([pieces[i] for i in order], jnp.stack([starts[i] for i in order]), total_keys, token)
+    keys = assembled([pieces[i] for i in order], jnp.stack([starts[i] for i in order]), total_keys)
     terms = None
     whitened = []
 
@@ -379,15 +347,14 @@
         nonlocal terms
         product = None
         if part is not None:
-            product = (keys, precision, [] if part else early, spans[part])
+            product = (keys, precision, spans[part], part == 0)
         if contract is not None:
             number, final, came = contract
             contract = (final, came, stored_keys, terms, spans[number][0], block)
         joined = whitened if contract is not None and number == count - 1 else []
         out = work(at, after, product, contract, joined)
         if contract is not None:
-            first = 1 if product else 0
-            terms = out[first]
+            terms = out[1 if product else 0]
             whitened.append(out[-1])
         return out
 
@@ -399,7 +366,7 @@
     else:
         after = at
         for part in range(count):
-            (wide,) = multiplied(part, after)
+            wide = multiplied(part, after)[0]
             every = lax.psum(wide, "row").astype(jnp.bfloat16)
             contracted(part, every, every, wide)
             after = whitened[-1]
@@ -419,17 +386,8 @@
         left = lax.dynamic_index_in_dim(pairs, 1 - mine, 2, keepdims=False)
         sums = kept + flipped(left, bit, col_count)
         bit *= 2
-    parts = [sums[None, :, 0]]
-    bit = 1
-    while bit < row_count:
-        sums = jnp.concatenate(parts)
-        pairs = sums.reshape(bit, sums.shape[1] // 2, 2, share, sums.shape[3])
-        mine = (row_index // bit) % 2
-        kept = lax.dynamic_index_in_dim(pairs, mine, 2, keepdims=False)
-        left = lax.dynamic_index_in_dim(pairs, 1 - mine, 2, keepdims=False)
-        parts = [kept, lax.ppermute(left, "row", [(r, r ^ bit) for r in range(row_count)])]
-        bit *= 2
-    shares = selected(*parts, row_index, pair_batch, pair_count, batch_length, batch_slot, batches)
+    sums = lax.all_to_all(sums[:, 0], "row", split_axis=0, concat_axis=0, tiled=True)
+    shares = selected(sums, row_index, pair_batch, pair_count, batch_length, batch_slot, batches)
     return (whitened[-1], shares)
 
 

time: 139 us -> 135 us (0.971)
  blocking collectives: 0 us -> 8.78 us
  waiting for transfers between devices: 57.3 us -> 50.3 us
  Pallas kernels: 42.6 us -> 39.9 us
  local copies, waits for them, and re-layouts: 5.19 us -> 3.23 us
    all_to_all x0 -> x1, blocking collectives: none -> 8.78 us  [shards(): lax.all_to_all(sums[:, 0], 'row', split_axis=0, concat_axis=0, tiled=True)]
    ppermute x2 -> x1, waiting for transfers between devices: 8.67 us -> 2.94 us  [along_line(): outer = lax.ppermute(sent, 'row', [(0, 1), (3, 2)])]
    ppermute x6 -> x5, waiting for transfers between devices: 31 us -> 26 us  [along_line(): outer = lax.ppermute(sent, 'row', pairs)]
    ppermute x13, waiting for transfers between devices: 17.6 us -> 21.3 us  [flipped(): return lax.ppermute(array, 'col', [(c, c ^ bit) for c in range(count)])]
    ppermute x6 -> x5, starting transfers between devices: 18.1 us -> 14.5 us  [along_line(): outer = lax.ppermute(sent, 'row', pairs)]
    ppermute x2 -> x1, starting transfers between devices: 0.07 us -> 3.51 us  [along_line(): outer = lax.ppermute(sent, 'row', [(0, 1), (3, 2)])]
    pallas_call x3 -> x2, Pallas kernels: 4.12 us -> 1.57 us  [the longest x1 1.51 us: selected(): pl.pallas_call(select_kernel, in_specs=[SMEM] * 5 + [VMEM], out_specs=VME...]
    unnamed x12 -> x6, local copies, waits for them, and re-layouts: 5.05 us -> 3.06 us
  transfers between devices with their start and end apart: 25 -> 23, of which waited for: 17 -> 15; matrix products, arithmetic and copies ran while one was open for 0% -> 0% of each run, Pallas kernels for 20% -> 19%
where the time goes in v6:
time: 135 us
  waiting for transfers between devices  50.3 us (37%)
  Pallas kernels  39.9 us (30%)
  starting transfers between devices  31.8 us (24%)
  blocking collectives  8.78 us (7%)
  local copies, waits for them, and re-layouts  3.23 us (2%)
    pallas_call x8, Pallas kernels, work(): pl.pallas_call(functools.partial(work_kernel, product_at, contract_at, le...  33.3 us
    ppermute x5, waiting for transfers between devices, along_line(): outer = lax.ppermute(sent, 'row', pairs)  26 us
    ppermute x13, waiting for transfers between devices, flipped(): return lax.ppermute(array, 'col', [(c, c ^ bit) for c in range(count)])  21.3 us
    ppermute x5, starting transfers between devices, along_line(): outer = lax.ppermute(sent, 'row', pairs)  14.5 us
    ppermute x13, starting transfers between devices, flipped(): return lax.ppermute(array, 'col', [(c, c ^ bit) for c in range(count)])  10.8 us
    all_to_all x1, blocking collectives, shards(): lax.all_to_all(sums[:, 0], 'row', split_axis=0, concat_axis=0, tiled=True)  8.78 us
    pallas_call x5, Pallas kernels, tick(): pl.pallas_call(functools.partial(tick_kernel, tuple(given), outs), in_spe...  3.8 us
    ppermute x1, starting transfers between devices, along_line(): outer = lax.ppermute(sent, 'row', [(0, 1), (3, 2)])  3.51 us
  transfers between devices with their start and end apart: 23, of which 15 were waited for; matrix products, arithmetic and copies ran while one was open for 0% of the time, Pallas kernels for 19%

profile of v6, /device:TPU:0, one launch (start us, length us, event | category | flops | bytes accessed | tf_op | source)
XLA Modules:
  0.0 134.9 jit_solution(17612360577794174295)
XLA Ops:
  0.6 3.0 %collective-permute-start.1 = (bf16[32,7168]{1,0:T(8,128)(2,1)}, bf16[32,7168]{1,0:T(8,128)(2,1)S(1)}, u32[]{:S(2)}, u32[]{:S(2)}) collective-permute-start(bf16[32,7168]{1,0:T(8,128)(2,1)} %own_ref.1), channel_id=1, source_target_pairs={{0,2},{1,3},{2,0},{3,1},{4,6},{5,7},{6,4},{7,5},{8,10},{9,11},{10,... | collective-permute-start | bytes 1376264 | tf_op jit(solution)/shard_map/ppermute | solution.py:20
  3.6 1.5 %collective-permute-start.3 = (bf16[32,7168]{1,0:T(8,128)(2,1)}, bf16[32,7168]{1,0:T(8,128)(2,1)S(1)}, u32[]{:S(2)}, u32[]{:S(2)}) collective-permute-start(bf16[32,7168]{1,0:T(8,128)(2,1)} %own_ref.1), channel_id=1, source_target_pairs={{0,4},{1,5},{2,6},{3,7},{4,0},{5,1},{6,2},{7,3},{8,12},{9,13},{10,... | collective-permute-start | bytes 1376264 | tf_op jit(solution)/shard_map/ppermute | solution.py:20
  5.2 0.0 collective-permute-start
  5.2 9.2 %collective-permute-done.1.x_ref.refs_1_ = bf16[32,7168]{1,0:T(8,128)(2,1)S(1)} collective-permute-done((bf16[32,7168]{1,0:T(8,128)(2,1)}, bf16[32,7168]{1,0:T(8,128)(2,1)S(1)}, u32[]{:S(2)}, u32[]{:S(2)}) %collective-permute-start.1) | collective-permute-done | bytes 458784 | tf_op jit(solution)/shard_map/ppermute | solution.py:20
  14.4 1.5 %collective-permute-done.3.y_ref.refs_3_ = bf16[32,7168]{1,0:T(8,128)(2,1)S(1)} collective-permute-done((bf16[32,7168]{1,0:T(8,128)(2,1)}, bf16[32,7168]{1,0:T(8,128)(2,1)S(1)}, u32[]{:S(2)}, u32[]{:S(2)}) %collective-permute-start.3) | collective-permute-done | bytes 458784 | tf_op jit(solution)/shard_map/ppermute | solution.py:20
  15.8 1.0 copy-done.2
  16.8 0.1 halved.1
  16.9 1.6 %collective-permute-start.5 = (bf16[16,7168]{1,0:T(8,128)(2,1)S(1)}, bf16[16,7168]{1,0:T(8,128)(2,1)S(1)}, u32[]{:S(2)}, u32[]{:S(2)}) collective-permute-start(bf16[16,7168]{1,0:T(8,128)(2,1)S(1)} %get-tuple-element.29), channel_id=1, source_target_pairs={{0,4},{1,5},{2,6},{3,7},{4,0},{5,1},{6,2},{7,3},{8,12},{9,13},{10,... | collective-permute-start | bytes 688136 | tf_op jit(solution)/shard_map/ppermute | solution.py:20
  18.5 0.5 collective-permute-start.6
  19.0 0.0 collective-permute-start.2
  19.0 0.5 collective-permute-start.4
  19.5 3.6 %collective-permute-done.5.refs_5_ = bf16[16,7168]{1,0:T(8,128)(2,1)S(1)} collective-permute-done((bf16[16,7168]{1,0:T(8,128)(2,1)S(1)}, bf16[16,7168]{1,0:T(8,128)(2,1)S(1)}, u32[]{:S(2)}, u32[]{:S(2)}) %collective-permute-start.5) | collective-permute-done | bytes 229408 | tf_op jit(solution)/shard_map/ppermute | solution.py:20
  23.1 0.0 collective-permute-start.7
  23.1 1.4 %collective-permute-done.6.refs_6_ = bf16[16,7168]{1,0:T(8,128)(2,1)S(1)} collective-permute-done((bf16[16,7168]{1,0:T(8,128)(2,1)S(1)}, bf16[16,7168]{1,0:T(8,128)(2,1)S(1)}, u32[]{:S(2)}, u32[]{:S(2)}) %collective-permute-start.6) | collective-permute-done | bytes 229408 | tf_op jit(solution)/shard_map/ppermute | solution.py:20
  24.5 0.0 collective-permute-start.8
  24.5 0.1 stack.59.starts_ref
  24.6 0.1 pad_add_fusion.at_ref.after_ref
  24.7 1.5 %collective-permute-done.8.refs_8_ = bf16[16,7168]{1,0:T(8,128)(2,1)} collective-permute-done((bf16[16,7168]{1,0:T(8,128)(2,1)S(1)}, bf16[16,7168]{1,0:T(8,128)(2,1)}, u32[]{:S(2)}, u32[]{:S(2)}) %collective-permute-start.8) | collective-permute-done | bytes 229408 | tf_op jit(solution)/shard_map/ppermute | solution.py:20
  26.1 0.0 collective-permute-done.2.refs_2_
  26.1 0.0 collective-permute-done.4.refs_4_
  26.1 1.2 assemble.1.refs_0_
  27.3 7.1 %work.8 = (f32[256,896]{1,0:T(8,128)S(1)}, bf16[256,896]{1,0:T(8,128)(2,1)S(1)}) custom-call(s32[2]{0:T(128)S(1)} %pad_add_fusion.at_ref.after_ref, s32[2]{0:T(128)S(1)} %pad_add_fusion.at_ref.after_ref, bf16[256,7168]{1,0:T(8,128)(2,1)S(1)} %assemble.1.refs_0_, bf16[7168,3584]{1,0:T(8,128)(2,1)} %refs_1_.7), custom_call_target="tpu_custom_call" | custom-call | flops 1 | bytes 1 | tf_op jit(solution)/shard_map/work/pallas_call | solution.py:209
  34.4 3.5 %collective-permute-start.9 = (bf16[256,896]{1,0:T(8,128)(2,1)S(1)}, bf16[256,896]{1,0:T(8,128)(2,1)S(1)}, u32[]{:S(2)}, u32[]{:S(2)}) collective-permute-start(bf16[256,896]{1,0:T(8,128)(2,1)S(1)} %get-tuple-element.32.after_ref), channel_id=1, source_target_pairs={{0,8},{24,16},{1,9},{25,17},{2,10},{26,18},{3,11},{27,19},{4,12},{... | collective-permute-start | bytes 1376264 | tf_op jit(solution)/shard_map/ppermute | solution.py:256
  38.0 7.1 %work.9.after_ref.refs_2_.refs_0_ = f32[256,896]{1,0:T(8,128)S(1)} custom-call(s32[2]{0:T(128)S(1)} %pad_add_fusion.at_ref.after_ref, bf16[256,896]{1,0:T(8,128)(2,1)S(1)} %get-tuple-element.32.after_ref, bf16[256,7168]{1,0:T(8,128)(2,1)S(1)} %assemble.1.refs_0_, bf16[7168,3584]{1,0:T(8,128)(2,1)} %refs_1_.7), custom_call_target="tpu_custom_call" | custom-call | flops 1 | bytes 1 | tf_op jit(solution)/shard_map/work/pallas_call | solution.py:209
  45.0 2.9 %collective-permute-done.9.refs_1_ = bf16[256,896]{1,0:T(8,128)(2,1)S(1)} collective-permute-done((bf16[256,896]{1,0:T(8,128)(2,1)S(1)}, bf16[256,896]{1,0:T(8,128)(2,1)S(1)}, u32[]{:S(2)}, u32[]{:S(2)}) %collective-permute-start.9) | collective-permute-done | bytes 458784 | tf_op jit(solution)/shard_map/ppermute | solution.py:256
  48.0 0.7 tick.5
  48.7 4.4 %collective-permute-start.10 = (bf16[256,896]{1,0:T(8,128)(2,1)S(1)}, bf16[256,896]{1,0:T(8,128)(2,1)S(1)}, u32[]{:S(2)}, u32[]{:S(2)}) collective-permute-start(bf16[256,896]{1,0:T(8,128)(2,1)S(1)} %get-tuple-element.34.after_ref), channel_id=1, source_target_pairs={{0,8},{24,16},{1,9},{25,17},{2,10},{26,18},{3,11},{27,19},{4,12},{... | collective-permute-start | bytes 1376264 | tf_op jit(solution)/shard_map/ppermute | solution.py:282
  53.1 0.9 collective-permute-start.11
  54.0 7.1 %work.10.after_ref.refs_4_.refs_0_ = f32[256,896]{1,0:T(8,128)S(1)} custom-call(s32[2]{0:T(128)S(1)} %pad_add_fusion.at_ref.after_ref, bf16[256,896]{1,0:T(8,128)(2,1)S(1)} %get-tuple-element.34.after_ref, bf16[256,7168]{1,0:T(8,128)(2,1)S(1)} %assemble.1.refs_0_, bf16[7168,3584]{1,0:T(8,128)(2,1)} %refs_1_.7), custom_call_target="tpu_custom_call" | custom-call | flops 1 | bytes 1 | tf_op jit(solution)/shard_map/work/pallas_call | solution.py:209
  61.1 1.2 collective-permute-done.10.refs_1_
  62.3 0.9 tick.6
  63.2 3.8 %collective-permute-start.12 = (bf16[256,896]{1,0:T(8,128)(2,1)S(1)}, bf16[256,896]{1,0:T(8,128)(2,1)S(1)}, u32[]{:S(2)}, u32[]{:S(2)}) collective-permute-start(bf16[256,896]{1,0:T(8,128)(2,1)S(1)} %get-tuple-element.37.after_ref), channel_id=1, source_target_pairs={{0,8},{24,16},{8,0},{16,24},{1,9},{25,17},{9,1},{17,25},{2,10},{26... | collective-permute-start | bytes 1376264 | tf_op jit(solution)/shard_map/ppermute | solution.py:282
  67.0 0.7 collective-permute-start.13
  67.7 7.1 %work.11.after_ref.refs_4_.refs_0_ = f32[256,896]{1,0:T(8,128)S(1)} custom-call(s32[2]{0:T(128)S(1)} %pad_add_fusion.at_ref.after_ref, bf16[256,896]{1,0:T(8,128)(2,1)S(1)} %get-tuple-element.37.after_ref, bf16[256,7168]{1,0:T(8,128)(2,1)S(1)} %assemble.1.refs_0_, bf16[7168,3584]{1,0:T(8,128)(2,1)} %refs_1_.7), custom_call_target="tpu_custom_call" | custom-call | flops 1 | bytes 1 | tf_op jit(solution)/shard_map/work/pallas_call | solution.py:209
  74.8 0.0 copy-start
  74.8 1.3 collective-permute-done.12.refs_1_
  76.1 0.0 collective-permute-done.13.refs_3_
  76.1 0.9 tick.7
  77.0 3.7 %collective-permute-start.14 = (bf16[256,896]{1,0:T(8,128)(2,1)S(1)}, bf16[256,896]{1,0:T(8,128)(2,1)S(1)}, u32[]{:S(2)}, u32[]{:S(2)}) collective-permute-start(bf16[256,896]{1,0:T(8,128)(2,1)S(1)} %get-tuple-element.40.after_ref), channel_id=1, source_target_pairs={{0,8},{24,16},{8,0},{16,24},{1,9},{25,17},{9,1},{17,25},{2,10},{26... | collective-permute-start | bytes 1376264 | tf_op jit(solution)/shard_map/ppermute | solution.py:282
  80.7 0.7 collective-permute-start.15
  81.4 1.1 work.12
  82.4 6.4 %collective-permute-done.14.refs_1_ = bf16[256,896]{1,0:T(8,128)(2,1)S(1)} collective-permute-done((bf16[256,896]{1,0:T(8,128)(2,1)S(1)}, bf16[256,896]{1,0:T(8,128)(2,1)S(1)}, u32[]{:S(2)}, u32[]{:S(2)}) %collective-permute-start.14) | collective-permute-done | bytes 458784 | tf_op jit(solution)/shard_map/ppermute | solution.py:282
  88.8 0.7 tick.8
  89.6 0.7 collective-permute-start.16
  90.3 1.3 collective-permute-start.17
  91.6 1.1 work.13
  92.6 0.0 collective-permute-done.16.refs_1_
  92.6 0.6 tick.9.after_ref.refs_0_
  93.3 1.3 collective-permute-start.18
  94.6 12.8 %collective-permute-done.17.refs_1_ = bf16[256,896]{1,0:T(8,128)(2,1)S(1)} collective-permute-done((bf16[256,896]{1,0:T(8,128)(2,1)S(1)}, bf16[256,896]{1,0:T(8,128)(2,1)S(1)}, u32[]{:S(2)}, u32[]{:S(2)}) %collective-permute-start.17) | collective-permute-done | bytes 458784 | tf_op jit(solution)/shard_map/ppermute | solution.py:282
  107.4 2.0 %copy-done.1 = bf16[2,256,3584]{2,1,0:T(8,128)(2,1)S(1)} copy-done((bf16[2,256,3584]{2,1,0:T(8,128)(2,1)S(1)}, bf16[2,256,3584]{2,1,0:T(8,128)(2,1)}, u32[]{:S(2)}) %copy-start.1) | copy-done | bytes 3670040
  109.4 1.1 work.14
  110.5 4.3 %collective-permute-done.18.refs_1_ = bf16[256,896]{1,0:T(8,128)(2,1)S(1)} collective-permute-done((bf16[256,896]{1,0:T(8,128)(2,1)S(1)}, bf16[256,896]{1,0:T(8,128)(2,1)S(1)}, u32[]{:S(2)}, u32[]{:S(2)}) %collective-permute-start.18) | collective-permute-done | bytes 458784 | tf_op jit(solution)/shard_map/ppermute | solution.py:282
  114.8 1.8 %work.15 = (f32[256,512]{1,0:T(8,128)S(1)}, bf16[64,896]{1,0:T(8,128)(2,1)}, bf16[64,3584]{1,0:T(8,128)(2,1)}) custom-call(s32[2]{0:T(128)S(1)} %pad_add_fusion.at_ref.after_ref, bf16[64,896]{1,0:T(8,128)(2,1)S(1)} %get-tuple-element.52.after_ref.refs_6_, bf16[256,896]{1,0:T(8,128)(2,1)S(1)} %tick.9.after_ref.refs_0_, ...), custom_call_target="tpu_custom_call" | custom-call | flops 1 | bytes 1 | tf_op jit(solution)/shard_map/work/pallas_call | solution.py:209
  116.6 0.1 collective-permute-start.19
  116.8 1.5 %collective-permute-done.19 = f32[4,4,8,512]{3,2,0,1:T(8,128)S(1)} collective-permute-done((f32[4,4,8,512]{3,2,0,1:T(8,128)S(1)}, f32[4,4,8,512]{3,2,0,1:T(8,128)S(1)}, u32[]{:S(2)}, u32[]{:S(2)}) %collective-permute-start.19) | collective-permute-done | bytes 262176 | tf_op jit(solution)/shard_map/ppermute | solution.py:20
  118.3 0.8 collective-permute-start.20
  119.1 1.2 collective-permute-start.21
  120.4 1.5 %collective-permute-start.22 = (f32[4,8,512]{2,1,0:T(8,128)S(1)}, f32[4,8,512]{2,1,0:T(8,128)S(1)}, u32[]{:S(2)}, u32[]{:S(2)}) collective-permute-start(f32[4,8,512]{2,1,0:T(8,128)S(1)} %get-tuple-element.59), channel_id=1, source_target_pairs={{0,2},{1,3},{2,0},{3,1},{4,6},{5,7},{6,4},{7,5},{8,10},{9,11},{10,... | collective-permute-start | bytes 196616 | tf_op jit(solution)/shard_map/ppermute | solution.py:20
  121.9 2.3 %collective-permute-done.20 = f32[4,8,512]{2,1,0:T(8,128)S(1)} collective-permute-done((f32[4,8,512]{2,1,0:T(8,128)S(1)}, f32[4,8,512]{2,1,0:T(8,128)S(1)}, u32[]{:S(2)}, u32[]{:S(2)}) %collective-permute-start.20) | collective-permute-done | bytes 65568 | tf_op jit(solution)/shard_map/ppermute | solution.py:20
  124.2 0.2 collective-permute-done.21
  124.4 0.3 collective-permute-done.22
  124.6 8.8 %all_to_all.5.sums_ref = f32[4,8,512]{2,1,0:T(8,128)} all-to-all(f32[4,8,512]{2,1,0:T(8,128)S(1)} %bitcast_add_fusion.1), channel_id=1, replica_groups=mesh['row'=4,'col'=8] {'row'}, dimensions={0} | all-to-all | bytes 131072 | tf_op jit(solution)/shard_map/all_to_all | solution.py:389
  133.4 1.5 %select.9 = f32[1,6,8,256]{3,2,1,0:T(8,128)} custom-call(s32[1]{0:T(128)} %bitcast.12.row_ref, s32[4,6]{1,0:T(4,128)} %batch_ref.1, s32[4]{0:T(128)} %used_ref.1, s32[8]{0:T(128)} %length_ref.1, s32[8]{0:T(128)} %slot_ref.1, f32[4,8,512]{2,1,0:T(8,128)} %all_to_all.5.sums_ref), custom_call_target="tpu_custom_call" | custom-call | flops 1 | bytes 1 | tf_op jit(solution)/shard_map/select/pallas_call | solution.py:314
  (12 shorter events, 0.1 us)
Async XLA Ops:
  0.6 13.7 %collective-permute-start.1 = (bf16[32,7168]{1,0:T(8,128)(2,1)}, bf16[32,7168]{1,0:T(8,128)(2,1)S(1)}, u32[]{:S(2)}, u32[]{:S(2)}) collective-permute-start(bf16[32,7168]{1,0:T(8,128)(2,1)} %own_ref.1), channel_id=1, source_target_pairs={{0,2},{1,3},{2,0},{3,1},{4,6},{5,7},{6,4},{7,5},{8,10},{9,11},{10,... | collective-permute-start | bytes 1376264 | tf_op jit(solution)/shard_map/ppermute | solution.py:20
  3.6 12.2 %collective-permute-start.3 = (bf16[32,7168]{1,0:T(8,128)(2,1)}, bf16[32,7168]{1,0:T(8,128)(2,1)S(1)}, u32[]{:S(2)}, u32[]{:S(2)}) collective-permute-start(bf16[32,7168]{1,0:T(8,128)(2,1)} %own_ref.1), channel_id=1, source_target_pairs={{0,4},{1,5},{2,6},{3,7},{4,0},{5,1},{6,2},{7,3},{8,12},{9,13},{10,... | collective-permute-start | bytes 1376264 | tf_op jit(solution)/shard_map/ppermute | solution.py:20
  5.2 19.5 %collective-permute-start = (bf16[32,7168]{1,0:T(8,128)(2,1)}, bf16[32,7168]{1,0:T(8,128)(2,1)S(1)}, u32[]{:S(2)}, u32[]{:S(2)}) collective-permute-start(bf16[32,7168]{1,0:T(8,128)(2,1)} %own_ref.1), channel_id=1, source_target_pairs={{0,1},{1,0},{2,3},{3,2},{4,5},{5,4},{6,7},{7,6},{8,9},{9,8},{10,11... | collective-permute-start | bytes 1376264 | tf_op jit(solution)/shard_map/ppermute | solution.py:20
  15.8 1.0 copy-start.2
  16.9 6.2 %collective-permute-start.5 = (bf16[16,7168]{1,0:T(8,128)(2,1)S(1)}, bf16[16,7168]{1,0:T(8,128)(2,1)S(1)}, u32[]{:S(2)}, u32[]{:S(2)}) collective-permute-start(bf16[16,7168]{1,0:T(8,128)(2,1)S(1)} %get-tuple-element.29), channel_id=1, source_target_pairs={{0,4},{1,5},{2,6},{3,7},{4,0},{5,1},{6,2},{7,3},{8,12},{9,13},{10,... | collective-permute-start | bytes 688136 | tf_op jit(solution)/shard_map/ppermute | solution.py:20
  18.5 6.0 %collective-permute-start.6 = (bf16[16,7168]{1,0:T(8,128)(2,1)S(1)}, bf16[16,7168]{1,0:T(8,128)(2,1)S(1)}, u32[]{:S(2)}, u32[]{:S(2)}) collective-permute-start(bf16[16,7168]{1,0:T(8,128)(2,1)S(1)} %get-tuple-element.30), channel_id=1, source_target_pairs={{0,2},{1,3},{2,0},{3,1},{4,6},{5,7},{6,4},{7,5},{8,10},{9,11},{10,... | collective-permute-start | bytes 688136 | tf_op jit(solution)/shard_map/ppermute | solution.py:20
  19.0 7.1 %collective-permute-start.2 = (bf16[32,7168]{1,0:T(8,128)(2,1)S(1)}, bf16[32,7168]{1,0:T(8,128)(2,1)S(1)}, u32[]{:S(2)}, u32[]{:S(2)}) collective-permute-start(bf16[32,7168]{1,0:T(8,128)(2,1)S(1)} %collective-permute-done.1.x_ref.refs_1_), channel_id=1, source_target_pairs={{0,1},{1,0},{2,3},{3,2},{4,5},{5,4},{6,7},{7,6},{8,9},{9,8},{10,11... | collective-permute-start | bytes 1376264 | tf_op jit(solution)/shard_map/ppermute | solution.py:20
  19.0 7.1 %collective-permute-start.4 = (bf16[32,7168]{1,0:T(8,128)(2,1)S(1)}, bf16[32,7168]{1,0:T(8,128)(2,1)S(1)}, u32[]{:S(2)}, u32[]{:S(2)}) collective-permute-start(bf16[32,7168]{1,0:T(8,128)(2,1)S(1)} %collective-permute-done.3.y_ref.refs_3_), channel_id=1, source_target_pairs={{0,1},{1,0},{2,3},{3,2},{4,5},{5,4},{6,7},{7,6},{8,9},{9,8},{10,11... | collective-permute-start | bytes 1376264 | tf_op jit(solution)/shard_map/ppermute | solution.py:20
  23.1 1.6 %collective-permute-start.7 = (bf16[16,7168]{1,0:T(8,128)(2,1)S(1)}, bf16[16,7168]{1,0:T(8,128)(2,1)S(1)}, u32[]{:S(2)}, u32[]{:S(2)}) collective-permute-start(bf16[16,7168]{1,0:T(8,128)(2,1)S(1)} %collective-permute-done.5.refs_5_), channel_id=1, source_target_pairs={{0,1},{1,0},{2,3},{3,2},{4,5},{5,4},{6,7},{7,6},{8,9},{9,8},{10,11... | collective-permute-start | bytes 688136 | tf_op jit(solution)/shard_map/ppermute | solution.py:20
  24.5 1.6 %collective-permute-start.8 = (bf16[16,7168]{1,0:T(8,128)(2,1)S(1)}, bf16[16,7168]{1,0:T(8,128)(2,1)}, u32[]{:S(2)}, u32[]{:S(2)}) collective-permute-start(bf16[16,7168]{1,0:T(8,128)(2,1)S(1)} %collective-permute-done.6.refs_6_), channel_id=1, source_target_pairs={{0,1},{1,0},{2,3},{3,2},{4,5},{5,4},{6,7},{7,6},{8,9},{9,8},{10,11... | collective-permute-start | bytes 688136 | tf_op jit(solution)/shard_map/ppermute | solution.py:20
  34.4 13.5 %collective-permute-start.9 = (bf16[256,896]{1,0:T(8,128)(2,1)S(1)}, bf16[256,896]{1,0:T(8,128)(2,1)S(1)}, u32[]{:S(2)}, u32[]{:S(2)}) collective-permute-start(bf16[256,896]{1,0:T(8,128)(2,1)S(1)} %get-tuple-element.32.after_ref), channel_id=1, source_target_pairs={{0,8},{24,16},{1,9},{25,17},{2,10},{26,18},{3,11},{27,19},{4,12},{... | collective-permute-start | bytes 1376264 | tf_op jit(solution)/shard_map/ppermute | solution.py:256
  48.7 13.6 %collective-permute-start.10 = (bf16[256,896]{1,0:T(8,128)(2,1)S(1)}, bf16[256,896]{1,0:T(8,128)(2,1)S(1)}, u32[]{:S(2)}, u32[]{:S(2)}) collective-permute-start(bf16[256,896]{1,0:T(8,128)(2,1)S(1)} %get-tuple-element.34.after_ref), channel_id=1, source_target_pairs={{0,8},{24,16},{1,9},{25,17},{2,10},{26,18},{3,11},{27,19},{4,12},{... | collective-permute-start | bytes 1376264 | tf_op jit(solution)/shard_map/ppermute | solution.py:282
  53.1 9.2 %collective-permute-start.11 = (bf16[256,896]{1,0:T(8,128)(2,1)S(1)}, bf16[256,896]{1,0:T(8,128)(2,1)S(1)}, u32[]{:S(2)}, u32[]{:S(2)}) collective-permute-start(bf16[256,896]{1,0:T(8,128)(2,1)S(1)} %get-tuple-element.36), channel_id=1, source_target_pairs={{8,16},{16,8},{9,17},{17,9},{10,18},{18,10},{11,19},{19,11},{12,20... | collective-permute-start | bytes 1376264 | tf_op jit(solution)/shard_map/ppermute | solution.py:278
  63.2 12.9 %collective-permute-start.12 = (bf16[256,896]{1,0:T(8,128)(2,1)S(1)}, bf16[256,896]{1,0:T(8,128)(2,1)S(1)}, u32[]{:S(2)}, u32[]{:S(2)}) collective-permute-start(bf16[256,896]{1,0:T(8,128)(2,1)S(1)} %get-tuple-element.37.after_ref), channel_id=1, source_target_pairs={{0,8},{24,16},{8,0},{16,24},{1,9},{25,17},{9,1},{17,25},{2,10},{26... | collective-permute-start | bytes 1376264 | tf_op jit(solution)/shard_map/ppermute | solution.py:282
  67.0 9.1 %collective-permute-start.13 = (bf16[256,896]{1,0:T(8,128)(2,1)S(1)}, bf16[256,896]{1,0:T(8,128)(2,1)S(1)}, u32[]{:S(2)}, u32[]{:S(2)}) collective-permute-start(bf16[256,896]{1,0:T(8,128)(2,1)S(1)} %get-tuple-element.39), channel_id=1, source_target_pairs={{8,16},{16,8},{9,17},{17,9},{10,18},{18,10},{11,19},{19,11},{12,20... | collective-permute-start | bytes 1376264 | tf_op jit(solution)/shard_map/ppermute | solution.py:278
  74.8 6.6 %copy-start = (bf16[2,256,3584]{2,1,0:T(8,128)(2,1)S(1)}, bf16[2,256,3584]{2,1,0:T(8,128)(2,1)}, u32[]{:S(2)}) copy-start(bf16[2,256,3584]{2,1,0:T(8,128)(2,1)} %refs_2_.7) | copy-start | bytes 11010052
  77.0 11.9 %collective-permute-start.14 = (bf16[256,896]{1,0:T(8,128)(2,1)S(1)}, bf16[256,896]{1,0:T(8,128)(2,1)S(1)}, u32[]{:S(2)}, u32[]{:S(2)}) collective-permute-start(bf16[256,896]{1,0:T(8,128)(2,1)S(1)} %get-tuple-element.40.after_ref), channel_id=1, source_target_pairs={{0,8},{24,16},{8,0},{16,24},{1,9},{25,17},{9,1},{17,25},{2,10},{26... | collective-permute-start | bytes 1376264 | tf_op jit(solution)/shard_map/ppermute | solution.py:282
  80.7 8.1 %collective-permute-start.15 = (bf16[256,896]{1,0:T(8,128)(2,1)S(1)}, bf16[256,896]{1,0:T(8,128)(2,1)S(1)}, u32[]{:S(2)}, u32[]{:S(2)}) collective-permute-start(bf16[256,896]{1,0:T(8,128)(2,1)S(1)} %get-tuple-element.44), channel_id=1, source_target_pairs={{8,16},{16,8},{9,17},{17,9},{10,18},{18,10},{11,19},{19,11},{12,20... | collective-permute-start | bytes 1376264 | tf_op jit(solution)/shard_map/ppermute | solution.py:278
  89.6 3.1 %collective-permute-start.16 = (bf16[256,896]{1,0:T(8,128)(2,1)S(1)}, bf16[256,896]{1,0:T(8,128)(2,1)S(1)}, u32[]{:S(2)}, u32[]{:S(2)}) collective-permute-start(bf16[256,896]{1,0:T(8,128)(2,1)S(1)} %get-tuple-element.50), channel_id=1, source_target_pairs={{8,16},{16,8},{9,17},{17,9},{10,18},{18,10},{11,19},{19,11},{12,20... | collective-permute-start | bytes 1376264 | tf_op jit(solution)/shard_map/ppermute | solution.py:278
  90.3 17.1 %collective-permute-start.17 = (bf16[256,896]{1,0:T(8,128)(2,1)S(1)}, bf16[256,896]{1,0:T(8,128)(2,1)S(1)}, u32[]{:S(2)}, u32[]{:S(2)}) collective-permute-start(bf16[256,896]{1,0:T(8,128)(2,1)S(1)} %get-tuple-element.45.after_ref.refs_0_), channel_id=1, source_target_pairs={{8,0},{16,24},{9,1},{17,25},{10,2},{18,26},{11,3},{19,27},{12,4},{... | collective-permute-start | bytes 1376264 | tf_op jit(solution)/shard_map/ppermute | solution.py:282
  93.3 21.5 %collective-permute-start.18 = (bf16[256,896]{1,0:T(8,128)(2,1)S(1)}, bf16[256,896]{1,0:T(8,128)(2,1)S(1)}, u32[]{:S(2)}, u32[]{:S(2)}) collective-permute-start(bf16[256,896]{1,0:T(8,128)(2,1)S(1)} %tick.9.after_ref.refs_0_), channel_id=1, source_target_pairs={{8,0},{16,24},{9,1},{17,25},{10,2},{18,26},{11,3},{19,27},{12,4},{... | collective-permute-start | bytes 1376264 | tf_op jit(solution)/shard_map/ppermute | solution.py:282
  107.4 2.0 %copy-start.1 = (bf16[2,256,3584]{2,1,0:T(8,128)(2,1)S(1)}, bf16[2,256,3584]{2,1,0:T(8,128)(2,1)}, u32[]{:S(2)}) copy-start(bf16[2,256,3584]{2,1,0:T(8,128)(2,1)} %refs_2_.7) | copy-start | bytes 11010052
  116.6 1.6 %collective-permute-start.19 = (f32[4,4,8,512]{3,2,0,1:T(8,128)S(1)}, f32[4,4,8,512]{3,2,0,1:T(8,128)S(1)}, u32[]{:S(2)}, u32[]{:S(2)}) collective-permute-start(f32[4,4,8,512]{3,2,0,1:T(8,128)S(1)} %bitcast.28), channel_id=1, source_target_pairs={{0,1},{1,0},{2,3},{3,2},{4,5},{5,4},{6,7},{7,6},{8,9},{9,8},{10,11... | collective-permute-start | bytes 786440 | tf_op jit(solution)/shard_map/ppermute | solution.py:20
  118.3 5.8 %collective-permute-start.20 = (f32[4,8,512]{2,1,0:T(8,128)S(1)}, f32[4,8,512]{2,1,0:T(8,128)S(1)}, u32[]{:S(2)}, u32[]{:S(2)}) collective-permute-start(f32[4,8,512]{2,1,0:T(8,128)S(1)} %get-tuple-element.60), channel_id=1, source_target_pairs={{0,6},{1,7},{2,4},{3,5},{4,2},{5,3},{6,0},{7,1},{8,14},{9,15},{10,... | collective-permute-start | bytes 196616 | tf_op jit(solution)/shard_map/ppermute | solution.py:20
  119.1 5.3 %collective-permute-start.21 = (f32[4,8,512]{2,1,0:T(8,128)S(1)}, f32[4,8,512]{2,1,0:T(8,128)S(1)}, u32[]{:S(2)}, u32[]{:S(2)}) collective-permute-start(f32[4,8,512]{2,1,0:T(8,128)S(1)} %get-tuple-element.58), channel_id=1, source_target_pairs={{0,4},{1,5},{2,6},{3,7},{4,0},{5,1},{6,2},{7,3},{8,12},{9,13},{10,... | collective-permute-start | bytes 196616 | tf_op jit(solution)/shard_map/ppermute | solution.py:20
  120.4 4.3 %collective-permute-start.22 = (f32[4,8,512]{2,1,0:T(8,128)S(1)}, f32[4,8,512]{2,1,0:T(8,128)S(1)}, u32[]{:S(2)}, u32[]{:S(2)}) collective-permute-start(f32[4,8,512]{2,1,0:T(8,128)S(1)} %get-tuple-element.59), channel_id=1, source_target_pairs={{0,2},{1,3},{2,0},{3,1},{4,6},{5,7},{6,4},{7,5},{8,10},{9,11},{10,... | collective-permute-start | bytes 196616 | tf_op jit(solution)/shard_map/ppermute | solution.py:20

commit v7 on v6

--- a/solution.py
+++ b/solution.py
@@ -25,44 +25,13 @@
     if col_count != 8:
         start = col_index * rows
         return [new_keys, lax.all_gather(new_keys, "col", axis=0, tiled=True)], [start, jnp.int32(0)]
-    half = rows // 2
-    by_x = flipped(new_keys, 2, 8)
-    by_y = flipped(new_keys, 4, 8)
-    by_core = flipped(new_keys, 1, 8)
-    own, low, high = halved(new_keys, by_x, by_y)
-    low = flipped(low, 4, 8)
-    high = flipped(high, 2, 8)
-    x_core = flipped(by_x, 1, 8)
-    y_core = flipped(by_y, 1, 8)
-    low_core = flipped(low, 1, 8)
-    high_core = flipped(high, 1, 8)
-    pieces = [own, by_core, by_x, x_core, by_y, y_core, low, high, low_core, high_core]
-    of = [0, 1, 2, 3, 4, 5, 6, 6, 7, 7]
-    within = [0] * 7 + [half, 0, half]
-    return pieces, [(col_index ^ f) * rows + w for f, w in zip(of, within)]
-
-
-def halved_kernel(own_ref, x_ref, y_ref, keys_ref, low_ref, high_ref):
-    keys_ref[...] = own_ref[...]
-    half = low_ref.shape[0]
-    low_ref[...] = x_ref[:half]
-    high_ref[...] = y_ref[half:]
-
-
-def halved(own, by_x, by_y):
-    rows, depth = by_x.shape
-    return pl.pallas_call(
-        halved_kernel,
-        in_specs=[VMEM] * 3,
-        out_specs=[VMEM] * 3,
-        out_shape=[
-            jax.ShapeDtypeStruct((rows, depth), own.dtype),
-            *[jax.ShapeDtypeStruct((rows // 2, depth), by_x.dtype)] * 2,
-        ],
-        compiler_params=params(),
-        cost_estimate=cost(),
-        name="halved",
-    )(own, by_x, by_y)
+    pieces = {0: new_keys}
+    for far in (2, 4, 6):
+        pieces[far] = flipped(new_keys, far, 8)
+    for far in (0, 2, 4, 6):
+        pieces[far + 1] = flipped(pieces[far], 1, 8)
+    order = sorted(pieces)
+    return [pieces[f] for f in order], [(col_index ^ f) * rows for f in order]
 
 
 def ranges(columns):
@@ -80,18 +49,24 @@
     return pltpu.CompilerParams(vmem_limit_bytes=18 * 2**20)
 
 
-def assemble_kernel(count, starts_ref, *refs):
-    keys_ref = refs[count]
+def assemble_kernel(count, starts_ref, own_ref, *refs):
+    keys_ref, held_ref, arrived = refs[count:]
+    copy = pltpu.make_async_copy(own_ref, held_ref, arrived)
+    copy.start()
     for i, piece in enumerate(refs[:count]):
-        keys_ref[pl.ds(pl.multiple_of(starts_ref[i], 16), piece.shape[0]), :] = piece[...]
+        keys_ref[pl.ds(pl.multiple_of(starts_ref[i + 1], 16), piece.shape[0]), :] = piece[...]
+    copy.wait()
+    keys_ref[pl.ds(pl.multiple_of(starts_ref[0], 16), own_ref.shape[0]), :] = held_ref[...]
 
 
 def assembled(pieces, starts, keys):
+    own = pieces[0]
     return pl.pallas_call(
-        functools.partial(assemble_kernel, len(pieces)),
-        in_specs=[SMEM] + [VMEM] * len(pieces),
+        functools.partial(assemble_kernel, len(pieces) - 1),
+        in_specs=[SMEM, ANY] + [VMEM] * (len(pieces) - 1),
         out_specs=VMEM,
-        out_shape=jax.ShapeDtypeStruct((keys, pieces[0].shape[1]), pieces[0].dtype),
+        out_shape=jax.ShapeDtypeStruct((keys, own.shape[1]), own.dtype),
+        scratch_shapes=[pltpu.VMEM(own.shape, own.dtype), pltpu.SemaphoreType.DMA],
         compiler_params=params(),
         cost_estimate=cost(),
         name="assemble",
@@ -338,8 +313,7 @@
     count = len(spans)
 
     pieces, starts = gathered(new_keys, col_count, col_index)
-    order = list(range(1, len(pieces))) + [0]
-    keys = assembled([pieces[i] for i in order], jnp.stack([starts[i] for i in order]), total_keys)
+    keys = assembled(pieces, jnp.stack(starts), total_keys)
     terms = None
     whitened = []
 

time: 135 us -> 139 us (1.030)
  waiting for transfers between devices: 50.3 us -> 55.7 us
  starting transfers between devices: 31.8 us -> 29.7 us
    ppermute x13 -> x11, waiting for transfers between devices: 21.3 us -> 26.7 us  [flipped(): return lax.ppermute(array, 'col', [(c, c ^ bit) for c in range(count)])]
    ppermute x13 -> x11, starting transfers between devices: 10.8 us -> 8.69 us  [flipped(): return lax.ppermute(array, 'col', [(c, c ^ bit) for c in range(count)])]
  transfers between devices with their start and end apart: 23 -> 21, of which waited for: 15 -> 13; matrix products, arithmetic and copies ran while one was open for 0% -> 0% of each run, Pallas kernels for 19% -> 18%
where the time goes in v7:
time: 139 us; the launch traced here: 138 us
  waiting for transfers between devices  55.7 us (40%)
  Pallas kernels  39.7 us (29%)
  starting transfers between devices  29.7 us (21%)
  blocking collectives  8.79 us (6%)
  local copies, waits for them, and re-layouts  3.23 us (2%)
    pallas_call x8, Pallas kernels, work(): pl.pallas_call(functools.partial(work_kernel, product_at, contract_at, le...  33.3 us
    ppermute x11, waiting for transfers between devices, flipped(): return lax.ppermute(array, 'col', [(c, c ^ bit) for c in range(count)])  26.7 us
    ppermute x5, waiting for transfers between devices, along_line(): outer = lax.ppermute(sent, 'row', pairs)  26 us
    ppermute x5, starting transfers between devices, along_line(): outer = lax.ppermute(sent, 'row', pairs)  14.5 us
    all_to_all x1, blocking collectives, shards(): lax.all_to_all(sums[:, 0], 'row', split_axis=0, concat_axis=0, tiled=True)  8.79 us
    ppermute x11, starting transfers between devices, flipped(): return lax.ppermute(array, 'col', [(c, c ^ bit) for c in range(count)])  8.69 us
    pallas_call x5, Pallas kernels, tick(): pl.pallas_call(functools.partial(tick_kernel, tuple(given), outs), in_spe...  3.8 us
    ppermute x1, starting transfers between devices, along_line(): outer = lax.ppermute(sent, 'row', [(0, 1), (3, 2)])  3.5 us
  transfers between devices with their start and end apart: 21, of which 13 were waited for; matrix products, arithmetic and copies ran while one was open for 0% of the time, Pallas kernels for 18%

profile of v7, /device:TPU:0, one launch (start us, length us, event | category | flops | bytes accessed | tf_op | source)
XLA Modules:
  0.0 138.1 jit_solution(489402592753579886)
XLA Ops:
  0.6 3.0 %collective-permute-start.1 = (bf16[32,7168]{1,0:T(8,128)(2,1)}, bf16[32,7168]{1,0:T(8,128)(2,1)S(1)}, u32[]{:S(2)}, u32[]{:S(2)}) collective-permute-start(bf16[32,7168]{1,0:T(8,128)(2,1)} %own_ref.1), channel_id=1, source_target_pairs={{0,2},{1,3},{2,0},{3,1},{4,6},{5,7},{6,4},{7,5},{8,10},{9,11},{10,... | collective-permute-start | bytes 1376264 | tf_op jit(solution)/shard_map/ppermute | solution.py:20
  3.6 1.5 %collective-permute-start.3 = (bf16[32,7168]{1,0:T(8,128)(2,1)}, bf16[32,7168]{1,0:T(8,128)(2,1)S(1)}, u32[]{:S(2)}, u32[]{:S(2)}) collective-permute-start(bf16[32,7168]{1,0:T(8,128)(2,1)} %own_ref.1), channel_id=1, source_target_pairs={{0,4},{1,5},{2,6},{3,7},{4,0},{5,1},{6,2},{7,3},{8,12},{9,13},{10,... | collective-permute-start | bytes 1376264 | tf_op jit(solution)/shard_map/ppermute | solution.py:20
  5.2 0.0 collective-permute-start.5
  5.2 0.0 collective-permute-start
  5.2 10.0 %collective-permute-done.1.refs_1_ = bf16[32,7168]{1,0:T(8,128)(2,1)S(1)} collective-permute-done((bf16[32,7168]{1,0:T(8,128)(2,1)}, bf16[32,7168]{1,0:T(8,128)(2,1)S(1)}, u32[]{:S(2)}, u32[]{:S(2)}) %collective-permute-start.1) | collective-permute-done | bytes 458784 | tf_op jit(solution)/shard_map/ppermute | solution.py:20
  15.2 0.0 collective-permute-start.2
  15.2 10.5 %collective-permute-done.3.refs_3_ = bf16[32,7168]{1,0:T(8,128)(2,1)S(1)} collective-permute-done((bf16[32,7168]{1,0:T(8,128)(2,1)}, bf16[32,7168]{1,0:T(8,128)(2,1)S(1)}, u32[]{:S(2)}, u32[]{:S(2)}) %collective-permute-start.3) | collective-permute-done | bytes 458784 | tf_op jit(solution)/shard_map/ppermute | solution.py:20
  25.7 0.0 collective-permute-start.4
  25.7 0.0 collective-permute-done.5.refs_5_
  25.7 0.5 collective-permute-start.6
  26.2 0.1 stack.51.starts_ref
  26.3 0.1 pad_add_fusion.at_ref.after_ref
  26.3 0.0 collective-permute-done.refs_0_
  26.3 0.0 collective-permute-done.2.refs_2_
  26.3 1.1 collective-permute-done.4.refs_4_
  27.5 0.7 collective-permute-done.6.refs_6_
  28.1 1.0 copy-done.2
  29.1 1.1 assemble.1.refs_0_
  30.2 7.1 %work.8 = (f32[256,896]{1,0:T(8,128)S(1)}, bf16[256,896]{1,0:T(8,128)(2,1)S(1)}) custom-call(s32[2]{0:T(128)S(1)} %pad_add_fusion.at_ref.after_ref, s32[2]{0:T(128)S(1)} %pad_add_fusion.at_ref.after_ref, bf16[256,7168]{1,0:T(8,128)(2,1)S(1)} %assemble.1.refs_0_, bf16[7168,3584]{1,0:T(8,128)(2,1)} %refs_1_.7), custom_call_target="tpu_custom_call" | custom-call | flops 1 | bytes 1 | tf_op jit(solution)/shard_map/work/pallas_call | solution.py:184
  37.3 3.5 %collective-permute-start.7 = (bf16[256,896]{1,0:T(8,128)(2,1)S(1)}, bf16[256,896]{1,0:T(8,128)(2,1)S(1)}, u32[]{:S(2)}, u32[]{:S(2)}) collective-permute-start(bf16[256,896]{1,0:T(8,128)(2,1)S(1)} %get-tuple-element.26.after_ref), channel_id=1, source_target_pairs={{0,8},{24,16},{1,9},{25,17},{2,10},{26,18},{3,11},{27,19},{4,12},{... | collective-permute-start | bytes 1376264 | tf_op jit(solution)/shard_map/ppermute | solution.py:231
  40.8 7.1 %work.9.after_ref.refs_2_.refs_0_ = f32[256,896]{1,0:T(8,128)S(1)} custom-call(s32[2]{0:T(128)S(1)} %pad_add_fusion.at_ref.after_ref, bf16[256,896]{1,0:T(8,128)(2,1)S(1)} %get-tuple-element.26.after_ref, bf16[256,7168]{1,0:T(8,128)(2,1)S(1)} %assemble.1.refs_0_, bf16[7168,3584]{1,0:T(8,128)(2,1)} %refs_1_.7), custom_call_target="tpu_custom_call" | custom-call | flops 1 | bytes 1 | tf_op jit(solution)/shard_map/work/pallas_call | solution.py:184
  47.9 2.9 %collective-permute-done.7.refs_1_ = bf16[256,896]{1,0:T(8,128)(2,1)S(1)} collective-permute-done((bf16[256,896]{1,0:T(8,128)(2,1)S(1)}, bf16[256,896]{1,0:T(8,128)(2,1)S(1)}, u32[]{:S(2)}, u32[]{:S(2)}) %collective-permute-start.7) | collective-permute-done | bytes 458784 | tf_op jit(solution)/shard_map/ppermute | solution.py:231
  50.9 0.7 tick.5
  51.6 4.4 %collective-permute-start.8 = (bf16[256,896]{1,0:T(8,128)(2,1)S(1)}, bf16[256,896]{1,0:T(8,128)(2,1)S(1)}, u32[]{:S(2)}, u32[]{:S(2)}) collective-permute-start(bf16[256,896]{1,0:T(8,128)(2,1)S(1)} %get-tuple-element.28.after_ref), channel_id=1, source_target_pairs={{0,8},{24,16},{1,9},{25,17},{2,10},{26,18},{3,11},{27,19},{4,12},{... | collective-permute-start | bytes 1376264 | tf_op jit(solution)/shard_map/ppermute | solution.py:257
  56.0 0.9 collective-permute-start.9
  56.9 7.1 %work.10.after_ref.refs_4_.refs_0_ = f32[256,896]{1,0:T(8,128)S(1)} custom-call(s32[2]{0:T(128)S(1)} %pad_add_fusion.at_ref.after_ref, bf16[256,896]{1,0:T(8,128)(2,1)S(1)} %get-tuple-element.28.after_ref, bf16[256,7168]{1,0:T(8,128)(2,1)S(1)} %assemble.1.refs_0_, bf16[7168,3584]{1,0:T(8,128)(2,1)} %refs_1_.7), custom_call_target="tpu_custom_call" | custom-call | flops 1 | bytes 1 | tf_op jit(solution)/shard_map/work/pallas_call | solution.py:184
  64.0 1.2 collective-permute-done.8.refs_1_
  65.2 0.0 collective-permute-done.9.refs_3_
  65.2 0.9 tick.6
  66.1 3.8 %collective-permute-start.10 = (bf16[256,896]{1,0:T(8,128)(2,1)S(1)}, bf16[256,896]{1,0:T(8,128)(2,1)S(1)}, u32[]{:S(2)}, u32[]{:S(2)}) collective-permute-start(bf16[256,896]{1,0:T(8,128)(2,1)S(1)} %get-tuple-element.31.after_ref), channel_id=1, source_target_pairs={{0,8},{24,16},{8,0},{16,24},{1,9},{25,17},{9,1},{17,25},{2,10},{26... | collective-permute-start | bytes 1376264 | tf_op jit(solution)/shard_map/ppermute | solution.py:257
  69.9 0.7 collective-permute-start.11
  70.6 7.1 %work.11.after_ref.refs_4_.refs_0_ = f32[256,896]{1,0:T(8,128)S(1)} custom-call(s32[2]{0:T(128)S(1)} %pad_add_fusion.at_ref.after_ref, bf16[256,896]{1,0:T(8,128)(2,1)S(1)} %get-tuple-element.31.after_ref, bf16[256,7168]{1,0:T(8,128)(2,1)S(1)} %assemble.1.refs_0_, bf16[7168,3584]{1,0:T(8,128)(2,1)} %refs_1_.7), custom_call_target="tpu_custom_call" | custom-call | flops 1 | bytes 1 | tf_op jit(solution)/shard_map/work/pallas_call | solution.py:184
  77.7 0.0 copy-start
  77.7 1.3 collective-permute-done.10.refs_1_
  79.0 0.0 collective-permute-done.11.refs_3_
  79.0 0.9 tick.7
  79.9 3.7 %collective-permute-start.12 = (bf16[256,896]{1,0:T(8,128)(2,1)S(1)}, bf16[256,896]{1,0:T(8,128)(2,1)S(1)}, u32[]{:S(2)}, u32[]{:S(2)}) collective-permute-start(bf16[256,896]{1,0:T(8,128)(2,1)S(1)} %get-tuple-element.34.after_ref), channel_id=1, source_target_pairs={{0,8},{24,16},{8,0},{16,24},{1,9},{25,17},{9,1},{17,25},{2,10},{26... | collective-permute-start | bytes 1376264 | tf_op jit(solution)/shard_map/ppermute | solution.py:257
  83.6 0.7 collective-permute-start.13
  84.3 0.0 copy-done
  84.3 1.1 work.12
  85.3 6.4 %collective-permute-done.12.refs_1_ = bf16[256,896]{1,0:T(8,128)(2,1)S(1)} collective-permute-done((bf16[256,896]{1,0:T(8,128)(2,1)S(1)}, bf16[256,896]{1,0:T(8,128)(2,1)S(1)}, u32[]{:S(2)}, u32[]{:S(2)}) %collective-permute-start.12) | collective-permute-done | bytes 458784 | tf_op jit(solution)/shard_map/ppermute | solution.py:257
  91.7 0.0 collective-permute-done.13.refs_3_
  91.7 0.7 tick.8
  92.5 0.7 collective-permute-start.14
  93.2 1.3 collective-permute-start.15
  94.5 1.1 work.13
  95.5 0.0 collective-permute-done.14.refs_1_
  95.6 0.6 tick.9.after_ref.refs_0_
  96.2 1.3 collective-permute-start.16
  97.5 12.8 %collective-permute-done.15.refs_1_ = bf16[256,896]{1,0:T(8,128)(2,1)S(1)} collective-permute-done((bf16[256,896]{1,0:T(8,128)(2,1)S(1)}, bf16[256,896]{1,0:T(8,128)(2,1)S(1)}, u32[]{:S(2)}, u32[]{:S(2)}) %collective-permute-start.15) | collective-permute-done | bytes 458784 | tf_op jit(solution)/shard_map/ppermute | solution.py:257
  110.3 2.0 %copy-done.1 = bf16[2,256,3584]{2,1,0:T(8,128)(2,1)S(1)} copy-done((bf16[2,256,3584]{2,1,0:T(8,128)(2,1)S(1)}, bf16[2,256,3584]{2,1,0:T(8,128)(2,1)}, u32[]{:S(2)}) %copy-start.1) | copy-done | bytes 3670040
  112.3 1.1 work.14
  113.4 4.3 %collective-permute-done.16.refs_1_ = bf16[256,896]{1,0:T(8,128)(2,1)S(1)} collective-permute-done((bf16[256,896]{1,0:T(8,128)(2,1)S(1)}, bf16[256,896]{1,0:T(8,128)(2,1)S(1)}, u32[]{:S(2)}, u32[]{:S(2)}) %collective-permute-start.16) | collective-permute-done | bytes 458784 | tf_op jit(solution)/shard_map/ppermute | solution.py:257
  117.7 1.8 %work.15 = (f32[256,512]{1,0:T(8,128)S(1)}, bf16[64,896]{1,0:T(8,128)(2,1)}, bf16[64,3584]{1,0:T(8,128)(2,1)}) custom-call(s32[2]{0:T(128)S(1)} %pad_add_fusion.at_ref.after_ref, bf16[64,896]{1,0:T(8,128)(2,1)S(1)} %get-tuple-element.46.after_ref.refs_6_, bf16[256,896]{1,0:T(8,128)(2,1)S(1)} %tick.9.after_ref.refs_0_, ...), custom_call_target="tpu_custom_call" | custom-call | flops 1 | bytes 1 | tf_op jit(solution)/shard_map/work/pallas_call | solution.py:184
  119.6 0.1 collective-permute-start.17
  119.7 1.5 %collective-permute-done.17 = f32[4,4,8,512]{3,2,0,1:T(8,128)S(1)} collective-permute-done((f32[4,4,8,512]{3,2,0,1:T(8,128)S(1)}, f32[4,4,8,512]{3,2,0,1:T(8,128)S(1)}, u32[]{:S(2)}, u32[]{:S(2)}) %collective-permute-start.17) | collective-permute-done | bytes 262176 | tf_op jit(solution)/shard_map/ppermute | solution.py:20
  121.2 1.6 %collective-permute-start.18 = (f32[4,8,512]{2,1,0:T(8,128)S(1)}, f32[4,8,512]{2,1,0:T(8,128)S(1)}, u32[]{:S(2)}, u32[]{:S(2)}) collective-permute-start(f32[4,8,512]{2,1,0:T(8,128)S(1)} %get-tuple-element.54), channel_id=1, source_target_pairs={{0,6},{1,7},{2,4},{3,5},{4,2},{5,3},{6,0},{7,1},{8,14},{9,15},{10,... | collective-permute-start | bytes 196616 | tf_op jit(solution)/shard_map/ppermute | solution.py:20
  122.8 0.6 collective-permute-start.19
  123.3 1.4 %collective-permute-start.20 = (f32[4,8,512]{2,1,0:T(8,128)S(1)}, f32[4,8,512]{2,1,0:T(8,128)S(1)}, u32[]{:S(2)}, u32[]{:S(2)}) collective-permute-start(f32[4,8,512]{2,1,0:T(8,128)S(1)} %get-tuple-element.53), channel_id=1, source_target_pairs={{0,2},{1,3},{2,0},{3,1},{4,6},{5,7},{6,4},{7,5},{8,10},{9,11},{10,... | collective-permute-start | bytes 196616 | tf_op jit(solution)/shard_map/ppermute | solution.py:20
  124.8 1.8 %collective-permute-done.18 = f32[4,8,512]{2,1,0:T(8,128)S(1)} collective-permute-done((f32[4,8,512]{2,1,0:T(8,128)S(1)}, f32[4,8,512]{2,1,0:T(8,128)S(1)}, u32[]{:S(2)}, u32[]{:S(2)}) %collective-permute-start.18) | collective-permute-done | bytes 65568 | tf_op jit(solution)/shard_map/ppermute | solution.py:20
  126.6 1.2 collective-permute-done.19
  127.7 0.0 collective-permute-done.20
  127.8 8.8 %all_to_all.5.sums_ref = f32[4,8,512]{2,1,0:T(8,128)} all-to-all(f32[4,8,512]{2,1,0:T(8,128)S(1)} %bitcast_add_fusion.1), channel_id=1, replica_groups=mesh['row'=4,'col'=8] {'row'}, dimensions={0} | all-to-all | bytes 131072 | tf_op jit(solution)/shard_map/all_to_all | solution.py:363
  136.6 1.5 %select.9 = f32[1,6,8,256]{3,2,1,0:T(8,128)} custom-call(s32[1]{0:T(128)} %bitcast.10.row_ref, s32[4,6]{1,0:T(4,128)} %batch_ref.1, s32[4]{0:T(128)} %used_ref.1, s32[8]{0:T(128)} %length_ref.1, s32[8]{0:T(128)} %slot_ref.1, f32[4,8,512]{2,1,0:T(8,128)} %all_to_all.5.sums_ref), custom_call_target="tpu_custom_call" | custom-call | flops 1 | bytes 1 | tf_op jit(solution)/shard_map/select/pallas_call | solution.py:289
  (7 shorter events, 0.1 us)
Async XLA Ops:
  0.6 14.6 %collective-permute-start.1 = (bf16[32,7168]{1,0:T(8,128)(2,1)}, bf16[32,7168]{1,0:T(8,128)(2,1)S(1)}, u32[]{:S(2)}, u32[]{:S(2)}) collective-permute-start(bf16[32,7168]{1,0:T(8,128)(2,1)} %own_ref.1), channel_id=1, source_target_pairs={{0,2},{1,3},{2,0},{3,1},{4,6},{5,7},{6,4},{7,5},{8,10},{9,11},{10,... | collective-permute-start | bytes 1376264 | tf_op jit(solution)/shard_map/ppermute | solution.py:20
  3.6 22.0 %collective-permute-start.3 = (bf16[32,7168]{1,0:T(8,128)(2,1)}, bf16[32,7168]{1,0:T(8,128)(2,1)S(1)}, u32[]{:S(2)}, u32[]{:S(2)}) collective-permute-start(bf16[32,7168]{1,0:T(8,128)(2,1)} %own_ref.1), channel_id=1, source_target_pairs={{0,4},{1,5},{2,6},{3,7},{4,0},{5,1},{6,2},{7,3},{8,12},{9,13},{10,... | collective-permute-start | bytes 1376264 | tf_op jit(solution)/shard_map/ppermute | solution.py:20
  5.2 20.5 %collective-permute-start.5 = (bf16[32,7168]{1,0:T(8,128)(2,1)}, bf16[32,7168]{1,0:T(8,128)(2,1)S(1)}, u32[]{:S(2)}, u32[]{:S(2)}) collective-permute-start(bf16[32,7168]{1,0:T(8,128)(2,1)} %own_ref.1), channel_id=1, source_target_pairs={{0,6},{1,7},{2,4},{3,5},{4,2},{5,3},{6,0},{7,1},{8,14},{9,15},{10,... | collective-permute-start | bytes 1376264 | tf_op jit(solution)/shard_map/ppermute | solution.py:20
  5.2 21.2 %collective-permute-start = (bf16[32,7168]{1,0:T(8,128)(2,1)}, bf16[32,7168]{1,0:T(8,128)(2,1)S(1)}, u32[]{:S(2)}, u32[]{:S(2)}) collective-permute-start(bf16[32,7168]{1,0:T(8,128)(2,1)} %own_ref.1), channel_id=1, source_target_pairs={{0,1},{1,0},{2,3},{3,2},{4,5},{5,4},{6,7},{7,6},{8,9},{9,8},{10,11... | collective-permute-start | bytes 1376264 | tf_op jit(solution)/shard_map/ppermute | solution.py:20
  15.2 11.1 %collective-permute-start.2 = (bf16[32,7168]{1,0:T(8,128)(2,1)S(1)}, bf16[32,7168]{1,0:T(8,128)(2,1)S(1)}, u32[]{:S(2)}, u32[]{:S(2)}) collective-permute-start(bf16[32,7168]{1,0:T(8,128)(2,1)S(1)} %collective-permute-done.1.refs_1_), channel_id=1, source_target_pairs={{0,1},{1,0},{2,3},{3,2},{4,5},{5,4},{6,7},{7,6},{8,9},{9,8},{10,11... | collective-permute-start | bytes 1376264 | tf_op jit(solution)/shard_map/ppermute | solution.py:20
  25.7 1.8 %collective-permute-start.4 = (bf16[32,7168]{1,0:T(8,128)(2,1)S(1)}, bf16[32,7168]{1,0:T(8,128)(2,1)S(1)}, u32[]{:S(2)}, u32[]{:S(2)}) collective-permute-start(bf16[32,7168]{1,0:T(8,128)(2,1)S(1)} %collective-permute-done.3.refs_3_), channel_id=1, source_target_pairs={{0,1},{1,0},{2,3},{3,2},{4,5},{5,4},{6,7},{7,6},{8,9},{9,8},{10,11... | collective-permute-start | bytes 1376264 | tf_op jit(solution)/shard_map/ppermute | solution.py:20
  25.7 2.5 %collective-permute-start.6 = (bf16[32,7168]{1,0:T(8,128)(2,1)S(1)}, bf16[32,7168]{1,0:T(8,128)(2,1)S(1)}, u32[]{:S(2)}, u32[]{:S(2)}) collective-permute-start(bf16[32,7168]{1,0:T(8,128)(2,1)S(1)} %collective-permute-done.5.refs_5_), channel_id=1, source_target_pairs={{0,1},{1,0},{2,3},{3,2},{4,5},{5,4},{6,7},{7,6},{8,9},{9,8},{10,11... | collective-permute-start | bytes 1376264 | tf_op jit(solution)/shard_map/ppermute | solution.py:20
  28.1 1.0 copy-start.2
  37.3 13.6 %collective-permute-start.7 = (bf16[256,896]{1,0:T(8,128)(2,1)S(1)}, bf16[256,896]{1,0:T(8,128)(2,1)S(1)}, u32[]{:S(2)}, u32[]{:S(2)}) collective-permute-start(bf16[256,896]{1,0:T(8,128)(2,1)S(1)} %get-tuple-element.26.after_ref), channel_id=1, source_target_pairs={{0,8},{24,16},{1,9},{25,17},{2,10},{26,18},{3,11},{27,19},{4,12},{... | collective-permute-start | bytes 1376264 | tf_op jit(solution)/shard_map/ppermute | solution.py:231
  51.6 13.6 %collective-permute-start.8 = (bf16[256,896]{1,0:T(8,128)(2,1)S(1)}, bf16[256,896]{1,0:T(8,128)(2,1)S(1)}, u32[]{:S(2)}, u32[]{:S(2)}) collective-permute-start(bf16[256,896]{1,0:T(8,128)(2,1)S(1)} %get-tuple-element.28.after_ref), channel_id=1, source_target_pairs={{0,8},{24,16},{1,9},{25,17},{2,10},{26,18},{3,11},{27,19},{4,12},{... | collective-permute-start | bytes 1376264 | tf_op jit(solution)/shard_map/ppermute | solution.py:257
  56.0 9.2 %collective-permute-start.9 = (bf16[256,896]{1,0:T(8,128)(2,1)S(1)}, bf16[256,896]{1,0:T(8,128)(2,1)S(1)}, u32[]{:S(2)}, u32[]{:S(2)}) collective-permute-start(bf16[256,896]{1,0:T(8,128)(2,1)S(1)} %get-tuple-element.30), channel_id=1, source_target_pairs={{8,16},{16,8},{9,17},{17,9},{10,18},{18,10},{11,19},{19,11},{12,20... | collective-permute-start | bytes 1376264 | tf_op jit(solution)/shard_map/ppermute | solution.py:253
  66.1 12.9 %collective-permute-start.10 = (bf16[256,896]{1,0:T(8,128)(2,1)S(1)}, bf16[256,896]{1,0:T(8,128)(2,1)S(1)}, u32[]{:S(2)}, u32[]{:S(2)}) collective-permute-start(bf16[256,896]{1,0:T(8,128)(2,1)S(1)} %get-tuple-element.31.after_ref), channel_id=1, source_target_pairs={{0,8},{24,16},{8,0},{16,24},{1,9},{25,17},{9,1},{17,25},{2,10},{26... | collective-permute-start | bytes 1376264 | tf_op jit(solution)/shard_map/ppermute | solution.py:257
  69.9 9.1 %collective-permute-start.11 = (bf16[256,896]{1,0:T(8,128)(2,1)S(1)}, bf16[256,896]{1,0:T(8,128)(2,1)S(1)}, u32[]{:S(2)}, u32[]{:S(2)}) collective-permute-start(bf16[256,896]{1,0:T(8,128)(2,1)S(1)} %get-tuple-element.33), channel_id=1, source_target_pairs={{8,16},{16,8},{9,17},{17,9},{10,18},{18,10},{11,19},{19,11},{12,20... | collective-permute-start | bytes 1376264 | tf_op jit(solution)/shard_map/ppermute | solution.py:253
  77.7 6.6 %copy-start = (bf16[2,256,3584]{2,1,0:T(8,128)(2,1)S(1)}, bf16[2,256,3584]{2,1,0:T(8,128)(2,1)}, u32[]{:S(2)}) copy-start(bf16[2,256,3584]{2,1,0:T(8,128)(2,1)} %refs_2_.7) | copy-start | bytes 11010052
  79.9 11.9 %collective-permute-start.12 = (bf16[256,896]{1,0:T(8,128)(2,1)S(1)}, bf16[256,896]{1,0:T(8,128)(2,1)S(1)}, u32[]{:S(2)}, u32[]{:S(2)}) collective-permute-start(bf16[256,896]{1,0:T(8,128)(2,1)S(1)} %get-tuple-element.34.after_ref), channel_id=1, source_target_pairs={{0,8},{24,16},{8,0},{16,24},{1,9},{25,17},{9,1},{17,25},{2,10},{26... | collective-permute-start | bytes 1376264 | tf_op jit(solution)/shard_map/ppermute | solution.py:257
  83.6 8.2 %collective-permute-start.13 = (bf16[256,896]{1,0:T(8,128)(2,1)S(1)}, bf16[256,896]{1,0:T(8,128)(2,1)S(1)}, u32[]{:S(2)}, u32[]{:S(2)}) collective-permute-start(bf16[256,896]{1,0:T(8,128)(2,1)S(1)} %get-tuple-element.38), channel_id=1, source_target_pairs={{8,16},{16,8},{9,17},{17,9},{10,18},{18,10},{11,19},{19,11},{12,20... | collective-permute-start | bytes 1376264 | tf_op jit(solution)/shard_map/ppermute | solution.py:253
  92.5 3.1 %collective-permute-start.14 = (bf16[256,896]{1,0:T(8,128)(2,1)S(1)}, bf16[256,896]{1,0:T(8,128)(2,1)S(1)}, u32[]{:S(2)}, u32[]{:S(2)}) collective-permute-start(bf16[256,896]{1,0:T(8,128)(2,1)S(1)} %get-tuple-element.44), channel_id=1, source_target_pairs={{8,16},{16,8},{9,17},{17,9},{10,18},{18,10},{11,19},{19,11},{12,20... | collective-permute-start | bytes 1376264 | tf_op jit(solution)/shard_map/ppermute | solution.py:253
  93.2 17.1 %collective-permute-start.15 = (bf16[256,896]{1,0:T(8,128)(2,1)S(1)}, bf16[256,896]{1,0:T(8,128)(2,1)S(1)}, u32[]{:S(2)}, u32[]{:S(2)}) collective-permute-start(bf16[256,896]{1,0:T(8,128)(2,1)S(1)} %get-tuple-element.39.after_ref.refs_0_), channel_id=1, source_target_pairs={{8,0},{16,24},{9,1},{17,25},{10,2},{18,26},{11,3},{19,27},{12,4},{... | collective-permute-start | bytes 1376264 | tf_op jit(solution)/shard_map/ppermute | solution.py:257
  96.2 21.5 %collective-permute-start.16 = (bf16[256,896]{1,0:T(8,128)(2,1)S(1)}, bf16[256,896]{1,0:T(8,128)(2,1)S(1)}, u32[]{:S(2)}, u32[]{:S(2)}) collective-permute-start(bf16[256,896]{1,0:T(8,128)(2,1)S(1)} %tick.9.after_ref.refs_0_), channel_id=1, source_target_pairs={{8,0},{16,24},{9,1},{17,25},{10,2},{18,26},{11,3},{19,27},{12,4},{... | collective-permute-start | bytes 1376264 | tf_op jit(solution)/shard_map/ppermute | solution.py:257
  110.3 2.0 %copy-start.1 = (bf16[2,256,3584]{2,1,0:T(8,128)(2,1)S(1)}, bf16[2,256,3584]{2,1,0:T(8,128)(2,1)}, u32[]{:S(2)}) copy-start(bf16[2,256,3584]{2,1,0:T(8,128)(2,1)} %refs_2_.7) | copy-start | bytes 11010052
  119.6 1.6 %collective-permute-start.17 = (f32[4,4,8,512]{3,2,0,1:T(8,128)S(1)}, f32[4,4,8,512]{3,2,0,1:T(8,128)S(1)}, u32[]{:S(2)}, u32[]{:S(2)}) collective-permute-start(f32[4,4,8,512]{3,2,0,1:T(8,128)S(1)} %bitcast.26), channel_id=1, source_target_pairs={{0,1},{1,0},{2,3},{3,2},{4,5},{5,4},{6,7},{7,6},{8,9},{9,8},{10,11... | collective-permute-start | bytes 786440 | tf_op jit(solution)/shard_map/ppermute | solution.py:20
  121.2 5.3 %collective-permute-start.18 = (f32[4,8,512]{2,1,0:T(8,128)S(1)}, f32[4,8,512]{2,1,0:T(8,128)S(1)}, u32[]{:S(2)}, u32[]{:S(2)}) collective-permute-start(f32[4,8,512]{2,1,0:T(8,128)S(1)} %get-tuple-element.54), channel_id=1, source_target_pairs={{0,6},{1,7},{2,4},{3,5},{4,2},{5,3},{6,0},{7,1},{8,14},{9,15},{10,... | collective-permute-start | bytes 196616 | tf_op jit(solution)/shard_map/ppermute | solution.py:20
  122.8 5.0 %collective-permute-start.19 = (f32[4,8,512]{2,1,0:T(8,128)S(1)}, f32[4,8,512]{2,1,0:T(8,128)S(1)}, u32[]{:S(2)}, u32[]{:S(2)}) collective-permute-start(f32[4,8,512]{2,1,0:T(8,128)S(1)} %get-tuple-element.52), channel_id=1, source_target_pairs={{0,4},{1,5},{2,6},{3,7},{4,0},{5,1},{6,2},{7,3},{8,12},{9,13},{10,... | collective-permute-start | bytes 196616 | tf_op jit(solution)/shard_map/ppermute | solution.py:20
  123.3 4.4 %collective-permute-start.20 = (f32[4,8,512]{2,1,0:T(8,128)S(1)}, f32[4,8,512]{2,1,0:T(8,128)S(1)}, u32[]{:S(2)}, u32[]{:S(2)}) collective-permute-start(f32[4,8,512]{2,1,0:T(8,128)S(1)} %get-tuple-element.53), channel_id=1, source_target_pairs={{0,2},{1,3},{2,0},{3,1},{4,6},{5,7},{6,4},{7,5},{8,10},{9,11},{10,... | collective-permute-start | bytes 196616 | tf_op jit(solution)/shard_map/ppermute | solution.py:20

commit v8 on v6

--- a/solution.py
+++ b/solution.py
@@ -260,12 +260,12 @@
         after = wide[1]
     for k in range(1, count + 2):
         outs, given = [], {}
+        if k >= 2:
+            outs += ["final"]
+            given.update(held=total[k - 2], middle=middle)
         if 1 <= k <= count:
             outs += ["total", "across"]
             given.update(wide=wide[k - 1], outer=outer)
-        if k >= 2:
-            outs += ["final"]
-            given.update(held=total[k - 2], middle=middle)
         if k < count:
             outs += ["along"]
             given.update(next=wide[k])

time: 135 us -> 137 us (1.015)
  starting transfers between devices: 31.8 us -> 35.9 us
  waiting for transfers between devices: 50.3 us -> 47.1 us
    ppermute x5, starting transfers between devices: 14.5 us -> 18.8 us  [along_line(): outer = lax.ppermute(sent, 'row', pairs)]
    ppermute x5, waiting for transfers between devices: 26 us -> 22.8 us  [along_line(): outer = lax.ppermute(sent, 'row', pairs)]
  transfers between devices with their start and end apart: 23 -> 23, of which waited for: 15 -> 15; matrix products, arithmetic and copies ran while one was open for 0% -> 0% of each run, Pallas kernels for 19% -> 18%
where the time goes in v8:
time: 137 us; the launch traced here: 136 us
  waiting for transfers between devices  47.1 us (34%)
  Pallas kernels  39.9 us (29%)
  starting transfers between devices  35.9 us (26%)
  blocking collectives  9.36 us (7%)
  local copies, waits for them, and re-layouts  3.23 us (2%)
    pallas_call x8, Pallas kernels, work(): pl.pallas_call(functools.partial(work_kernel, product_at, contract_at, le...  33.3 us
    ppermute x5, waiting for transfers between devices, along_line(): outer = lax.ppermute(sent, 'row', pairs)  22.8 us
    ppermute x13, waiting for transfers between devices, flipped(): return lax.ppermute(array, 'col', [(c, c ^ bit) for c in range(count)])  21.3 us
    ppermute x5, starting transfers between devices, along_line(): outer = lax.ppermute(sent, 'row', pairs)  18.8 us
    ppermute x13, starting transfers between devices, flipped(): return lax.ppermute(array, 'col', [(c, c ^ bit) for c in range(count)])  10.8 us
    all_to_all x1, blocking collectives, shards(): lax.all_to_all(sums[:, 0], 'row', split_axis=0, concat_axis=0, tiled=True)  9.36 us
    pallas_call x5, Pallas kernels, tick(): pl.pallas_call(functools.partial(tick_kernel, tuple(given), outs), in_spe...  3.79 us
    ppermute x1, starting transfers between devices, along_line(): outer = lax.ppermute(sent, 'row', [(0, 1), (3, 2)])  3.51 us
  transfers between devices with their start and end apart: 23, of which 15 were waited for; matrix products, arithmetic and copies ran while one was open for 0% of the time, Pallas kernels for 18%

profile of v8, /device:TPU:0, one launch (start us, length us, event | category | flops | bytes accessed | tf_op | source)
XLA Modules:
  0.0 136.5 jit_solution(17753961377178586923)
XLA Ops:
  0.6 3.0 %collective-permute-start.1 = (bf16[32,7168]{1,0:T(8,128)(2,1)}, bf16[32,7168]{1,0:T(8,128)(2,1)S(1)}, u32[]{:S(2)}, u32[]{:S(2)}) collective-permute-start(bf16[32,7168]{1,0:T(8,128)(2,1)} %own_ref.1), channel_id=1, source_target_pairs={{0,2},{1,3},{2,0},{3,1},{4,6},{5,7},{6,4},{7,5},{8,10},{9,11},{10,... | collective-permute-start | bytes 1376264 | tf_op jit(solution)/shard_map/ppermute | solution.py:20
  3.6 1.5 %collective-permute-start.3 = (bf16[32,7168]{1,0:T(8,128)(2,1)}, bf16[32,7168]{1,0:T(8,128)(2,1)S(1)}, u32[]{:S(2)}, u32[]{:S(2)}) collective-permute-start(bf16[32,7168]{1,0:T(8,128)(2,1)} %own_ref.1), channel_id=1, source_target_pairs={{0,4},{1,5},{2,6},{3,7},{4,0},{5,1},{6,2},{7,3},{8,12},{9,13},{10,... | collective-permute-start | bytes 1376264 | tf_op jit(solution)/shard_map/ppermute | solution.py:20
  5.2 0.0 collective-permute-start
  5.2 9.2 %collective-permute-done.1.x_ref.refs_1_ = bf16[32,7168]{1,0:T(8,128)(2,1)S(1)} collective-permute-done((bf16[32,7168]{1,0:T(8,128)(2,1)}, bf16[32,7168]{1,0:T(8,128)(2,1)S(1)}, u32[]{:S(2)}, u32[]{:S(2)}) %collective-permute-start.1) | collective-permute-done | bytes 458784 | tf_op jit(solution)/shard_map/ppermute | solution.py:20
  14.4 1.5 %collective-permute-done.3.y_ref.refs_3_ = bf16[32,7168]{1,0:T(8,128)(2,1)S(1)} collective-permute-done((bf16[32,7168]{1,0:T(8,128)(2,1)}, bf16[32,7168]{1,0:T(8,128)(2,1)S(1)}, u32[]{:S(2)}, u32[]{:S(2)}) %collective-permute-start.3) | collective-permute-done | bytes 458784 | tf_op jit(solution)/shard_map/ppermute | solution.py:20
  15.8 1.0 copy-done.2
  16.8 0.1 halved.1
  16.9 1.6 %collective-permute-start.5 = (bf16[16,7168]{1,0:T(8,128)(2,1)S(1)}, bf16[16,7168]{1,0:T(8,128)(2,1)S(1)}, u32[]{:S(2)}, u32[]{:S(2)}) collective-permute-start(bf16[16,7168]{1,0:T(8,128)(2,1)S(1)} %get-tuple-element.29), channel_id=1, source_target_pairs={{0,4},{1,5},{2,6},{3,7},{4,0},{5,1},{6,2},{7,3},{8,12},{9,13},{10,... | collective-permute-start | bytes 688136 | tf_op jit(solution)/shard_map/ppermute | solution.py:20
  18.5 0.5 collective-permute-start.6
  19.0 0.5 collective-permute-start.4
  19.5 3.6 %collective-permute-done.5.refs_5_ = bf16[16,7168]{1,0:T(8,128)(2,1)S(1)} collective-permute-done((bf16[16,7168]{1,0:T(8,128)(2,1)S(1)}, bf16[16,7168]{1,0:T(8,128)(2,1)S(1)}, u32[]{:S(2)}, u32[]{:S(2)}) %collective-permute-start.5) | collective-permute-done | bytes 229408 | tf_op jit(solution)/shard_map/ppermute | solution.py:20
  23.1 0.0 collective-permute-start.7
  23.1 1.4 %collective-permute-done.6.refs_6_ = bf16[16,7168]{1,0:T(8,128)(2,1)S(1)} collective-permute-done((bf16[16,7168]{1,0:T(8,128)(2,1)S(1)}, bf16[16,7168]{1,0:T(8,128)(2,1)S(1)}, u32[]{:S(2)}, u32[]{:S(2)}) %collective-permute-start.6) | collective-permute-done | bytes 229408 | tf_op jit(solution)/shard_map/ppermute | solution.py:20
  24.5 0.0 collective-permute-start.8
  24.5 0.1 stack.59.starts_ref
  24.6 0.1 pad_add_fusion.at_ref.after_ref
  24.7 1.5 %collective-permute-done.8.refs_8_ = bf16[16,7168]{1,0:T(8,128)(2,1)} collective-permute-done((bf16[16,7168]{1,0:T(8,128)(2,1)S(1)}, bf16[16,7168]{1,0:T(8,128)(2,1)}, u32[]{:S(2)}, u32[]{:S(2)}) %collective-permute-start.8) | collective-permute-done | bytes 229408 | tf_op jit(solution)/shard_map/ppermute | solution.py:20
  26.1 0.0 collective-permute-done.2.refs_2_
  26.1 0.0 collective-permute-done.4.refs_4_
  26.1 1.2 assemble.1.refs_0_
  27.3 7.1 %work.8 = (f32[256,896]{1,0:T(8,128)S(1)}, bf16[256,896]{1,0:T(8,128)(2,1)S(1)}) custom-call(s32[2]{0:T(128)S(1)} %pad_add_fusion.at_ref.after_ref, s32[2]{0:T(128)S(1)} %pad_add_fusion.at_ref.after_ref, bf16[256,7168]{1,0:T(8,128)(2,1)S(1)} %assemble.1.refs_0_, bf16[7168,3584]{1,0:T(8,128)(2,1)} %refs_1_.7), custom_call_target="tpu_custom_call" | custom-call | flops 1 | bytes 1 | tf_op jit(solution)/shard_map/work/pallas_call | solution.py:209
  34.4 3.5 %collective-permute-start.9 = (bf16[256,896]{1,0:T(8,128)(2,1)S(1)}, bf16[256,896]{1,0:T(8,128)(2,1)S(1)}, u32[]{:S(2)}, u32[]{:S(2)}) collective-permute-start(bf16[256,896]{1,0:T(8,128)(2,1)S(1)} %get-tuple-element.32.after_ref), channel_id=1, source_target_pairs={{0,8},{24,16},{1,9},{25,17},{2,10},{26,18},{3,11},{27,19},{4,12},{... | collective-permute-start | bytes 1376264 | tf_op jit(solution)/shard_map/ppermute | solution.py:256
  38.0 7.1 %work.9.after_ref.refs_2_ = f32[256,896]{1,0:T(8,128)S(1)} custom-call(s32[2]{0:T(128)S(1)} %pad_add_fusion.at_ref.after_ref, bf16[256,896]{1,0:T(8,128)(2,1)S(1)} %get-tuple-element.32.after_ref, bf16[256,7168]{1,0:T(8,128)(2,1)S(1)} %assemble.1.refs_0_, bf16[7168,3584]{1,0:T(8,128)(2,1)} %refs_1_.7), custom_call_target="tpu_custom_call" | custom-call | flops 1 | bytes 1 | tf_op jit(solution)/shard_map/work/pallas_call | solution.py:209
  45.0 2.9 %collective-permute-done.9.refs_1_ = bf16[256,896]{1,0:T(8,128)(2,1)S(1)} collective-permute-done((bf16[256,896]{1,0:T(8,128)(2,1)S(1)}, bf16[256,896]{1,0:T(8,128)(2,1)S(1)}, u32[]{:S(2)}, u32[]{:S(2)}) %collective-permute-start.9) | collective-permute-done | bytes 458784 | tf_op jit(solution)/shard_map/ppermute | solution.py:256
  48.0 0.7 tick.5
  48.7 0.7 collective-permute-start.10
  49.4 7.4 %collective-permute-start.11 = (bf16[256,896]{1,0:T(8,128)(2,1)S(1)}, bf16[256,896]{1,0:T(8,128)(2,1)S(1)}, u32[]{:S(2)}, u32[]{:S(2)}) collective-permute-start(bf16[256,896]{1,0:T(8,128)(2,1)S(1)} %get-tuple-element.34.after_ref), channel_id=1, source_target_pairs={{0,8},{24,16},{1,9},{25,17},{2,10},{26,18},{3,11},{27,19},{4,12},{... | collective-permute-start | bytes 1376264 | tf_op jit(solution)/shard_map/ppermute | solution.py:282
  56.8 7.1 %work.10.after_ref.refs_4_.refs_2_ = f32[256,896]{1,0:T(8,128)S(1)} custom-call(s32[2]{0:T(128)S(1)} %pad_add_fusion.at_ref.after_ref, bf16[256,896]{1,0:T(8,128)(2,1)S(1)} %get-tuple-element.34.after_ref, bf16[256,7168]{1,0:T(8,128)(2,1)S(1)} %assemble.1.refs_0_, bf16[7168,3584]{1,0:T(8,128)(2,1)} %refs_1_.7), custom_call_target="tpu_custom_call" | custom-call | flops 1 | bytes 1 | tf_op jit(solution)/shard_map/work/pallas_call | solution.py:209
  63.9 0.0 collective-permute-done.10.refs_1_
  63.9 1.7 %collective-permute-done.11.refs_3_ = bf16[256,896]{1,0:T(8,128)(2,1)S(1)} collective-permute-done((bf16[256,896]{1,0:T(8,128)(2,1)S(1)}, bf16[256,896]{1,0:T(8,128)(2,1)S(1)}, u32[]{:S(2)}, u32[]{:S(2)}) %collective-permute-start.11) | collective-permute-done | bytes 458784 | tf_op jit(solution)/shard_map/ppermute | solution.py:282
  65.5 0.9 tick.6
  66.4 0.7 collective-permute-start.12
  67.1 4.2 %collective-permute-start.13 = (bf16[256,896]{1,0:T(8,128)(2,1)S(1)}, bf16[256,896]{1,0:T(8,128)(2,1)S(1)}, u32[]{:S(2)}, u32[]{:S(2)}) collective-permute-start(bf16[256,896]{1,0:T(8,128)(2,1)S(1)} %get-tuple-element.37.after_ref), channel_id=1, source_target_pairs={{0,8},{24,16},{8,0},{16,24},{1,9},{25,17},{9,1},{17,25},{2,10},{26... | collective-permute-start | bytes 1376264 | tf_op jit(solution)/shard_map/ppermute | solution.py:282
  71.3 7.1 %work.11.after_ref.refs_4_.refs_2_ = f32[256,896]{1,0:T(8,128)S(1)} custom-call(s32[2]{0:T(128)S(1)} %pad_add_fusion.at_ref.after_ref, bf16[256,896]{1,0:T(8,128)(2,1)S(1)} %get-tuple-element.37.after_ref, bf16[256,7168]{1,0:T(8,128)(2,1)S(1)} %assemble.1.refs_0_, bf16[7168,3584]{1,0:T(8,128)(2,1)} %refs_1_.7), custom_call_target="tpu_custom_call" | custom-call | flops 1 | bytes 1 | tf_op jit(solution)/shard_map/work/pallas_call | solution.py:209
  78.4 0.0 copy-start
  78.4 0.0 collective-permute-done.12.refs_1_
  78.4 1.4 %collective-permute-done.13.refs_3_.refs_1_ = bf16[256,896]{1,0:T(8,128)(2,1)S(1)} collective-permute-done((bf16[256,896]{1,0:T(8,128)(2,1)S(1)}, bf16[256,896]{1,0:T(8,128)(2,1)S(1)}, u32[]{:S(2)}, u32[]{:S(2)}) %collective-permute-start.13) | collective-permute-done | bytes 458784 | tf_op jit(solution)/shard_map/ppermute | solution.py:282
  79.8 0.9 tick.7
  80.7 0.7 collective-permute-start.14
  81.4 4.6 %collective-permute-start.15 = (bf16[256,896]{1,0:T(8,128)(2,1)S(1)}, bf16[256,896]{1,0:T(8,128)(2,1)S(1)}, u32[]{:S(2)}, u32[]{:S(2)}) collective-permute-start(bf16[256,896]{1,0:T(8,128)(2,1)S(1)} %get-tuple-element.40.after_ref), channel_id=1, source_target_pairs={{0,8},{24,16},{8,0},{16,24},{1,9},{25,17},{9,1},{17,25},{2,10},{26... | collective-permute-start | bytes 1376264 | tf_op jit(solution)/shard_map/ppermute | solution.py:282
  86.0 1.1 work.12
  87.1 0.0 collective-permute-done.14.refs_1_
  87.1 6.2 %collective-permute-done.15.refs_3_.refs_1_ = bf16[256,896]{1,0:T(8,128)(2,1)S(1)} collective-permute-done((bf16[256,896]{1,0:T(8,128)(2,1)S(1)}, bf16[256,896]{1,0:T(8,128)(2,1)S(1)}, u32[]{:S(2)}, u32[]{:S(2)}) %collective-permute-start.15) | collective-permute-done | bytes 458784 | tf_op jit(solution)/shard_map/ppermute | solution.py:282
  93.3 0.7 tick.8
  94.1 0.7 collective-permute-start.16
  94.8 1.3 collective-permute-start.17
  96.1 1.1 work.13
  97.1 0.6 tick.9.after_ref.refs_0_
  97.8 1.3 collective-permute-start.18
  99.1 9.2 %collective-permute-done.17.refs_1_ = bf16[256,896]{1,0:T(8,128)(2,1)S(1)} collective-permute-done((bf16[256,896]{1,0:T(8,128)(2,1)S(1)}, bf16[256,896]{1,0:T(8,128)(2,1)S(1)}, u32[]{:S(2)}, u32[]{:S(2)}) %collective-permute-start.17) | collective-permute-done | bytes 458784 | tf_op jit(solution)/shard_map/ppermute | solution.py:282
  108.3 2.0 %copy-done.1 = bf16[2,256,3584]{2,1,0:T(8,128)(2,1)S(1)} copy-done((bf16[2,256,3584]{2,1,0:T(8,128)(2,1)S(1)}, bf16[2,256,3584]{2,1,0:T(8,128)(2,1)}, u32[]{:S(2)}) %copy-start.1) | copy-done | bytes 3670040
  110.3 1.1 work.14
  111.4 4.4 %collective-permute-done.18.refs_1_ = bf16[256,896]{1,0:T(8,128)(2,1)S(1)} collective-permute-done((bf16[256,896]{1,0:T(8,128)(2,1)S(1)}, bf16[256,896]{1,0:T(8,128)(2,1)S(1)}, u32[]{:S(2)}, u32[]{:S(2)}) %collective-permute-start.18) | collective-permute-done | bytes 458784 | tf_op jit(solution)/shard_map/ppermute | solution.py:282
  115.8 1.8 %work.15 = (f32[256,512]{1,0:T(8,128)S(1)}, bf16[64,896]{1,0:T(8,128)(2,1)}, bf16[64,3584]{1,0:T(8,128)(2,1)}) custom-call(s32[2]{0:T(128)S(1)} %pad_add_fusion.at_ref.after_ref, bf16[64,896]{1,0:T(8,128)(2,1)S(1)} %get-tuple-element.52.after_ref.refs_6_, bf16[256,896]{1,0:T(8,128)(2,1)S(1)} %tick.9.after_ref.refs_0_, ...), custom_call_target="tpu_custom_call" | custom-call | flops 1 | bytes 1 | tf_op jit(solution)/shard_map/work/pallas_call | solution.py:209
  117.6 0.1 collective-permute-start.19
  117.7 1.5 %collective-permute-done.19 = f32[4,4,8,512]{3,2,0,1:T(8,128)S(1)} collective-permute-done((f32[4,4,8,512]{3,2,0,1:T(8,128)S(1)}, f32[4,4,8,512]{3,2,0,1:T(8,128)S(1)}, u32[]{:S(2)}, u32[]{:S(2)}) %collective-permute-start.19) | collective-permute-done | bytes 262176 | tf_op jit(solution)/shard_map/ppermute | solution.py:20
  119.3 0.7 collective-permute-start.20
  120.0 1.3 collective-permute-start.21
  121.3 1.5 %collective-permute-start.22 = (f32[4,8,512]{2,1,0:T(8,128)S(1)}, f32[4,8,512]{2,1,0:T(8,128)S(1)}, u32[]{:S(2)}, u32[]{:S(2)}) collective-permute-start(f32[4,8,512]{2,1,0:T(8,128)S(1)} %get-tuple-element.59), channel_id=1, source_target_pairs={{0,2},{1,3},{2,0},{3,1},{4,6},{5,7},{6,4},{7,5},{8,10},{9,11},{10,... | collective-permute-start | bytes 196616 | tf_op jit(solution)/shard_map/ppermute | solution.py:20
  122.8 2.3 %collective-permute-done.20 = f32[4,8,512]{2,1,0:T(8,128)S(1)} collective-permute-done((f32[4,8,512]{2,1,0:T(8,128)S(1)}, f32[4,8,512]{2,1,0:T(8,128)S(1)}, u32[]{:S(2)}, u32[]{:S(2)}) %collective-permute-start.20) | collective-permute-done | bytes 65568 | tf_op jit(solution)/shard_map/ppermute | solution.py:20
  125.1 0.2 collective-permute-done.21
  125.3 0.3 collective-permute-done.22
  125.6 9.4 %all_to_all.5.sums_ref = f32[4,8,512]{2,1,0:T(8,128)} all-to-all(f32[4,8,512]{2,1,0:T(8,128)S(1)} %bitcast_add_fusion.1), channel_id=1, replica_groups=mesh['row'=4,'col'=8] {'row'}, dimensions={0} | all-to-all | bytes 131072 | tf_op jit(solution)/shard_map/all_to_all | solution.py:389
  135.0 1.5 %select.9 = f32[1,6,8,256]{3,2,1,0:T(8,128)} custom-call(s32[1]{0:T(128)} %bitcast.12.row_ref, s32[4,6]{1,0:T(4,128)} %batch_ref.1, s32[4]{0:T(128)} %used_ref.1, s32[8]{0:T(128)} %length_ref.1, s32[8]{0:T(128)} %slot_ref.1, f32[4,8,512]{2,1,0:T(8,128)} %all_to_all.5.sums_ref), custom_call_target="tpu_custom_call" | custom-call | flops 1 | bytes 1 | tf_op jit(solution)/shard_map/select/pallas_call | solution.py:314
  (12 shorter events, 0.1 us)
Async XLA Ops:
  0.6 13.7 %collective-permute-start.1 = (bf16[32,7168]{1,0:T(8,128)(2,1)}, bf16[32,7168]{1,0:T(8,128)(2,1)S(1)}, u32[]{:S(2)}, u32[]{:S(2)}) collective-permute-start(bf16[32,7168]{1,0:T(8,128)(2,1)} %own_ref.1), channel_id=1, source_target_pairs={{0,2},{1,3},{2,0},{3,1},{4,6},{5,7},{6,4},{7,5},{8,10},{9,11},{10,... | collective-permute-start | bytes 1376264 | tf_op jit(solution)/shard_map/ppermute | solution.py:20
  3.6 12.2 %collective-permute-start.3 = (bf16[32,7168]{1,0:T(8,128)(2,1)}, bf16[32,7168]{1,0:T(8,128)(2,1)S(1)}, u32[]{:S(2)}, u32[]{:S(2)}) collective-permute-start(bf16[32,7168]{1,0:T(8,128)(2,1)} %own_ref.1), channel_id=1, source_target_pairs={{0,4},{1,5},{2,6},{3,7},{4,0},{5,1},{6,2},{7,3},{8,12},{9,13},{10,... | collective-permute-start | bytes 1376264 | tf_op jit(solution)/shard_map/ppermute | solution.py:20
  5.2 19.5 %collective-permute-start = (bf16[32,7168]{1,0:T(8,128)(2,1)}, bf16[32,7168]{1,0:T(8,128)(2,1)S(1)}, u32[]{:S(2)}, u32[]{:S(2)}) collective-permute-start(bf16[32,7168]{1,0:T(8,128)(2,1)} %own_ref.1), channel_id=1, source_target_pairs={{0,1},{1,0},{2,3},{3,2},{4,5},{5,4},{6,7},{7,6},{8,9},{9,8},{10,11... | collective-permute-start | bytes 1376264 | tf_op jit(solution)/shard_map/ppermute | solution.py:20
  15.8 1.0 copy-start.2
  16.9 6.2 %collective-permute-start.5 = (bf16[16,7168]{1,0:T(8,128)(2,1)S(1)}, bf16[16,7168]{1,0:T(8,128)(2,1)S(1)}, u32[]{:S(2)}, u32[]{:S(2)}) collective-permute-start(bf16[16,7168]{1,0:T(8,128)(2,1)S(1)} %get-tuple-element.29), channel_id=1, source_target_pairs={{0,4},{1,5},{2,6},{3,7},{4,0},{5,1},{6,2},{7,3},{8,12},{9,13},{10,... | collective-permute-start | bytes 688136 | tf_op jit(solution)/shard_map/ppermute | solution.py:20
  18.5 6.0 %collective-permute-start.6 = (bf16[16,7168]{1,0:T(8,128)(2,1)S(1)}, bf16[16,7168]{1,0:T(8,128)(2,1)S(1)}, u32[]{:S(2)}, u32[]{:S(2)}) collective-permute-start(bf16[16,7168]{1,0:T(8,128)(2,1)S(1)} %get-tuple-element.30), channel_id=1, source_target_pairs={{0,2},{1,3},{2,0},{3,1},{4,6},{5,7},{6,4},{7,5},{8,10},{9,11},{10,... | collective-permute-start | bytes 688136 | tf_op jit(solution)/shard_map/ppermute | solution.py:20
  19.0 7.1 %collective-permute-start.2 = (bf16[32,7168]{1,0:T(8,128)(2,1)S(1)}, bf16[32,7168]{1,0:T(8,128)(2,1)S(1)}, u32[]{:S(2)}, u32[]{:S(2)}) collective-permute-start(bf16[32,7168]{1,0:T(8,128)(2,1)S(1)} %collective-permute-done.1.x_ref.refs_1_), channel_id=1, source_target_pairs={{0,1},{1,0},{2,3},{3,2},{4,5},{5,4},{6,7},{7,6},{8,9},{9,8},{10,11... | collective-permute-start | bytes 1376264 | tf_op jit(solution)/shard_map/ppermute | solution.py:20
  19.0 7.1 %collective-permute-start.4 = (bf16[32,7168]{1,0:T(8,128)(2,1)S(1)}, bf16[32,7168]{1,0:T(8,128)(2,1)S(1)}, u32[]{:S(2)}, u32[]{:S(2)}) collective-permute-start(bf16[32,7168]{1,0:T(8,128)(2,1)S(1)} %collective-permute-done.3.y_ref.refs_3_), channel_id=1, source_target_pairs={{0,1},{1,0},{2,3},{3,2},{4,5},{5,4},{6,7},{7,6},{8,9},{9,8},{10,11... | collective-permute-start | bytes 1376264 | tf_op jit(solution)/shard_map/ppermute | solution.py:20
  23.1 1.6 %collective-permute-start.7 = (bf16[16,7168]{1,0:T(8,128)(2,1)S(1)}, bf16[16,7168]{1,0:T(8,128)(2,1)S(1)}, u32[]{:S(2)}, u32[]{:S(2)}) collective-permute-start(bf16[16,7168]{1,0:T(8,128)(2,1)S(1)} %collective-permute-done.5.refs_5_), channel_id=1, source_target_pairs={{0,1},{1,0},{2,3},{3,2},{4,5},{5,4},{6,7},{7,6},{8,9},{9,8},{10,11... | collective-permute-start | bytes 688136 | tf_op jit(solution)/shard_map/ppermute | solution.py:20
  24.5 1.6 %collective-permute-start.8 = (bf16[16,7168]{1,0:T(8,128)(2,1)S(1)}, bf16[16,7168]{1,0:T(8,128)(2,1)}, u32[]{:S(2)}, u32[]{:S(2)}) collective-permute-start(bf16[16,7168]{1,0:T(8,128)(2,1)S(1)} %collective-permute-done.6.refs_6_), channel_id=1, source_target_pairs={{0,1},{1,0},{2,3},{3,2},{4,5},{5,4},{6,7},{7,6},{8,9},{9,8},{10,11... | collective-permute-start | bytes 688136 | tf_op jit(solution)/shard_map/ppermute | solution.py:20
  34.4 13.5 %collective-permute-start.9 = (bf16[256,896]{1,0:T(8,128)(2,1)S(1)}, bf16[256,896]{1,0:T(8,128)(2,1)S(1)}, u32[]{:S(2)}, u32[]{:S(2)}) collective-permute-start(bf16[256,896]{1,0:T(8,128)(2,1)S(1)} %get-tuple-element.32.after_ref), channel_id=1, source_target_pairs={{0,8},{24,16},{1,9},{25,17},{2,10},{26,18},{3,11},{27,19},{4,12},{... | collective-permute-start | bytes 1376264 | tf_op jit(solution)/shard_map/ppermute | solution.py:256
  48.7 15.2 %collective-permute-start.10 = (bf16[256,896]{1,0:T(8,128)(2,1)S(1)}, bf16[256,896]{1,0:T(8,128)(2,1)S(1)}, u32[]{:S(2)}, u32[]{:S(2)}) collective-permute-start(bf16[256,896]{1,0:T(8,128)(2,1)S(1)} %get-tuple-element.36), channel_id=1, source_target_pairs={{8,16},{16,8},{9,17},{17,9},{10,18},{18,10},{11,19},{19,11},{12,20... | collective-permute-start | bytes 1376264 | tf_op jit(solution)/shard_map/ppermute | solution.py:278
  49.4 16.1 %collective-permute-start.11 = (bf16[256,896]{1,0:T(8,128)(2,1)S(1)}, bf16[256,896]{1,0:T(8,128)(2,1)S(1)}, u32[]{:S(2)}, u32[]{:S(2)}) collective-permute-start(bf16[256,896]{1,0:T(8,128)(2,1)S(1)} %get-tuple-element.34.after_ref), channel_id=1, source_target_pairs={{0,8},{24,16},{1,9},{25,17},{2,10},{26,18},{3,11},{27,19},{4,12},{... | collective-permute-start | bytes 1376264 | tf_op jit(solution)/shard_map/ppermute | solution.py:282
  66.4 12.0 %collective-permute-start.12 = (bf16[256,896]{1,0:T(8,128)(2,1)S(1)}, bf16[256,896]{1,0:T(8,128)(2,1)S(1)}, u32[]{:S(2)}, u32[]{:S(2)}) collective-permute-start(bf16[256,896]{1,0:T(8,128)(2,1)S(1)} %get-tuple-element.39), channel_id=1, source_target_pairs={{8,16},{16,8},{9,17},{17,9},{10,18},{18,10},{11,19},{19,11},{12,20... | collective-permute-start | bytes 1376264 | tf_op jit(solution)/shard_map/ppermute | solution.py:278
  67.1 12.7 %collective-permute-start.13 = (bf16[256,896]{1,0:T(8,128)(2,1)S(1)}, bf16[256,896]{1,0:T(8,128)(2,1)S(1)}, u32[]{:S(2)}, u32[]{:S(2)}) collective-permute-start(bf16[256,896]{1,0:T(8,128)(2,1)S(1)} %get-tuple-element.37.after_ref), channel_id=1, source_target_pairs={{0,8},{24,16},{8,0},{16,24},{1,9},{25,17},{9,1},{17,25},{2,10},{26... | collective-permute-start | bytes 1376264 | tf_op jit(solution)/shard_map/ppermute | solution.py:282
  78.4 7.6 %copy-start = (bf16[2,256,3584]{2,1,0:T(8,128)(2,1)S(1)}, bf16[2,256,3584]{2,1,0:T(8,128)(2,1)}, u32[]{:S(2)}) copy-start(bf16[2,256,3584]{2,1,0:T(8,128)(2,1)} %refs_2_.7) | copy-start | bytes 11010052
  80.7 6.4 %collective-permute-start.14 = (bf16[256,896]{1,0:T(8,128)(2,1)S(1)}, bf16[256,896]{1,0:T(8,128)(2,1)S(1)}, u32[]{:S(2)}, u32[]{:S(2)}) collective-permute-start(bf16[256,896]{1,0:T(8,128)(2,1)S(1)} %get-tuple-element.44), channel_id=1, source_target_pairs={{8,16},{16,8},{9,17},{17,9},{10,18},{18,10},{11,19},{19,11},{12,20... | collective-permute-start | bytes 1376264 | tf_op jit(solution)/shard_map/ppermute | solution.py:278
  81.4 11.9 %collective-permute-start.15 = (bf16[256,896]{1,0:T(8,128)(2,1)S(1)}, bf16[256,896]{1,0:T(8,128)(2,1)S(1)}, u32[]{:S(2)}, u32[]{:S(2)}) collective-permute-start(bf16[256,896]{1,0:T(8,128)(2,1)S(1)} %get-tuple-element.40.after_ref), channel_id=1, source_target_pairs={{0,8},{24,16},{8,0},{16,24},{1,9},{25,17},{9,1},{17,25},{2,10},{26... | collective-permute-start | bytes 1376264 | tf_op jit(solution)/shard_map/ppermute | solution.py:282
  94.1 3.1 %collective-permute-start.16 = (bf16[256,896]{1,0:T(8,128)(2,1)S(1)}, bf16[256,896]{1,0:T(8,128)(2,1)S(1)}, u32[]{:S(2)}, u32[]{:S(2)}) collective-permute-start(bf16[256,896]{1,0:T(8,128)(2,1)S(1)} %get-tuple-element.50), channel_id=1, source_target_pairs={{8,16},{16,8},{9,17},{17,9},{10,18},{18,10},{11,19},{19,11},{12,20... | collective-permute-start | bytes 1376264 | tf_op jit(solution)/shard_map/ppermute | solution.py:278
  94.8 13.5 %collective-permute-start.17 = (bf16[256,896]{1,0:T(8,128)(2,1)S(1)}, bf16[256,896]{1,0:T(8,128)(2,1)S(1)}, u32[]{:S(2)}, u32[]{:S(2)}) collective-permute-start(bf16[256,896]{1,0:T(8,128)(2,1)S(1)} %get-tuple-element.45.after_ref.refs_0_), channel_id=1, source_target_pairs={{8,0},{16,24},{9,1},{17,25},{10,2},{18,26},{11,3},{19,27},{12,4},{... | collective-permute-start | bytes 1376264 | tf_op jit(solution)/shard_map/ppermute | solution.py:282
  97.8 18.0 %collective-permute-start.18 = (bf16[256,896]{1,0:T(8,128)(2,1)S(1)}, bf16[256,896]{1,0:T(8,128)(2,1)S(1)}, u32[]{:S(2)}, u32[]{:S(2)}) collective-permute-start(bf16[256,896]{1,0:T(8,128)(2,1)S(1)} %tick.9.after_ref.refs_0_), channel_id=1, source_target_pairs={{8,0},{16,24},{9,1},{17,25},{10,2},{18,26},{11,3},{19,27},{12,4},{... | collective-permute-start | bytes 1376264 | tf_op jit(solution)/shard_map/ppermute | solution.py:282
  108.3 2.0 %copy-start.1 = (bf16[2,256,3584]{2,1,0:T(8,128)(2,1)S(1)}, bf16[2,256,3584]{2,1,0:T(8,128)(2,1)}, u32[]{:S(2)}) copy-start(bf16[2,256,3584]{2,1,0:T(8,128)(2,1)} %refs_2_.7) | copy-start | bytes 11010052
  117.6 1.6 %collective-permute-start.19 = (f32[4,4,8,512]{3,2,0,1:T(8,128)S(1)}, f32[4,4,8,512]{3,2,0,1:T(8,128)S(1)}, u32[]{:S(2)}, u32[]{:S(2)}) collective-permute-start(f32[4,4,8,512]{3,2,0,1:T(8,128)S(1)} %bitcast.28), channel_id=1, source_target_pairs={{0,1},{1,0},{2,3},{3,2},{4,5},{5,4},{6,7},{7,6},{8,9},{9,8},{10,11... | collective-permute-start | bytes 786440 | tf_op jit(solution)/shard_map/ppermute | solution.py:20
  119.3 5.8 %collective-permute-start.20 = (f32[4,8,512]{2,1,0:T(8,128)S(1)}, f32[4,8,512]{2,1,0:T(8,128)S(1)}, u32[]{:S(2)}, u32[]{:S(2)}) collective-permute-start(f32[4,8,512]{2,1,0:T(8,128)S(1)} %get-tuple-element.60), channel_id=1, source_target_pairs={{0,6},{1,7},{2,4},{3,5},{4,2},{5,3},{6,0},{7,1},{8,14},{9,15},{10,... | collective-permute-start | bytes 196616 | tf_op jit(solution)/shard_map/ppermute | solution.py:20
  120.0 5.3 %collective-permute-start.21 = (f32[4,8,512]{2,1,0:T(8,128)S(1)}, f32[4,8,512]{2,1,0:T(8,128)S(1)}, u32[]{:S(2)}, u32[]{:S(2)}) collective-permute-start(f32[4,8,512]{2,1,0:T(8,128)S(1)} %get-tuple-element.58), channel_id=1, source_target_pairs={{0,4},{1,5},{2,6},{3,7},{4,0},{5,1},{6,2},{7,3},{8,12},{9,13},{10,... | collective-permute-start | bytes 196616 | tf_op jit(solution)/shard_map/ppermute | solution.py:20
  121.3 4.3 %collective-permute-start.22 = (f32[4,8,512]{2,1,0:T(8,128)S(1)}, f32[4,8,512]{2,1,0:T(8,128)S(1)}, u32[]{:S(2)}, u32[]{:S(2)}) collective-permute-start(f32[4,8,512]{2,1,0:T(8,128)S(1)} %get-tuple-element.59), channel_id=1, source_target_pairs={{0,2},{1,3},{2,0},{3,1},{4,6},{5,7},{6,4},{7,5},{8,10},{9,11},{10,... | collective-permute-start | bytes 196616 | tf_op jit(solution)/shard_map/ppermute | solution.py:20
